TPU v7x, 256 devices: a whole 4x4x8 slice. The times are simulated.
256 devices in a mesh: tile: 64 (over y, z, core), mode: 4 (over x).
Axes of the slice: x: 4, y: 4, z: 8, core: 2. Of those that a mesh axis runs over, the one named last changes fastest.
Arguments:
- object_pieces: float32 [1536, 2, 64, 128], P('tile'), may hold values from -5 to 5
- probe_modes: float32 [12, 2, 256, 256], P('mode'), may hold values from -1.6 to 1.6
- intensity: float32 [128, 256, 256], P('tile'), may hold values from 0.05 to 5
- positions: int32 [128, 2], P('tile'), may hold values from 0 to 3840, as said below
- counts: int32 [64], P('tile'), may hold values from 0 to 2, as said below
Outputs:
- object_new: float32 [1536, 2, 64, 128], P('tile')
- probe_grad: float32 [12, 2, 256, 256], P('mode')
Inputs may be any that keep to these rules, and one draw needn't show every extreme that they name: `positions`: rows are multiples of 64 and columns multiples of 128; every live patch lies inside the object, and its top-left piece lies in its own device's tile (device d holds piece rows from (d // 8) * 6 and piece columns from (d mod 8) * 4, 6 x 4 of them); slots at or past their device's count hold zeros. counts[d] + counts[d + 32] = 2 for d < 32, and some device has 2.
All inputs are finite; a program needn't handle non-finite values.
Results may differ from a plain program's by a relative error of at most 0.0052.
Values sent between devices are 32-bit elements; how exact they have to be, the bound alone decides.
No kernel may reach another device: no remote copies, remote signals or barrier semaphores. Data moves between devices by JAX's collectives and lax.ppermute only.
A program may use at most 64 MiB of HBM per device.

v0:
```python
import math

import jax
import jax.numpy as jnp
from jax import lax
from jax.sharding import PartitionSpec as P

DEV_COLS = 8
TILE_R = 6
TILE_C = 4


far_floor = 0.1
object_floor = 0.1


def shifted(block, axis, distance):
    devices = range(lax.axis_size(axis))
    route = [(i - distance, i) for i in devices if i - distance in devices]
    return lax.ppermute(block, axis, route)


def fourier_tables(length):
    indices = jnp.arange(length, dtype=jnp.int32)
    phases = (indices[:, None] * indices[None, :] % length).astype(jnp.float32) * (
        2.0 * math.pi / length
    )
    scaling = 1.0 / math.sqrt(length)
    return (
        (jnp.cos(phases) * scaling).astype(jnp.bfloat16),
        (-jnp.sin(phases) * scaling).astype(jnp.bfloat16),
    )


def product_left(table_part, data_part):
    return jnp.einsum("ux,skxy->skuy", table_part, data_part, preferred_element_type=jnp.float32)


def product_right(data_part, table_part):
    return jnp.einsum("skuy,yv->skuv", data_part, table_part, preferred_element_type=jnp.float32)


def left_apply(tables, data_re, data_im, conj_sign):
    table_re, table_im = tables
    real_part = product_left(table_re, data_re) - conj_sign * product_left(table_im, data_im)
    imag_part = product_left(table_re, data_im) + conj_sign * product_left(table_im, data_re)
    return (real_part, imag_part)


def right_apply(tables, data_re, data_im, conj_sign):
    table_re, table_im = tables
    real_part = product_right(data_re, table_re) - conj_sign * product_right(data_im, table_im)
    imag_part = conj_sign * product_right(data_re, table_im) + product_right(data_im, table_re)
    return (real_part, imag_part)


def body(object_pieces, probe_modes, intensity, positions, counts):
    tile_index = lax.axis_index("tile")
    piece_rows = object_pieces.shape[2]
    piece_cols = object_pieces.shape[3]
    patch_side = probe_modes.shape[-1]
    slot_count = positions.shape[0]
    own_count = counts[0]
    anchor = jnp.zeros((), jnp.int32)
    tile_grid = object_pieces.reshape(TILE_R, TILE_C, 2, piece_rows, piece_cols)
    right_column = shifted(tile_grid[:, 0], "tile", -1)
    lower_rows = shifted(tile_grid[:3], "tile", -DEV_COLS)
    corner_rows = shifted(tile_grid[:3, 0], "tile", -DEV_COLS - 1)
    below_rows = jnp.concatenate([lower_rows, corner_rows[:, None]], axis=1)
    canvas = jnp.concatenate(
        [jnp.concatenate([tile_grid, right_column[:, None]], axis=1), below_rows], axis=0
    )
    dev_row = tile_index // DEV_COLS
    dev_col = tile_index % DEV_COLS
    patch_rows = jnp.clip(positions[:, 0] // piece_rows - dev_row * TILE_R, 0, TILE_R - 1)
    patch_cols = jnp.clip(positions[:, 1] // piece_cols - dev_col * TILE_C, 0, TILE_C - 1)

    def cut_patch(top_row, left_col):
        piece_block = lax.dynamic_slice(
            canvas, (top_row, left_col, anchor, anchor, anchor), (4, 2, 2, piece_rows, piece_cols)
        )
        return piece_block.transpose(2, 0, 3, 1, 4).reshape(2, patch_side, patch_side)

    patches = jax.vmap(cut_patch)(patch_rows, patch_cols)
    slot_live = jnp.arange(slot_count, dtype=jnp.int32) < own_count
    work_live = slot_live.astype(jnp.float32)
    work_slots = patches.shape[0]
    tables = fourier_tables(patch_side)
    probe_re = probe_modes[:, 0]
    probe_im = probe_modes[:, 1]
    patch_re = patches[:, 0:1]
    patch_im = patches[:, 1:2]
    exit_re = (probe_re * patch_re - probe_im * patch_im).astype(jnp.bfloat16)
    exit_im = (probe_re * patch_im + probe_im * patch_re).astype(jnp.bfloat16)
    half_re, half_im = left_apply(tables, exit_re, exit_im, 1.0)
    far_re, far_im = right_apply(
        tables, half_re.astype(jnp.bfloat16), half_im.astype(jnp.bfloat16), 1.0
    )
    model_local = jnp.sum(far_re * far_re + far_im * far_im, axis=1)
    light_local = jnp.sum(probe_re * probe_re + probe_im * probe_im, axis=0)
    model_power, light_sum = lax.psum((model_local, light_local), "mode")
    factor = work_live[:, None, None] * (
        jnp.sqrt(intensity) / jnp.sqrt(model_power + far_floor) - 1.0
    )
    change_re = (factor[:, None] * far_re).astype(jnp.bfloat16)
    change_im = (factor[:, None] * far_im).astype(jnp.bfloat16)
    back_re, back_im = left_apply(tables, change_re, change_im, -1.0)
    delta_re, delta_im = right_apply(
        tables, back_re.astype(jnp.bfloat16), back_im.astype(jnp.bfloat16), -1.0
    )
    grad_re = jnp.sum(probe_re * delta_re + probe_im * delta_im, axis=1)
    grad_im = jnp.sum(probe_re * delta_im - probe_im * delta_re, axis=1)
    term_re = jnp.sum(patch_re * delta_re + patch_im * delta_im, axis=0)
    term_im = jnp.sum(patch_re * delta_im - patch_im * delta_re, axis=0)
    probe_grad = lax.psum(jnp.stack([term_re, term_im], axis=1), "tile")
    grad_image = jnp.stack([grad_re, grad_im], axis=1)
    grad_blocks = grad_image.reshape(work_slots, 2, 4, piece_rows, 2, piece_cols).transpose(
        0, 2, 4, 1, 3, 5
    )
    light_blocks = light_sum.reshape(4, piece_rows, 2, piece_cols).transpose(0, 2, 1, 3)
    reduced = lax.psum(grad_blocks, "mode")
    light_live = slot_live.astype(jnp.float32)
    grad_canvas = jnp.zeros((TILE_R + 3, TILE_C + 1, 2, piece_rows, piece_cols), jnp.float32)
    weight_canvas = jnp.zeros((TILE_R + 3, TILE_C + 1, piece_rows, piece_cols), jnp.float32)

    def add_slot(index, running):
        grads_now, weights_now = running
        grad_at = (patch_rows[index], patch_cols[index], anchor, anchor, anchor)
        weight_at = (patch_rows[index], patch_cols[index], anchor, anchor)
        grad_piece = (
            lax.dynamic_slice(grads_now, grad_at, (4, 2, 2, piece_rows, piece_cols))
            + reduced[index]
        )
        weight_piece = (
            lax.dynamic_slice(weights_now, weight_at, (4, 2, piece_rows, piece_cols))
            + light_live[index] * light_blocks
        )
        return (
            lax.dynamic_update_slice(grads_now, grad_piece, grad_at),
            lax.dynamic_update_slice(weights_now, weight_piece, weight_at),
        )

    grad_canvas, weight_canvas = lax.fori_loop(
        0, slot_count, add_slot, (grad_canvas, weight_canvas)
    )
    from_above = shifted(
        (grad_canvas[TILE_R:, :TILE_C], weight_canvas[TILE_R:, :TILE_C]), "tile", DEV_COLS
    )
    from_corner = shifted(
        (grad_canvas[TILE_R:, TILE_C], weight_canvas[TILE_R:, TILE_C]), "tile", DEV_COLS + 1
    )
    grad_canvas = grad_canvas.at[:3, :TILE_C].add(from_above[0]).at[:3, 0].add(from_corner[0])
    weight_canvas = weight_canvas.at[:3, :TILE_C].add(from_above[1]).at[:3, 0].add(from_corner[1])
    from_left = shifted((grad_canvas[:TILE_R, TILE_C], weight_canvas[:TILE_R, TILE_C]), "tile", 1)
    grad_own = grad_canvas[:TILE_R, :TILE_C].at[:, 0].add(from_left[0])
    weight_own = weight_canvas[:TILE_R, :TILE_C].at[:, 0].add(from_left[1])
    new_share = tile_grid + grad_own / (weight_own[:, :, None] + object_floor)
    new_pieces = new_share.reshape(TILE_R * TILE_C, 2, piece_rows, piece_cols)
    return (new_pieces, probe_grad)


def solution(mesh):
    return jax.shard_map(
        body,
        mesh=mesh,
        in_specs=(
            P("tile", None, None, None),
            P("mode", None, None, None),
            P("tile", None, None),
            P("tile", None),
            P("tile"),
        ),
        out_specs=(P("tile", None, None, None), P("mode", None, None, None)),
        check_vma=False,
    )
```

profile of v0, /device:TPU:39, one launch (start us, length us, event | category | flops | bytes accessed | tf_op | source)
XLA Modules:
  0.0 463.8 jit_solution(4767293222380516442)
XLA Ops:
  7.2 2.2 slice.259
  9.4 1.3 collective-permute-start.1
  10.7 0.7 slice_bitcast_fusion.10
  11.4 1.3 collective-permute-start.2
  12.7 0.8 slice_bitcast_fusion.7
  13.5 2.7 collective-permute-start
  16.2 1.5 slice_bitcast_fusion.2
  17.9 42.7 %collective-permute-done.2 = f32[3,2,64,128]{3,2,1,0:T(8,128)} collective-permute-done((f32[3,2,64,128]{3,2,1,0:T(8,128)}, f32[3,2,64,128]{3,2,1,0:T(8,128)}, u32[]{:S(2)}, u32[]{:S(2)}) %collective-permute-start.2) | collective-permute-done | bytes 196640 | tf_op jit(solution)/shard_map/ppermute | solution.py:20
  60.6 3.1 maximum_maximum_fusion
  63.7 2.4 gather_fusion
  66.2 1.8 copy.39
  68.0 2.1 reshape.274
  70.2 1.5 fusion.5
  71.7 1.5 fusion.4
  73.2 1.5 fusion
  74.7 1.3 fusion.41
  76.0 1.3 fusion.55
  77.4 1.5 fusion.1
  78.8 1.5 convolution_subtract_fusion
  80.4 3.4 add_reduce_fusion.2
  84.6 1.5 add_reduce_fusion.3
  86.1 0.8 reshape.275
  86.9 46.4 %all-reduce.5.cloned.1.call-done = f32[2,256,256]{2,1,0:T(8,128)} async-done(((f32[2,256,256]{2,1,0:T(8,128)}), f32[2,256,256]{2,1,0:T(8,128)}) %all-reduce.5.cloned.1.call-update) | async-done | bytes 524304 | tf_op jit(solution)/shard_map/psum | solution.py:101
  133.3 1.4 add_multiply_fusion
  134.8 1.4 fusion.51
  136.2 1.4 fusion.47
  137.5 1.4 fusion.2
  138.9 1.3 fusion.36
  140.2 1.3 fusion.49
  141.6 1.4 fusion.3
  143.0 1.3 multiply_subtract_fusion
  144.3 4.0 add_reduce_fusion
  148.4 1.3 stack.19
  149.7 1.3 stack.18
  151.0 1.4 maximum_bitcast_fusion
  152.5 1.2 pad_maximum_fusion
  153.8 53.4 %all-reduce.9.cloned.1.call-done = (f32[2,4,2,2,64,128]{5,2,4,1,0,3:T(2,128)}, f32[4,2,64,128]{3,1,2,0:T(2,128)}) async-done(((f32[2,4,2,2,64,128]{5,2,4,1,0,3:T(2,128)}, f32[4,2,64,128]{3,1,2,0:T(2,128)}), (f32[2,4,2,2,64,128]{5,2,4,1,0,3:T(2,128)}, f32[4,2,64,128]{3,1,2,0:T(2,128)})) %all-reduce.9.cloned.1.call-update) | async-done | bytes 1310736 | tf_op jit(solution)/shard_map/psum | solution.py:121
  207.2 1.0 copy.57
  208.2 1.3 broadcast_in_dim.25
  209.8 17.3 %while.21 = (s32[]{:T(128)}, f32[9,5,2,64,128]{4,3,2,0,1:T(8,128)S(1)}, f32[9,5,64,128]{3,2,1,0:T(8,128)}, s32[2]{0:T(128)S(1)}, s32[2]{0:T(128)S(1)}, /*index=5...) while((s32[]{:T(128)}, ...), condition=%wide.region_8.9_spmd, body=%wide.region_7.8_spmd.sunk | while | flops 262152 | bytes 4457217 | solution.py:143
  209.9 0.6 dynamic_slice.56
  212.1 0.6 dynamic_slice.57
  214.4 0.6 dynamic_slice.58
  215.0 1.1 constant_dynamic-slice_fusion.5
  216.1 2.3 add_dynamic-update-slice_fusion.2
  218.5 0.6 dynamic_slice.56
  220.7 0.6 dynamic_slice.57
  223.0 0.6 dynamic_slice.58
  223.6 1.1 constant_dynamic-slice_fusion.5
  224.8 2.3 add_dynamic-update-slice_fusion.2
  227.1 1.6 copy.64
  228.8 6.5 %collective-permute-start.6 = (f32[3,4,64,128]{3,2,0,1:T(8,128)S(1)}, f32[3,4,64,128]{3,2,0,1:T(8,128)S(1)}, u32[]{:S(2)}, u32[]{:S(2)}) collective-permute-start(f32[3,4,64,128]{3,2,0,1:T(8,128)S(1)} %slice.295), channel_id=1, source_target_pairs={{0,32},{4,36},{8,40},{12,44},{16,48},{20,52},{24,56},{28,60},{32,6... | collective-permute-start | bytes 1179656 | tf_op jit(solution)/shard_map/ppermute | solution.py:20
  235.3 4.9 %collective-permute-start.7 = (f32[3,64,128]{2,1,0:T(8,128)S(1)}, f32[3,64,128]{2,1,0:T(8,128)S(1)}, u32[]{:S(2)}, u32[]{:S(2)}) collective-permute-start(f32[3,64,128]{2,1,0:T(8,128)S(1)} %slice_bitcast_fusion.12), channel_id=1, source_target_pairs={{0,36},{4,40},{8,44},{12,48},{16,52},{20,56},{24,60},{28,64},{32,6... | collective-permute-start | bytes 294920 | tf_op jit(solution)/shard_map/ppermute | solution.py:20
  240.3 4.7 %collective-permute-start.4 = (f32[3,2,64,128]{3,2,1,0:T(8,128)S(1)}, f32[3,2,64,128]{3,2,1,0:T(8,128)S(1)}, u32[]{:S(2)}, u32[]{:S(2)}) collective-permute-start(f32[3,2,64,128]{3,2,1,0:T(8,128)S(1)} %slice_bitcast_fusion.11), channel_id=1, source_target_pairs={{0,36},{4,40},{8,44},{12,48},{16,52},{20,56},{24,60},{28,64},{32,6... | collective-permute-start | bytes 589832 | tf_op jit(solution)/shard_map/ppermute | solution.py:20
  245.0 4.6 collective-permute-start.3
  249.6 5.2 %collective-permute-done.6 = f32[3,4,64,128]{3,2,0,1:T(8,128)S(1)} collective-permute-done((f32[3,4,64,128]{3,2,0,1:T(8,128)S(1)}, f32[3,4,64,128]{3,2,0,1:T(8,128)S(1)}, u32[]{:S(2)}, u32[]{:S(2)}) %collective-permute-start.6) | collective-permute-done | bytes 393248 | tf_op jit(solution)/shard_map/ppermute | solution.py:20
  254.8 3.8 collective-permute-done.7
  258.7 10.2 %collective-permute-start.8 = (f32[6,64,128]{2,1,0:T(8,128)S(1)}, f32[6,64,128]{2,1,0:T(8,128)S(1)}, u32[]{:S(2)}, u32[]{:S(2)}) collective-permute-start(f32[6,64,128]{2,1,0:T(8,128)S(1)} %slice_bitcast_fusion.8), channel_id=1, source_target_pairs={{0,4},{4,8},{8,12},{12,16},{16,20},{20,24},{24,28},{28,32},{32,36}... | collective-permute-start | bytes 589832 | tf_op jit(solution)/shard_map/ppermute | solution.py:20
  269.0 35.7 %collective-permute-done.3 = f32[3,4,2,64,128]{4,3,2,0,1:T(8,128)S(1)} collective-permute-done((f32[3,4,2,64,128]{4,3,2,0,1:T(8,128)S(1)}, f32[3,4,2,64,128]{4,3,2,0,1:T(8,128)S(1)}, u32[]{:S(2)}, u32[]{:S(2)}) %collective-permute-start.3) | collective-permute-done | bytes 786464 | tf_op jit(solution)/shard_map/ppermute | solution.py:20
  305.1 1.9 collective-permute-start.5
  307.5 4.6 collective-permute-done.5
  312.1 1.5 divide_add_fusion
  313.7 140.8 %all-reduce.7.cloned.1.call-done = f32[3,2,256,256]{3,2,1,0:T(8,128)} async-done(((f32[3,2,256,256]{3,2,1,0:T(8,128)}), f32[3,2,256,256]{3,2,1,0:T(8,128)}) %all-reduce.7.cloned.1.call-update) | async-done | bytes 1572880 | tf_op jit(solution)/shard_map/psum | solution.py:115
  454.5 2.7 copy.140
  (54 shorter events, 2.3 us)
Async XLA Ops:
  7.2 3.5 copy-start.6
  7.2 126.2 %all-reduce.5.cloned.1.call-start = ((), (), s32[]{:S(2)}) async-start(), calls=%async_computation | async-start | bytes 1048576 | tf_op jit(solution)/shard_map/psum | solution.py:101
  9.4 51.2 %collective-permute-start.1 = (f32[3,4,2,64,128]{4,3,2,1,0:T(8,128)}, f32[3,4,2,64,128]{4,3,2,1,0:T(8,128)}, u32[]{:S(2)}, u32[]{:S(2)}) collective-permute-start(f32[3,4,2,64,128]{4,3,2,1,0:T(8,128)} %bitcast.9), channel_id=1, source_target_pairs={{32,0},{36,4},{40,8},{44,12},{48,16},{52,20},{56,24},{60,28},{64,3... | collective-permute-start | bytes 2359304 | tf_op jit(solution)/shard_map/ppermute | solution.py:20
  11.4 49.2 %collective-permute-start.2 = (f32[3,2,64,128]{3,2,1,0:T(8,128)}, f32[3,2,64,128]{3,2,1,0:T(8,128)}, u32[]{:S(2)}, u32[]{:S(2)}) collective-permute-start(f32[3,2,64,128]{3,2,1,0:T(8,128)} %slice_bitcast_fusion.10), channel_id=1, source_target_pairs={{36,0},{40,4},{44,8},{48,12},{52,16},{56,20},{60,24},{64,28},{68,3... | collective-permute-start | bytes 589832 | tf_op jit(solution)/shard_map/ppermute | solution.py:20
  13.5 4.2 copy-start.8
  13.5 47.2 %collective-permute-start = (f32[6,2,64,128]{3,2,1,0:T(8,128)}, f32[6,2,64,128]{3,2,1,0:T(8,128)S(1)}, u32[]{:S(2)}, u32[]{:S(2)}) collective-permute-start(f32[6,2,64,128]{3,2,1,0:T(8,128)} %slice_bitcast_fusion.7), channel_id=1, source_target_pairs={{4,0},{8,4},{12,8},{16,12},{20,16},{24,20},{28,24},{32,28},{36,32}... | collective-permute-start | bytes 1179656 | tf_op jit(solution)/shard_map/ppermute | solution.py:20
  70.1 7.2 %copy-start.1 = (f32[2,256,256]{2,1,0:T(8,128)}, f32[2,256,256]{2,1,0:T(8,128)S(1)}, u32[]{:S(2)}) copy-start(f32[2,256,256]{2,1,0:T(8,128)S(1)} %get-tuple-element.255) | copy-start | bytes 1572868
  70.1 7.2 %copy-start.3 = (f32[2,256,256]{2,1,0:T(8,128)}, f32[2,256,256]{2,1,0:T(8,128)S(1)}, u32[]{:S(2)}) copy-start(f32[2,256,256]{2,1,0:T(8,128)S(1)} %get-tuple-element.256) | copy-start | bytes 1572868
  83.9 123.4 %all-reduce.9.cloned.1.call-start = ((), (), s32[]{:S(2)}) async-start(), calls=%async_computation.2 | async-start | bytes 2621440 | tf_op jit(solution)/shard_map/psum | solution.py:121
  134.7 1.4 copy-start.5
  142.9 1.4 copy-start.2
  142.9 1.4 copy-start.4
  152.4 302.1 %all-reduce.7.cloned.1.call-start = ((), (), s32[]{:S(2)}) async-start(), calls=%async_computation.1 | async-start | bytes 3145728 | tf_op jit(solution)/shard_map/psum | solution.py:115
  227.1 8.1 %copy-start = (f32[9,5,64,128]{3,2,1,0:T(8,128)S(1)}, f32[9,5,64,128]{3,2,1,0:T(8,128)}, u32[]{:S(2)}) copy-start(f32[9,5,64,128]{3,2,1,0:T(8,128)} %get-tuple-element.215) | copy-start | bytes 4423684
  228.8 26.0 %collective-permute-start.6 = (f32[3,4,64,128]{3,2,0,1:T(8,128)S(1)}, f32[3,4,64,128]{3,2,0,1:T(8,128)S(1)}, u32[]{:S(2)}, u32[]{:S(2)}) collective-permute-start(f32[3,4,64,128]{3,2,0,1:T(8,128)S(1)} %slice.295), channel_id=1, source_target_pairs={{0,32},{4,36},{8,40},{12,44},{16,48},{20,52},{24,56},{28,60},{32,6... | collective-permute-start | bytes 1179656 | tf_op jit(solution)/shard_map/ppermute | solution.py:20
  235.3 23.4 %collective-permute-start.7 = (f32[3,64,128]{2,1,0:T(8,128)S(1)}, f32[3,64,128]{2,1,0:T(8,128)S(1)}, u32[]{:S(2)}, u32[]{:S(2)}) collective-permute-start(f32[3,64,128]{2,1,0:T(8,128)S(1)} %slice_bitcast_fusion.12), channel_id=1, source_target_pairs={{0,36},{4,40},{8,44},{12,48},{16,52},{20,56},{24,60},{28,64},{32,6... | collective-permute-start | bytes 294920 | tf_op jit(solution)/shard_map/ppermute | solution.py:20
  240.3 64.8 %collective-permute-start.4 = (f32[3,2,64,128]{3,2,1,0:T(8,128)S(1)}, f32[3,2,64,128]{3,2,1,0:T(8,128)S(1)}, u32[]{:S(2)}, u32[]{:S(2)}) collective-permute-start(f32[3,2,64,128]{3,2,1,0:T(8,128)S(1)} %slice_bitcast_fusion.11), channel_id=1, source_target_pairs={{0,36},{4,40},{8,44},{12,48},{16,52},{20,56},{24,60},{28,64},{32,6... | collective-permute-start | bytes 589832 | tf_op jit(solution)/shard_map/ppermute | solution.py:20
  245.0 59.7 %collective-permute-start.3 = (f32[3,4,2,64,128]{4,3,2,0,1:T(8,128)S(1)}, f32[3,4,2,64,128]{4,3,2,0,1:T(8,128)S(1)}, u32[]{:S(2)}, u32[]{:S(2)}) collective-permute-start(f32[3,4,2,64,128]{4,3,2,0,1:T(8,128)S(1)} %slice.266), channel_id=1, source_target_pairs={{0,32},{4,36},{8,40},{12,44},{16,48},{20,52},{24,56},{28,60},{32,6... | collective-permute-start | bytes 2359304 | tf_op jit(solution)/shard_map/ppermute | solution.py:20
  258.7 48.3 %collective-permute-start.8 = (f32[6,64,128]{2,1,0:T(8,128)S(1)}, f32[6,64,128]{2,1,0:T(8,128)S(1)}, u32[]{:S(2)}, u32[]{:S(2)}) collective-permute-start(f32[6,64,128]{2,1,0:T(8,128)S(1)} %slice_bitcast_fusion.8), channel_id=1, source_target_pairs={{0,4},{4,8},{8,12},{12,16},{16,20},{20,24},{24,28},{28,32},{32,36}... | collective-permute-start | bytes 589832 | tf_op jit(solution)/shard_map/ppermute | solution.py:20
  305.1 7.0 %collective-permute-start.5 = (f32[6,2,64,128]{3,2,1,0:T(8,128)S(1)}, f32[6,2,64,128]{3,2,1,0:T(8,128)S(1)}, u32[]{:S(2)}, u32[]{:S(2)}) collective-permute-start(f32[6,2,64,128]{3,2,1,0:T(8,128)S(1)} %slice_bitcast_fusion.5), channel_id=1, source_target_pairs={{0,4},{4,8},{8,12},{12,16},{16,20},{20,24},{24,28},{28,32},{32,36}... | collective-permute-start | bytes 1179656 | tf_op jit(solution)/shard_map/ppermute | solution.py:20
  307.3 4.8 %copy-start.7 = (f32[24,2,64,128]{3,2,1,0:T(8,128)S(1)}, f32[24,2,64,128]{3,2,1,0:T(8,128)}, u32[]{:S(2)}) copy-start(f32[24,2,64,128]{3,2,1,0:T(8,128)} %param.19) | copy-start | bytes 4718596
Sparse Core Ops, SparseCore 0:
  84.0 49.2 all-reduce.4
  152.6 54.6 all-reduce.8
  211.2 243.2 all-reduce.6
where the time goes:
time: 467 us; the launch traced here: 464 us
  waiting for transfers between devices  333 us (71%)
  starting transfers between devices  38.1 us (8%)
  local copies, waits for them, and re-layouts  28.3 us (6%)
  matrix products  27.1 us (6%)
  other arithmetic  15.7 us (3%)
  between operations  14.9 us (3%)
  loops' own time  6.81 us (1%)
    psum x1, waiting for transfers between devices, body(): probe_grad = lax.psum(jnp.stack([term_re, term_im], axis=1), 'tile')  141 us
    ppermute x9, waiting for transfers between devices, shifted(): return lax.ppermute(block, axis, route)  92.1 us
    psum x1, waiting for transfers between devices, body(): reduced = lax.psum(grad_blocks, 'mode')  53.4 us
    psum x1, waiting for transfers between devices, body(): model_power, light_sum = lax.psum((model_local, light_local), 'mode')  46.4 us
    ppermute x9, starting transfers between devices, shifted(): return lax.ppermute(block, axis, route)  38 us
    dot_general x8, matrix products, product_right(): jnp.einsum('skuy,yv->skuv', data_part, table_part, preferred_element_type...  15.7 us
    dot_general x8, matrix products, product_left(): jnp.einsum('ux,skxy->skuy', table_part, data_part, preferred_element_type...  11.4 us
  transfers between devices with their start and end apart: 12, of which 8 were waited for; matrix products, arithmetic and copies ran while one was open for 5% of the time, Pallas kernels for 0%

commit v1 on v0

v1 whole, which is shorter than its diff:
```python
import math

import jax
import jax.numpy as jnp
import numpy as np
from jax import lax
from jax.experimental import pallas as pl
from jax.experimental.pallas import tpu as pltpu
from jax.sharding import PartitionSpec as P

DEV_COLS = 8
TILE_R = 6
TILE_C = 4
SIDE = 256
PIECE_R = 64
PIECE_C = 128
N_MODE = 4
N_TILE = 64
SUB = PIECE_R // N_MODE

far_floor = 0.1
object_floor = 0.1

F32 = jnp.float32
BF16 = jnp.bfloat16
ANY = pl.BlockSpec(memory_space=pl.ANY)
SMEM = pl.BlockSpec(memory_space=pltpu.SMEM)
VMEM = pl.BlockSpec(memory_space=pltpu.VMEM)


def shifted(block, axis, distance):
    devices = range(lax.axis_size(axis))
    route = [(i - distance, i) for i in devices if i - distance in devices]
    return lax.ppermute(block, axis, route)


def turned(block, distance):
    return lax.ppermute(block, "mode", [(i, (i + distance) % N_MODE) for i in range(N_MODE)])


def core_swap(block):
    return lax.ppermute(block, "tile", [(d, d ^ 1) for d in range(N_TILE)])


def fourier_blocks():
    indices = np.arange(SIDE)
    phases = (indices[:, None] * indices[None, :] % SIDE) * (2.0 * math.pi / SIDE)
    scaling = 1.0 / math.sqrt(SIDE)
    re = (np.cos(phases) * scaling).astype(np.float32)
    im = (-np.sin(phases) * scaling).astype(np.float32)
    left = np.block([[re, -im], [im, re]])
    right = np.block([[re, im], [-im, re]])
    return jnp.asarray(left.astype(jnp.bfloat16)), jnp.asarray(right.astype(jnp.bfloat16))


def canvas_index(row, col):
    inside = jnp.where(col < TILE_C, row * TILE_C + col, 24 + row)
    below = jnp.where(col < TILE_C, 30 + (row - TILE_R) * TILE_C + col, 42 + row - TILE_R)
    return jnp.where(row < TILE_R, inside, below)


def forward_kernel(info, own, right, low, corner, probe, left_table, right_table,
                   far, patch, p0, p1, p2, p3, power, sems):
    slot = pl.program_id(0)
    mode = pl.program_id(1)

    def piece_copy(s, q, source, index):
        target = patch.at[s, :, pl.ds(PIECE_R * (q // 2), PIECE_R), pl.ds(PIECE_C * (q % 2), PIECE_C)]
        return pltpu.make_async_copy(source.at[index], target, sems.at[s, q])

    @pl.when((slot == 0) & (mode == 0))
    def _():
        for s in range(2):
            for q in range(8):
                row = info[2 * s] + q // 2
                col = info[2 * s + 1] + q % 2
                upper = row < TILE_R
                inner = col < TILE_C

                @pl.when(upper & inner)
                def _():
                    piece_copy(s, q, own, row * TILE_C + col).start()

                @pl.when(upper & jnp.logical_not(inner))
                def _():
                    piece_copy(s, q, right, row).start()

                @pl.when(jnp.logical_not(upper) & inner)
                def _():
                    piece_copy(s, q, low, (row - TILE_R) * TILE_C + col).start()

                @pl.when(jnp.logical_not(upper) & jnp.logical_not(inner))
                def _():
                    piece_copy(s, q, corner, row - TILE_R).start()

    for s in range(2):

        @pl.when((slot == s) & (mode == 0))
        def _():
            for q in range(8):
                piece_copy(s, q, own, 0).wait()

    probe_re, probe_im = probe[0, 0], probe[0, 1]
    patch_re, patch_im = patch[slot, 0], patch[slot, 1]
    exit_re = (probe_re * patch_re - probe_im * patch_im).astype(BF16)
    exit_im = (probe_re * patch_im + probe_im * patch_re).astype(BF16)
    half = jnp.dot(left_table[...], jnp.concatenate([exit_re, exit_im], axis=0),
                   preferred_element_type=F32).astype(BF16)
    half = jnp.concatenate([half[:SIDE], half[SIDE:]], axis=1)
    both = jnp.dot(half, right_table[...], preferred_element_type=F32)
    far_re, far_im = both[:, :SIDE], both[:, SIDE:]
    far[0, 0, 0] = far_re
    far[0, 0, 1] = far_im
    local = far_re * far_re + far_im * far_im

    @pl.when(mode == 0)
    def _():
        power[...] = local

    @pl.when(mode > 0)
    def _():
        power[...] += local

    @pl.when(mode == 2)
    def _():
        me = info[5]
        for j, out in enumerate((p0, p1, p2, p3)):
            start = pl.multiple_of(lax.rem(me + j, N_MODE) * 64, 64)
            out[slot] = power[pl.ds(start, 64), :]


def forward(info, own, right, low, corner, probe, tables):
    full = lambda *shape: pl.BlockSpec(shape, lambda s, k: (0,) * len(shape))
    return pl.pallas_call(
        forward_kernel,
        grid=(2, 3),
        in_specs=[SMEM, ANY, ANY, ANY, ANY,
                  pl.BlockSpec((1, 2, SIDE, SIDE), lambda s, k: (k, 0, 0, 0)),
                  full(512, 512), full(512, 512)],
        out_specs=[pl.BlockSpec((1, 1, 2, SIDE, SIDE), lambda s, k: (s, k, 0, 0, 0)),
                   full(2, 2, SIDE, SIDE)] + [full(2, 64, SIDE)] * 4,
        out_shape=[jax.ShapeDtypeStruct((2, 3, 2, SIDE, SIDE), F32),
                   jax.ShapeDtypeStruct((2, 2, SIDE, SIDE), F32)]
        + [jax.ShapeDtypeStruct((2, 64, SIDE), F32)] * 4,
        scratch_shapes=[pltpu.VMEM((SIDE, SIDE), F32), pltpu.SemaphoreType.DMA((2, 8))],
        compiler_params=pltpu.CompilerParams(vmem_limit_bytes=32 * 1024 * 1024),
        cost_estimate=pl.CostEstimate(flops=1700000000, bytes_accessed=12000000, transcendentals=0),
        name="forward",
    )(info, own, right, low, corner, probe, *tables)


def backward_kernel(info, far, probe, patch, f0, f1, f2, f3, left_table, right_table,
                    mine, theirs, g0, g1, g2, g3, factor, grad):
    mode = pl.program_id(0)
    slot = pl.program_id(1)
    me = info[5]
    core = info[6]

    @pl.when((slot == 0) & (mode == 0))
    def _():
        for j, part in enumerate((f0, f1, f2, f3)):
            start = pl.multiple_of(lax.rem(me + N_MODE - j, N_MODE) * 64, 64)
            factor[:, pl.ds(start, 64), :] = part[...]

    scale = factor[slot]
    change_re = (scale * far[0, 0, 0]).astype(BF16)
    change_im = (scale * far[0, 0, 1]).astype(BF16)
    back = jnp.dot(right_table[...], jnp.concatenate([change_re, change_im], axis=0),
                   preferred_element_type=F32).astype(BF16)
    back = jnp.concatenate([back[:SIDE], back[SIDE:]], axis=1)
    both = jnp.dot(back, left_table[...], preferred_element_type=F32)
    delta_re, delta_im = both[:, :SIDE], both[:, SIDE:]
    patch_re, patch_im = patch[slot, 0], patch[slot, 1]
    term_re = patch_re * delta_re + patch_im * delta_im
    term_im = patch_re * delta_im - patch_im * delta_re
    first = core == 0
    own_term = jnp.where(first, term_re, term_im)
    other_term = jnp.where(first, term_im, term_re)

    @pl.when(slot == 0)
    def _():
        mine[0] = own_term
        theirs[0] = other_term

    @pl.when(slot == 1)
    def _():
        mine[0] += own_term
        theirs[0] += other_term

    probe_re, probe_im = probe[0, 0], probe[0, 1]
    grad_re = probe_re * delta_re + probe_im * delta_im
    grad_im = probe_re * delta_im - probe_im * delta_re

    @pl.when(mode == 0)
    def _():
        grad[slot, 0] = grad_re
        grad[slot, 1] = grad_im

    @pl.when(mode > 0)
    def _():
        grad[slot, 0] += grad_re
        grad[slot, 1] += grad_im

    @pl.when(mode == 2)
    def _():
        for j, out in enumerate((g0, g1, g2, g3)):
            base = lax.rem(me + j, N_MODE) * SUB
            for q in range(8):
                start = pl.multiple_of(base + PIECE_R * (q // 2), SUB)
                for channel in range(2):
                    out[slot, q, channel] = grad[
                        slot, channel, pl.ds(start, SUB),
                        PIECE_C * (q % 2):PIECE_C * (q % 2 + 1)]


def backward(info, far, probe, patch, factors, tables):
    full = lambda *shape: pl.BlockSpec(shape, lambda k, s: (0,) * len(shape))
    return pl.pallas_call(
        backward_kernel,
        grid=(3, 2),
        in_specs=[SMEM,
                  pl.BlockSpec((1, 1, 2, SIDE, SIDE), lambda k, s: (s, k, 0, 0, 0)),
                  pl.BlockSpec((1, 2, SIDE, SIDE), lambda k, s: (k, 0, 0, 0)),
                  full(2, 2, SIDE, SIDE)] + [full(2, 64, SIDE)] * 4
        + [full(512, 512), full(512, 512)],
        out_specs=[pl.BlockSpec((1, SIDE, SIDE), lambda k, s: (k, 0, 0))] * 2
        + [full(2, 8, 2, SUB, PIECE_C)] * 4,
        out_shape=[jax.ShapeDtypeStruct((3, SIDE, SIDE), F32)] * 2
        + [jax.ShapeDtypeStruct((2, 8, 2, SUB, PIECE_C), F32)] * 4,
        scratch_shapes=[pltpu.VMEM((2, SIDE, SIDE), F32), pltpu.VMEM((2, 2, SIDE, SIDE), F32)],
        compiler_params=pltpu.CompilerParams(vmem_limit_bytes=32 * 1024 * 1024),
        cost_estimate=pl.CostEstimate(flops=1700000000, bytes_accessed=12000000, transcendentals=0),
        name="backward",
    )(info, far, probe, patch, *factors, *tables)


def scatter_kernel(info, g0, g1, g2, g3, own, right, low, corner, canvas):
    canvas[...] = jnp.zeros_like(canvas)
    for s in range(2):
        for q in range(8):
            index = canvas_index(info[2 * s] + q // 2, info[2 * s + 1] + q % 2)
            canvas[index] += (g0[s, q] + g1[s, q]) + (g2[s, q] + g3[s, q])
    own[...] = canvas[:24]
    right[...] = canvas[24:30]
    low[...] = canvas[30:42]
    corner[...] = canvas[42:45]


def scatter(info, parts):
    pieces = lambda n: jax.ShapeDtypeStruct((n, 2, SUB, PIECE_C), F32)
    return pl.pallas_call(
        scatter_kernel,
        in_specs=[SMEM] + [VMEM] * 4,
        out_specs=[VMEM] * 4,
        out_shape=[pieces(24), pieces(6), pieces(12), pieces(3)],
        scratch_shapes=[pltpu.VMEM((45, 2, SUB, PIECE_C), F32)],
        cost_estimate=pl.CostEstimate(flops=1000000, bytes_accessed=2000000, transcendentals=0),
        name="scatter",
    )(info, *parts)


def weight_kernel(info, from_left, from_above, from_corner, light, weight):
    weight[...] = jnp.zeros_like(weight)
    sources = ((info, 0, 0), (from_left, 0, TILE_C), (from_above, TILE_R, 0),
               (from_corner, TILE_R, TILE_C))
    for source, down, across in sources:
        for s in range(2):
            top = source[2 * s] - down
            left = source[2 * s + 1] - across
            live = s < source[4]
            for q in range(8):
                row = top + q // 2
                col = left + q % 2
                inside = (row >= 0) & (row < TILE_R) & (col >= 0) & (col < TILE_C)

                @pl.when(live & inside)
                def _():
                    weight[row * TILE_C + col] += light[
                        q // 2, :, PIECE_C * (q % 2):PIECE_C * (q % 2 + 1)]


def weights(info, neighbours, light):
    return pl.pallas_call(
        weight_kernel,
        in_specs=[SMEM] * 4 + [VMEM],
        out_specs=VMEM,
        out_shape=jax.ShapeDtypeStruct((TILE_R * TILE_C, SUB, PIECE_C), F32),
        cost_estimate=pl.CostEstimate(flops=1000000, bytes_accessed=500000, transcendentals=0),
        name="weights",
    )(info, *neighbours, light)


def update_kernel(info, pieces, own, right, low, corner, weight, new, old, sem):
    start = pl.multiple_of(info[5] * SUB, SUB)
    fetch = pltpu.make_async_copy(pieces.at[:, :, pl.ds(start, SUB), :], old, sem)
    fetch.start()
    fetch.wait()
    for p in range(TILE_R * TILE_C):
        row, col = p // TILE_C, p % TILE_C
        total = own[p]
        if row < 3:
            total = total + low[p]
        if col == 0:
            total = total + right[row]
        if row < 3 and col == 0:
            total = total + corner[row]
        new[p] = old[p] + total / (weight[p] + object_floor)[None]


def update(info, pieces, own, right, low, corner, weight):
    shape = (TILE_R * TILE_C, 2, SUB, PIECE_C)
    return pl.pallas_call(
        update_kernel,
        in_specs=[SMEM, ANY] + [VMEM] * 5,
        out_specs=VMEM,
        out_shape=jax.ShapeDtypeStruct(shape, F32),
        scratch_shapes=[pltpu.VMEM(shape, F32), pltpu.SemaphoreType.DMA],
        cost_estimate=pl.CostEstimate(flops=1000000, bytes_accessed=2000000, transcendentals=0),
        name="update",
    )(info, pieces, own, right, low, corner, weight)


def join_pieces_kernel(info, n0, n1, n2, n3, out, sems):
    copies = []
    for j, part in enumerate((n0, n1, n2, n3)):
        start = pl.multiple_of(lax.rem(info[5] + N_MODE - j, N_MODE) * SUB, SUB)
        copies.append(pltpu.make_async_copy(part, out.at[:, :, pl.ds(start, SUB), :], sems.at[j]))
    for copy in copies:
        copy.start()
    for copy in copies:
        copy.wait()


def join_pieces(info, parts):
    return pl.pallas_call(
        join_pieces_kernel,
        in_specs=[SMEM] + [ANY] * 4,
        out_specs=ANY,
        out_shape=jax.ShapeDtypeStruct((TILE_R * TILE_C, 2, PIECE_R, PIECE_C), F32),
        scratch_shapes=[pltpu.SemaphoreType.DMA((4,))],
        cost_estimate=pl.CostEstimate(flops=0, bytes_accessed=3000000, transcendentals=0),
        name="join_pieces",
    )(info, *parts)


def join_channels_kernel(info, mine, theirs, out, sems):
    core = info[6]
    copies = [pltpu.make_async_copy(mine, out.at[:, core], sems.at[0]),
              pltpu.make_async_copy(theirs, out.at[:, 1 - core], sems.at[1])]
    for copy in copies:
        copy.start()
    for copy in copies:
        copy.wait()


def join_channels(info, mine, theirs):
    return pl.pallas_call(
        join_channels_kernel,
        in_specs=[SMEM, ANY, ANY],
        out_specs=ANY,
        out_shape=jax.ShapeDtypeStruct((3, 2, SIDE, SIDE), F32),
        scratch_shapes=[pltpu.SemaphoreType.DMA((2,))],
        cost_estimate=pl.CostEstimate(flops=0, bytes_accessed=3000000, transcendentals=0),
        name="join_channels",
    )(info, mine, theirs)


def body(object_pieces, probe_modes, intensity, positions, counts):
    tile_index = lax.axis_index("tile")
    mode_index = lax.axis_index("mode")
    tables = fourier_blocks()
    tile_grid = object_pieces.reshape(TILE_R, TILE_C, 2, PIECE_R, PIECE_C)
    low = shifted(object_pieces[:12], "tile", -DEV_COLS)
    right = shifted(tile_grid[:, 0], "tile", -1)
    corner = shifted(tile_grid[:3, 0], "tile", -DEV_COLS - 1)

    dev_row = tile_index // DEV_COLS
    dev_col = tile_index % DEV_COLS
    rows = jnp.clip(positions[:, 0] // PIECE_R - dev_row * TILE_R, 0, TILE_R - 1)
    cols = jnp.clip(positions[:, 1] // PIECE_C - dev_col * TILE_C, 0, TILE_C - 1)
    info = jnp.stack([rows[0], cols[0], rows[1], cols[1], counts[0], mode_index, tile_index % 2,
                      tile_index]).astype(jnp.int32)
    neighbours = [shifted(info, "tile", d) for d in (1, DEV_COLS, DEV_COLS + 1)]

    light_local = jnp.sum(probe_modes * probe_modes, axis=(0, 1))
    light_parts = light_local.reshape(4, N_MODE, SUB, SIDE).transpose(1, 0, 2, 3)
    light = lax.psum_scatter(light_parts, "mode", scatter_dimension=0, tiled=True)[0]
    weight = weights(info, neighbours, light)

    far, patch, *powers = forward(info, object_pieces, right, low, corner, probe_modes, tables)
    received = [turned(powers[j], j) for j in (1, 2, 3)]
    power = (powers[0] + received[0]) + (received[1] + received[2])
    own_intensity = lax.dynamic_slice_in_dim(intensity, mode_index * 64, 64, axis=1)
    live = (jnp.arange(2, dtype=jnp.int32) < counts[0]).astype(F32)
    factor = live[:, None, None] * (jnp.sqrt(own_intensity) / jnp.sqrt(power + far_floor) - 1.0)
    factors = [factor] + [turned(factor, j) for j in (1, 2, 3)]

    mine, theirs, *grads = backward(info, far, probe_modes, patch, factors, tables)

    summed = mine + core_swap(theirs)
    groups = [[y * 16 + z * 2 + c for y in range(4) for z in range(8)] for c in range(2)]
    pieces = lax.all_to_all(summed.reshape(32, 24, SIDE), "tile", 0, 0, axis_index_groups=groups, tiled=True)
    share = jnp.sum(pieces, axis=0)
    gathered = lax.all_to_all(jnp.broadcast_to(share[None], (32, 24, SIDE)), "tile", 0, 0,
                              axis_index_groups=groups, tiled=True).reshape(3, SIDE, SIDE)
    probe_grad = join_channels(info, gathered, core_swap(gathered))

    parts = [grads[0]] + [turned(grads[j], j) for j in (1, 2, 3)]
    own, to_right, to_low, to_corner = scatter(info, parts)
    from_above = shifted(to_low, "tile", DEV_COLS)
    from_left = shifted(to_right, "tile", 1)
    from_corner = shifted(to_corner, "tile", DEV_COLS + 1)
    new = update(info, object_pieces, own, from_left, from_above, from_corner, weight)
    new_parts = [new] + [turned(new, j) for j in (1, 2, 3)]
    return (join_pieces(info, new_parts), probe_grad)


def solution(mesh):
    return jax.shard_map(
        body,
        mesh=mesh,
        in_specs=(
            P("tile", None, None, None),
            P("mode", None, None, None),
            P("tile", None, None),
            P("tile", None),
            P("tile"),
        ),
        out_specs=(P("tile", None, None, None), P("mode", None, None, None)),
        check_vma=False,
    )
```

time: 467 us -> 351 us (0.75)
  waiting for transfers between devices: 333 us -> 95.6 us
  Pallas kernels: 0 us -> 119 us
  blocking collectives: 0 us -> 34.9 us
  matrix products: 27.1 us -> 0 us
  starting transfers between devices: 38.1 us -> 54 us
  other arithmetic: 15.7 us -> 1.34 us
  loops' own time: 6.81 us -> 0 us
  local copies, waits for them, and re-layouts: 28.3 us -> 23.5 us
    psum x3 -> x0, waiting for transfers between devices: 241 us -> none  [the longest x1 141 us: body(): probe_grad = lax.psum(jnp.stack([term_re, term_im], axis=1), 'tile')]
    pallas_call x0 -> x7, Pallas kernels: none -> 119 us  [the longest x1 49.4 us: join_pieces(): pl.pallas_call(join_pieces_kernel, in_specs=[SMEM] + [ANY] * 4, out_specs...]
    ppermute x9, waiting for transfers between devices: 92.1 us -> 44.8 us  [shifted(): return lax.ppermute(block, axis, route)]
    ppermute x0 -> x14, waiting for transfers between devices: none -> 35.2 us  [the longest x12 33.3 us: turned(): lax.ppermute(block, 'mode', [(i, (i + distance) % N_MODE) for i in range(...]
    all_to_all x0 -> x1, blocking collectives: none -> 34.9 us  [body(): lax.all_to_all(summed.reshape(32, 24, SIDE), 'tile', 0, 0, axis_index_gro...]
    dot_general x16 -> x0, matrix products: 27.1 us -> none  [the longest x8 15.7 us: product_right(): jnp.einsum('skuy,yv->skuv', data_part, table_part, preferred_element_type...]
    all_to_all x0 -> x1, waiting for transfers between devices: none -> 15.6 us  [body(): lax.all_to_all(jnp.broadcast_to(share[None], (32, 24, SIDE)), 'tile', 0,...]
    ppermute x0 -> x14, starting transfers between devices: none -> 15.3 us  [the longest x12 11.1 us: turned(): lax.ppermute(block, 'mode', [(i, (i + distance) % N_MODE) for i in range(...]
  transfers between devices with their start and end apart: 12 -> 25, of which waited for: 8 -> 15; matrix products, arithmetic and copies ran while one was open for 5% -> 2% of each run, Pallas kernels for 0% -> 17%
where the time goes in v1:
time: 351 us; the launch traced here: 344 us
  Pallas kernels  119 us (34%)
  waiting for transfers between devices  95.6 us (27%)
  starting transfers between devices  54 us (15%)
  blocking collectives  34.9 us (10%)
  local copies, waits for them, and re-layouts  23.5 us (7%)
  between operations  15.1 us (4%)
    pallas_call x1, Pallas kernels, join_pieces(): pl.pallas_call(join_pieces_kernel, in_specs=[SMEM] + [ANY] * 4, out_specs...  49.4 us
    pallas_call x1, Pallas kernels, join_channels(): pl.pallas_call(join_channels_kernel, in_specs=[SMEM, ANY, ANY], out_specs...  49.4 us
    ppermute x9, waiting for transfers between devices, shifted(): return lax.ppermute(block, axis, route)  44.8 us
    all_to_all x1, blocking collectives, body(): lax.all_to_all(summed.reshape(32, 24, SIDE), 'tile', 0, 0, axis_index_gro...  34.9 us
    ppermute x12, waiting for transfers between devices, turned(): lax.ppermute(block, 'mode', [(i, (i + distance) % N_MODE) for i in range(...  33.3 us
    ppermute x9, starting transfers between devices, shifted(): return lax.ppermute(block, axis, route)  32.8 us
    all_to_all x1, waiting for transfers between devices, body(): lax.all_to_all(jnp.broadcast_to(share[None], (32, 24, SIDE)), 'tile', 0,...  15.6 us
    unnamed x62, local copies, waits for them, and re-layouts  12.7 us
  transfers between devices with their start and end apart: 25, of which 15 were waited for; matrix products, arithmetic and copies ran while one was open for 2% of the time, Pallas kernels for 17%

profile of v1, /device:TPU:39, one launch (start us, length us, event | category | flops | bytes accessed | tf_op | source)
XLA Modules:
  0.0 343.6 jit_solution(4209482466388134565)
XLA Ops:
  7.2 1.9 slice_bitcast_fusion
  9.1 2.6 collective-permute-start
  11.7 2.1 slice.34
  13.8 1.3 collective-permute-start.1
  15.1 0.9 slice_bitcast_fusion.1
  16.0 1.3 collective-permute-start.2
  18.2 0.7 fusion
  18.9 0.7 fusion.1
  19.5 2.7 stack.15.info
  22.2 42.7 %collective-permute-done.2.corner = f32[3,2,64,128]{3,2,1,0:T(8,128)S(1)} collective-permute-done((f32[3,2,64,128]{3,2,1,0:T(8,128)S(1)}, f32[3,2,64,128]{3,2,1,0:T(8,128)S(1)}, u32[]{:S(2)}, u32[]{:S(2)}) %collective-permute-start.2) | collective-permute-done | bytes 196640 | tf_op jit(solution)/shard_map/ppermute | solution.py:34
  64.9 0.9 copy-done.10
  65.8 1.4 copy-done.1
  67.2 1.0 copy-done.5
  68.2 1.1 copy-done.11
  69.4 6.6 %forward.1 = (f32[2,3,2,256,256]{4,3,2,1,0:T(8,128)S(1)}, f32[2,2,256,256]{3,2,1,0:T(8,128)S(1)}, f32[2,64,256]{2,1,0:T(8,128)S(1)}, f32[2,64,256]{2,1,0:T(8,128...) custom-call(s32[8]{0:T(128)S(1)} %stack.15.info, f32[24,2,64,128]{3,2,1,0:T(8,128)S(1)} %copy-done.1, ...), custom_call_target="tpu_custom_call" | custom-call | flops 1700000000 | bytes 12000000 | tf_op jit(solution)/shard_map/forward/pallas_call | solution.py:134
  76.0 1.6 copy-done.2
  77.8 2.1 collective-permute-start.4
  79.9 2.8 collective-permute-done.3
  82.7 1.7 collective-permute-done.4
  84.4 1.8 collective-permute-done.5
  86.2 1.0 add_multiply_fusion.f0
  87.3 0.4 collective-permute-start.6
  87.6 1.7 collective-permute-start.7
  89.5 3.0 collective-permute-done.6.f1
  92.5 1.8 collective-permute-done.7.f2
  94.3 3.1 collective-permute-done.8.f3
  97.4 1.9 copy-done.3
  99.3 1.0 copy-done.6
  100.4 6.4 %backward.1 = (f32[3,256,256]{2,1,0:T(8,128)S(1)}, f32[3,256,256]{2,1,0:T(8,128)S(1)}, f32[2,8,2,16,128]{4,3,2,1,0:T(8,128)S(1)}, f32[2,8,2,16,128]{4,3,2,1,0:T(...) custom-call(s32[8]{0:T(128)S(1)} %stack.15.info, f32[2,3,2,256,256]{4,3,2,1,0:T(8,128)S(1)} %copy-done.3, ...), custom_call_target="tpu_custom_call" | custom-call | flops 1700000000 | bytes 12000000 | tf_op jit(solution)/shard_map/backward/pallas_call | solution.py:218
  106.8 0.5 collective-permute-start.21
  107.3 1.9 collective-permute-done.21
  109.4 34.9 %all_to_all.10 = f32[32,24,256]{2,1,0:T(8,128)S(1)} all-to-all(f32[32,24,256]{2,1,0:T(8,128)S(1)} %bitcast.23), channel_id=1, replica_groups={{0,8,16,24,32,40,48,56,64,72,80,88,96,104,112,120,128,136,144,152,160,1..., dimensions={0} | all-to-all | bytes 1572864 | tf_op jit(solution)/shard_map/all_to_all | solution.py:402
  144.3 0.9 broadcast_in_dim.2
  145.2 5.9 %all-to-all-start.1 = ((f32[32,24,256]{2,1,0:T(8,128)}), f32[32,24,256]{2,1,0:T(8,128)S(1)}, u32[]{:S(2)}, u32[]{:S(2)}) async-start(f32[32,24,256]{2,1,0:T(8,128)} %broadcast_in_dim.2), calls=%async_computation.2 | async-start | bytes 1572864 | tf_op jit(solution)/shard_map/all_to_all | solution.py:404
  151.4 0.7 copy.15
  152.1 1.5 collective-permute-start.10
  153.6 2.7 collective-permute-start.9
  156.3 15.6 %all-to-all-done.1 = f32[32,24,256]{2,1,0:T(8,128)S(1)} async-done(((f32[32,24,256]{2,1,0:T(8,128)}), f32[32,24,256]{2,1,0:T(8,128)S(1)}, u32[]{:S(2)}, u32[]{:S(2)}) %all-to-all-start.1) | async-done | bytes 786464 | tf_op jit(solution)/shard_map/all_to_all | solution.py:404
  171.9 3.7 %collective-permute-start.22 = (f32[3,256,256]{2,1,0:T(8,128)S(1)}, f32[3,256,256]{2,1,0:T(8,128)S(1)}, u32[]{:S(2)}, u32[]{:S(2)}) collective-permute-start(f32[3,256,256]{2,1,0:T(8,128)S(1)} %bitcast.24), channel_id=1, source_target_pairs={{0,4},{4,0},{8,12},{12,8},{16,20},{20,16},{24,28},{28,24},{32,36},... | collective-permute-start | bytes 2359304 | tf_op jit(solution)/shard_map/ppermute | solution.py:42
  175.6 0.7 copy-done.21
  176.5 2.2 scatter.1
  178.6 2.5 collective-permute-start.13
  181.1 3.8 %collective-permute-start.12 = (f32[6,2,16,128]{3,2,1,0:T(8,128)}, f32[6,2,16,128]{3,2,1,0:T(8,128)S(1)}, u32[]{:S(2)}, u32[]{:S(2)}) collective-permute-start(f32[6,2,16,128]{3,2,1,0:T(8,128)} %get-tuple-element.29), channel_id=1, source_target_pairs={{0,4},{4,8},{8,12},{12,16},{16,20},{20,24},{24,28},{28,32},{32,36}... | collective-permute-start | bytes 294920 | tf_op jit(solution)/shard_map/ppermute | solution.py:34
  185.0 3.7 %collective-permute-start.14 = (f32[3,2,16,128]{3,2,1,0:T(8,128)}, f32[3,2,16,128]{3,2,1,0:T(8,128)S(1)}, u32[]{:S(2)}, u32[]{:S(2)}) collective-permute-start(f32[3,2,16,128]{3,2,1,0:T(8,128)} %get-tuple-element.31), channel_id=1, source_target_pairs={{0,36},{4,40},{8,44},{12,48},{16,52},{20,56},{24,60},{28,64},{32,6... | collective-permute-start | bytes 147464 | tf_op jit(solution)/shard_map/ppermute | solution.py:34
  188.6 4.7 %collective-permute-start.15 = (s32[8]{0:T(128)S(1)}, s32[8]{0:T(128)S(1)}, u32[]{:S(2)}, u32[]{:S(2)}) collective-permute-start(s32[8]{0:T(128)S(1)} %copy-done.9), channel_id=1, source_target_pairs={{0,4},{4,8},{8,12},{12,16},{16,20},{20,24},{24,28},{28,32},{32,36}... | collective-permute-start | bytes 104 | tf_op jit(solution)/shard_map/ppermute | solution.py:34
  193.3 0.7 collective-permute-done.15.from_left
  194.0 3.2 collective-permute-start.16
  197.3 0.7 collective-permute-done.16.from_above
  198.0 9.7 %collective-permute-start.17 = (s32[8]{0:T(128)S(1)}, s32[8]{0:T(128)S(1)}, u32[]{:S(2)}, u32[]{:S(2)}) collective-permute-start(s32[8]{0:T(128)S(1)} %copy-done.9), channel_id=1, source_target_pairs={{0,36},{4,40},{8,44},{12,48},{16,52},{20,56},{24,60},{28,64},{32,6... | collective-permute-start | bytes 104 | tf_op jit(solution)/shard_map/ppermute | solution.py:34
  207.7 0.7 collective-permute-done.17.from_corner
  208.4 0.5 copy-done.30
  208.9 2.1 weights.1.weight
  211.1 0.6 copy-done.26
  211.8 3.0 update.1.n0
  214.8 0.7 collective-permute-start.18
  215.5 1.0 collective-permute-start.19
  216.6 0.6 collective-permute-start.20
  217.1 9.0 %collective-permute-done.18.n1 = f32[24,2,16,128]{3,2,1,0:T(8,128)S(1)} collective-permute-done((f32[24,2,16,128]{3,2,1,0:T(8,128)}, f32[24,2,16,128]{3,2,1,0:T(8,128)S(1)}, u32[]{:S(2)}, u32[]{:S(2)}) %collective-permute-start.18) | collective-permute-done | bytes 393248 | tf_op jit(solution)/shard_map/ppermute | solution.py:38
  226.2 1.9 collective-permute-done.19.n2
  228.1 8.2 %collective-permute-done.20.n3 = f32[24,2,16,128]{3,2,1,0:T(8,128)S(1)} collective-permute-done((f32[24,2,16,128]{3,2,1,0:T(8,128)}, f32[24,2,16,128]{3,2,1,0:T(8,128)S(1)}, u32[]{:S(2)}, u32[]{:S(2)}) %collective-permute-start.20) | collective-permute-done | bytes 393248 | tf_op jit(solution)/shard_map/ppermute | solution.py:38
  236.2 0.7 copy-done.20
  237.0 49.4 %join_pieces.1 = f32[24,2,64,128]{3,2,1,0:T(8,128)} custom-call(s32[8]{0:T(128)} %copy-done.8, f32[24,2,16,128]{3,2,1,0:T(8,128)} %update.1.n0, f32[24,2,16,128]{3,2,1,0:T(8,128)} %copy-done.18, f32[24,2,16,128]{3,2,1,0:T(8,128)} %copy-done.19, f32[24,2,16,128]{3,2,1,0:T(8,128)} %copy-done.20), custom_call_target="tpu_custom_call" | custom-call | bytes 3000000 | tf_op jit(solution)/shard_map/join_pieces/pallas_call | solution.py:335
  286.4 0.9 copy-done.17
  287.3 49.4 %join_channels.1 = f32[3,2,256,256]{3,2,1,0:T(8,128)} custom-call(s32[8]{0:T(128)} %copy-done.8, f32[3,256,256]{2,1,0:T(8,128)} %bitcast.25, f32[3,256,256]{2,1,0:T(8,128)} %copy-done.17), custom_call_target="tpu_custom_call" | custom-call | bytes 3000000 | tf_op jit(solution)/shard_map/join_channels/pallas_call | solution.py:357
  (72 shorter events, 1.3 us)
Async XLA Ops:
  7.2 58.6 %copy-start.4 = (bf16[512,512]{1,0:T(8,128)(2,1)S(1)}, bf16[512,512]{1,0:T(8,128)(2,1)}, u32[]{:S(2)}) copy-start(bf16[512,512]{1,0:T(8,128)(2,1)} %constant.88.clone.left_table) | copy-start | bytes 1572868
  7.2 10.8 %copy-start.27 = (s32[2,2]{1,0:T(2,128)S(1)}, s32[2,2]{1,0:T(2,128)}, u32[]{:S(2)}) copy-start(s32[2,2]{1,0:T(2,128)} %param.10) | copy-start | bytes 52
  7.2 58.6 %copy-start = (f32[3,2,256,256]{3,2,1,0:T(8,128)S(1)}, f32[3,2,256,256]{3,2,1,0:T(8,128)}, u32[]{:S(2)}) copy-start(f32[3,2,256,256]{3,2,1,0:T(8,128)} %probe.3) | copy-start | bytes 4718596
  9.1 55.8 %collective-permute-start = (f32[6,2,64,128]{3,2,1,0:T(8,128)}, f32[6,2,64,128]{3,2,1,0:T(8,128)}, u32[]{:S(2)}, u32[]{:S(2)}) collective-permute-start(f32[6,2,64,128]{3,2,1,0:T(8,128)} %slice_bitcast_fusion), channel_id=1, source_target_pairs={{4,0},{8,4},{12,8},{16,12},{20,16},{24,20},{28,24},{32,28},{36,32}... | collective-permute-start | bytes 1179656 | tf_op jit(solution)/shard_map/ppermute | solution.py:34
  13.8 51.1 %collective-permute-start.1 = (f32[12,2,64,128]{3,2,1,0:T(8,128)}, f32[12,2,64,128]{3,2,1,0:T(8,128)S(1)}, u32[]{:S(2)}, u32[]{:S(2)}) collective-permute-start(f32[12,2,64,128]{3,2,1,0:T(8,128)} %slice.34), channel_id=1, source_target_pairs={{32,0},{36,4},{40,8},{44,12},{48,16},{52,20},{56,24},{60,28},{64,3... | collective-permute-start | bytes 2359304 | tf_op jit(solution)/shard_map/ppermute | solution.py:34
  16.0 48.9 %collective-permute-start.2 = (f32[3,2,64,128]{3,2,1,0:T(8,128)S(1)}, f32[3,2,64,128]{3,2,1,0:T(8,128)S(1)}, u32[]{:S(2)}, u32[]{:S(2)}) collective-permute-start(f32[3,2,64,128]{3,2,1,0:T(8,128)S(1)} %slice_bitcast_fusion.1), channel_id=1, source_target_pairs={{36,0},{40,4},{44,8},{48,12},{52,16},{56,20},{60,24},{64,28},{68,3... | collective-permute-start | bytes 589832 | tf_op jit(solution)/shard_map/ppermute | solution.py:34
  22.2 75.2 %copy-start.8 = (s32[8]{0:T(128)}, s32[8]{0:T(128)S(1)}, u32[]{:S(2)}) copy-start(s32[8]{0:T(128)S(1)} %stack.15.info) | copy-start | bytes 100
  64.9 0.9 copy-start.10
  65.8 1.4 copy-start.1
  67.2 1.0 copy-start.5
  68.2 1.1 copy-start.11
  75.9 1.6 copy-start.2
  77.6 5.1 %collective-permute-start.3 = (f32[2,64,256]{2,1,0:T(8,128)}, f32[2,64,256]{2,1,0:T(8,128)S(1)}, u32[]{:S(2)}, u32[]{:S(2)}) collective-permute-start(f32[2,64,256]{2,1,0:T(8,128)} %get-tuple-element.21), channel_id=1, source_target_pairs={{0,1},{1,2},{2,3},{3,0},{4,5},{5,6},{6,7},{7,4},{8,9},{9,10},{10,1... | collective-permute-start | bytes 393224 | tf_op jit(solution)/shard_map/ppermute | solution.py:38
  77.8 6.6 %collective-permute-start.4 = (f32[2,64,256]{2,1,0:T(8,128)}, f32[2,64,256]{2,1,0:T(8,128)S(1)}, u32[]{:S(2)}, u32[]{:S(2)}) collective-permute-start(f32[2,64,256]{2,1,0:T(8,128)} %get-tuple-element.22), channel_id=1, source_target_pairs={{0,2},{1,3},{2,0},{3,1},{4,6},{5,7},{6,4},{7,5},{8,10},{9,11},{10,... | collective-permute-start | bytes 393224 | tf_op jit(solution)/shard_map/ppermute | solution.py:38
  79.9 6.3 %collective-permute-start.5 = (f32[2,64,256]{2,1,0:T(8,128)}, f32[2,64,256]{2,1,0:T(8,128)}, u32[]{:S(2)}, u32[]{:S(2)}) collective-permute-start(f32[2,64,256]{2,1,0:T(8,128)} %get-tuple-element.23), channel_id=1, source_target_pairs={{0,3},{1,0},{2,1},{3,2},{4,7},{5,4},{6,5},{7,6},{8,11},{9,8},{10,9... | collective-permute-start | bytes 393224 | tf_op jit(solution)/shard_map/ppermute | solution.py:38
  87.3 5.3 %collective-permute-start.6 = (f32[2,64,256]{2,1,0:T(8,128)S(1)}, f32[2,64,256]{2,1,0:T(8,128)S(1)}, u32[]{:S(2)}, u32[]{:S(2)}) collective-permute-start(f32[2,64,256]{2,1,0:T(8,128)S(1)} %add_multiply_fusion.f0), channel_id=1, source_target_pairs={{0,1},{1,2},{2,3},{3,0},{4,5},{5,6},{6,7},{7,4},{8,9},{9,10},{10,1... | collective-permute-start | bytes 393224 | tf_op jit(solution)/shard_map/ppermute | solution.py:38
  87.6 6.7 %collective-permute-start.7 = (f32[2,64,256]{2,1,0:T(8,128)S(1)}, f32[2,64,256]{2,1,0:T(8,128)S(1)}, u32[]{:S(2)}, u32[]{:S(2)}) collective-permute-start(f32[2,64,256]{2,1,0:T(8,128)S(1)} %add_multiply_fusion.f0), channel_id=1, source_target_pairs={{0,2},{1,3},{2,0},{3,1},{4,6},{5,7},{6,4},{7,5},{8,10},{9,11},{10,... | collective-permute-start | bytes 393224 | tf_op jit(solution)/shard_map/ppermute | solution.py:38
  89.4 8.1 %collective-permute-start.8 = (f32[2,64,256]{2,1,0:T(8,128)S(1)}, f32[2,64,256]{2,1,0:T(8,128)S(1)}, u32[]{:S(2)}, u32[]{:S(2)}) collective-permute-start(f32[2,64,256]{2,1,0:T(8,128)S(1)} %add_multiply_fusion.f0), channel_id=1, source_target_pairs={{0,3},{1,0},{2,1},{3,2},{4,7},{5,4},{6,5},{7,6},{8,11},{9,8},{10,9... | collective-permute-start | bytes 393224 | tf_op jit(solution)/shard_map/ppermute | solution.py:38
  97.4 1.9 copy-start.3
  99.3 1.0 copy-start.6
  106.8 2.6 copy-start.7
  106.8 2.6 copy-start.12
  106.8 2.6 copy-start.14
  106.8 2.4 collective-permute-start.21
  145.2 26.6 %all-to-all-start.1 = ((f32[32,24,256]{2,1,0:T(8,128)}), f32[32,24,256]{2,1,0:T(8,128)S(1)}, u32[]{:S(2)}, u32[]{:S(2)}) async-start(f32[32,24,256]{2,1,0:T(8,128)} %broadcast_in_dim.2), calls=%async_computation.2 | async-start | bytes 1572864 | tf_op jit(solution)/shard_map/all_to_all | solution.py:404
  151.2 1.0 copy-start.15
  151.2 2.5 copy-start.13
  151.2 37.5 %copy-start.9 = (s32[8]{0:T(128)S(1)}, s32[8]{0:T(128)}, u32[]{:S(2)}) copy-start(s32[8]{0:T(128)} %copy-done.8) | copy-start | bytes 100
  151.2 57.2 %reduce-scatter.2.cloned.1.call-start = ((), (), s32[]{:S(2)}) async-start(), calls=%async_computation.3 | async-start | bytes 327680 | tf_op jit(solution)/shard_map/reduce_scatter | solution.py:387
  152.1 23.5 %collective-permute-start.10 = (f32[2,8,2,16,128]{4,3,2,1,0:T(8,128)S(1)}, f32[2,8,2,16,128]{4,3,2,1,0:T(8,128)S(1)}, u32[]{:S(2)}, u32[]{:S(2)}) collective-permute-start(f32[2,8,2,16,128]{4,3,2,1,0:T(8,128)S(1)} %copy-done.15), channel_id=1, source_target_pairs={{0,2},{1,3},{2,0},{3,1},{4,6},{5,7},{6,4},{7,5},{8,10},{9,11},{10,... | collective-permute-start | bytes 786440 | tf_op jit(solution)/shard_map/ppermute | solution.py:38
  153.6 22.0 %collective-permute-start.11 = (f32[2,8,2,16,128]{4,3,2,1,0:T(8,128)S(1)}, f32[2,8,2,16,128]{4,3,2,1,0:T(8,128)S(1)}, u32[]{:S(2)}, u32[]{:S(2)}) collective-permute-start(f32[2,8,2,16,128]{4,3,2,1,0:T(8,128)S(1)} %copy-done.13), channel_id=1, source_target_pairs={{0,3},{1,0},{2,1},{3,2},{4,7},{5,4},{6,5},{7,6},{8,11},{9,8},{10,9... | collective-permute-start | bytes 786440 | tf_op jit(solution)/shard_map/ppermute | solution.py:38
  153.6 22.0 %collective-permute-start.9 = (f32[2,8,2,16,128]{4,3,2,1,0:T(8,128)S(1)}, f32[2,8,2,16,128]{4,3,2,1,0:T(8,128)S(1)}, u32[]{:S(2)}, u32[]{:S(2)}) collective-permute-start(f32[2,8,2,16,128]{4,3,2,1,0:T(8,128)S(1)} %get-tuple-element.25), channel_id=1, source_target_pairs={{0,1},{1,2},{2,3},{3,0},{4,5},{5,6},{6,7},{7,4},{8,9},{9,10},{10,1... | collective-permute-start | bytes 786440 | tf_op jit(solution)/shard_map/ppermute | solution.py:38
  171.9 42.9 %copy-start.16 = (f32[32,24,256]{2,1,0:T(8,128)}, f32[32,24,256]{2,1,0:T(8,128)S(1)}, u32[]{:S(2)}) copy-start(f32[32,24,256]{2,1,0:T(8,128)S(1)} %all-to-all-done.1) | copy-start | bytes 2359300
  171.9 114.5 %collective-permute-start.22 = (f32[3,256,256]{2,1,0:T(8,128)S(1)}, f32[3,256,256]{2,1,0:T(8,128)S(1)}, u32[]{:S(2)}, u32[]{:S(2)}) collective-permute-start(f32[3,256,256]{2,1,0:T(8,128)S(1)} %bitcast.24), channel_id=1, source_target_pairs={{0,4},{4,0},{8,12},{12,8},{16,20},{20,16},{24,28},{28,24},{32,36},... | collective-permute-start | bytes 2359304 | tf_op jit(solution)/shard_map/ppermute | solution.py:42
  175.6 0.7 copy-start.21
  175.6 0.8 copy-start.22
  175.6 0.9 copy-start.23
  178.6 32.4 %collective-permute-start.13 = (f32[12,2,16,128]{3,2,1,0:T(8,128)}, f32[12,2,16,128]{3,2,1,0:T(8,128)S(1)}, u32[]{:S(2)}, u32[]{:S(2)}) collective-permute-start(f32[12,2,16,128]{3,2,1,0:T(8,128)} %get-tuple-element.30), channel_id=1, source_target_pairs={{0,32},{4,36},{8,40},{12,44},{16,48},{20,52},{24,56},{28,60},{32,6... | collective-permute-start | bytes 589832 | tf_op jit(solution)/shard_map/ppermute | solution.py:34
  181.1 29.9 %collective-permute-start.12 = (f32[6,2,16,128]{3,2,1,0:T(8,128)}, f32[6,2,16,128]{3,2,1,0:T(8,128)S(1)}, u32[]{:S(2)}, u32[]{:S(2)}) collective-permute-start(f32[6,2,16,128]{3,2,1,0:T(8,128)} %get-tuple-element.29), channel_id=1, source_target_pairs={{0,4},{4,8},{8,12},{12,16},{16,20},{20,24},{24,28},{28,32},{32,36}... | collective-permute-start | bytes 294920 | tf_op jit(solution)/shard_map/ppermute | solution.py:34
  185.0 26.1 %collective-permute-start.14 = (f32[3,2,16,128]{3,2,1,0:T(8,128)}, f32[3,2,16,128]{3,2,1,0:T(8,128)S(1)}, u32[]{:S(2)}, u32[]{:S(2)}) collective-permute-start(f32[3,2,16,128]{3,2,1,0:T(8,128)} %get-tuple-element.31), channel_id=1, source_target_pairs={{0,36},{4,40},{8,44},{12,48},{16,52},{20,56},{24,60},{28,64},{32,6... | collective-permute-start | bytes 147464 | tf_op jit(solution)/shard_map/ppermute | solution.py:34
  188.6 5.4 %collective-permute-start.15 = (s32[8]{0:T(128)S(1)}, s32[8]{0:T(128)S(1)}, u32[]{:S(2)}, u32[]{:S(2)}) collective-permute-start(s32[8]{0:T(128)S(1)} %copy-done.9), channel_id=1, source_target_pairs={{0,4},{4,8},{8,12},{12,16},{16,20},{20,24},{24,28},{28,32},{32,36}... | collective-permute-start | bytes 104 | tf_op jit(solution)/shard_map/ppermute | solution.py:34
  194.0 14.4 %copy-start.28 = (s32[8]{0:T(128)}, s32[8]{0:T(128)S(1)}, u32[]{:S(2)}) copy-start(s32[8]{0:T(128)S(1)} %collective-permute-done.15.from_left) | copy-start | bytes 100
  194.0 4.0 %collective-permute-start.16 = (s32[8]{0:T(128)S(1)}, s32[8]{0:T(128)S(1)}, u32[]{:S(2)}, u32[]{:S(2)}) collective-permute-start(s32[8]{0:T(128)S(1)} %copy-done.9), channel_id=1, source_target_pairs={{0,32},{4,36},{8,40},{12,44},{16,48},{20,52},{24,56},{28,60},{32,6... | collective-permute-start | bytes 104 | tf_op jit(solution)/shard_map/ppermute | solution.py:34
  198.0 10.5 %copy-start.29 = (s32[8]{0:T(128)}, s32[8]{0:T(128)S(1)}, u32[]{:S(2)}) copy-start(s32[8]{0:T(128)S(1)} %collective-permute-done.16.from_above) | copy-start | bytes 100
  198.0 10.4 %collective-permute-start.17 = (s32[8]{0:T(128)S(1)}, s32[8]{0:T(128)S(1)}, u32[]{:S(2)}, u32[]{:S(2)}) collective-permute-start(s32[8]{0:T(128)S(1)} %copy-done.9), channel_id=1, source_target_pairs={{0,36},{4,40},{8,44},{12,48},{16,52},{20,56},{24,60},{28,64},{32,6... | collective-permute-start | bytes 104 | tf_op jit(solution)/shard_map/ppermute | solution.py:34
  208.4 0.5 copy-start.30
  211.0 0.6 copy-start.26
  211.0 0.7 copy-start.25
  211.1 0.7 copy-start.24
  214.8 11.4 %collective-permute-start.18 = (f32[24,2,16,128]{3,2,1,0:T(8,128)}, f32[24,2,16,128]{3,2,1,0:T(8,128)S(1)}, u32[]{:S(2)}, u32[]{:S(2)}) collective-permute-start(f32[24,2,16,128]{3,2,1,0:T(8,128)} %update.1.n0), channel_id=1, source_target_pairs={{0,1},{1,2},{2,3},{3,0},{4,5},{5,6},{6,7},{7,4},{8,9},{9,10},{10,1... | collective-permute-start | bytes 1179656 | tf_op jit(solution)/shard_map/ppermute | solution.py:38
  215.5 12.5 %collective-permute-start.19 = (f32[24,2,16,128]{3,2,1,0:T(8,128)}, f32[24,2,16,128]{3,2,1,0:T(8,128)S(1)}, u32[]{:S(2)}, u32[]{:S(2)}) collective-permute-start(f32[24,2,16,128]{3,2,1,0:T(8,128)} %update.1.n0), channel_id=1, source_target_pairs={{0,2},{1,3},{2,0},{3,1},{4,6},{5,7},{6,4},{7,5},{8,10},{9,11},{10,... | collective-permute-start | bytes 1179656 | tf_op jit(solution)/shard_map/ppermute | solution.py:38
  216.6 19.6 %collective-permute-start.20 = (f32[24,2,16,128]{3,2,1,0:T(8,128)}, f32[24,2,16,128]{3,2,1,0:T(8,128)S(1)}, u32[]{:S(2)}, u32[]{:S(2)}) collective-permute-start(f32[24,2,16,128]{3,2,1,0:T(8,128)} %update.1.n0), channel_id=1, source_target_pairs={{0,3},{1,0},{2,1},{3,2},{4,7},{5,4},{6,5},{7,6},{8,11},{9,8},{10,9... | collective-permute-start | bytes 1179656 | tf_op jit(solution)/shard_map/ppermute | solution.py:38
  226.2 10.0 %copy-start.18 = (f32[24,2,16,128]{3,2,1,0:T(8,128)}, f32[24,2,16,128]{3,2,1,0:T(8,128)S(1)}, u32[]{:S(2)}) copy-start(f32[24,2,16,128]{3,2,1,0:T(8,128)S(1)} %collective-permute-done.18.n1) | copy-start | bytes 1179652
  228.1 8.2 %copy-start.19 = (f32[24,2,16,128]{3,2,1,0:T(8,128)}, f32[24,2,16,128]{3,2,1,0:T(8,128)S(1)}, u32[]{:S(2)}) copy-start(f32[24,2,16,128]{3,2,1,0:T(8,128)S(1)} %collective-permute-done.19.n2) | copy-start | bytes 1179652
  236.2 0.7 copy-start.20
  286.4 0.9 copy-start.17
Sparse Core Ops, SparseCore 0:
  154.5 21.5 reduce-scatter.1

commit v2 on v1

v2 whole, which is shorter than its diff:
```python
import math

import jax
import jax.numpy as jnp
import numpy as np
from jax import lax
from jax.experimental import pallas as pl
from jax.experimental.pallas import tpu as pltpu
from jax.sharding import PartitionSpec as P

DEV_COLS = 8
TILE_R = 6
TILE_C = 4
SIDE = 256
PIECE_R = 64
PIECE_C = 128
N_MODE = 4
N_TILE = 64
SUB = PIECE_R // N_MODE
N_CHIP = N_TILE // 2
PART = 3 * SIDE // N_CHIP
VMEM_BYTES = 56 * 1024 * 1024

far_floor = 0.1
object_floor = 0.1

F32 = jnp.float32
BF16 = jnp.bfloat16
ANY = pl.BlockSpec(memory_space=pl.ANY)
SMEM = pl.BlockSpec(memory_space=pltpu.SMEM)
VMEM = pl.BlockSpec(memory_space=pltpu.VMEM)


def shifted(block, axis, distance):
    devices = range(lax.axis_size(axis))
    route = [(i - distance, i) for i in devices if i - distance in devices]
    return lax.ppermute(block, axis, route)


def turned(block, distance):
    return lax.ppermute(block, "mode", [(i, (i + distance) % N_MODE) for i in range(N_MODE)])


def core_swap(block):
    return lax.ppermute(block, "tile", [(d, d ^ 1) for d in range(N_TILE)])


def fourier_blocks():
    indices = np.arange(SIDE)
    phases = (indices[:, None] * indices[None, :] % SIDE) * (2.0 * math.pi / SIDE)
    scaling = 1.0 / math.sqrt(SIDE)
    re = (np.cos(phases) * scaling).astype(np.float32)
    im = (-np.sin(phases) * scaling).astype(np.float32)
    left = np.block([[re, -im], [im, re]])
    right = np.block([[re, im], [-im, re]])
    return jnp.asarray(left.astype(jnp.bfloat16)), jnp.asarray(right.astype(jnp.bfloat16))


def canvas_index(row, col):
    inside = jnp.where(col < TILE_C, row * TILE_C + col, 24 + row)
    below = jnp.where(col < TILE_C, 30 + (row - TILE_R) * TILE_C + col, 42 + row - TILE_R)
    return jnp.where(row < TILE_R, inside, below)


def forward_kernel(info, own, right, b0, b1, b2, b3, probe, left_table, right_table,
                   far, patch, p0, p1, p2, p3, power, sems):
    mode = pl.program_id(0)

    def piece_copy(s, q, source, index):
        target = patch.at[s, :, pl.ds(PIECE_R * (q // 2), PIECE_R), pl.ds(PIECE_C * (q % 2), PIECE_C)]
        return pltpu.make_async_copy(source.at[index], target, sems.at[s, q])

    @pl.when(mode == 0)
    def _():
        for s in range(2):
            for q in range(8):
                row = info[2 * s] + q // 2
                col = info[2 * s + 1] + q % 2
                upper = row < TILE_R
                inner = col < TILE_C

                @pl.when(upper & inner)
                def _():
                    piece_copy(s, q, own, row * TILE_C + col).start()

                @pl.when(upper & jnp.logical_not(inner))
                def _():
                    piece_copy(s, q, right, row).start()

                @pl.when(jnp.logical_not(upper))
                def _():
                    below = jnp.where(inner, (row - TILE_R) * TILE_C + col, 12 + row - TILE_R)
                    for j, source in enumerate((b0, b1, b2, b3)):
                        start = lax.rem(info[5] + N_MODE - j, N_MODE) * SUB + PIECE_R * (q // 2)
                        target = patch.at[s, :, pl.ds(pl.multiple_of(start, SUB), SUB),
                                          pl.ds(PIECE_C * (q % 2), PIECE_C)]
                        pltpu.make_async_copy(source.at[below], target, sems.at[s, q]).start()

        for s in range(2):
            for q in range(8):
                piece_copy(s, q, own, 0).wait()

    probe_re, probe_im = probe[0, 0], probe[0, 1]
    for s in range(2):
        patch_re, patch_im = patch[s, 0], patch[s, 1]
        exit_re = (probe_re * patch_re - probe_im * patch_im).astype(BF16)
        exit_im = (probe_re * patch_im + probe_im * patch_re).astype(BF16)
        half = jnp.dot(left_table[...], jnp.concatenate([exit_re, exit_im], axis=0),
                       preferred_element_type=F32).astype(BF16)
        half = jnp.concatenate([half[:SIDE], half[SIDE:]], axis=1)
        both = jnp.dot(half, right_table[...], preferred_element_type=F32)
        far_re, far_im = both[:, :SIDE], both[:, SIDE:]
        far[s, 0, 0] = far_re
        far[s, 0, 1] = far_im
        local = far_re * far_re + far_im * far_im
        power[s] = jnp.where(mode == 0, local, power[s] + local)

    @pl.when(mode == 2)
    def _():
        for j, out in enumerate((p0, p1, p2, p3)):
            start = pl.multiple_of(lax.rem(info[5] + j, N_MODE) * 64, 64)
            out[...] = power[:, pl.ds(start, 64), :]


def forward(info, own, right, below, probe, tables):
    full = lambda *shape: pl.BlockSpec(shape, lambda k: (0,) * len(shape))
    return pl.pallas_call(
        forward_kernel,
        grid=(3,),
        in_specs=[SMEM] + [ANY] * 6 + [
                  pl.BlockSpec((1, 2, SIDE, SIDE), lambda k: (k, 0, 0, 0)),
                  full(512, 512), full(512, 512)],
        out_specs=[pl.BlockSpec((2, 1, 2, SIDE, SIDE), lambda k: (0, k, 0, 0, 0)),
                   full(2, 2, SIDE, SIDE)] + [full(2, 64, SIDE)] * 4,
        out_shape=[jax.ShapeDtypeStruct((2, 3, 2, SIDE, SIDE), F32),
                   jax.ShapeDtypeStruct((2, 2, SIDE, SIDE), F32)]
        + [jax.ShapeDtypeStruct((2, 64, SIDE), F32)] * 4,
        scratch_shapes=[pltpu.VMEM((2, SIDE, SIDE), F32), pltpu.SemaphoreType.DMA((2, 8))],
        compiler_params=pltpu.CompilerParams(vmem_limit_bytes=VMEM_BYTES),
        cost_estimate=pl.CostEstimate(flops=1700000000, bytes_accessed=12000000, transcendentals=0),
        name="forward",
    )(info, own, right, *below, probe, *tables)


def backward_kernel(info, far, probe, patch, f0, f1, f2, f3, left_table, right_table,
                    mine, theirs, g0, g1, g2, g3, factor, grad):
    mode = pl.program_id(0)
    me = info[5]
    first = info[6] == 0

    @pl.when(mode == 0)
    def _():
        for j, part in enumerate((f0, f1, f2, f3)):
            start = pl.multiple_of(lax.rem(me + N_MODE - j, N_MODE) * 64, 64)
            factor[:, pl.ds(start, 64), :] = part[...]

    probe_re, probe_im = probe[0, 0], probe[0, 1]
    own_term, other_term = 0.0, 0.0
    for s in range(2):
        change_re = (factor[s] * far[s, 0, 0]).astype(BF16)
        change_im = (factor[s] * far[s, 0, 1]).astype(BF16)
        back = jnp.dot(right_table[...], jnp.concatenate([change_re, change_im], axis=0),
                       preferred_element_type=F32).astype(BF16)
        back = jnp.concatenate([back[:SIDE], back[SIDE:]], axis=1)
        both = jnp.dot(back, left_table[...], preferred_element_type=F32)
        delta_re, delta_im = both[:, :SIDE], both[:, SIDE:]
        patch_re, patch_im = patch[s, 0], patch[s, 1]
        term_re = patch_re * delta_re + patch_im * delta_im
        term_im = patch_re * delta_im - patch_im * delta_re
        own_term += jnp.where(first, term_re, term_im)
        other_term += jnp.where(first, term_im, term_re)
        grad_re = probe_re * delta_re + probe_im * delta_im
        grad_im = probe_re * delta_im - probe_im * delta_re
        grad[s, 0] = jnp.where(mode == 0, grad_re, grad[s, 0] + grad_re)
        grad[s, 1] = jnp.where(mode == 0, grad_im, grad[s, 1] + grad_im)
    mine[0] = own_term
    theirs[0] = other_term

    @pl.when(mode == 2)
    def _():
        for j, out in enumerate((g0, g1, g2, g3)):
            base = lax.rem(me + j, N_MODE) * SUB
            for q in range(8):
                start = pl.multiple_of(base + PIECE_R * (q // 2), SUB)
                out[:, q] = grad[:, :, pl.ds(start, SUB), PIECE_C * (q % 2):PIECE_C * (q % 2 + 1)]


def backward(info, far, probe, patch, factors, tables):
    full = lambda *shape: pl.BlockSpec(shape, lambda k: (0,) * len(shape))
    return pl.pallas_call(
        backward_kernel,
        grid=(3,),
        in_specs=[SMEM,
                  pl.BlockSpec((2, 1, 2, SIDE, SIDE), lambda k: (0, k, 0, 0, 0)),
                  pl.BlockSpec((1, 2, SIDE, SIDE), lambda k: (k, 0, 0, 0)),
                  full(2, 2, SIDE, SIDE)] + [full(2, 64, SIDE)] * 4
        + [full(512, 512), full(512, 512)],
        out_specs=[pl.BlockSpec((1, SIDE, SIDE), lambda k: (k, 0, 0))] * 2
        + [full(2, 8, 2, SUB, PIECE_C)] * 4,
        out_shape=[jax.ShapeDtypeStruct((3, SIDE, SIDE), F32)] * 2
        + [jax.ShapeDtypeStruct((2, 8, 2, SUB, PIECE_C), F32)] * 4,
        scratch_shapes=[pltpu.VMEM((2, SIDE, SIDE), F32), pltpu.VMEM((2, 2, SIDE, SIDE), F32)],
        compiler_params=pltpu.CompilerParams(vmem_limit_bytes=VMEM_BYTES),
        cost_estimate=pl.CostEstimate(flops=1700000000, bytes_accessed=12000000, transcendentals=0),
        name="backward",
    )(info, far, probe, patch, *factors, *tables)


def scatter_kernel(info, g0, g1, g2, g3, own, right, low, corner, canvas):
    canvas[...] = jnp.zeros_like(canvas)
    for s in range(2):
        for q in range(8):
            index = canvas_index(info[2 * s] + q // 2, info[2 * s + 1] + q % 2)
            canvas[index] += (g0[s, q] + g1[s, q]) + (g2[s, q] + g3[s, q])
    own[...] = canvas[:24]
    rows = lax.broadcasted_iota(jnp.int32, (2, SUB, PIECE_C), 1)
    note = jnp.zeros((2, SUB, PIECE_C), F32)
    for i in range(5):
        note = jnp.where(rows == i, info[i].astype(F32), note)
    for out, begin, size in ((right, 24, 6), (low, 30, 12), (corner, 42, 3)):
        out[:size] = canvas[begin:begin + size]
        out[size] = note


def scatter(info, parts):
    pieces = lambda n: jax.ShapeDtypeStruct((n, 2, SUB, PIECE_C), F32)
    return pl.pallas_call(
        scatter_kernel,
        in_specs=[SMEM] + [VMEM] * 4,
        out_specs=[VMEM] * 4,
        out_shape=[pieces(24), pieces(7), pieces(13), pieces(4)],
        scratch_shapes=[pltpu.VMEM((45, 2, SUB, PIECE_C), F32)],
        cost_estimate=pl.CostEstimate(flops=1000000, bytes_accessed=2000000, transcendentals=0),
        name="scatter",
    )(info, *parts)


def update_kernel(info, pieces, own, right, low, corner, light, new, old, weight, notes, sems):
    start = pl.multiple_of(info[5] * SUB, SUB)
    fetch = pltpu.make_async_copy(pieces.at[:, :, pl.ds(start, SUB), :], old, sems.at[3])
    fetch.start()
    reads = [pltpu.make_async_copy(part.at[size, 0], notes.at[n], sems.at[n])
             for n, (part, size) in enumerate(((right, 6), (low, 12), (corner, 3)))]
    for read in reads:
        read.start()
    weight[...] = jnp.zeros_like(weight)

    def add_slot(top, left, live, classes):
        @pl.when(live)
        def _():
            for q in classes:
                row = top + q // 2
                col = left + q % 2

                @pl.when((row >= 0) & (row < TILE_R) & (col >= 0) & (col < TILE_C))
                def _():
                    weight[row * TILE_C + col] += light[
                        q // 2, :, PIECE_C * (q % 2):PIECE_C * (q % 2 + 1)]

    for s in range(2):
        add_slot(info[2 * s], info[2 * s + 1], s < info[4], range(8))
    for read in reads:
        read.wait()
    for n, (down, across, classes) in enumerate((
            (0, TILE_C, (1, 3, 5, 7)), (TILE_R, 0, (2, 3, 4, 5, 6, 7)), (TILE_R, TILE_C, (3, 5, 7)))):
        for s in range(2):
            top = notes[n, 2 * s, 0].astype(jnp.int32) - down
            left = notes[n, 2 * s + 1, 0].astype(jnp.int32) - across
            live = s < notes[n, 4, 0].astype(jnp.int32)
            add_slot(top, left, live & (top > -4) & (left > -2), classes)
    fetch.wait()
    for p in range(TILE_R * TILE_C):
        row, col = p // TILE_C, p % TILE_C
        total = own[p]
        if row < 3:
            total = total + low[p]
        if col == 0:
            total = total + right[row]
        if row < 3 and col == 0:
            total = total + corner[row]
        new[p] = old[p] + total / (weight[p] + object_floor)[None]


def update(info, pieces, own, right, low, corner, light):
    shape = (TILE_R * TILE_C, 2, SUB, PIECE_C)
    return pl.pallas_call(
        update_kernel,
        in_specs=[SMEM, ANY] + [VMEM] * 5,
        out_specs=VMEM,
        out_shape=jax.ShapeDtypeStruct(shape, F32),
        scratch_shapes=[pltpu.VMEM(shape, F32), pltpu.VMEM((TILE_R * TILE_C, SUB, PIECE_C), F32),
                        pltpu.SMEM((3, SUB, PIECE_C), F32), pltpu.SemaphoreType.DMA((4,))],
        compiler_params=pltpu.CompilerParams(vmem_limit_bytes=VMEM_BYTES),
        cost_estimate=pl.CostEstimate(flops=1000000, bytes_accessed=2000000, transcendentals=0),
        name="update",
    )(info, pieces, own, right, low, corner, light)


def join_pieces_kernel(info, n0, n1, n2, n3, out):
    for j, part in enumerate((n0, n1, n2, n3)):
        start = pl.multiple_of(lax.rem(info[5] + N_MODE - j, N_MODE) * SUB, SUB)
        out[:, :, pl.ds(start, SUB), :] = part[...]


def join_pieces(info, parts):
    block = lambda rows: pl.BlockSpec((6, 2, rows, PIECE_C), lambda i: (i, 0, 0, 0))
    return pl.pallas_call(
        join_pieces_kernel,
        grid=(4,),
        in_specs=[SMEM] + [block(SUB)] * 4,
        out_specs=block(PIECE_R),
        out_shape=jax.ShapeDtypeStruct((TILE_R * TILE_C, 2, PIECE_R, PIECE_C), F32),
        compiler_params=pltpu.CompilerParams(vmem_limit_bytes=VMEM_BYTES),
        cost_estimate=pl.CostEstimate(flops=0, bytes_accessed=3000000, transcendentals=0),
        name="join_pieces",
    )(info, *parts)


def join_channels_kernel(info, mine, theirs, out):
    core = info[6]
    out[0, core] = mine[0]
    out[0, 1 - core] = theirs[0]


def join_channels(info, mine, theirs):
    block = pl.BlockSpec((1, SIDE, SIDE), lambda k: (k, 0, 0))
    return pl.pallas_call(
        join_channels_kernel,
        grid=(3,),
        in_specs=[SMEM, block, block],
        out_specs=pl.BlockSpec((1, 2, SIDE, SIDE), lambda k: (k, 0, 0, 0)),
        out_shape=jax.ShapeDtypeStruct((3, 2, SIDE, SIDE), F32),
        compiler_params=pltpu.CompilerParams(vmem_limit_bytes=VMEM_BYTES),
        cost_estimate=pl.CostEstimate(flops=0, bytes_accessed=3000000, transcendentals=0),
        name="join_channels",
    )(info, mine, theirs)


def body(object_pieces, probe_modes, intensity, positions, counts):
    tile_index = lax.axis_index("tile")
    mode_index = lax.axis_index("mode")
    tables = fourier_blocks()
    tile_grid = object_pieces.reshape(TILE_R, TILE_C, 2, PIECE_R, PIECE_C)
    own_rows = lax.dynamic_slice_in_dim(object_pieces[:12], mode_index * SUB, SUB, axis=2)
    low = shifted(own_rows, "tile", -DEV_COLS)
    corner = shifted(own_rows[::TILE_C], "tile", -DEV_COLS - 1)
    right = shifted(tile_grid[:, 0], "tile", -1)
    below = jnp.concatenate([low, corner], axis=0)
    dev_row = tile_index // DEV_COLS
    dev_col = tile_index % DEV_COLS
    rows = jnp.clip(positions[:, 0] // PIECE_R - dev_row * TILE_R, 0, TILE_R - 1)
    cols = jnp.clip(positions[:, 1] // PIECE_C - dev_col * TILE_C, 0, TILE_C - 1)
    info = jnp.stack([rows[0], cols[0], rows[1], cols[1], counts[0], mode_index,
                      tile_index % 2, tile_index]).astype(jnp.int32)
    below = [below] + [turned(below, j) for j in (1, 2, 3)]

    light_local = jnp.sum(probe_modes * probe_modes, axis=(0, 1))
    light_parts = light_local.reshape(4, N_MODE, SUB, SIDE).transpose(1, 0, 2, 3)
    light = lax.psum_scatter(light_parts, "mode", scatter_dimension=0, tiled=True)
    light, right = lax.optimization_barrier((light, right))

    far, patch, *powers = forward(info, object_pieces, right, below, probe_modes, tables)
    received = [turned(powers[j], j) for j in (1, 2, 3)]
    power = (powers[0] + received[0]) + (received[1] + received[2])
    own_intensity = lax.dynamic_slice_in_dim(intensity, mode_index * 64, 64, axis=1)
    live = (jnp.arange(2, dtype=jnp.int32) < counts[0]).astype(F32)
    factor = live[:, None, None] * (jnp.sqrt(own_intensity) / jnp.sqrt(power + far_floor) - 1.0)
    factors = [factor] + [turned(factor, j) for j in (1, 2, 3)]

    mine, theirs, *grads = backward(info, far, probe_modes, patch, factors, tables)

    parts = [grads[0]] + [turned(grads[j], j) for j in (1, 2, 3)]
    groups = [list(range(core, N_TILE, 2)) for core in range(2)]
    exchange = lambda blocks: lax.all_to_all(
        blocks, "tile", 0, 0, axis_index_groups=groups, tiled=True)
    summed = mine + core_swap(theirs)
    own, to_right, to_low, to_corner = scatter(info, parts)
    summed, own = lax.optimization_barrier((summed, own))
    pieces = exchange(summed.reshape(N_CHIP, PART, SIDE))

    from_above = shifted(to_low, "tile", DEV_COLS)
    from_corner = shifted(to_corner, "tile", DEV_COLS + 1)
    from_left = shifted(to_right, "tile", 1)

    new = update(info, object_pieces, own, from_left, from_above, from_corner, light[0])
    share = jnp.sum(pieces, axis=0)
    share, new = lax.optimization_barrier((share, new))
    gathered = exchange(jnp.broadcast_to(share[None], (N_CHIP, PART, SIDE)))
    new_parts = [new] + [turned(new, j) for j in (1, 2, 3)]
    gathered = gathered.reshape(3, SIDE, SIDE)
    probe_grad = join_channels(info, gathered, core_swap(gathered))
    return (join_pieces(info, new_parts), probe_grad)


def solution(mesh):
    return jax.shard_map(
        body,
        mesh=mesh,
        in_specs=(
            P("tile", None, None, None),
            P("mode", None, None, None),
            P("tile", None, None),
            P("tile", None),
            P("tile"),
        ),
        out_specs=(P("tile", None, None, None), P("mode", None, None, None)),
        check_vma=False,
    )
```

time: 351 us -> 225 us (0.64); the launches traced: 344 us -> 222 us
  Pallas kernels: 119 us -> 27.9 us
  waiting for transfers between devices: 95.6 us -> 82.7 us
  local copies, waits for them, and re-layouts: 23.5 us -> 11.6 us
  starting transfers between devices: 54 us -> 48.6 us
    pallas_call x5 -> x4, Pallas kernels: 114 us -> 22.7 us  [the longest x1 8.28 us: forward(): pl.pallas_call(forward_kernel, grid=(3,), in_specs=[SMEM] + [ANY] * 6 + [...]
    ppermute x12 -> x15, waiting for transfers between devices: 33.3 us -> 53.3 us  [turned(): lax.ppermute(block, 'mode', [(i, (i + distance) % N_MODE) for i in range(...]
    all_to_all x1, waiting for transfers between devices: 15.6 us -> 0.01 us  [body(): lax.all_to_all(blocks, 'tile', 0, 0, axis_index_groups=groups, tiled=True)]
    ppermute x9 -> x6, waiting for transfers between devices: 44.8 us -> 29.4 us  [shifted(): return lax.ppermute(block, axis, route)]
    ppermute x9 -> x6, starting transfers between devices: 32.8 us -> 18.7 us  [shifted(): return lax.ppermute(block, axis, route)]
    unnamed x62 -> x55, local copies, waits for them, and re-layouts: 12.7 us -> 5.84 us
    all_to_all x1, starting transfers between devices: 5.92 us -> 11.1 us  [body(): lax.all_to_all(blocks, 'tile', 0, 0, axis_index_groups=groups, tiled=True)]
    ppermute x12 -> x15, starting transfers between devices: 11.1 us -> 14.3 us  [turned(): lax.ppermute(block, 'mode', [(i, (i + distance) % N_MODE) for i in range(...]
  transfers between devices with their start and end apart: 25 -> 25, of which waited for: 15 -> 13; matrix products, arithmetic and copies ran while one was open for 2% -> 2% of each run, Pallas kernels for 17% -> 4%
where the time goes in v2:
time: 225 us; the launch traced here: 222 us
  waiting for transfers between devices  82.7 us (37%)
  starting transfers between devices  48.6 us (22%)
  blocking collectives  32.6 us (14%)
  Pallas kernels  27.9 us (12%)
  between operations  15.1 us (7%)
  local copies, waits for them, and re-layouts  11.6 us (5%)
  other arithmetic  3.65 us (2%)
    ppermute x15, waiting for transfers between devices, turned(): lax.ppermute(block, 'mode', [(i, (i + distance) % N_MODE) for i in range(...  53.3 us
    all_to_all x1, blocking collectives, body(): lax.all_to_all(blocks, 'tile', 0, 0, axis_index_groups=groups, tiled=True)  32.6 us
    ppermute x6, waiting for transfers between devices, shifted(): return lax.ppermute(block, axis, route)  29.4 us
    ppermute x6, starting transfers between devices, shifted(): return lax.ppermute(block, axis, route)  18.7 us
    ppermute x15, starting transfers between devices, turned(): lax.ppermute(block, 'mode', [(i, (i + distance) % N_MODE) for i in range(...  14.3 us
    all_to_all x1, starting transfers between devices, body(): lax.all_to_all(blocks, 'tile', 0, 0, axis_index_groups=groups, tiled=True)  11.1 us
    pallas_call x1, Pallas kernels, forward(): pl.pallas_call(forward_kernel, grid=(3,), in_specs=[SMEM] + [ANY] * 6 + [...  8.28 us
    pallas_call x1, Pallas kernels, backward(): pl.pallas_call(backward_kernel, grid=(3,), in_specs=[SMEM, pl.BlockSpec((...  7.38 us
  transfers between devices with their start and end apart: 25, of which 13 were waited for; matrix products, arithmetic and copies ran while one was open for 2% of the time, Pallas kernels for 4%

profile of v2, /device:TPU:39, one launch (start us, length us, event | category | flops | bytes accessed | tf_op | source)
XLA Modules:
  0.0 222.1 jit_solution(2376339394877539799)
XLA Ops:
  7.2 1.5 multiply_reduce_fusion
  8.8 0.7 copy.13
  9.5 0.5 slice-done
  10.0 1.3 collective-permute-start.1
  11.3 2.6 %collective-permute-start = (f32[6,2,64,128]{3,2,1,0:T(8,128)S(1)}, f32[6,2,64,128]{3,2,1,0:T(8,128)S(1)}, u32[]{:S(2)}, u32[]{:S(2)}) collective-permute-start(f32[6,2,64,128]{3,2,1,0:T(8,128)S(1)} %slice_bitcast_fusion), channel_id=1, source_target_pairs={{4,0},{8,4},{12,8},{16,12},{20,16},{24,20},{28,24},{32,28},{36,32}... | collective-permute-start | bytes 1179656 | tf_op jit(solution)/shard_map/ppermute | solution.py:37
  14.0 1.3 collective-permute-start.2
  15.3 0.2 slice_reduce_fusion
  15.5 11.8 %collective-permute-done.1 = f32[12,2,16,128]{3,2,1,0:T(8,128)S(1)} collective-permute-done((f32[12,2,16,128]{3,2,1,0:T(8,128)S(1)}, f32[12,2,16,128]{3,2,1,0:T(8,128)S(1)}, u32[]{:S(2)}, u32[]{:S(2)}) %collective-permute-start.1) | collective-permute-done | bytes 196640 | tf_op jit(solution)/shard_map/ppermute | solution.py:37
  27.3 2.0 collective-permute-done.2
  29.3 0.6 collective-permute-start.5
  29.9 0.8 collective-permute-start.4
  30.8 1.8 collective-permute-start.3
  33.3 0.6 fusion
  33.9 0.6 fusion.1
  34.4 3.1 %stack.15.info = s32[8]{0:T(128)} concatenate(s32[1]{0:T(128)} %get-tuple-element.51, s32[1]{0:T(128)} %get-tuple-element.49, s32[1]{0:T(128)} %get-tuple-element.50, s32[1]{0:T(128)} %get-tuple-element.48, s32[1]{0:T(128)} %copy.15, s32[1]{0:T(128)} %bitcast, s32[1]{0:T(128)} %bitcast.1, s32[1]{0:T(128)} %bitcast.2), dimensions={0} | concatenate | bytes 64 | tf_op jit(solution)/shard_map/stack | solution.py:353
  37.6 6.4 %collective-permute-done.5.b3 = f32[15,2,16,128]{3,2,1,0:T(8,128)S(1)} collective-permute-done((f32[15,2,16,128]{3,2,1,0:T(8,128)S(1)}, f32[15,2,16,128]{3,2,1,0:T(8,128)S(1)}, u32[]{:S(2)}, u32[]{:S(2)}) %collective-permute-start.5) | collective-permute-done | bytes 245792 | tf_op jit(solution)/shard_map/ppermute | solution.py:41
  44.0 0.7 copy-done.21
  44.6 0.1 copy-done.22
  44.7 0.7 copy-done.23
  45.4 8.3 %forward.1 = (f32[2,3,2,256,256]{4,3,2,1,0:T(8,128)}, f32[2,2,256,256]{3,2,1,0:T(8,128)}, f32[2,64,256]{2,1,0:T(8,128)}, f32[2,64,256]{2,1,0:T(8,128)}, f32[2,64,256]{2,1,0:T(8,128)}, /*index=5*/f32[2,64,256]{2,1,0:T(8,128)}) custom-call(s32[8]{0:T(128)} %stack.15.info, f32[24,2,64,128]{3,2,1,0:T(8,128)} %pieces.1, f32[6,2,64,128]{3,2,1,0:T(8,128)} %copy-done.20, ...), custom_call_target="tpu_custom_call" | custom-call | flops 1700000000 | bytes 12000000 | tf_op jit(solution)/shard_map/forward/pallas_call | solution.py:127
  53.7 2.2 %collective-permute-start.6 = (f32[2,64,256]{2,1,0:T(8,128)}, f32[2,64,256]{2,1,0:T(8,128)S(1)}, u32[]{:S(2)}, u32[]{:S(2)}) collective-permute-start(f32[2,64,256]{2,1,0:T(8,128)} %get-tuple-element.28), channel_id=1, source_target_pairs={{0,1},{1,2},{2,3},{3,0},{4,5},{5,6},{6,7},{7,4},{8,9},{9,10},{10,1... | collective-permute-start | bytes 393224 | tf_op jit(solution)/shard_map/ppermute | solution.py:41
  55.9 0.7 collective-permute-start.8
  56.6 3.0 %collective-permute-done.6 = f32[2,64,256]{2,1,0:T(8,128)S(1)} collective-permute-done((f32[2,64,256]{2,1,0:T(8,128)}, f32[2,64,256]{2,1,0:T(8,128)S(1)}, u32[]{:S(2)}, u32[]{:S(2)}) %collective-permute-start.6) | collective-permute-done | bytes 131104 | tf_op jit(solution)/shard_map/ppermute | solution.py:41
  59.6 2.4 %collective-permute-done.7 = f32[2,64,256]{2,1,0:T(8,128)S(1)} collective-permute-done((f32[2,64,256]{2,1,0:T(8,128)}, f32[2,64,256]{2,1,0:T(8,128)S(1)}, u32[]{:S(2)}, u32[]{:S(2)}) %collective-permute-start.7) | collective-permute-done | bytes 131104 | tf_op jit(solution)/shard_map/ppermute | solution.py:41
  62.0 3.2 %collective-permute-done.8 = f32[2,64,256]{2,1,0:T(8,128)S(1)} collective-permute-done((f32[2,64,256]{2,1,0:T(8,128)}, f32[2,64,256]{2,1,0:T(8,128)S(1)}, u32[]{:S(2)}, u32[]{:S(2)}) %collective-permute-start.8) | collective-permute-done | bytes 131104 | tf_op jit(solution)/shard_map/ppermute | solution.py:41
  65.2 1.0 add_multiply_fusion.f0
  66.3 0.1 collective-permute-start.11
  66.4 1.1 collective-permute-start.10
  67.4 1.6 collective-permute-start.9
  69.0 6.0 %collective-permute-done.11.f3 = f32[2,64,256]{2,1,0:T(8,128)S(1)} collective-permute-done((f32[2,64,256]{2,1,0:T(8,128)S(1)}, f32[2,64,256]{2,1,0:T(8,128)S(1)}, u32[]{:S(2)}, u32[]{:S(2)}) %collective-permute-start.11) | collective-permute-done | bytes 131104 | tf_op jit(solution)/shard_map/ppermute | solution.py:41
  75.1 0.6 copy-done.14
  75.7 0.1 copy-done.15
  75.8 7.4 %backward.1 = (f32[3,256,256]{2,1,0:T(8,128)}, f32[3,256,256]{2,1,0:T(8,128)}, f32[2,8,2,16,128]{4,3,2,1,0:T(8,128)}, f32[2,8,2,16,128]{4,3,2,1,0:T(8,128)}, f32...) custom-call(s32[8]{0:T(128)} %stack.15.info, f32[2,3,2,256,256]{4,3,2,1,0:T(8,128)} %get-tuple-element.25.far, ...), custom_call_target="tpu_custom_call" | custom-call | flops 1700000000 | bytes 12000000 | tf_op jit(solution)/shard_map/backward/pallas_call | solution.py:190
  83.2 1.9 collective-permute-start.12
  85.0 2.1 collective-permute-start.13
  87.1 0.6 collective-permute-start.15
  87.7 5.7 %collective-permute-done.13.g1 = f32[2,8,2,16,128]{4,3,2,1,0:T(8,128)S(1)} collective-permute-done((f32[2,8,2,16,128]{4,3,2,1,0:T(8,128)}, f32[2,8,2,16,128]{4,3,2,1,0:T(8,128)S(1)}, u32[]{:S(2)}, u32[]{:S(2)}) %collective-permute-start.13) | collective-permute-done | bytes 262176 | tf_op jit(solution)/shard_map/ppermute | solution.py:41
  93.4 3.0 %collective-permute-done.14.g2 = f32[2,8,2,16,128]{4,3,2,1,0:T(8,128)S(1)} collective-permute-done((f32[2,8,2,16,128]{4,3,2,1,0:T(8,128)}, f32[2,8,2,16,128]{4,3,2,1,0:T(8,128)S(1)}, u32[]{:S(2)}, u32[]{:S(2)}) %collective-permute-start.14) | collective-permute-done | bytes 262176 | tf_op jit(solution)/shard_map/ppermute | solution.py:41
  96.4 5.7 %collective-permute-done.15.g3 = f32[2,8,2,16,128]{4,3,2,1,0:T(8,128)S(1)} collective-permute-done((f32[2,8,2,16,128]{4,3,2,1,0:T(8,128)}, f32[2,8,2,16,128]{4,3,2,1,0:T(8,128)S(1)}, u32[]{:S(2)}, u32[]{:S(2)}) %collective-permute-start.15) | collective-permute-done | bytes 262176 | tf_op jit(solution)/shard_map/ppermute | solution.py:41
  102.1 0.7 copy-done.11
  102.8 2.2 scatter.1
  105.0 1.0 add.46
  106.0 11.1 %all-to-all-start = ((f32[32,24,256]{2,1,0:T(8,128)}), f32[32,24,256]{2,1,0:T(8,128)S(1)}, u32[]{:S(2)}, u32[]{:S(2)}) async-start(f32[32,24,256]{2,1,0:T(8,128)} %bitcast.8), calls=%async_computation.1 | async-start | bytes 1572864 | tf_op jit(solution)/shard_map/all_to_all | solution.py:374
  117.2 6.1 %collective-permute-start.17 = (f32[13,2,16,128]{3,2,1,0:T(8,128)S(1)}, f32[13,2,16,128]{3,2,1,0:T(8,128)S(1)}, u32[]{:S(2)}, u32[]{:S(2)}) collective-permute-start(f32[13,2,16,128]{3,2,1,0:T(8,128)S(1)} %copy-done.24), channel_id=1, source_target_pairs={{0,32},{4,36},{8,40},{12,44},{16,48},{20,52},{24,56},{28,60},{32,6... | collective-permute-start | bytes 638984 | tf_op jit(solution)/shard_map/ppermute | solution.py:37
  123.3 3.7 %collective-permute-start.16 = (f32[7,2,16,128]{3,2,1,0:T(8,128)S(1)}, f32[7,2,16,128]{3,2,1,0:T(8,128)S(1)}, u32[]{:S(2)}, u32[]{:S(2)}) collective-permute-start(f32[7,2,16,128]{3,2,1,0:T(8,128)S(1)} %copy-done.25), channel_id=1, source_target_pairs={{0,4},{4,8},{8,12},{12,16},{16,20},{20,24},{24,28},{28,32},{32,36}... | collective-permute-start | bytes 344072 | tf_op jit(solution)/shard_map/ppermute | solution.py:37
  127.0 3.7 %collective-permute-start.18 = (f32[4,2,16,128]{3,2,1,0:T(8,128)S(1)}, f32[4,2,16,128]{3,2,1,0:T(8,128)S(1)}, u32[]{:S(2)}, u32[]{:S(2)}) collective-permute-start(f32[4,2,16,128]{3,2,1,0:T(8,128)S(1)} %copy-done.26), channel_id=1, source_target_pairs={{0,36},{4,40},{8,44},{12,48},{16,52},{20,56},{24,60},{28,64},{32,6... | collective-permute-start | bytes 196616 | tf_op jit(solution)/shard_map/ppermute | solution.py:37
  130.7 15.5 %collective-permute-done.18.corner = f32[4,2,16,128]{3,2,1,0:T(8,128)S(1)} collective-permute-done((f32[4,2,16,128]{3,2,1,0:T(8,128)S(1)}, f32[4,2,16,128]{3,2,1,0:T(8,128)S(1)}, u32[]{:S(2)}, u32[]{:S(2)}) %collective-permute-start.18) | collective-permute-done | bytes 65568 | tf_op jit(solution)/shard_map/ppermute | solution.py:37
  146.3 0.6 copy-done.18
  146.9 0.1 copy-done.17
  146.9 0.1 copy-done.12
  147.0 3.0 %update.1.n0 = f32[24,2,16,128]{3,2,1,0:T(8,128)} custom-call(s32[8]{0:T(128)} %stack.15.info, f32[24,2,64,128]{3,2,1,0:T(8,128)} %pieces.1, f32[24,2,16,128]{3,2,1,0:T(8,128)} %get-tuple-element.39.own, f32[7,2,16,128]{3,2,1,0:T(8,128)} %copy-done.17, f32[13,2,16,128]{3,2,1,0:T(8,128)} %copy-done.12, f32[4,2,16,128]{3,2,1,0:T(8,128)} %copy-done.18, ...), custom_call_target="tpu_custom_call" | custom-call | flops 1000000 | bytes 2000000 | tf_op jit(solution)/shard_map/update/pallas_call | solution.py:286
  150.1 0.1 reduce_sum.19
  150.2 32.6 %all_to_all.10 = f32[32,24,256]{2,1,0:T(8,128)S(1)} all-to-all(f32[32,24,256]{2,1,0:T(8,128)S(1)} %broadcast_in_dim.2), channel_id=1, replica_groups={{0,8,16,24,32,40,48,56,64,72,80,88,96,104,112,120,128,136,144,152,160,1..., dimensions={0} | all-to-all | bytes 1572864 | tf_op jit(solution)/shard_map/all_to_all | solution.py:374
  182.7 2.6 %collective-permute-start.22 = (f32[3,256,256]{2,1,0:T(8,128)S(1)}, f32[3,256,256]{2,1,0:T(8,128)S(1)}, u32[]{:S(2)}, u32[]{:S(2)}) collective-permute-start(f32[3,256,256]{2,1,0:T(8,128)S(1)} %bitcast.18), channel_id=1, source_target_pairs={{0,4},{4,0},{8,12},{12,8},{16,20},{20,16},{24,28},{28,24},{32,36},... | collective-permute-start | bytes 2359304 | tf_op jit(solution)/shard_map/ppermute | solution.py:45
  185.3 1.1 collective-permute-start.20
  186.5 1.6 collective-permute-start.19
  188.0 17.6 %collective-permute-done.21.n3 = f32[24,2,16,128]{3,2,1,0:T(8,128)S(1)} collective-permute-done((f32[24,2,16,128]{3,2,1,0:T(8,128)S(1)}, f32[24,2,16,128]{3,2,1,0:T(8,128)S(1)}, u32[]{:S(2)}, u32[]{:S(2)}) %collective-permute-start.21) | collective-permute-done | bytes 393248 | tf_op jit(solution)/shard_map/ppermute | solution.py:41
  205.7 0.3 collective-permute-done.19.n1
  205.9 0.4 copy-done.6
  206.4 0.2 copy-done.7
  206.5 0.7 copy-done.8
  207.3 3.7 %join_pieces.1 = f32[24,2,64,128]{3,2,1,0:T(8,128)} custom-call(s32[8]{0:T(128)} %stack.15.info, f32[24,2,16,128]{3,2,1,0:T(8,128)} %update.1.n0, f32[24,2,16,128]{3,2,1,0:T(8,128)} %copy-done.8, f32[24,2,16,128]{3,2,1,0:T(8,128)} %copy-done.7, f32[24,2,16,128]{3,2,1,0:T(8,128)} %copy-done.6), custom_call_target="tpu_custom_call" | custom-call | bytes 3000000 | tf_op jit(solution)/shard_map/join_pieces/pallas_call | solution.py:307
  211.0 0.9 copy-done.4
  211.9 3.4 %join_channels.1 = f32[3,2,256,256]{3,2,1,0:T(8,128)} custom-call(s32[8]{0:T(128)} %stack.15.info, f32[3,256,256]{2,1,0:T(8,128)} %bitcast.19, f32[3,256,256]{2,1,0:T(8,128)} %copy-done.4), custom_call_target="tpu_custom_call" | custom-call | bytes 3000000 | tf_op jit(solution)/shard_map/join_channels/pallas_call | solution.py:327
  (67 shorter events, 0.3 us)
Async XLA Ops:
  7.2 30.4 %reduce-scatter.2.cloned.1.call-start = ((), (), s32[]{:S(2)}) async-start(), calls=%async_computation.3 | async-start | bytes 327680 | tf_op jit(solution)/shard_map/reduce_scatter | solution.py:359
  8.8 1.2 slice-start
  8.8 2.5 %copy-start = (f32[24,2,64,128]{3,2,1,0:T(8,128)S(1)}, f32[24,2,64,128]{3,2,1,0:T(8,128)}, u32[]{:S(2)}) copy-start(f32[24,2,64,128]{3,2,1,0:T(8,128)} %pieces.1) | copy-start | bytes 4718596
  9.5 5.8 %copy-start.19 = (s32[2,2]{1,0:T(2,128)S(1)}, s32[2,2]{1,0:T(2,128)}, u32[]{:S(2)}) copy-start(s32[2,2]{1,0:T(2,128)} %param.10) | copy-start | bytes 52
  10.0 17.3 %collective-permute-start.1 = (f32[12,2,16,128]{3,2,1,0:T(8,128)S(1)}, f32[12,2,16,128]{3,2,1,0:T(8,128)S(1)}, u32[]{:S(2)}, u32[]{:S(2)}) collective-permute-start(f32[12,2,16,128]{3,2,1,0:T(8,128)S(1)} %constant_dynamic-slice_fusion), channel_id=1, source_target_pairs={{32,0},{36,4},{40,8},{44,12},{48,16},{52,20},{56,24},{60,28},{64,3... | collective-permute-start | bytes 589832 | tf_op jit(solution)/shard_map/ppermute | solution.py:37
  11.3 26.2 %collective-permute-start = (f32[6,2,64,128]{3,2,1,0:T(8,128)S(1)}, f32[6,2,64,128]{3,2,1,0:T(8,128)S(1)}, u32[]{:S(2)}, u32[]{:S(2)}) collective-permute-start(f32[6,2,64,128]{3,2,1,0:T(8,128)S(1)} %slice_bitcast_fusion), channel_id=1, source_target_pairs={{4,0},{8,4},{12,8},{16,12},{20,16},{24,20},{28,24},{32,28},{36,32}... | collective-permute-start | bytes 1179656 | tf_op jit(solution)/shard_map/ppermute | solution.py:37
  14.0 15.4 %collective-permute-start.2 = (f32[3,2,16,128]{3,2,1,0:T(8,128)S(1)}, f32[3,2,16,128]{3,2,1,0:T(8,128)S(1)}, u32[]{:S(2)}, u32[]{:S(2)}) collective-permute-start(f32[3,2,16,128]{3,2,1,0:T(8,128)S(1)} %slice.35), channel_id=1, source_target_pairs={{36,0},{40,4},{44,8},{48,12},{52,16},{56,20},{60,24},{64,28},{68,3... | collective-permute-start | bytes 147464 | tf_op jit(solution)/shard_map/ppermute | solution.py:37
  29.3 14.6 %copy-start.13 = (f32[15,2,16,128]{3,2,1,0:T(8,128)}, f32[15,2,16,128]{3,2,1,0:T(8,128)S(1)}, u32[]{:S(2)}) copy-start(f32[15,2,16,128]{3,2,1,0:T(8,128)S(1)} %constant_dynamic-update-slice_fusion.b0) | copy-start | bytes 737284
  29.3 14.6 %collective-permute-start.5 = (f32[15,2,16,128]{3,2,1,0:T(8,128)S(1)}, f32[15,2,16,128]{3,2,1,0:T(8,128)S(1)}, u32[]{:S(2)}, u32[]{:S(2)}) collective-permute-start(f32[15,2,16,128]{3,2,1,0:T(8,128)S(1)} %constant_dynamic-update-slice_fusion.b0), channel_id=1, source_target_pairs={{0,3},{1,0},{2,1},{3,2},{4,7},{5,4},{6,5},{7,6},{8,11},{9,8},{10,9... | collective-permute-start | bytes 737288 | tf_op jit(solution)/shard_map/ppermute | solution.py:41
  29.9 14.0 %collective-permute-start.4 = (f32[15,2,16,128]{3,2,1,0:T(8,128)S(1)}, f32[15,2,16,128]{3,2,1,0:T(8,128)S(1)}, u32[]{:S(2)}, u32[]{:S(2)}) collective-permute-start(f32[15,2,16,128]{3,2,1,0:T(8,128)S(1)} %constant_dynamic-update-slice_fusion.b0), channel_id=1, source_target_pairs={{0,2},{1,3},{2,0},{3,1},{4,6},{5,7},{6,4},{7,5},{8,10},{9,11},{10,... | collective-permute-start | bytes 737288 | tf_op jit(solution)/shard_map/ppermute | solution.py:41
  30.8 13.2 %collective-permute-start.3 = (f32[15,2,16,128]{3,2,1,0:T(8,128)S(1)}, f32[15,2,16,128]{3,2,1,0:T(8,128)S(1)}, u32[]{:S(2)}, u32[]{:S(2)}) collective-permute-start(f32[15,2,16,128]{3,2,1,0:T(8,128)S(1)} %constant_dynamic-update-slice_fusion.b0), channel_id=1, source_target_pairs={{0,1},{1,2},{2,3},{3,0},{4,5},{5,6},{6,7},{7,4},{8,9},{9,10},{10,1... | collective-permute-start | bytes 737288 | tf_op jit(solution)/shard_map/ppermute | solution.py:41
  37.6 6.4 %copy-start.20 = (f32[6,2,64,128]{3,2,1,0:T(8,128)}, f32[6,2,64,128]{3,2,1,0:T(8,128)S(1)}, u32[]{:S(2)}) copy-start(f32[6,2,64,128]{3,2,1,0:T(8,128)S(1)} %collective-permute-done.right) | copy-start | bytes 1179652
  43.9 0.7 copy-start.21
  43.9 0.8 copy-start.22
  44.7 0.7 copy-start.23
  53.7 5.9 %collective-permute-start.6 = (f32[2,64,256]{2,1,0:T(8,128)}, f32[2,64,256]{2,1,0:T(8,128)S(1)}, u32[]{:S(2)}, u32[]{:S(2)}) collective-permute-start(f32[2,64,256]{2,1,0:T(8,128)} %get-tuple-element.28), channel_id=1, source_target_pairs={{0,1},{1,2},{2,3},{3,0},{4,5},{5,6},{6,7},{7,4},{8,9},{9,10},{10,1... | collective-permute-start | bytes 393224 | tf_op jit(solution)/shard_map/ppermute | solution.py:41
  55.9 6.1 %collective-permute-start.7 = (f32[2,64,256]{2,1,0:T(8,128)}, f32[2,64,256]{2,1,0:T(8,128)S(1)}, u32[]{:S(2)}, u32[]{:S(2)}) collective-permute-start(f32[2,64,256]{2,1,0:T(8,128)} %get-tuple-element.29), channel_id=1, source_target_pairs={{0,2},{1,3},{2,0},{3,1},{4,6},{5,7},{6,4},{7,5},{8,10},{9,11},{10,... | collective-permute-start | bytes 393224 | tf_op jit(solution)/shard_map/ppermute | solution.py:41
  55.9 9.3 %collective-permute-start.8 = (f32[2,64,256]{2,1,0:T(8,128)}, f32[2,64,256]{2,1,0:T(8,128)S(1)}, u32[]{:S(2)}, u32[]{:S(2)}) collective-permute-start(f32[2,64,256]{2,1,0:T(8,128)} %get-tuple-element.30), channel_id=1, source_target_pairs={{0,3},{1,0},{2,1},{3,2},{4,7},{5,4},{6,5},{7,6},{8,11},{9,8},{10,9... | collective-permute-start | bytes 393224 | tf_op jit(solution)/shard_map/ppermute | solution.py:41
  66.3 8.8 %copy-start.5 = (f32[2,64,256]{2,1,0:T(8,128)}, f32[2,64,256]{2,1,0:T(8,128)S(1)}, u32[]{:S(2)}) copy-start(f32[2,64,256]{2,1,0:T(8,128)S(1)} %add_multiply_fusion.f0) | copy-start | bytes 393220
  66.3 8.7 %collective-permute-start.11 = (f32[2,64,256]{2,1,0:T(8,128)S(1)}, f32[2,64,256]{2,1,0:T(8,128)S(1)}, u32[]{:S(2)}, u32[]{:S(2)}) collective-permute-start(f32[2,64,256]{2,1,0:T(8,128)S(1)} %add_multiply_fusion.f0), channel_id=1, source_target_pairs={{0,3},{1,0},{2,1},{3,2},{4,7},{5,4},{6,5},{7,6},{8,11},{9,8},{10,9... | collective-permute-start | bytes 393224 | tf_op jit(solution)/shard_map/ppermute | solution.py:41
  66.4 8.7 %collective-permute-start.10 = (f32[2,64,256]{2,1,0:T(8,128)S(1)}, f32[2,64,256]{2,1,0:T(8,128)S(1)}, u32[]{:S(2)}, u32[]{:S(2)}) collective-permute-start(f32[2,64,256]{2,1,0:T(8,128)S(1)} %add_multiply_fusion.f0), channel_id=1, source_target_pairs={{0,2},{1,3},{2,0},{3,1},{4,6},{5,7},{6,4},{7,5},{8,10},{9,11},{10,... | collective-permute-start | bytes 393224 | tf_op jit(solution)/shard_map/ppermute | solution.py:41
  67.4 7.6 %collective-permute-start.9 = (f32[2,64,256]{2,1,0:T(8,128)S(1)}, f32[2,64,256]{2,1,0:T(8,128)S(1)}, u32[]{:S(2)}, u32[]{:S(2)}) collective-permute-start(f32[2,64,256]{2,1,0:T(8,128)S(1)} %add_multiply_fusion.f0), channel_id=1, source_target_pairs={{0,1},{1,2},{2,3},{3,0},{4,5},{5,6},{6,7},{7,4},{8,9},{9,10},{10,1... | collective-permute-start | bytes 393224 | tf_op jit(solution)/shard_map/ppermute | solution.py:41
  75.0 0.6 copy-start.14
  75.0 0.7 copy-start.15
  75.0 0.7 copy-start.16
  83.1 21.9 %copy-start.3 = (f32[3,256,256]{2,1,0:T(8,128)S(1)}, f32[3,256,256]{2,1,0:T(8,128)}, u32[]{:S(2)}) copy-start(f32[3,256,256]{2,1,0:T(8,128)} %get-tuple-element.31) | copy-start | bytes 2359300
  83.2 21.9 %collective-permute-start.12 = (f32[3,256,256]{2,1,0:T(8,128)}, f32[3,256,256]{2,1,0:T(8,128)S(1)}, u32[]{:S(2)}, u32[]{:S(2)}) collective-permute-start(f32[3,256,256]{2,1,0:T(8,128)} %get-tuple-element.32), channel_id=1, source_target_pairs={{0,4},{4,0},{8,12},{12,8},{16,20},{20,16},{24,28},{28,24},{32,36},... | collective-permute-start | bytes 2359304 | tf_op jit(solution)/shard_map/ppermute | solution.py:45
  85.0 8.4 %collective-permute-start.13 = (f32[2,8,2,16,128]{4,3,2,1,0:T(8,128)}, f32[2,8,2,16,128]{4,3,2,1,0:T(8,128)S(1)}, u32[]{:S(2)}, u32[]{:S(2)}) collective-permute-start(f32[2,8,2,16,128]{4,3,2,1,0:T(8,128)} %get-tuple-element.34), channel_id=1, source_target_pairs={{0,1},{1,2},{2,3},{3,0},{4,5},{5,6},{6,7},{7,4},{8,9},{9,10},{10,1... | collective-permute-start | bytes 786440 | tf_op jit(solution)/shard_map/ppermute | solution.py:41
  87.1 9.3 %collective-permute-start.14 = (f32[2,8,2,16,128]{4,3,2,1,0:T(8,128)}, f32[2,8,2,16,128]{4,3,2,1,0:T(8,128)S(1)}, u32[]{:S(2)}, u32[]{:S(2)}) collective-permute-start(f32[2,8,2,16,128]{4,3,2,1,0:T(8,128)} %get-tuple-element.35), channel_id=1, source_target_pairs={{0,2},{1,3},{2,0},{3,1},{4,6},{5,7},{6,4},{7,5},{8,10},{9,11},{10,... | collective-permute-start | bytes 786440 | tf_op jit(solution)/shard_map/ppermute | solution.py:41
  87.1 15.0 %collective-permute-start.15 = (f32[2,8,2,16,128]{4,3,2,1,0:T(8,128)}, f32[2,8,2,16,128]{4,3,2,1,0:T(8,128)S(1)}, u32[]{:S(2)}, u32[]{:S(2)}) collective-permute-start(f32[2,8,2,16,128]{4,3,2,1,0:T(8,128)} %get-tuple-element.36), channel_id=1, source_target_pairs={{0,3},{1,0},{2,1},{3,2},{4,7},{5,4},{6,5},{7,6},{8,11},{9,8},{10,9... | collective-permute-start | bytes 786440 | tf_op jit(solution)/shard_map/ppermute | solution.py:41
  93.4 8.7 %copy-start.9 = (f32[2,8,2,16,128]{4,3,2,1,0:T(8,128)}, f32[2,8,2,16,128]{4,3,2,1,0:T(8,128)S(1)}, u32[]{:S(2)}) copy-start(f32[2,8,2,16,128]{4,3,2,1,0:T(8,128)S(1)} %collective-permute-done.13.g1) | copy-start | bytes 786436
  96.4 5.7 %copy-start.10 = (f32[2,8,2,16,128]{4,3,2,1,0:T(8,128)}, f32[2,8,2,16,128]{4,3,2,1,0:T(8,128)S(1)}, u32[]{:S(2)}) copy-start(f32[2,8,2,16,128]{4,3,2,1,0:T(8,128)S(1)} %collective-permute-done.14.g2) | copy-start | bytes 786436
  102.1 0.7 copy-start.11
  105.0 12.2 %copy-start.24 = (f32[13,2,16,128]{3,2,1,0:T(8,128)S(1)}, f32[13,2,16,128]{3,2,1,0:T(8,128)}, u32[]{:S(2)}) copy-start(f32[13,2,16,128]{3,2,1,0:T(8,128)} %get-tuple-element.41) | copy-start | bytes 638980
  105.0 18.3 %copy-start.25 = (f32[7,2,16,128]{3,2,1,0:T(8,128)S(1)}, f32[7,2,16,128]{3,2,1,0:T(8,128)}, u32[]{:S(2)}) copy-start(f32[7,2,16,128]{3,2,1,0:T(8,128)} %get-tuple-element.40) | copy-start | bytes 344068
  105.0 22.0 %copy-start.26 = (f32[4,2,16,128]{3,2,1,0:T(8,128)S(1)}, f32[4,2,16,128]{3,2,1,0:T(8,128)}, u32[]{:S(2)}) copy-start(f32[4,2,16,128]{3,2,1,0:T(8,128)} %get-tuple-element.42) | copy-start | bytes 196612
  106.0 44.0 %all-to-all-start = ((f32[32,24,256]{2,1,0:T(8,128)}), f32[32,24,256]{2,1,0:T(8,128)S(1)}, u32[]{:S(2)}, u32[]{:S(2)}) async-start(f32[32,24,256]{2,1,0:T(8,128)} %bitcast.8), calls=%async_computation.1 | async-start | bytes 1572864 | tf_op jit(solution)/shard_map/all_to_all | solution.py:374
  117.2 29.1 %collective-permute-start.17 = (f32[13,2,16,128]{3,2,1,0:T(8,128)S(1)}, f32[13,2,16,128]{3,2,1,0:T(8,128)S(1)}, u32[]{:S(2)}, u32[]{:S(2)}) collective-permute-start(f32[13,2,16,128]{3,2,1,0:T(8,128)S(1)} %copy-done.24), channel_id=1, source_target_pairs={{0,32},{4,36},{8,40},{12,44},{16,48},{20,52},{24,56},{28,60},{32,6... | collective-permute-start | bytes 638984 | tf_op jit(solution)/shard_map/ppermute | solution.py:37
  123.3 22.9 %collective-permute-start.16 = (f32[7,2,16,128]{3,2,1,0:T(8,128)S(1)}, f32[7,2,16,128]{3,2,1,0:T(8,128)S(1)}, u32[]{:S(2)}, u32[]{:S(2)}) collective-permute-start(f32[7,2,16,128]{3,2,1,0:T(8,128)S(1)} %copy-done.25), channel_id=1, source_target_pairs={{0,4},{4,8},{8,12},{12,16},{16,20},{20,24},{24,28},{28,32},{32,36}... | collective-permute-start | bytes 344072 | tf_op jit(solution)/shard_map/ppermute | solution.py:37
  127.0 19.3 %collective-permute-start.18 = (f32[4,2,16,128]{3,2,1,0:T(8,128)S(1)}, f32[4,2,16,128]{3,2,1,0:T(8,128)S(1)}, u32[]{:S(2)}, u32[]{:S(2)}) collective-permute-start(f32[4,2,16,128]{3,2,1,0:T(8,128)S(1)} %copy-done.26), channel_id=1, source_target_pairs={{0,36},{4,40},{8,44},{12,48},{16,52},{20,56},{24,60},{28,64},{32,6... | collective-permute-start | bytes 196616 | tf_op jit(solution)/shard_map/ppermute | solution.py:37
  146.3 0.6 copy-start.18
  146.3 0.7 copy-start.17
  146.3 0.7 copy-start.12
  150.0 35.3 %copy-start.2 = (f32[24,2,16,128]{3,2,1,0:T(8,128)S(1)}, f32[24,2,16,128]{3,2,1,0:T(8,128)}, u32[]{:S(2)}) copy-start(f32[24,2,16,128]{3,2,1,0:T(8,128)} %update.1.n0) | copy-start | bytes 1179652
  182.7 28.2 %copy-start.1 = (f32[32,24,256]{2,1,0:T(8,128)}, f32[32,24,256]{2,1,0:T(8,128)S(1)}, u32[]{:S(2)}) copy-start(f32[32,24,256]{2,1,0:T(8,128)S(1)} %all_to_all.10) | copy-start | bytes 2359300
  182.7 28.2 %collective-permute-start.22 = (f32[3,256,256]{2,1,0:T(8,128)S(1)}, f32[3,256,256]{2,1,0:T(8,128)S(1)}, u32[]{:S(2)}, u32[]{:S(2)}) collective-permute-start(f32[3,256,256]{2,1,0:T(8,128)S(1)} %bitcast.18), channel_id=1, source_target_pairs={{0,4},{4,0},{8,12},{12,8},{16,20},{20,16},{24,28},{28,24},{32,36},... | collective-permute-start | bytes 2359304 | tf_op jit(solution)/shard_map/ppermute | solution.py:45
  185.3 20.3 %collective-permute-start.21 = (f32[24,2,16,128]{3,2,1,0:T(8,128)S(1)}, f32[24,2,16,128]{3,2,1,0:T(8,128)S(1)}, u32[]{:S(2)}, u32[]{:S(2)}) collective-permute-start(f32[24,2,16,128]{3,2,1,0:T(8,128)S(1)} %copy-done.2), channel_id=1, source_target_pairs={{0,3},{1,0},{2,1},{3,2},{4,7},{5,4},{6,5},{7,6},{8,11},{9,8},{10,9... | collective-permute-start | bytes 1179656 | tf_op jit(solution)/shard_map/ppermute | solution.py:41
  185.3 20.3 %collective-permute-start.20 = (f32[24,2,16,128]{3,2,1,0:T(8,128)S(1)}, f32[24,2,16,128]{3,2,1,0:T(8,128)S(1)}, u32[]{:S(2)}, u32[]{:S(2)}) collective-permute-start(f32[24,2,16,128]{3,2,1,0:T(8,128)S(1)} %copy-done.2), channel_id=1, source_target_pairs={{0,2},{1,3},{2,0},{3,1},{4,6},{5,7},{6,4},{7,5},{8,10},{9,11},{10,... | collective-permute-start | bytes 1179656 | tf_op jit(solution)/shard_map/ppermute | solution.py:41
  186.5 19.5 %collective-permute-start.19 = (f32[24,2,16,128]{3,2,1,0:T(8,128)S(1)}, f32[24,2,16,128]{3,2,1,0:T(8,128)S(1)}, u32[]{:S(2)}, u32[]{:S(2)}) collective-permute-start(f32[24,2,16,128]{3,2,1,0:T(8,128)S(1)} %copy-done.2), channel_id=1, source_target_pairs={{0,1},{1,2},{2,3},{3,0},{4,5},{5,6},{6,7},{7,4},{8,9},{9,10},{10,1... | collective-permute-start | bytes 1179656 | tf_op jit(solution)/shard_map/ppermute | solution.py:41
  205.6 0.7 copy-start.6
  205.7 0.9 copy-start.7
  206.5 0.7 copy-start.8
  211.0 0.9 copy-start.4
Sparse Core Ops, SparseCore 0:
  11.1 22.0 reduce-scatter.1

commit v3 on v2

--- a/solution.py
+++ b/solution.py
@@ -296,40 +296,62 @@
     )(info, pieces, own, right, low, corner, light)
 
 
-def join_pieces_kernel(info, n0, n1, n2, n3, out):
-    for j, part in enumerate((n0, n1, n2, n3)):
+def join_pieces_kernel(info, n0, n1, n2, n3, out, held, in_sems, out_sems):
+    parts = (n0, n1, n2, n3)
+    reads = [pltpu.make_async_copy(part, held.at[j], in_sems.at[j]) for j, part in enumerate(parts)]
+    for read in reads:
+        read.start()
+    writes = []
+    for j, read in enumerate(reads):
         start = pl.multiple_of(lax.rem(info[5] + N_MODE - j, N_MODE) * SUB, SUB)
-        out[:, :, pl.ds(start, SUB), :] = part[...]
+        read.wait()
+        writes.append(pltpu.make_async_copy(
+            held.at[j], out.at[:, :, pl.ds(start, SUB), :], out_sems.at[j]))
+        writes[j].start()
+    for write in writes:
+        write.wait()
 
 
 def join_pieces(info, parts):
-    block = lambda rows: pl.BlockSpec((6, 2, rows, PIECE_C), lambda i: (i, 0, 0, 0))
     return pl.pallas_call(
         join_pieces_kernel,
-        grid=(4,),
-        in_specs=[SMEM] + [block(SUB)] * 4,
-        out_specs=block(PIECE_R),
+        in_specs=[SMEM] + [ANY] * 4,
+        out_specs=pl.BlockSpec(memory_space=pltpu.HBM),
         out_shape=jax.ShapeDtypeStruct((TILE_R * TILE_C, 2, PIECE_R, PIECE_C), F32),
+        scratch_shapes=[pltpu.VMEM((N_MODE, TILE_R * TILE_C, 2, SUB, PIECE_C), F32),
+                        pltpu.SemaphoreType.DMA((N_MODE,)), pltpu.SemaphoreType.DMA((N_MODE,))],
         compiler_params=pltpu.CompilerParams(vmem_limit_bytes=VMEM_BYTES),
         cost_estimate=pl.CostEstimate(flops=0, bytes_accessed=3000000, transcendentals=0),
         name="join_pieces",
     )(info, *parts)
 
 
-def join_channels_kernel(info, mine, theirs, out):
+def join_channels_kernel(info, mine, theirs, out, held, in_sems, out_sems):
     core = info[6]
-    out[0, core] = mine[0]
-    out[0, 1 - core] = theirs[0]
+    steps = [(source, half, k) for k in range(3) for half, source in enumerate((mine, theirs))]
+    reads = [pltpu.make_async_copy(source.at[k], held.at[half, k], in_sems.at[half, k])
+             for source, half, k in steps]
+    for read in reads:
+        read.start()
+    writes = []
+    for (source, half, k), read in zip(steps, reads):
+        read.wait()
+        channel = core if half == 0 else 1 - core
+        writes.append(pltpu.make_async_copy(
+            held.at[half, k], out.at[k, channel], out_sems.at[half, k]))
+        writes[-1].start()
+    for write in writes:
+        write.wait()
 
 
 def join_channels(info, mine, theirs):
-    block = pl.BlockSpec((1, SIDE, SIDE), lambda k: (k, 0, 0))
     return pl.pallas_call(
         join_channels_kernel,
-        grid=(3,),
-        in_specs=[SMEM, block, block],
-        out_specs=pl.BlockSpec((1, 2, SIDE, SIDE), lambda k: (k, 0, 0, 0)),
+        in_specs=[SMEM, ANY, ANY],
+        out_specs=pl.BlockSpec(memory_space=pltpu.HBM),
         out_shape=jax.ShapeDtypeStruct((3, 2, SIDE, SIDE), F32),
+        scratch_shapes=[pltpu.VMEM((2, 3, SIDE, SIDE), F32),
+                        pltpu.SemaphoreType.DMA((2, 3)), pltpu.SemaphoreType.DMA((2, 3))],
         compiler_params=pltpu.CompilerParams(vmem_limit_bytes=VMEM_BYTES),
         cost_estimate=pl.CostEstimate(flops=0, bytes_accessed=3000000, transcendentals=0),
         name="join_channels",
@@ -369,24 +391,25 @@
 
     mine, theirs, *grads = backward(info, far, probe_modes, patch, factors, tables)
 
-    parts = [grads[0]] + [turned(grads[j], j) for j in (1, 2, 3)]
     groups = [list(range(core, N_TILE, 2)) for core in range(2)]
     exchange = lambda blocks: lax.all_to_all(
         blocks, "tile", 0, 0, axis_index_groups=groups, tiled=True)
     summed = mine + core_swap(theirs)
+    pieces = exchange(summed.reshape(N_CHIP, PART, SIDE))
+    parts = [grads[0]] + [turned(grads[j], j) for j in (1, 2, 3)]
     own, to_right, to_low, to_corner = scatter(info, parts)
-    summed, own = lax.optimization_barrier((summed, own))
-    pieces = exchange(summed.reshape(N_CHIP, PART, SIDE))
-
     from_above = shifted(to_low, "tile", DEV_COLS)
     from_corner = shifted(to_corner, "tile", DEV_COLS + 1)
     from_left = shifted(to_right, "tile", 1)
+    pieces, from_left, from_above, from_corner = lax.optimization_barrier(
+        (pieces, from_left, from_above, from_corner))
+    share = jnp.sum(pieces, axis=0)
 
     new = update(info, object_pieces, own, from_left, from_above, from_corner, light[0])
-    share = jnp.sum(pieces, axis=0)
     share, new = lax.optimization_barrier((share, new))
     gathered = exchange(jnp.broadcast_to(share[None], (N_CHIP, PART, SIDE)))
     new_parts = [new] + [turned(new, j) for j in (1, 2, 3)]
+    gathered, *new_parts = lax.optimization_barrier((gathered, *new_parts))
     gathered = gathered.reshape(3, SIDE, SIDE)
     probe_grad = join_channels(info, gathered, core_swap(gathered))
     return (join_pieces(info, new_parts), probe_grad)

time: 225 us -> 195 us (0.87)
  blocking collectives: 32.6 us -> 0 us
  starting transfers between devices: 48.6 us -> 58.8 us
  waiting for transfers between devices: 82.7 us -> 75.9 us
    all_to_all x1 -> x0, blocking collectives: 32.6 us -> none  [body(): lax.all_to_all(blocks, 'tile', 0, 0, axis_index_groups=groups, tiled=True)]
    all_to_all x1 -> x2, starting transfers between devices: 11.1 us -> 21.8 us  [body(): lax.all_to_all(blocks, 'tile', 0, 0, axis_index_groups=groups, tiled=True)]
    ppermute x6, waiting for transfers between devices: 29.4 us -> 19.7 us  [shifted(): return lax.ppermute(block, axis, route)]
    unnamed x55 -> x53, local copies, waits for them, and re-layouts: 5.84 us -> 4.5 us
  transfers between devices with their start and end apart: 25 -> 26, of which waited for: 13 -> 16; matrix products, arithmetic and copies ran while one was open for 2% -> 2% of each run, Pallas kernels for 4% -> 3%
where the time goes in v3:
time: 195 us; the launch traced here: 193 us
  waiting for transfers between devices  75.9 us (39%)
  starting transfers between devices  58.8 us (30%)
  Pallas kernels  26.7 us (14%)
  between operations  15.1 us (8%)
  local copies, waits for them, and re-layouts  11.4 us (6%)
  other arithmetic  4.85 us (2%)
    ppermute x15, waiting for transfers between devices, turned(): lax.ppermute(block, 'mode', [(i, (i + distance) % N_MODE) for i in range(...  52 us
    all_to_all x2, starting transfers between devices, body(): lax.all_to_all(blocks, 'tile', 0, 0, axis_index_groups=groups, tiled=True)  21.8 us
    ppermute x6, waiting for transfers between devices, shifted(): return lax.ppermute(block, axis, route)  19.7 us
    ppermute x6, starting transfers between devices, shifted(): return lax.ppermute(block, axis, route)  18 us
    ppermute x15, starting transfers between devices, turned(): lax.ppermute(block, 'mode', [(i, (i + distance) % N_MODE) for i in range(...  14.7 us
    pallas_call x1, Pallas kernels, forward(): pl.pallas_call(forward_kernel, grid=(3,), in_specs=[SMEM] + [ANY] * 6 + [...  8.3 us
    pallas_call x1, Pallas kernels, backward(): pl.pallas_call(backward_kernel, grid=(3,), in_specs=[SMEM, pl.BlockSpec((...  7.42 us
    unnamed x53, local copies, waits for them, and re-layouts  4.5 us
  transfers between devices with their start and end apart: 26, of which 16 were waited for; matrix products, arithmetic and copies ran while one was open for 2% of the time, Pallas kernels for 3%

profile of v3, /device:TPU:39, one launch (start us, length us, event | category | flops | bytes accessed | tf_op | source)
XLA Modules:
  0.0 192.7 jit_solution(675163131702500911)
XLA Ops:
  7.2 1.5 multiply_reduce_fusion
  8.8 0.7 copy.13
  9.5 0.5 slice-done
  10.0 1.3 collective-permute-start.1
  11.3 2.6 %collective-permute-start = (f32[6,2,64,128]{3,2,1,0:T(8,128)S(1)}, f32[6,2,64,128]{3,2,1,0:T(8,128)S(1)}, u32[]{:S(2)}, u32[]{:S(2)}) collective-permute-start(f32[6,2,64,128]{3,2,1,0:T(8,128)S(1)} %slice_bitcast_fusion), channel_id=1, source_target_pairs={{4,0},{8,4},{12,8},{16,12},{20,16},{24,20},{28,24},{32,28},{36,32}... | collective-permute-start | bytes 1179656 | tf_op jit(solution)/shard_map/ppermute | solution.py:37
  14.0 1.3 collective-permute-start.2
  15.3 0.2 slice_reduce_fusion
  15.5 11.8 %collective-permute-done.1 = f32[12,2,16,128]{3,2,1,0:T(8,128)S(1)} collective-permute-done((f32[12,2,16,128]{3,2,1,0:T(8,128)S(1)}, f32[12,2,16,128]{3,2,1,0:T(8,128)S(1)}, u32[]{:S(2)}, u32[]{:S(2)}) %collective-permute-start.1) | collective-permute-done | bytes 196640 | tf_op jit(solution)/shard_map/ppermute | solution.py:37
  27.3 2.0 %collective-permute-done.2 = f32[3,2,16,128]{3,2,1,0:T(8,128)S(1)} collective-permute-done((f32[3,2,16,128]{3,2,1,0:T(8,128)S(1)}, f32[3,2,16,128]{3,2,1,0:T(8,128)S(1)}, u32[]{:S(2)}, u32[]{:S(2)}) %collective-permute-start.2) | collective-permute-done | bytes 49184 | tf_op jit(solution)/shard_map/ppermute | solution.py:37
  29.3 0.6 collective-permute-start.5
  29.9 0.8 collective-permute-start.4
  30.8 1.8 collective-permute-start.3
  33.3 0.6 fusion
  33.9 0.6 fusion.1
  34.5 3.2 %stack.15.info = s32[8]{0:T(128)} concatenate(s32[1]{0:T(128)} %get-tuple-element.65, s32[1]{0:T(128)} %get-tuple-element.63, s32[1]{0:T(128)} %get-tuple-element.64, s32[1]{0:T(128)} %get-tuple-element.62, s32[1]{0:T(128)} %copy.15, s32[1]{0:T(128)} %bitcast, s32[1]{0:T(128)} %bitcast.1, s32[1]{0:T(128)} %bitcast.2), dimensions={0} | concatenate | bytes 64 | tf_op jit(solution)/shard_map/stack | solution.py:375
  37.8 6.2 %collective-permute-done.5.b3 = f32[15,2,16,128]{3,2,1,0:T(8,128)S(1)} collective-permute-done((f32[15,2,16,128]{3,2,1,0:T(8,128)S(1)}, f32[15,2,16,128]{3,2,1,0:T(8,128)S(1)}, u32[]{:S(2)}, u32[]{:S(2)}) %collective-permute-start.5) | collective-permute-done | bytes 245792 | tf_op jit(solution)/shard_map/ppermute | solution.py:41
  44.0 0.7 copy-done.23
  44.6 0.1 copy-done.24
  44.7 0.7 copy-done.25
  45.4 8.3 %forward.1 = (f32[2,3,2,256,256]{4,3,2,1,0:T(8,128)}, f32[2,2,256,256]{3,2,1,0:T(8,128)}, f32[2,64,256]{2,1,0:T(8,128)}, f32[2,64,256]{2,1,0:T(8,128)}, f32[2,64,256]{2,1,0:T(8,128)}, /*index=5*/f32[2,64,256]{2,1,0:T(8,128)}) custom-call(s32[8]{0:T(128)} %stack.15.info, f32[24,2,64,128]{3,2,1,0:T(8,128)} %pieces.1, f32[6,2,64,128]{3,2,1,0:T(8,128)} %copy-done.19, ...), custom_call_target="tpu_custom_call" | custom-call | flops 1700000000 | bytes 12000000 | tf_op jit(solution)/shard_map/forward/pallas_call | solution.py:127
  53.7 2.2 %collective-permute-start.6 = (f32[2,64,256]{2,1,0:T(8,128)}, f32[2,64,256]{2,1,0:T(8,128)S(1)}, u32[]{:S(2)}, u32[]{:S(2)}) collective-permute-start(f32[2,64,256]{2,1,0:T(8,128)} %get-tuple-element.35), channel_id=1, source_target_pairs={{0,1},{1,2},{2,3},{3,0},{4,5},{5,6},{6,7},{7,4},{8,9},{9,10},{10,1... | collective-permute-start | bytes 393224 | tf_op jit(solution)/shard_map/ppermute | solution.py:41
  55.9 0.7 collective-permute-start.8
  56.6 2.9 %collective-permute-done.6 = f32[2,64,256]{2,1,0:T(8,128)S(1)} collective-permute-done((f32[2,64,256]{2,1,0:T(8,128)}, f32[2,64,256]{2,1,0:T(8,128)S(1)}, u32[]{:S(2)}, u32[]{:S(2)}) %collective-permute-start.6) | collective-permute-done | bytes 131104 | tf_op jit(solution)/shard_map/ppermute | solution.py:41
  59.6 2.5 %collective-permute-done.7 = f32[2,64,256]{2,1,0:T(8,128)S(1)} collective-permute-done((f32[2,64,256]{2,1,0:T(8,128)}, f32[2,64,256]{2,1,0:T(8,128)S(1)}, u32[]{:S(2)}, u32[]{:S(2)}) %collective-permute-start.7) | collective-permute-done | bytes 131104 | tf_op jit(solution)/shard_map/ppermute | solution.py:41
  62.0 3.2 %collective-permute-done.8 = f32[2,64,256]{2,1,0:T(8,128)S(1)} collective-permute-done((f32[2,64,256]{2,1,0:T(8,128)}, f32[2,64,256]{2,1,0:T(8,128)S(1)}, u32[]{:S(2)}, u32[]{:S(2)}) %collective-permute-start.8) | collective-permute-done | bytes 131104 | tf_op jit(solution)/shard_map/ppermute | solution.py:41
  65.2 1.0 add_multiply_fusion.f0
  66.3 0.1 collective-permute-start.11
  66.4 1.1 collective-permute-start.10
  67.5 1.6 collective-permute-start.9
  69.1 6.0 %collective-permute-done.11.f3 = f32[2,64,256]{2,1,0:T(8,128)S(1)} collective-permute-done((f32[2,64,256]{2,1,0:T(8,128)S(1)}, f32[2,64,256]{2,1,0:T(8,128)S(1)}, u32[]{:S(2)}, u32[]{:S(2)}) %collective-permute-start.11) | collective-permute-done | bytes 131104 | tf_op jit(solution)/shard_map/ppermute | solution.py:41
  75.1 0.6 copy-done.13
  75.8 7.4 %backward.1 = (f32[3,256,256]{2,1,0:T(8,128)}, f32[3,256,256]{2,1,0:T(8,128)}, f32[2,8,2,16,128]{4,3,2,1,0:T(8,128)}, f32[2,8,2,16,128]{4,3,2,1,0:T(8,128)}, f32...) custom-call(s32[8]{0:T(128)} %stack.15.info, f32[2,3,2,256,256]{4,3,2,1,0:T(8,128)} %get-tuple-element.32.far, ...), custom_call_target="tpu_custom_call" | custom-call | flops 1700000000 | bytes 12000000 | tf_op jit(solution)/shard_map/backward/pallas_call | solution.py:190
  83.2 1.9 collective-permute-start.12
  85.1 2.1 %collective-permute-done.12 = f32[3,256,256]{2,1,0:T(8,128)S(1)} collective-permute-done((f32[3,256,256]{2,1,0:T(8,128)}, f32[3,256,256]{2,1,0:T(8,128)S(1)}, u32[]{:S(2)}, u32[]{:S(2)}) %collective-permute-start.12) | collective-permute-done | bytes 786464 | tf_op jit(solution)/shard_map/ppermute | solution.py:45
  87.2 2.2 %add.46 = f32[3,256,256]{2,1,0:T(8,128)} add(f32[3,256,256]{2,1,0:T(8,128)} %get-tuple-element.38, f32[3,256,256]{2,1,0:T(8,128)S(1)} %collective-permute-done.12) | non-fusion elementwise | flops 196608 | bytes 2359296 | tf_op jit(solution)/shard_map/add | solution.py:397
  89.4 11.1 %all-to-all-start = ((f32[32,24,256]{2,1,0:T(8,128)}), f32[32,24,256]{2,1,0:T(8,128)S(1)}, u32[]{:S(2)}, u32[]{:S(2)}) async-start(f32[32,24,256]{2,1,0:T(8,128)} %bitcast.8), calls=%async_computation.1 | async-start | bytes 1572864 | tf_op jit(solution)/shard_map/all_to_all | solution.py:395
  100.6 2.3 %collective-permute-start.13 = (f32[2,8,2,16,128]{4,3,2,1,0:T(8,128)S(1)}, f32[2,8,2,16,128]{4,3,2,1,0:T(8,128)S(1)}, u32[]{:S(2)}, u32[]{:S(2)}) collective-permute-start(f32[2,8,2,16,128]{4,3,2,1,0:T(8,128)S(1)} %copy-done.22), channel_id=1, source_target_pairs={{0,1},{1,2},{2,3},{3,0},{4,5},{5,6},{6,7},{7,4},{8,9},{9,10},{10,1... | collective-permute-start | bytes 786440 | tf_op jit(solution)/shard_map/ppermute | solution.py:41
  102.9 0.7 collective-permute-start.15
  103.6 4.4 %collective-permute-done.13.g1 = f32[2,8,2,16,128]{4,3,2,1,0:T(8,128)S(1)} collective-permute-done((f32[2,8,2,16,128]{4,3,2,1,0:T(8,128)S(1)}, f32[2,8,2,16,128]{4,3,2,1,0:T(8,128)S(1)}, u32[]{:S(2)}, u32[]{:S(2)}) %collective-permute-start.13) | collective-permute-done | bytes 262176 | tf_op jit(solution)/shard_map/ppermute | solution.py:41
  107.9 3.1 %collective-permute-done.14.g2 = f32[2,8,2,16,128]{4,3,2,1,0:T(8,128)S(1)} collective-permute-done((f32[2,8,2,16,128]{4,3,2,1,0:T(8,128)S(1)}, f32[2,8,2,16,128]{4,3,2,1,0:T(8,128)S(1)}, u32[]{:S(2)}, u32[]{:S(2)}) %collective-permute-start.14) | collective-permute-done | bytes 262176 | tf_op jit(solution)/shard_map/ppermute | solution.py:41
  111.1 6.8 %collective-permute-done.15.g3 = f32[2,8,2,16,128]{4,3,2,1,0:T(8,128)S(1)} collective-permute-done((f32[2,8,2,16,128]{4,3,2,1,0:T(8,128)S(1)}, f32[2,8,2,16,128]{4,3,2,1,0:T(8,128)S(1)}, u32[]{:S(2)}, u32[]{:S(2)}) %collective-permute-start.15) | collective-permute-done | bytes 262176 | tf_op jit(solution)/shard_map/ppermute | solution.py:41
  117.8 0.7 copy-done.10
  118.5 2.2 %scatter.1 = (f32[24,2,16,128]{3,2,1,0:T(8,128)}, f32[7,2,16,128]{3,2,1,0:T(8,128)}, f32[13,2,16,128]{3,2,1,0:T(8,128)}, f32[4,2,16,128]{3,2,1,0:T(8,128)}) custom-call(s32[8]{0:T(128)} %stack.15.info, f32[2,8,2,16,128]{4,3,2,1,0:T(8,128)} %get-tuple-element.40.g0, f32[2,8,2,16,128]{4,3,2,1,0:T(8,128)} %copy-done.8, f32[2,8,2,16,128]{4,3,2,1,0:T(8,128)} %copy-done.9, ...), custom_call_target="tpu_custom_call" | custom-call | flops 1000000 | bytes 2000000 | tf_op jit(solution)/shard_map/scatter/pallas_call | solution.py:227
  120.7 6.1 %collective-permute-start.17 = (f32[13,2,16,128]{3,2,1,0:T(8,128)}, f32[13,2,16,128]{3,2,1,0:T(8,128)S(1)}, u32[]{:S(2)}, u32[]{:S(2)}) collective-permute-start(f32[13,2,16,128]{3,2,1,0:T(8,128)} %get-tuple-element.45), channel_id=1, source_target_pairs={{0,32},{4,36},{8,40},{12,44},{16,48},{20,52},{24,56},{28,60},{32,6... | collective-permute-start | bytes 638984 | tf_op jit(solution)/shard_map/ppermute | solution.py:37
  126.8 3.1 %collective-permute-start.16 = (f32[7,2,16,128]{3,2,1,0:T(8,128)}, f32[7,2,16,128]{3,2,1,0:T(8,128)S(1)}, u32[]{:S(2)}, u32[]{:S(2)}) collective-permute-start(f32[7,2,16,128]{3,2,1,0:T(8,128)} %get-tuple-element.44), channel_id=1, source_target_pairs={{0,4},{4,8},{8,12},{12,16},{16,20},{20,24},{24,28},{28,32},{32,36}... | collective-permute-start | bytes 344072 | tf_op jit(solution)/shard_map/ppermute | solution.py:37
  129.9 3.7 %collective-permute-start.18 = (f32[4,2,16,128]{3,2,1,0:T(8,128)}, f32[4,2,16,128]{3,2,1,0:T(8,128)S(1)}, u32[]{:S(2)}, u32[]{:S(2)}) collective-permute-start(f32[4,2,16,128]{3,2,1,0:T(8,128)} %get-tuple-element.46), channel_id=1, source_target_pairs={{0,36},{4,40},{8,44},{12,48},{16,52},{20,56},{24,60},{28,64},{32,6... | collective-permute-start | bytes 196616 | tf_op jit(solution)/shard_map/ppermute | solution.py:37
  133.6 5.8 %collective-permute-done.18.corner = f32[4,2,16,128]{3,2,1,0:T(8,128)S(1)} collective-permute-done((f32[4,2,16,128]{3,2,1,0:T(8,128)}, f32[4,2,16,128]{3,2,1,0:T(8,128)S(1)}, u32[]{:S(2)}, u32[]{:S(2)}) %collective-permute-start.18) | collective-permute-done | bytes 65568 | tf_op jit(solution)/shard_map/ppermute | solution.py:37
  139.5 0.1 reduce_sum.19
  139.6 0.5 copy-done.17
  140.1 0.1 copy-done.11
  140.2 3.1 %update.1.n0 = f32[24,2,16,128]{3,2,1,0:T(8,128)} custom-call(s32[8]{0:T(128)} %stack.15.info, f32[24,2,64,128]{3,2,1,0:T(8,128)} %pieces.1, f32[24,2,16,128]{3,2,1,0:T(8,128)} %get-tuple-element.48.own, f32[7,2,16,128]{3,2,1,0:T(8,128)} %copy-done.16, f32[13,2,16,128]{3,2,1,0:T(8,128)} %copy-done.11, f32[4,2,16,128]{3,2,1,0:T(8,128)} %copy-done.17, ...), custom_call_target="tpu_custom_call" | custom-call | flops 1000000 | bytes 2000000 | tf_op jit(solution)/shard_map/update/pallas_call | solution.py:286
  143.4 0.9 broadcast_in_dim.2
  144.3 10.7 %all-to-all-start.1 = ((f32[32,24,256]{2,1,0:T(8,128)}), f32[32,24,256]{2,1,0:T(8,128)S(1)}, u32[]{:S(2)}, u32[]{:S(2)}) async-start(f32[32,24,256]{2,1,0:T(8,128)} %broadcast_in_dim.2), calls=%async_computation.2 | async-start | bytes 1572864 | tf_op jit(solution)/shard_map/all_to_all | solution.py:395
  155.0 0.1 collective-permute-start.21
  155.1 1.4 collective-permute-start.20
  156.5 1.3 collective-permute-start.19
  157.8 9.8 %collective-permute-done.21.n3 = f32[24,2,16,128]{3,2,1,0:T(8,128)S(1)} collective-permute-done((f32[24,2,16,128]{3,2,1,0:T(8,128)S(1)}, f32[24,2,16,128]{3,2,1,0:T(8,128)S(1)}, u32[]{:S(2)}, u32[]{:S(2)}) %collective-permute-start.21) | collective-permute-done | bytes 393248 | tf_op jit(solution)/shard_map/ppermute | solution.py:41
  167.5 5.4 %collective-permute-done.20.n2 = f32[24,2,16,128]{3,2,1,0:T(8,128)S(1)} collective-permute-done((f32[24,2,16,128]{3,2,1,0:T(8,128)S(1)}, f32[24,2,16,128]{3,2,1,0:T(8,128)S(1)}, u32[]{:S(2)}, u32[]{:S(2)}) %collective-permute-start.20) | collective-permute-done | bytes 393248 | tf_op jit(solution)/shard_map/ppermute | solution.py:41
  172.9 1.8 collective-permute-done.19.n1
  174.8 2.0 %all-to-all-done.1 = f32[32,24,256]{2,1,0:T(8,128)S(1)} async-done(((f32[32,24,256]{2,1,0:T(8,128)}), f32[32,24,256]{2,1,0:T(8,128)S(1)}, u32[]{:S(2)}, u32[]{:S(2)}) %all-to-all-start.1) | async-done | bytes 786464 | tf_op jit(solution)/shard_map/all_to_all | solution.py:395
  176.8 2.4 %collective-permute-start.22 = (f32[3,256,256]{2,1,0:T(8,128)S(1)}, f32[3,256,256]{2,1,0:T(8,128)S(1)}, u32[]{:S(2)}, u32[]{:S(2)}) collective-permute-start(f32[3,256,256]{2,1,0:T(8,128)S(1)} %bitcast.18), channel_id=1, source_target_pairs={{0,4},{4,0},{8,12},{12,8},{16,20},{20,16},{24,28},{28,24},{32,36},... | collective-permute-start | bytes 2359304 | tf_op jit(solution)/shard_map/ppermute | solution.py:45
  179.2 2.9 %join_pieces.1 = f32[24,2,64,128]{3,2,1,0:T(8,128)} custom-call(s32[8]{0:T(128)} %stack.15.info, f32[24,2,16,128]{3,2,1,0:T(8,128)} %update.1.n0, f32[24,2,16,128]{3,2,1,0:T(8,128)} %copy-done.7, f32[24,2,16,128]{3,2,1,0:T(8,128)} %copy-done.6, f32[24,2,16,128]{3,2,1,0:T(8,128)} %copy-done.5), custom_call_target="tpu_custom_call" | custom-call | bytes 3000000 | tf_op jit(solution)/shard_map/join_pieces/pallas_call | solution.py:316
  182.1 0.9 copy-done.3
  183.0 2.8 %join_channels.1 = f32[3,2,256,256]{3,2,1,0:T(8,128)} custom-call(s32[8]{0:T(128)} %stack.15.info, f32[3,256,256]{2,1,0:T(8,128)} %bitcast.19, f32[3,256,256]{2,1,0:T(8,128)} %copy-done.3), custom_call_target="tpu_custom_call" | custom-call | bytes 3000000 | tf_op jit(solution)/shard_map/join_channels/pallas_call | solution.py:348
  (66 shorter events, 0.4 us)
Async XLA Ops:
  7.2 30.6 %reduce-scatter.2.cloned.1.call-start = ((), (), s32[]{:S(2)}) async-start(), calls=%async_computation.3 | async-start | bytes 327680 | tf_op jit(solution)/shard_map/reduce_scatter | solution.py:381
  8.8 1.2 slice-start
  8.8 2.5 %copy-start = (f32[24,2,64,128]{3,2,1,0:T(8,128)S(1)}, f32[24,2,64,128]{3,2,1,0:T(8,128)}, u32[]{:S(2)}) copy-start(f32[24,2,64,128]{3,2,1,0:T(8,128)} %pieces.1) | copy-start | bytes 4718596
  9.5 5.8 %copy-start.18 = (s32[2,2]{1,0:T(2,128)S(1)}, s32[2,2]{1,0:T(2,128)}, u32[]{:S(2)}) copy-start(s32[2,2]{1,0:T(2,128)} %param.10) | copy-start | bytes 52
  10.0 17.3 %collective-permute-start.1 = (f32[12,2,16,128]{3,2,1,0:T(8,128)S(1)}, f32[12,2,16,128]{3,2,1,0:T(8,128)S(1)}, u32[]{:S(2)}, u32[]{:S(2)}) collective-permute-start(f32[12,2,16,128]{3,2,1,0:T(8,128)S(1)} %constant_dynamic-slice_fusion), channel_id=1, source_target_pairs={{32,0},{36,4},{40,8},{44,12},{48,16},{52,20},{56,24},{60,28},{64,3... | collective-permute-start | bytes 589832 | tf_op jit(solution)/shard_map/ppermute | solution.py:37
  11.3 26.4 %collective-permute-start = (f32[6,2,64,128]{3,2,1,0:T(8,128)S(1)}, f32[6,2,64,128]{3,2,1,0:T(8,128)S(1)}, u32[]{:S(2)}, u32[]{:S(2)}) collective-permute-start(f32[6,2,64,128]{3,2,1,0:T(8,128)S(1)} %slice_bitcast_fusion), channel_id=1, source_target_pairs={{4,0},{8,4},{12,8},{16,12},{20,16},{24,20},{28,24},{32,28},{36,32}... | collective-permute-start | bytes 1179656 | tf_op jit(solution)/shard_map/ppermute | solution.py:37
  14.0 15.4 %collective-permute-start.2 = (f32[3,2,16,128]{3,2,1,0:T(8,128)S(1)}, f32[3,2,16,128]{3,2,1,0:T(8,128)S(1)}, u32[]{:S(2)}, u32[]{:S(2)}) collective-permute-start(f32[3,2,16,128]{3,2,1,0:T(8,128)S(1)} %slice.35), channel_id=1, source_target_pairs={{36,0},{40,4},{44,8},{48,12},{52,16},{56,20},{60,24},{64,28},{68,3... | collective-permute-start | bytes 147464 | tf_op jit(solution)/shard_map/ppermute | solution.py:37
  29.3 14.6 %copy-start.12 = (f32[15,2,16,128]{3,2,1,0:T(8,128)}, f32[15,2,16,128]{3,2,1,0:T(8,128)S(1)}, u32[]{:S(2)}) copy-start(f32[15,2,16,128]{3,2,1,0:T(8,128)S(1)} %constant_dynamic-update-slice_fusion.b0) | copy-start | bytes 737284
  29.3 14.6 %collective-permute-start.5 = (f32[15,2,16,128]{3,2,1,0:T(8,128)S(1)}, f32[15,2,16,128]{3,2,1,0:T(8,128)S(1)}, u32[]{:S(2)}, u32[]{:S(2)}) collective-permute-start(f32[15,2,16,128]{3,2,1,0:T(8,128)S(1)} %constant_dynamic-update-slice_fusion.b0), channel_id=1, source_target_pairs={{0,3},{1,0},{2,1},{3,2},{4,7},{5,4},{6,5},{7,6},{8,11},{9,8},{10,9... | collective-permute-start | bytes 737288 | tf_op jit(solution)/shard_map/ppermute | solution.py:41
  29.9 14.0 %collective-permute-start.4 = (f32[15,2,16,128]{3,2,1,0:T(8,128)S(1)}, f32[15,2,16,128]{3,2,1,0:T(8,128)S(1)}, u32[]{:S(2)}, u32[]{:S(2)}) collective-permute-start(f32[15,2,16,128]{3,2,1,0:T(8,128)S(1)} %constant_dynamic-update-slice_fusion.b0), channel_id=1, source_target_pairs={{0,2},{1,3},{2,0},{3,1},{4,6},{5,7},{6,4},{7,5},{8,10},{9,11},{10,... | collective-permute-start | bytes 737288 | tf_op jit(solution)/shard_map/ppermute | solution.py:41
  30.8 13.2 %collective-permute-start.3 = (f32[15,2,16,128]{3,2,1,0:T(8,128)S(1)}, f32[15,2,16,128]{3,2,1,0:T(8,128)S(1)}, u32[]{:S(2)}, u32[]{:S(2)}) collective-permute-start(f32[15,2,16,128]{3,2,1,0:T(8,128)S(1)} %constant_dynamic-update-slice_fusion.b0), channel_id=1, source_target_pairs={{0,1},{1,2},{2,3},{3,0},{4,5},{5,6},{6,7},{7,4},{8,9},{9,10},{10,1... | collective-permute-start | bytes 737288 | tf_op jit(solution)/shard_map/ppermute | solution.py:41
  37.8 6.2 %copy-start.19 = (f32[6,2,64,128]{3,2,1,0:T(8,128)}, f32[6,2,64,128]{3,2,1,0:T(8,128)S(1)}, u32[]{:S(2)}) copy-start(f32[6,2,64,128]{3,2,1,0:T(8,128)S(1)} %collective-permute-done.right) | copy-start | bytes 1179652
  43.9 0.7 copy-start.23
  43.9 0.8 copy-start.24
  44.7 0.7 copy-start.25
  53.7 5.8 %collective-permute-start.6 = (f32[2,64,256]{2,1,0:T(8,128)}, f32[2,64,256]{2,1,0:T(8,128)S(1)}, u32[]{:S(2)}, u32[]{:S(2)}) collective-permute-start(f32[2,64,256]{2,1,0:T(8,128)} %get-tuple-element.35), channel_id=1, source_target_pairs={{0,1},{1,2},{2,3},{3,0},{4,5},{5,6},{6,7},{7,4},{8,9},{9,10},{10,1... | collective-permute-start | bytes 393224 | tf_op jit(solution)/shard_map/ppermute | solution.py:41
  55.9 6.1 %collective-permute-start.7 = (f32[2,64,256]{2,1,0:T(8,128)}, f32[2,64,256]{2,1,0:T(8,128)S(1)}, u32[]{:S(2)}, u32[]{:S(2)}) collective-permute-start(f32[2,64,256]{2,1,0:T(8,128)} %get-tuple-element.36), channel_id=1, source_target_pairs={{0,2},{1,3},{2,0},{3,1},{4,6},{5,7},{6,4},{7,5},{8,10},{9,11},{10,... | collective-permute-start | bytes 393224 | tf_op jit(solution)/shard_map/ppermute | solution.py:41
  55.9 9.3 %collective-permute-start.8 = (f32[2,64,256]{2,1,0:T(8,128)}, f32[2,64,256]{2,1,0:T(8,128)S(1)}, u32[]{:S(2)}, u32[]{:S(2)}) collective-permute-start(f32[2,64,256]{2,1,0:T(8,128)} %get-tuple-element.37), channel_id=1, source_target_pairs={{0,3},{1,0},{2,1},{3,2},{4,7},{5,4},{6,5},{7,6},{8,11},{9,8},{10,9... | collective-permute-start | bytes 393224 | tf_op jit(solution)/shard_map/ppermute | solution.py:41
  66.3 8.8 %copy-start.4 = (f32[2,64,256]{2,1,0:T(8,128)}, f32[2,64,256]{2,1,0:T(8,128)S(1)}, u32[]{:S(2)}) copy-start(f32[2,64,256]{2,1,0:T(8,128)S(1)} %add_multiply_fusion.f0) | copy-start | bytes 393220
  66.3 8.7 %collective-permute-start.11 = (f32[2,64,256]{2,1,0:T(8,128)S(1)}, f32[2,64,256]{2,1,0:T(8,128)S(1)}, u32[]{:S(2)}, u32[]{:S(2)}) collective-permute-start(f32[2,64,256]{2,1,0:T(8,128)S(1)} %add_multiply_fusion.f0), channel_id=1, source_target_pairs={{0,3},{1,0},{2,1},{3,2},{4,7},{5,4},{6,5},{7,6},{8,11},{9,8},{10,9... | collective-permute-start | bytes 393224 | tf_op jit(solution)/shard_map/ppermute | solution.py:41
  66.4 8.7 %collective-permute-start.10 = (f32[2,64,256]{2,1,0:T(8,128)S(1)}, f32[2,64,256]{2,1,0:T(8,128)S(1)}, u32[]{:S(2)}, u32[]{:S(2)}) collective-permute-start(f32[2,64,256]{2,1,0:T(8,128)S(1)} %add_multiply_fusion.f0), channel_id=1, source_target_pairs={{0,2},{1,3},{2,0},{3,1},{4,6},{5,7},{6,4},{7,5},{8,10},{9,11},{10,... | collective-permute-start | bytes 393224 | tf_op jit(solution)/shard_map/ppermute | solution.py:41
  67.5 7.6 %collective-permute-start.9 = (f32[2,64,256]{2,1,0:T(8,128)S(1)}, f32[2,64,256]{2,1,0:T(8,128)S(1)}, u32[]{:S(2)}, u32[]{:S(2)}) collective-permute-start(f32[2,64,256]{2,1,0:T(8,128)S(1)} %add_multiply_fusion.f0), channel_id=1, source_target_pairs={{0,1},{1,2},{2,3},{3,0},{4,5},{5,6},{6,7},{7,4},{8,9},{9,10},{10,1... | collective-permute-start | bytes 393224 | tf_op jit(solution)/shard_map/ppermute | solution.py:41
  75.0 0.7 copy-start.13
  75.0 0.7 copy-start.14
  75.1 0.7 copy-start.15
  83.2 4.0 %collective-permute-start.12 = (f32[3,256,256]{2,1,0:T(8,128)}, f32[3,256,256]{2,1,0:T(8,128)S(1)}, u32[]{:S(2)}, u32[]{:S(2)}) collective-permute-start(f32[3,256,256]{2,1,0:T(8,128)} %get-tuple-element.39), channel_id=1, source_target_pairs={{0,4},{4,0},{8,12},{12,8},{16,20},{20,16},{24,28},{28,24},{32,36},... | collective-permute-start | bytes 2359304 | tf_op jit(solution)/shard_map/ppermute | solution.py:45
  87.2 13.3 %copy-start.22 = (f32[2,8,2,16,128]{4,3,2,1,0:T(8,128)S(1)}, f32[2,8,2,16,128]{4,3,2,1,0:T(8,128)}, u32[]{:S(2)}) copy-start(f32[2,8,2,16,128]{4,3,2,1,0:T(8,128)} %get-tuple-element.41) | copy-start | bytes 786436
  87.2 15.7 %copy-start.21 = (f32[2,8,2,16,128]{4,3,2,1,0:T(8,128)S(1)}, f32[2,8,2,16,128]{4,3,2,1,0:T(8,128)}, u32[]{:S(2)}) copy-start(f32[2,8,2,16,128]{4,3,2,1,0:T(8,128)} %get-tuple-element.42) | copy-start | bytes 786436
  87.2 15.7 %copy-start.20 = (f32[2,8,2,16,128]{4,3,2,1,0:T(8,128)S(1)}, f32[2,8,2,16,128]{4,3,2,1,0:T(8,128)}, u32[]{:S(2)}) copy-start(f32[2,8,2,16,128]{4,3,2,1,0:T(8,128)} %get-tuple-element.43) | copy-start | bytes 786436
  89.4 50.1 %all-to-all-start = ((f32[32,24,256]{2,1,0:T(8,128)}), f32[32,24,256]{2,1,0:T(8,128)S(1)}, u32[]{:S(2)}, u32[]{:S(2)}) async-start(f32[32,24,256]{2,1,0:T(8,128)} %bitcast.8), calls=%async_computation.1 | async-start | bytes 1572864 | tf_op jit(solution)/shard_map/all_to_all | solution.py:395
  100.6 7.4 %collective-permute-start.13 = (f32[2,8,2,16,128]{4,3,2,1,0:T(8,128)S(1)}, f32[2,8,2,16,128]{4,3,2,1,0:T(8,128)S(1)}, u32[]{:S(2)}, u32[]{:S(2)}) collective-permute-start(f32[2,8,2,16,128]{4,3,2,1,0:T(8,128)S(1)} %copy-done.22), channel_id=1, source_target_pairs={{0,1},{1,2},{2,3},{3,0},{4,5},{5,6},{6,7},{7,4},{8,9},{9,10},{10,1... | collective-permute-start | bytes 786440 | tf_op jit(solution)/shard_map/ppermute | solution.py:41
  102.9 8.2 %collective-permute-start.14 = (f32[2,8,2,16,128]{4,3,2,1,0:T(8,128)S(1)}, f32[2,8,2,16,128]{4,3,2,1,0:T(8,128)S(1)}, u32[]{:S(2)}, u32[]{:S(2)}) collective-permute-start(f32[2,8,2,16,128]{4,3,2,1,0:T(8,128)S(1)} %copy-done.21), channel_id=1, source_target_pairs={{0,2},{1,3},{2,0},{3,1},{4,6},{5,7},{6,4},{7,5},{8,10},{9,11},{10,... | collective-permute-start | bytes 786440 | tf_op jit(solution)/shard_map/ppermute | solution.py:41
  102.9 14.9 %collective-permute-start.15 = (f32[2,8,2,16,128]{4,3,2,1,0:T(8,128)S(1)}, f32[2,8,2,16,128]{4,3,2,1,0:T(8,128)S(1)}, u32[]{:S(2)}, u32[]{:S(2)}) collective-permute-start(f32[2,8,2,16,128]{4,3,2,1,0:T(8,128)S(1)} %copy-done.20), channel_id=1, source_target_pairs={{0,3},{1,0},{2,1},{3,2},{4,7},{5,4},{6,5},{7,6},{8,11},{9,8},{10,9... | collective-permute-start | bytes 786440 | tf_op jit(solution)/shard_map/ppermute | solution.py:41
  107.9 9.9 %copy-start.8 = (f32[2,8,2,16,128]{4,3,2,1,0:T(8,128)}, f32[2,8,2,16,128]{4,3,2,1,0:T(8,128)S(1)}, u32[]{:S(2)}) copy-start(f32[2,8,2,16,128]{4,3,2,1,0:T(8,128)S(1)} %collective-permute-done.13.g1) | copy-start | bytes 786436
  111.1 6.8 %copy-start.9 = (f32[2,8,2,16,128]{4,3,2,1,0:T(8,128)}, f32[2,8,2,16,128]{4,3,2,1,0:T(8,128)S(1)}, u32[]{:S(2)}) copy-start(f32[2,8,2,16,128]{4,3,2,1,0:T(8,128)S(1)} %collective-permute-done.14.g2) | copy-start | bytes 786436
  117.8 0.7 copy-start.10
  120.7 18.7 %collective-permute-start.17 = (f32[13,2,16,128]{3,2,1,0:T(8,128)}, f32[13,2,16,128]{3,2,1,0:T(8,128)S(1)}, u32[]{:S(2)}, u32[]{:S(2)}) collective-permute-start(f32[13,2,16,128]{3,2,1,0:T(8,128)} %get-tuple-element.45), channel_id=1, source_target_pairs={{0,32},{4,36},{8,40},{12,44},{16,48},{20,52},{24,56},{28,60},{32,6... | collective-permute-start | bytes 638984 | tf_op jit(solution)/shard_map/ppermute | solution.py:37
  126.8 12.6 %collective-permute-start.16 = (f32[7,2,16,128]{3,2,1,0:T(8,128)}, f32[7,2,16,128]{3,2,1,0:T(8,128)S(1)}, u32[]{:S(2)}, u32[]{:S(2)}) collective-permute-start(f32[7,2,16,128]{3,2,1,0:T(8,128)} %get-tuple-element.44), channel_id=1, source_target_pairs={{0,4},{4,8},{8,12},{12,16},{16,20},{20,24},{24,28},{28,32},{32,36}... | collective-permute-start | bytes 344072 | tf_op jit(solution)/shard_map/ppermute | solution.py:37
  129.9 9.5 %collective-permute-start.18 = (f32[4,2,16,128]{3,2,1,0:T(8,128)}, f32[4,2,16,128]{3,2,1,0:T(8,128)S(1)}, u32[]{:S(2)}, u32[]{:S(2)}) collective-permute-start(f32[4,2,16,128]{3,2,1,0:T(8,128)} %get-tuple-element.46), channel_id=1, source_target_pairs={{0,36},{4,40},{8,44},{12,48},{16,52},{20,56},{24,60},{28,64},{32,6... | collective-permute-start | bytes 196616 | tf_op jit(solution)/shard_map/ppermute | solution.py:37
  139.5 0.6 copy-start.17
  139.5 0.7 copy-start.16
  139.5 0.8 copy-start.11
  143.3 11.6 %copy-start.2 = (f32[24,2,16,128]{3,2,1,0:T(8,128)S(1)}, f32[24,2,16,128]{3,2,1,0:T(8,128)}, u32[]{:S(2)}) copy-start(f32[24,2,16,128]{3,2,1,0:T(8,128)} %update.1.n0) | copy-start | bytes 1179652
  144.3 32.5 %all-to-all-start.1 = ((f32[32,24,256]{2,1,0:T(8,128)}), f32[32,24,256]{2,1,0:T(8,128)S(1)}, u32[]{:S(2)}, u32[]{:S(2)}) async-start(f32[32,24,256]{2,1,0:T(8,128)} %broadcast_in_dim.2), calls=%async_computation.2 | async-start | bytes 1572864 | tf_op jit(solution)/shard_map/all_to_all | solution.py:395
  155.0 12.5 %collective-permute-start.21 = (f32[24,2,16,128]{3,2,1,0:T(8,128)S(1)}, f32[24,2,16,128]{3,2,1,0:T(8,128)S(1)}, u32[]{:S(2)}, u32[]{:S(2)}) collective-permute-start(f32[24,2,16,128]{3,2,1,0:T(8,128)S(1)} %copy-done.2), channel_id=1, source_target_pairs={{0,3},{1,0},{2,1},{3,2},{4,7},{5,4},{6,5},{7,6},{8,11},{9,8},{10,9... | collective-permute-start | bytes 1179656 | tf_op jit(solution)/shard_map/ppermute | solution.py:41
  155.1 17.9 %collective-permute-start.20 = (f32[24,2,16,128]{3,2,1,0:T(8,128)S(1)}, f32[24,2,16,128]{3,2,1,0:T(8,128)S(1)}, u32[]{:S(2)}, u32[]{:S(2)}) collective-permute-start(f32[24,2,16,128]{3,2,1,0:T(8,128)S(1)} %copy-done.2), channel_id=1, source_target_pairs={{0,2},{1,3},{2,0},{3,1},{4,6},{5,7},{6,4},{7,5},{8,10},{9,11},{10,... | collective-permute-start | bytes 1179656 | tf_op jit(solution)/shard_map/ppermute | solution.py:41
  156.5 18.3 %collective-permute-start.19 = (f32[24,2,16,128]{3,2,1,0:T(8,128)S(1)}, f32[24,2,16,128]{3,2,1,0:T(8,128)S(1)}, u32[]{:S(2)}, u32[]{:S(2)}) collective-permute-start(f32[24,2,16,128]{3,2,1,0:T(8,128)S(1)} %copy-done.2), channel_id=1, source_target_pairs={{0,1},{1,2},{2,3},{3,0},{4,5},{5,6},{6,7},{7,4},{8,9},{9,10},{10,1... | collective-permute-start | bytes 1179656 | tf_op jit(solution)/shard_map/ppermute | solution.py:41
  167.5 11.7 %copy-start.5 = (f32[24,2,16,128]{3,2,1,0:T(8,128)}, f32[24,2,16,128]{3,2,1,0:T(8,128)S(1)}, u32[]{:S(2)}) copy-start(f32[24,2,16,128]{3,2,1,0:T(8,128)S(1)} %collective-permute-done.21.n3) | copy-start | bytes 1179652
  172.9 6.3 %copy-start.6 = (f32[24,2,16,128]{3,2,1,0:T(8,128)}, f32[24,2,16,128]{3,2,1,0:T(8,128)S(1)}, u32[]{:S(2)}) copy-start(f32[24,2,16,128]{3,2,1,0:T(8,128)S(1)} %collective-permute-done.20.n2) | copy-start | bytes 1179652
  174.8 4.4 %copy-start.7 = (f32[24,2,16,128]{3,2,1,0:T(8,128)}, f32[24,2,16,128]{3,2,1,0:T(8,128)S(1)}, u32[]{:S(2)}) copy-start(f32[24,2,16,128]{3,2,1,0:T(8,128)S(1)} %collective-permute-done.19.n1) | copy-start | bytes 1179652
  176.8 5.3 %copy-start.1 = (f32[32,24,256]{2,1,0:T(8,128)}, f32[32,24,256]{2,1,0:T(8,128)S(1)}, u32[]{:S(2)}) copy-start(f32[32,24,256]{2,1,0:T(8,128)S(1)} %all-to-all-done.1) | copy-start | bytes 2359300
  176.8 5.3 %collective-permute-start.22 = (f32[3,256,256]{2,1,0:T(8,128)S(1)}, f32[3,256,256]{2,1,0:T(8,128)S(1)}, u32[]{:S(2)}, u32[]{:S(2)}) collective-permute-start(f32[3,256,256]{2,1,0:T(8,128)S(1)} %bitcast.18), channel_id=1, source_target_pairs={{0,4},{4,0},{8,12},{12,8},{16,20},{20,16},{24,28},{28,24},{32,36},... | collective-permute-start | bytes 2359304 | tf_op jit(solution)/shard_map/ppermute | solution.py:45
  182.1 0.9 copy-start.3
Sparse Core Ops, SparseCore 0:
  11.1 22.0 reduce-scatter.1

commit v4 on v3

--- a/solution.py
+++ b/solution.py
@@ -31,10 +31,8 @@
 VMEM = pl.BlockSpec(memory_space=pltpu.VMEM)
 
 
-def shifted(block, axis, distance):
-    devices = range(lax.axis_size(axis))
-    route = [(i - distance, i) for i in devices if i - distance in devices]
-    return lax.ppermute(block, axis, route)
+def shifted(block, distance):
+    return lax.ppermute(block, "tile", [(d, (d + distance) % N_TILE) for d in range(N_TILE)])
 
 
 def turned(block, distance):
@@ -364,9 +362,9 @@
     tables = fourier_blocks()
     tile_grid = object_pieces.reshape(TILE_R, TILE_C, 2, PIECE_R, PIECE_C)
     own_rows = lax.dynamic_slice_in_dim(object_pieces[:12], mode_index * SUB, SUB, axis=2)
-    low = shifted(own_rows, "tile", -DEV_COLS)
-    corner = shifted(own_rows[::TILE_C], "tile", -DEV_COLS - 1)
-    right = shifted(tile_grid[:, 0], "tile", -1)
+    low = shifted(own_rows, -DEV_COLS)
+    corner = shifted(own_rows[::TILE_C], -DEV_COLS - 1)
+    right = shifted(tile_grid[:, 0], -1)
     below = jnp.concatenate([low, corner], axis=0)
     dev_row = tile_index // DEV_COLS
     dev_col = tile_index % DEV_COLS
@@ -374,12 +372,11 @@
     cols = jnp.clip(positions[:, 1] // PIECE_C - dev_col * TILE_C, 0, TILE_C - 1)
     info = jnp.stack([rows[0], cols[0], rows[1], cols[1], counts[0], mode_index,
                       tile_index % 2, tile_index]).astype(jnp.int32)
-    below = [below] + [turned(below, j) for j in (1, 2, 3)]
-
-    light_local = jnp.sum(probe_modes * probe_modes, axis=(0, 1))
+    late_modes, below = lax.optimization_barrier((probe_modes, below))
+    light_local = jnp.sum(late_modes * late_modes, axis=(0, 1))
     light_parts = light_local.reshape(4, N_MODE, SUB, SIDE).transpose(1, 0, 2, 3)
     light = lax.psum_scatter(light_parts, "mode", scatter_dimension=0, tiled=True)
-    light, right = lax.optimization_barrier((light, right))
+    below = [below] + [turned(below, j) for j in (1, 2, 3)]
 
     far, patch, *powers = forward(info, object_pieces, right, below, probe_modes, tables)
     received = [turned(powers[j], j) for j in (1, 2, 3)]
@@ -398,9 +395,9 @@
     pieces = exchange(summed.reshape(N_CHIP, PART, SIDE))
     parts = [grads[0]] + [turned(grads[j], j) for j in (1, 2, 3)]
     own, to_right, to_low, to_corner = scatter(info, parts)
-    from_above = shifted(to_low, "tile", DEV_COLS)
-    from_corner = shifted(to_corner, "tile", DEV_COLS + 1)
-    from_left = shifted(to_right, "tile", 1)
+    from_above = shifted(to_low, DEV_COLS)
+    from_corner = shifted(to_corner, DEV_COLS + 1)
+    from_left = shifted(to_right, 1)
     pieces, from_left, from_above, from_corner = lax.optimization_barrier(
         (pieces, from_left, from_above, from_corner))
     share = jnp.sum(pieces, axis=0)

time: 195 us -> 187 us (0.959)
  starting transfers between devices: 58.8 us -> 50.9 us
  waiting for transfers between devices: 75.9 us -> 78.1 us
    ppermute x15, starting transfers between devices: 14.7 us -> 11.4 us  [turned(): lax.ppermute(block, 'mode', [(i, (i + distance) % N_MODE) for i in range(...]
    all_to_all x2, starting transfers between devices: 21.8 us -> 19.2 us  [body(): lax.all_to_all(blocks, 'tile', 0, 0, axis_index_groups=groups, tiled=True)]
    unnamed x53 -> x52, local copies, waits for them, and re-layouts: 4.5 us -> 3.66 us
  transfers between devices with their start and end apart: 26 -> 26, of which waited for: 16 -> 18; matrix products, arithmetic and copies ran while one was open for 2% -> 3% of each run, Pallas kernels for 3% -> 3%
where the time goes in v4:
time: 187 us; the launch traced here: 186 us
  waiting for transfers between devices  78.1 us (42%)
  starting transfers between devices  50.9 us (27%)
  Pallas kernels  26.7 us (14%)
  between operations  15 us (8%)
  local copies, waits for them, and re-layouts  12 us (6%)
  other arithmetic  3.49 us (2%)
    ppermute x15, waiting for transfers between devices, turned(): lax.ppermute(block, 'mode', [(i, (i + distance) % N_MODE) for i in range(...  52.7 us
    ppermute x6, waiting for transfers between devices, shifted(): lax.ppermute(block, 'tile', [(d, (d + distance) % N_TILE) for d in range(...  21 us
    all_to_all x2, starting transfers between devices, body(): lax.all_to_all(blocks, 'tile', 0, 0, axis_index_groups=groups, tiled=True)  19.2 us
    ppermute x6, starting transfers between devices, shifted(): lax.ppermute(block, 'tile', [(d, (d + distance) % N_TILE) for d in range(...  16.4 us
    ppermute x15, starting transfers between devices, turned(): lax.ppermute(block, 'mode', [(i, (i + distance) % N_MODE) for i in range(...  11.4 us
    pallas_call x1, Pallas kernels, forward(): pl.pallas_call(forward_kernel, grid=(3,), in_specs=[SMEM] + [ANY] * 6 + [...  8.29 us
    pallas_call x1, Pallas kernels, backward(): pl.pallas_call(backward_kernel, grid=(3,), in_specs=[SMEM, pl.BlockSpec((...  7.42 us
    ppermute x2, starting transfers between devices, core_swap(): return lax.ppermute(block, 'tile', [(d, d ^ 1) for d in range(N_TILE)])  3.88 us
  transfers between devices with their start and end apart: 26, of which 18 were waited for; matrix products, arithmetic and copies ran while one was open for 3% of the time, Pallas kernels for 3%

profile of v4, /device:TPU:39, one launch (start us, length us, event | category | flops | bytes accessed | tf_op | source)
XLA Modules:
  0.0 186.2 jit_solution(10856228460879062127)
XLA Ops:
  7.2 1.1 slice-done
  8.3 8.5 %collective-permute-start.1 = (f32[12,2,16,128]{3,2,1,0:T(8,128)S(1)}, f32[12,2,16,128]{3,2,1,0:T(8,128)S(1)}, u32[]{:S(2)}, u32[]{:S(2)}) collective-permute-start(f32[12,2,16,128]{3,2,1,0:T(8,128)S(1)} %constant_dynamic-slice_fusion), channel_id=1, source_target_pairs={{0,224},{4,228},{8,232},{12,236},{16,240},{20,244},{24,248},{28,25... | collective-permute-start | bytes 589832 | tf_op jit(solution)/shard_map/ppermute | solution.py:35
  16.9 0.7 collective-permute-start.2
  17.5 1.0 slice_bitcast_fusion
  18.5 0.4 collective-permute-start
  18.9 0.2 slice_reduce_fusion
  19.1 7.3 %collective-permute-done.2 = f32[3,2,16,128]{3,2,1,0:T(8,128)S(1)} collective-permute-done((f32[3,2,16,128]{3,2,1,0:T(8,128)S(1)}, f32[3,2,16,128]{3,2,1,0:T(8,128)S(1)}, u32[]{:S(2)}, u32[]{:S(2)}) %collective-permute-start.2) | collective-permute-done | bytes 49184 | tf_op jit(solution)/shard_map/ppermute | solution.py:35
  26.5 0.3 collective-permute-start.3
  26.7 2.1 %collective-permute-start.4 = (f32[15,2,16,128]{3,2,1,0:T(8,128)S(1)}, f32[15,2,16,128]{3,2,1,0:T(8,128)S(1)}, u32[]{:S(2)}, u32[]{:S(2)}) collective-permute-start(f32[15,2,16,128]{3,2,1,0:T(8,128)S(1)} %pad_maximum_fusion.b0), channel_id=1, source_target_pairs={{0,2},{1,3},{2,0},{3,1},{4,6},{5,7},{6,4},{7,5},{8,10},{9,11},{10,... | collective-permute-start | bytes 737288 | tf_op jit(solution)/shard_map/ppermute | solution.py:39
  29.6 0.6 fusion
  30.2 0.6 fusion.1
  30.7 3.2 %stack.15.info = s32[8]{0:T(128)} concatenate(s32[1]{0:T(128)} %get-tuple-element.65, s32[1]{0:T(128)} %get-tuple-element.63, s32[1]{0:T(128)} %get-tuple-element.64, s32[1]{0:T(128)} %get-tuple-element.62, s32[1]{0:T(128)} %copy.14, s32[1]{0:T(128)} %bitcast, s32[1]{0:T(128)} %bitcast.1, s32[1]{0:T(128)} %bitcast.2), dimensions={0} | concatenate | bytes 64 | tf_op jit(solution)/shard_map/stack | solution.py:373
  33.9 0.5 collective-permute-done.4.b2
  34.5 6.8 %collective-permute-done.5.b3 = f32[15,2,16,128]{3,2,1,0:T(8,128)S(1)} collective-permute-done((f32[15,2,16,128]{3,2,1,0:T(8,128)S(1)}, f32[15,2,16,128]{3,2,1,0:T(8,128)S(1)}, u32[]{:S(2)}, u32[]{:S(2)}) %collective-permute-start.5) | collective-permute-done | bytes 245792 | tf_op jit(solution)/shard_map/ppermute | solution.py:39
  41.4 0.7 copy-done.25
  42.1 8.3 %forward.1 = (f32[2,3,2,256,256]{4,3,2,1,0:T(8,128)}, f32[2,2,256,256]{3,2,1,0:T(8,128)}, f32[2,64,256]{2,1,0:T(8,128)}, f32[2,64,256]{2,1,0:T(8,128)}, f32[2,64,256]{2,1,0:T(8,128)}, /*index=5*/f32[2,64,256]{2,1,0:T(8,128)}) custom-call(s32[8]{0:T(128)} %stack.15.info, f32[24,2,64,128]{3,2,1,0:T(8,128)} %pieces.1, f32[6,2,64,128]{3,2,1,0:T(8,128)} %copy-done.19, ...), custom_call_target="tpu_custom_call" | custom-call | flops 1700000000 | bytes 12000000 | tf_op jit(solution)/shard_map/forward/pallas_call | solution.py:125
  50.4 0.1 collective-permute-start.6
  50.5 0.9 collective-permute-start.7
  51.4 0.7 collective-permute-start.8
  52.1 3.1 %collective-permute-done.6 = f32[2,64,256]{2,1,0:T(8,128)S(1)} collective-permute-done((f32[2,64,256]{2,1,0:T(8,128)}, f32[2,64,256]{2,1,0:T(8,128)S(1)}, u32[]{:S(2)}, u32[]{:S(2)}) %collective-permute-start.6) | collective-permute-done | bytes 131104 | tf_op jit(solution)/shard_map/ppermute | solution.py:39
  55.1 1.0 collective-permute-done.7
  56.1 1.9 %collective-permute-done.8 = f32[2,64,256]{2,1,0:T(8,128)S(1)} collective-permute-done((f32[2,64,256]{2,1,0:T(8,128)}, f32[2,64,256]{2,1,0:T(8,128)S(1)}, u32[]{:S(2)}, u32[]{:S(2)}) %collective-permute-start.8) | collective-permute-done | bytes 131104 | tf_op jit(solution)/shard_map/ppermute | solution.py:39
  58.1 1.0 add_multiply_fusion.f0
  59.1 0.6 collective-permute-start.10
  59.7 2.4 %collective-permute-start.11 = (f32[2,64,256]{2,1,0:T(8,128)S(1)}, f32[2,64,256]{2,1,0:T(8,128)S(1)}, u32[]{:S(2)}, u32[]{:S(2)}) collective-permute-start(f32[2,64,256]{2,1,0:T(8,128)S(1)} %add_multiply_fusion.f0), channel_id=1, source_target_pairs={{0,3},{1,0},{2,1},{3,2},{4,7},{5,4},{6,5},{7,6},{8,11},{9,8},{10,9... | collective-permute-start | bytes 393224 | tf_op jit(solution)/shard_map/ppermute | solution.py:39
  62.1 0.3 collective-permute-start.9
  62.4 2.2 %collective-permute-done.10.f2 = f32[2,64,256]{2,1,0:T(8,128)S(1)} collective-permute-done((f32[2,64,256]{2,1,0:T(8,128)S(1)}, f32[2,64,256]{2,1,0:T(8,128)S(1)}, u32[]{:S(2)}, u32[]{:S(2)}) %collective-permute-start.10) | collective-permute-done | bytes 131104 | tf_op jit(solution)/shard_map/ppermute | solution.py:39
  64.6 1.3 collective-permute-done.11.f3
  65.9 1.3 collective-permute-done.9.f1
  67.2 0.7 copy-done.15
  67.9 7.4 %backward.1 = (f32[3,256,256]{2,1,0:T(8,128)}, f32[3,256,256]{2,1,0:T(8,128)}, f32[2,8,2,16,128]{4,3,2,1,0:T(8,128)}, f32[2,8,2,16,128]{4,3,2,1,0:T(8,128)}, f32...) custom-call(s32[8]{0:T(128)} %stack.15.info, f32[2,3,2,256,256]{4,3,2,1,0:T(8,128)} %get-tuple-element.32.far, ...), custom_call_target="tpu_custom_call" | custom-call | flops 1700000000 | bytes 12000000 | tf_op jit(solution)/shard_map/backward/pallas_call | solution.py:188
  75.3 3.2 %collective-permute-start.12 = (f32[3,256,256]{2,1,0:T(8,128)}, f32[3,256,256]{2,1,0:T(8,128)S(1)}, u32[]{:S(2)}, u32[]{:S(2)}) collective-permute-start(f32[3,256,256]{2,1,0:T(8,128)} %get-tuple-element.39), channel_id=1, source_target_pairs={{0,4},{4,0},{8,12},{12,8},{16,20},{20,16},{24,28},{28,24},{32,36},... | collective-permute-start | bytes 2359304 | tf_op jit(solution)/shard_map/ppermute | solution.py:43
  78.5 2.1 %collective-permute-done.12 = f32[3,256,256]{2,1,0:T(8,128)S(1)} collective-permute-done((f32[3,256,256]{2,1,0:T(8,128)}, f32[3,256,256]{2,1,0:T(8,128)S(1)}, u32[]{:S(2)}, u32[]{:S(2)}) %collective-permute-start.12) | collective-permute-done | bytes 786464 | tf_op jit(solution)/shard_map/ppermute | solution.py:43
  80.6 2.2 %add.46 = f32[3,256,256]{2,1,0:T(8,128)} add(f32[3,256,256]{2,1,0:T(8,128)} %get-tuple-element.38, f32[3,256,256]{2,1,0:T(8,128)S(1)} %collective-permute-done.12) | non-fusion elementwise | flops 196608 | bytes 2359296 | tf_op jit(solution)/shard_map/add | solution.py:394
  82.8 12.6 %all-to-all-start = ((f32[32,24,256]{2,1,0:T(8,128)}), f32[32,24,256]{2,1,0:T(8,128)S(1)}, u32[]{:S(2)}, u32[]{:S(2)}) async-start(f32[32,24,256]{2,1,0:T(8,128)} %bitcast.6), calls=%async_computation | async-start | bytes 1572864 | tf_op jit(solution)/shard_map/all_to_all | solution.py:392
  95.5 0.1 multiply_reduce_fusion
  95.6 0.7 copy.13
  96.4 1.3 collective-permute-start.13
  97.6 0.6 collective-permute-start.14
  98.3 0.5 collective-permute-start.15
  98.8 4.5 %collective-permute-done.13.g1 = f32[2,8,2,16,128]{4,3,2,1,0:T(8,128)S(1)} collective-permute-done((f32[2,8,2,16,128]{4,3,2,1,0:T(8,128)S(1)}, f32[2,8,2,16,128]{4,3,2,1,0:T(8,128)S(1)}, u32[]{:S(2)}, u32[]{:S(2)}) %collective-permute-start.13) | collective-permute-done | bytes 262176 | tf_op jit(solution)/shard_map/ppermute | solution.py:39
  103.3 2.4 %collective-permute-done.14.g2 = f32[2,8,2,16,128]{4,3,2,1,0:T(8,128)S(1)} collective-permute-done((f32[2,8,2,16,128]{4,3,2,1,0:T(8,128)S(1)}, f32[2,8,2,16,128]{4,3,2,1,0:T(8,128)S(1)}, u32[]{:S(2)}, u32[]{:S(2)}) %collective-permute-start.14) | collective-permute-done | bytes 262176 | tf_op jit(solution)/shard_map/ppermute | solution.py:39
  105.8 8.0 %collective-permute-done.15.g3 = f32[2,8,2,16,128]{4,3,2,1,0:T(8,128)S(1)} collective-permute-done((f32[2,8,2,16,128]{4,3,2,1,0:T(8,128)S(1)}, f32[2,8,2,16,128]{4,3,2,1,0:T(8,128)S(1)}, u32[]{:S(2)}, u32[]{:S(2)}) %collective-permute-start.15) | collective-permute-done | bytes 262176 | tf_op jit(solution)/shard_map/ppermute | solution.py:39
  113.8 0.7 copy-done.10
  114.5 2.2 %scatter.1 = (f32[24,2,16,128]{3,2,1,0:T(8,128)}, f32[7,2,16,128]{3,2,1,0:T(8,128)}, f32[13,2,16,128]{3,2,1,0:T(8,128)}, f32[4,2,16,128]{3,2,1,0:T(8,128)}) custom-call(s32[8]{0:T(128)} %stack.15.info, f32[2,8,2,16,128]{4,3,2,1,0:T(8,128)} %get-tuple-element.40.g0, f32[2,8,2,16,128]{4,3,2,1,0:T(8,128)} %copy-done.8, f32[2,8,2,16,128]{4,3,2,1,0:T(8,128)} %copy-done.9, ...), custom_call_target="tpu_custom_call" | custom-call | flops 1000000 | bytes 2000000 | tf_op jit(solution)/shard_map/scatter/pallas_call | solution.py:225
  116.7 3.8 %collective-permute-start.17 = (f32[13,2,16,128]{3,2,1,0:T(8,128)}, f32[13,2,16,128]{3,2,1,0:T(8,128)S(1)}, u32[]{:S(2)}, u32[]{:S(2)}) collective-permute-start(f32[13,2,16,128]{3,2,1,0:T(8,128)} %get-tuple-element.45), channel_id=1, source_target_pairs={{0,32},{4,36},{8,40},{12,44},{16,48},{20,52},{24,56},{28,60},{32,6... | collective-permute-start | bytes 638984 | tf_op jit(solution)/shard_map/ppermute | solution.py:35
  120.5 0.9 collective-permute-start.16
  121.5 2.1 %collective-permute-start.18 = (f32[4,2,16,128]{3,2,1,0:T(8,128)}, f32[4,2,16,128]{3,2,1,0:T(8,128)S(1)}, u32[]{:S(2)}, u32[]{:S(2)}) collective-permute-start(f32[4,2,16,128]{3,2,1,0:T(8,128)} %get-tuple-element.46), channel_id=1, source_target_pairs={{0,36},{4,40},{8,44},{12,48},{16,52},{20,56},{24,60},{28,64},{32,6... | collective-permute-start | bytes 196616 | tf_op jit(solution)/shard_map/ppermute | solution.py:35
  123.5 13.7 %collective-permute-done.18.corner = f32[4,2,16,128]{3,2,1,0:T(8,128)S(1)} collective-permute-done((f32[4,2,16,128]{3,2,1,0:T(8,128)}, f32[4,2,16,128]{3,2,1,0:T(8,128)S(1)}, u32[]{:S(2)}, u32[]{:S(2)}) %collective-permute-start.18) | collective-permute-done | bytes 65568 | tf_op jit(solution)/shard_map/ppermute | solution.py:35
  137.3 0.5 copy-done.17
  137.9 0.1 copy-done.12
  138.0 3.1 %update.1.n0 = f32[24,2,16,128]{3,2,1,0:T(8,128)} custom-call(s32[8]{0:T(128)} %stack.15.info, f32[24,2,64,128]{3,2,1,0:T(8,128)} %pieces.1, f32[24,2,16,128]{3,2,1,0:T(8,128)} %get-tuple-element.48.own, f32[7,2,16,128]{3,2,1,0:T(8,128)} %copy-done.16, f32[13,2,16,128]{3,2,1,0:T(8,128)} %copy-done.12, f32[4,2,16,128]{3,2,1,0:T(8,128)} %copy-done.17, ...), custom_call_target="tpu_custom_call" | custom-call | flops 1000000 | bytes 2000000 | tf_op jit(solution)/shard_map/update/pallas_call | solution.py:284
  141.1 0.9 broadcast_in_dim.2
  142.0 6.6 %all-to-all-start.1 = ((f32[32,24,256]{2,1,0:T(8,128)}), f32[32,24,256]{2,1,0:T(8,128)S(1)}, u32[]{:S(2)}, u32[]{:S(2)}) async-start(f32[32,24,256]{2,1,0:T(8,128)} %broadcast_in_dim.2), calls=%async_computation.2 | async-start | bytes 1572864 | tf_op jit(solution)/shard_map/all_to_all | solution.py:392
  148.7 0.4 collective-permute-start.20
  149.1 1.1 collective-permute-start.21
  150.2 8.8 %collective-permute-done.19.n1 = f32[24,2,16,128]{3,2,1,0:T(8,128)S(1)} collective-permute-done((f32[24,2,16,128]{3,2,1,0:T(8,128)S(1)}, f32[24,2,16,128]{3,2,1,0:T(8,128)S(1)}, u32[]{:S(2)}, u32[]{:S(2)}) %collective-permute-start.19) | collective-permute-done | bytes 393248 | tf_op jit(solution)/shard_map/ppermute | solution.py:39
  159.0 1.6 collective-permute-done.20.n2
  160.6 9.2 %collective-permute-done.21.n3 = f32[24,2,16,128]{3,2,1,0:T(8,128)S(1)} collective-permute-done((f32[24,2,16,128]{3,2,1,0:T(8,128)S(1)}, f32[24,2,16,128]{3,2,1,0:T(8,128)S(1)}, u32[]{:S(2)}, u32[]{:S(2)}) %collective-permute-start.21) | collective-permute-done | bytes 393248 | tf_op jit(solution)/shard_map/ppermute | solution.py:39
  169.8 2.2 %all-to-all-done.1 = f32[32,24,256]{2,1,0:T(8,128)S(1)} async-done(((f32[32,24,256]{2,1,0:T(8,128)}), f32[32,24,256]{2,1,0:T(8,128)S(1)}, u32[]{:S(2)}, u32[]{:S(2)}) %all-to-all-start.1) | async-done | bytes 786464 | tf_op jit(solution)/shard_map/all_to_all | solution.py:392
  172.0 0.7 collective-permute-start.22
  172.7 2.9 %join_pieces.1 = f32[24,2,64,128]{3,2,1,0:T(8,128)} custom-call(s32[8]{0:T(128)} %stack.15.info, f32[24,2,16,128]{3,2,1,0:T(8,128)} %update.1.n0, f32[24,2,16,128]{3,2,1,0:T(8,128)} %copy-done.5, f32[24,2,16,128]{3,2,1,0:T(8,128)} %copy-done.6, f32[24,2,16,128]{3,2,1,0:T(8,128)} %copy-done.7), custom_call_target="tpu_custom_call" | custom-call | bytes 3000000 | tf_op jit(solution)/shard_map/join_pieces/pallas_call | solution.py:314
  175.6 0.9 copy-done.3
  176.5 2.8 %join_channels.1 = f32[3,2,256,256]{3,2,1,0:T(8,128)} custom-call(s32[8]{0:T(128)} %stack.15.info, f32[3,256,256]{2,1,0:T(8,128)} %bitcast.19, f32[3,256,256]{2,1,0:T(8,128)} %copy-done.3), custom_call_target="tpu_custom_call" | custom-call | bytes 3000000 | tf_op jit(solution)/shard_map/join_channels/pallas_call | solution.py:346
  (65 shorter events, 0.4 us)
Async XLA Ops:
  7.2 1.1 slice-start
  7.2 11.7 %copy-start.18 = (s32[2,2]{1,0:T(2,128)S(1)}, s32[2,2]{1,0:T(2,128)}, u32[]{:S(2)}) copy-start(s32[2,2]{1,0:T(2,128)} %param.10) | copy-start | bytes 52
  8.3 18.1 %collective-permute-start.1 = (f32[12,2,16,128]{3,2,1,0:T(8,128)S(1)}, f32[12,2,16,128]{3,2,1,0:T(8,128)S(1)}, u32[]{:S(2)}, u32[]{:S(2)}) collective-permute-start(f32[12,2,16,128]{3,2,1,0:T(8,128)S(1)} %constant_dynamic-slice_fusion), channel_id=1, source_target_pairs={{0,224},{4,228},{8,232},{12,236},{16,240},{20,244},{24,248},{28,25... | collective-permute-start | bytes 589832 | tf_op jit(solution)/shard_map/ppermute | solution.py:35
  16.9 9.6 %collective-permute-start.2 = (f32[3,2,16,128]{3,2,1,0:T(8,128)S(1)}, f32[3,2,16,128]{3,2,1,0:T(8,128)S(1)}, u32[]{:S(2)}, u32[]{:S(2)}) collective-permute-start(f32[3,2,16,128]{3,2,1,0:T(8,128)S(1)} %slice.35), channel_id=1, source_target_pairs={{0,220},{4,224},{8,228},{12,232},{16,236},{20,240},{24,244},{28,24... | collective-permute-start | bytes 147464 | tf_op jit(solution)/shard_map/ppermute | solution.py:35
  18.5 15.4 %collective-permute-start = (f32[6,2,64,128]{3,2,1,0:T(8,128)S(1)}, f32[6,2,64,128]{3,2,1,0:T(8,128)S(1)}, u32[]{:S(2)}, u32[]{:S(2)}) collective-permute-start(f32[6,2,64,128]{3,2,1,0:T(8,128)S(1)} %slice_bitcast_fusion), channel_id=1, source_target_pairs={{0,252},{4,0},{8,4},{12,8},{16,12},{20,16},{24,20},{28,24},{32,28}... | collective-permute-start | bytes 1179656 | tf_op jit(solution)/shard_map/ppermute | solution.py:35
  26.5 14.9 %copy-start.11 = (f32[15,2,16,128]{3,2,1,0:T(8,128)}, f32[15,2,16,128]{3,2,1,0:T(8,128)S(1)}, u32[]{:S(2)}) copy-start(f32[15,2,16,128]{3,2,1,0:T(8,128)S(1)} %pad_maximum_fusion.b0) | copy-start | bytes 737284
  26.5 7.5 %collective-permute-start.3 = (f32[15,2,16,128]{3,2,1,0:T(8,128)S(1)}, f32[15,2,16,128]{3,2,1,0:T(8,128)S(1)}, u32[]{:S(2)}, u32[]{:S(2)}) collective-permute-start(f32[15,2,16,128]{3,2,1,0:T(8,128)S(1)} %pad_maximum_fusion.b0), channel_id=1, source_target_pairs={{0,1},{1,2},{2,3},{3,0},{4,5},{5,6},{6,7},{7,4},{8,9},{9,10},{10,1... | collective-permute-start | bytes 737288 | tf_op jit(solution)/shard_map/ppermute | solution.py:39
  26.7 7.7 %collective-permute-start.4 = (f32[15,2,16,128]{3,2,1,0:T(8,128)S(1)}, f32[15,2,16,128]{3,2,1,0:T(8,128)S(1)}, u32[]{:S(2)}, u32[]{:S(2)}) collective-permute-start(f32[15,2,16,128]{3,2,1,0:T(8,128)S(1)} %pad_maximum_fusion.b0), channel_id=1, source_target_pairs={{0,2},{1,3},{2,0},{3,1},{4,6},{5,7},{6,4},{7,5},{8,10},{9,11},{10,... | collective-permute-start | bytes 737288 | tf_op jit(solution)/shard_map/ppermute | solution.py:39
  28.9 12.4 %collective-permute-start.5 = (f32[15,2,16,128]{3,2,1,0:T(8,128)S(1)}, f32[15,2,16,128]{3,2,1,0:T(8,128)S(1)}, u32[]{:S(2)}, u32[]{:S(2)}) collective-permute-start(f32[15,2,16,128]{3,2,1,0:T(8,128)S(1)} %pad_maximum_fusion.b0), channel_id=1, source_target_pairs={{0,3},{1,0},{2,1},{3,2},{4,7},{5,4},{6,5},{7,6},{8,11},{9,8},{10,9... | collective-permute-start | bytes 737288 | tf_op jit(solution)/shard_map/ppermute | solution.py:39
  33.9 7.4 %copy-start.19 = (f32[6,2,64,128]{3,2,1,0:T(8,128)}, f32[6,2,64,128]{3,2,1,0:T(8,128)S(1)}, u32[]{:S(2)}) copy-start(f32[6,2,64,128]{3,2,1,0:T(8,128)S(1)} %collective-permute-done.right) | copy-start | bytes 1179652
  33.9 7.4 %copy-start.23 = (f32[15,2,16,128]{3,2,1,0:T(8,128)}, f32[15,2,16,128]{3,2,1,0:T(8,128)S(1)}, u32[]{:S(2)}) copy-start(f32[15,2,16,128]{3,2,1,0:T(8,128)S(1)} %collective-permute-done.3.b1) | copy-start | bytes 737284
  34.5 6.8 %copy-start.24 = (f32[15,2,16,128]{3,2,1,0:T(8,128)}, f32[15,2,16,128]{3,2,1,0:T(8,128)S(1)}, u32[]{:S(2)}) copy-start(f32[15,2,16,128]{3,2,1,0:T(8,128)S(1)} %collective-permute-done.4.b2) | copy-start | bytes 737284
  41.3 0.7 copy-start.25
  50.4 4.8 %collective-permute-start.6 = (f32[2,64,256]{2,1,0:T(8,128)}, f32[2,64,256]{2,1,0:T(8,128)S(1)}, u32[]{:S(2)}, u32[]{:S(2)}) collective-permute-start(f32[2,64,256]{2,1,0:T(8,128)} %get-tuple-element.35), channel_id=1, source_target_pairs={{0,1},{1,2},{2,3},{3,0},{4,5},{5,6},{6,7},{7,4},{8,9},{9,10},{10,1... | collective-permute-start | bytes 393224 | tf_op jit(solution)/shard_map/ppermute | solution.py:39
  50.5 5.6 %collective-permute-start.7 = (f32[2,64,256]{2,1,0:T(8,128)}, f32[2,64,256]{2,1,0:T(8,128)S(1)}, u32[]{:S(2)}, u32[]{:S(2)}) collective-permute-start(f32[2,64,256]{2,1,0:T(8,128)} %get-tuple-element.36), channel_id=1, source_target_pairs={{0,2},{1,3},{2,0},{3,1},{4,6},{5,7},{6,4},{7,5},{8,10},{9,11},{10,... | collective-permute-start | bytes 393224 | tf_op jit(solution)/shard_map/ppermute | solution.py:39
  51.4 6.7 %collective-permute-start.8 = (f32[2,64,256]{2,1,0:T(8,128)}, f32[2,64,256]{2,1,0:T(8,128)S(1)}, u32[]{:S(2)}, u32[]{:S(2)}) collective-permute-start(f32[2,64,256]{2,1,0:T(8,128)} %get-tuple-element.37), channel_id=1, source_target_pairs={{0,3},{1,0},{2,1},{3,2},{4,7},{5,4},{6,5},{7,6},{8,11},{9,8},{10,9... | collective-permute-start | bytes 393224 | tf_op jit(solution)/shard_map/ppermute | solution.py:39
  59.1 8.1 %copy-start.4 = (f32[2,64,256]{2,1,0:T(8,128)}, f32[2,64,256]{2,1,0:T(8,128)S(1)}, u32[]{:S(2)}) copy-start(f32[2,64,256]{2,1,0:T(8,128)S(1)} %add_multiply_fusion.f0) | copy-start | bytes 393220
  59.1 5.5 %collective-permute-start.10 = (f32[2,64,256]{2,1,0:T(8,128)S(1)}, f32[2,64,256]{2,1,0:T(8,128)S(1)}, u32[]{:S(2)}, u32[]{:S(2)}) collective-permute-start(f32[2,64,256]{2,1,0:T(8,128)S(1)} %add_multiply_fusion.f0), channel_id=1, source_target_pairs={{0,2},{1,3},{2,0},{3,1},{4,6},{5,7},{6,4},{7,5},{8,10},{9,11},{10,... | collective-permute-start | bytes 393224 | tf_op jit(solution)/shard_map/ppermute | solution.py:39
  59.7 6.2 %collective-permute-start.11 = (f32[2,64,256]{2,1,0:T(8,128)S(1)}, f32[2,64,256]{2,1,0:T(8,128)S(1)}, u32[]{:S(2)}, u32[]{:S(2)}) collective-permute-start(f32[2,64,256]{2,1,0:T(8,128)S(1)} %add_multiply_fusion.f0), channel_id=1, source_target_pairs={{0,3},{1,0},{2,1},{3,2},{4,7},{5,4},{6,5},{7,6},{8,11},{9,8},{10,9... | collective-permute-start | bytes 393224 | tf_op jit(solution)/shard_map/ppermute | solution.py:39
  62.1 5.1 %collective-permute-start.9 = (f32[2,64,256]{2,1,0:T(8,128)S(1)}, f32[2,64,256]{2,1,0:T(8,128)S(1)}, u32[]{:S(2)}, u32[]{:S(2)}) collective-permute-start(f32[2,64,256]{2,1,0:T(8,128)S(1)} %add_multiply_fusion.f0), channel_id=1, source_target_pairs={{0,1},{1,2},{2,3},{3,0},{4,5},{5,6},{6,7},{7,4},{8,9},{9,10},{10,1... | collective-permute-start | bytes 393224 | tf_op jit(solution)/shard_map/ppermute | solution.py:39
  64.6 2.6 %copy-start.13 = (f32[2,64,256]{2,1,0:T(8,128)}, f32[2,64,256]{2,1,0:T(8,128)S(1)}, u32[]{:S(2)}) copy-start(f32[2,64,256]{2,1,0:T(8,128)S(1)} %collective-permute-done.10.f2) | copy-start | bytes 393220
  65.9 1.3 copy-start.14
  67.2 0.7 copy-start.15
  75.3 5.3 %collective-permute-start.12 = (f32[3,256,256]{2,1,0:T(8,128)}, f32[3,256,256]{2,1,0:T(8,128)S(1)}, u32[]{:S(2)}, u32[]{:S(2)}) collective-permute-start(f32[3,256,256]{2,1,0:T(8,128)} %get-tuple-element.39), channel_id=1, source_target_pairs={{0,4},{4,0},{8,12},{12,8},{16,20},{20,16},{24,28},{28,24},{32,36},... | collective-permute-start | bytes 2359304 | tf_op jit(solution)/shard_map/ppermute | solution.py:43
  80.6 14.9 %copy-start = (f32[3,2,256,256]{3,2,1,0:T(8,128)S(1)}, f32[3,2,256,256]{3,2,1,0:T(8,128)}, u32[]{:S(2)}) copy-start(f32[3,2,256,256]{3,2,1,0:T(8,128)} %probe.3) | copy-start | bytes 4718596
  82.8 54.4 %all-to-all-start = ((f32[32,24,256]{2,1,0:T(8,128)}), f32[32,24,256]{2,1,0:T(8,128)S(1)}, u32[]{:S(2)}, u32[]{:S(2)}) async-start(f32[32,24,256]{2,1,0:T(8,128)} %bitcast.6), calls=%async_computation | async-start | bytes 1572864 | tf_op jit(solution)/shard_map/all_to_all | solution.py:392
  95.4 1.0 copy-start.22
  95.4 2.2 %copy-start.21 = (f32[2,8,2,16,128]{4,3,2,1,0:T(8,128)S(1)}, f32[2,8,2,16,128]{4,3,2,1,0:T(8,128)}, u32[]{:S(2)}) copy-start(f32[2,8,2,16,128]{4,3,2,1,0:T(8,128)} %get-tuple-element.42) | copy-start | bytes 786436
  95.4 2.8 %copy-start.20 = (f32[2,8,2,16,128]{4,3,2,1,0:T(8,128)S(1)}, f32[2,8,2,16,128]{4,3,2,1,0:T(8,128)}, u32[]{:S(2)}) copy-start(f32[2,8,2,16,128]{4,3,2,1,0:T(8,128)} %get-tuple-element.43) | copy-start | bytes 786436
  95.4 41.9 %reduce-scatter.2.cloned.1.call-start = ((), (), s32[]{:S(2)}) async-start(), calls=%async_computation.3 | async-start | bytes 327680 | tf_op jit(solution)/shard_map/reduce_scatter | solution.py:378
  96.4 7.0 %collective-permute-start.13 = (f32[2,8,2,16,128]{4,3,2,1,0:T(8,128)S(1)}, f32[2,8,2,16,128]{4,3,2,1,0:T(8,128)S(1)}, u32[]{:S(2)}, u32[]{:S(2)}) collective-permute-start(f32[2,8,2,16,128]{4,3,2,1,0:T(8,128)S(1)} %copy-done.22), channel_id=1, source_target_pairs={{0,1},{1,2},{2,3},{3,0},{4,5},{5,6},{6,7},{7,4},{8,9},{9,10},{10,1... | collective-permute-start | bytes 786440 | tf_op jit(solution)/shard_map/ppermute | solution.py:39
  97.6 8.1 %collective-permute-start.14 = (f32[2,8,2,16,128]{4,3,2,1,0:T(8,128)S(1)}, f32[2,8,2,16,128]{4,3,2,1,0:T(8,128)S(1)}, u32[]{:S(2)}, u32[]{:S(2)}) collective-permute-start(f32[2,8,2,16,128]{4,3,2,1,0:T(8,128)S(1)} %copy-done.21), channel_id=1, source_target_pairs={{0,2},{1,3},{2,0},{3,1},{4,6},{5,7},{6,4},{7,5},{8,10},{9,11},{10,... | collective-permute-start | bytes 786440 | tf_op jit(solution)/shard_map/ppermute | solution.py:39
  98.3 15.5 %collective-permute-start.15 = (f32[2,8,2,16,128]{4,3,2,1,0:T(8,128)S(1)}, f32[2,8,2,16,128]{4,3,2,1,0:T(8,128)S(1)}, u32[]{:S(2)}, u32[]{:S(2)}) collective-permute-start(f32[2,8,2,16,128]{4,3,2,1,0:T(8,128)S(1)} %copy-done.20), channel_id=1, source_target_pairs={{0,3},{1,0},{2,1},{3,2},{4,7},{5,4},{6,5},{7,6},{8,11},{9,8},{10,9... | collective-permute-start | bytes 786440 | tf_op jit(solution)/shard_map/ppermute | solution.py:39
  103.3 10.5 %copy-start.8 = (f32[2,8,2,16,128]{4,3,2,1,0:T(8,128)}, f32[2,8,2,16,128]{4,3,2,1,0:T(8,128)S(1)}, u32[]{:S(2)}) copy-start(f32[2,8,2,16,128]{4,3,2,1,0:T(8,128)S(1)} %collective-permute-done.13.g1) | copy-start | bytes 786436
  105.8 8.0 %copy-start.9 = (f32[2,8,2,16,128]{4,3,2,1,0:T(8,128)}, f32[2,8,2,16,128]{4,3,2,1,0:T(8,128)S(1)}, u32[]{:S(2)}) copy-start(f32[2,8,2,16,128]{4,3,2,1,0:T(8,128)S(1)} %collective-permute-done.14.g2) | copy-start | bytes 786436
  113.8 0.7 copy-start.10
  116.7 20.5 %collective-permute-start.17 = (f32[13,2,16,128]{3,2,1,0:T(8,128)}, f32[13,2,16,128]{3,2,1,0:T(8,128)S(1)}, u32[]{:S(2)}, u32[]{:S(2)}) collective-permute-start(f32[13,2,16,128]{3,2,1,0:T(8,128)} %get-tuple-element.45), channel_id=1, source_target_pairs={{0,32},{4,36},{8,40},{12,44},{16,48},{20,52},{24,56},{28,60},{32,6... | collective-permute-start | bytes 638984 | tf_op jit(solution)/shard_map/ppermute | solution.py:35
  120.5 16.7 %collective-permute-start.16 = (f32[7,2,16,128]{3,2,1,0:T(8,128)}, f32[7,2,16,128]{3,2,1,0:T(8,128)S(1)}, u32[]{:S(2)}, u32[]{:S(2)}) collective-permute-start(f32[7,2,16,128]{3,2,1,0:T(8,128)} %get-tuple-element.44), channel_id=1, source_target_pairs={{0,4},{4,8},{8,12},{12,16},{16,20},{20,24},{24,28},{28,32},{32,36}... | collective-permute-start | bytes 344072 | tf_op jit(solution)/shard_map/ppermute | solution.py:35
  121.5 15.7 %collective-permute-start.18 = (f32[4,2,16,128]{3,2,1,0:T(8,128)}, f32[4,2,16,128]{3,2,1,0:T(8,128)S(1)}, u32[]{:S(2)}, u32[]{:S(2)}) collective-permute-start(f32[4,2,16,128]{3,2,1,0:T(8,128)} %get-tuple-element.46), channel_id=1, source_target_pairs={{0,36},{4,40},{8,44},{12,48},{16,52},{20,56},{24,60},{28,64},{32,6... | collective-permute-start | bytes 196616 | tf_op jit(solution)/shard_map/ppermute | solution.py:35
  137.2 0.6 copy-start.17
  137.2 0.7 copy-start.16
  137.2 0.8 copy-start.12
  141.0 7.6 %copy-start.2 = (f32[24,2,16,128]{3,2,1,0:T(8,128)S(1)}, f32[24,2,16,128]{3,2,1,0:T(8,128)}, u32[]{:S(2)}) copy-start(f32[24,2,16,128]{3,2,1,0:T(8,128)} %update.1.n0) | copy-start | bytes 1179652
  142.0 30.0 %all-to-all-start.1 = ((f32[32,24,256]{2,1,0:T(8,128)}), f32[32,24,256]{2,1,0:T(8,128)S(1)}, u32[]{:S(2)}, u32[]{:S(2)}) async-start(f32[32,24,256]{2,1,0:T(8,128)} %broadcast_in_dim.2), calls=%async_computation.2 | async-start | bytes 1572864 | tf_op jit(solution)/shard_map/all_to_all | solution.py:392
  148.6 10.3 %collective-permute-start.19 = (f32[24,2,16,128]{3,2,1,0:T(8,128)S(1)}, f32[24,2,16,128]{3,2,1,0:T(8,128)S(1)}, u32[]{:S(2)}, u32[]{:S(2)}) collective-permute-start(f32[24,2,16,128]{3,2,1,0:T(8,128)S(1)} %copy-done.2), channel_id=1, source_target_pairs={{0,1},{1,2},{2,3},{3,0},{4,5},{5,6},{6,7},{7,4},{8,9},{9,10},{10,1... | collective-permute-start | bytes 1179656 | tf_op jit(solution)/shard_map/ppermute | solution.py:39
  148.7 11.9 %collective-permute-start.20 = (f32[24,2,16,128]{3,2,1,0:T(8,128)S(1)}, f32[24,2,16,128]{3,2,1,0:T(8,128)S(1)}, u32[]{:S(2)}, u32[]{:S(2)}) collective-permute-start(f32[24,2,16,128]{3,2,1,0:T(8,128)S(1)} %copy-done.2), channel_id=1, source_target_pairs={{0,2},{1,3},{2,0},{3,1},{4,6},{5,7},{6,4},{7,5},{8,10},{9,11},{10,... | collective-permute-start | bytes 1179656 | tf_op jit(solution)/shard_map/ppermute | solution.py:39
  149.1 20.7 %collective-permute-start.21 = (f32[24,2,16,128]{3,2,1,0:T(8,128)S(1)}, f32[24,2,16,128]{3,2,1,0:T(8,128)S(1)}, u32[]{:S(2)}, u32[]{:S(2)}) collective-permute-start(f32[24,2,16,128]{3,2,1,0:T(8,128)S(1)} %copy-done.2), channel_id=1, source_target_pairs={{0,3},{1,0},{2,1},{3,2},{4,7},{5,4},{6,5},{7,6},{8,11},{9,8},{10,9... | collective-permute-start | bytes 1179656 | tf_op jit(solution)/shard_map/ppermute | solution.py:39
  159.0 13.7 %copy-start.5 = (f32[24,2,16,128]{3,2,1,0:T(8,128)}, f32[24,2,16,128]{3,2,1,0:T(8,128)S(1)}, u32[]{:S(2)}) copy-start(f32[24,2,16,128]{3,2,1,0:T(8,128)S(1)} %collective-permute-done.19.n1) | copy-start | bytes 1179652
  160.6 12.1 %copy-start.6 = (f32[24,2,16,128]{3,2,1,0:T(8,128)}, f32[24,2,16,128]{3,2,1,0:T(8,128)S(1)}, u32[]{:S(2)}) copy-start(f32[24,2,16,128]{3,2,1,0:T(8,128)S(1)} %collective-permute-done.20.n2) | copy-start | bytes 1179652
  169.8 2.9 %copy-start.7 = (f32[24,2,16,128]{3,2,1,0:T(8,128)}, f32[24,2,16,128]{3,2,1,0:T(8,128)S(1)}, u32[]{:S(2)}) copy-start(f32[24,2,16,128]{3,2,1,0:T(8,128)S(1)} %collective-permute-done.21.n3) | copy-start | bytes 1179652
  172.0 3.6 %copy-start.1 = (f32[32,24,256]{2,1,0:T(8,128)}, f32[32,24,256]{2,1,0:T(8,128)S(1)}, u32[]{:S(2)}) copy-start(f32[32,24,256]{2,1,0:T(8,128)S(1)} %all-to-all-done.1) | copy-start | bytes 2359300
  172.0 3.6 %collective-permute-start.22 = (f32[3,256,256]{2,1,0:T(8,128)S(1)}, f32[3,256,256]{2,1,0:T(8,128)S(1)}, u32[]{:S(2)}, u32[]{:S(2)}) collective-permute-start(f32[3,256,256]{2,1,0:T(8,128)S(1)} %bitcast.18), channel_id=1, source_target_pairs={{0,4},{4,0},{8,12},{12,8},{16,20},{20,16},{24,28},{28,24},{32,36},... | collective-permute-start | bytes 2359304 | tf_op jit(solution)/shard_map/ppermute | solution.py:43
  175.6 0.9 copy-start.3
Sparse Core Ops, SparseCore 0:
  98.8 21.0 reduce-scatter.1

commit v5 on v4

--- a/solution.py
+++ b/solution.py
@@ -19,7 +19,9 @@
 SUB = PIECE_R // N_MODE
 N_CHIP = N_TILE // 2
 PART = 3 * SIDE // N_CHIP
-VMEM_BYTES = 56 * 1024 * 1024
+VMEM_BYTES = 24 * 1024 * 1024
+FORWARD_BYTES = 56 * 1024 * 1024
+SMALL_BYTES = 8 * 1024 * 1024
 
 far_floor = 0.1
 object_floor = 0.1
@@ -27,6 +29,7 @@
 F32 = jnp.float32
 BF16 = jnp.bfloat16
 ANY = pl.BlockSpec(memory_space=pl.ANY)
+HBM = pl.BlockSpec(memory_space=pltpu.HBM)
 SMEM = pl.BlockSpec(memory_space=pltpu.SMEM)
 VMEM = pl.BlockSpec(memory_space=pltpu.VMEM)
 
@@ -43,15 +46,26 @@
     return lax.ppermute(block, "tile", [(d, d ^ 1) for d in range(N_TILE)])
 
 
-def fourier_blocks():
+def fourier_table():
     indices = np.arange(SIDE)
     phases = (indices[:, None] * indices[None, :] % SIDE) * (2.0 * math.pi / SIDE)
     scaling = 1.0 / math.sqrt(SIDE)
-    re = (np.cos(phases) * scaling).astype(np.float32)
-    im = (-np.sin(phases) * scaling).astype(np.float32)
-    left = np.block([[re, -im], [im, re]])
-    right = np.block([[re, im], [-im, re]])
-    return jnp.asarray(left.astype(jnp.bfloat16)), jnp.asarray(right.astype(jnp.bfloat16))
+    both = np.stack([np.cos(phases) * scaling, -np.sin(phases) * scaling])
+    return jnp.asarray(both.astype(np.float32).astype(jnp.bfloat16))
+
+
+def expand_table(table, held, left, right, sem):
+    fetch = pltpu.make_async_copy(table, held, sem)
+    fetch.start()
+    fetch.wait()
+    re, im = held[0], held[1]
+    for out in (left, right):
+        out[:SIDE, :SIDE] = re
+        out[SIDE:, SIDE:] = re
+    left[:SIDE, SIDE:] = -im
+    left[SIDE:, :SIDE] = im
+    right[:SIDE, SIDE:] = im
+    right[SIDE:, :SIDE] = -im
 
 
 def canvas_index(row, col):
@@ -60,8 +74,8 @@
     return jnp.where(row < TILE_R, inside, below)
 
 
-def forward_kernel(info, own, right, b0, b1, b2, b3, probe, left_table, right_table,
-                   far, patch, p0, p1, p2, p3, power, sems):
+def forward_kernel(info, own, right, b0, b1, b2, b3, probe, table,
+                   far, patch, p0, p1, p2, p3, power, held, left_table, right_table, sems, table_sem):
     mode = pl.program_id(0)
 
     def piece_copy(s, q, source, index):
@@ -94,6 +108,7 @@
                                           pl.ds(PIECE_C * (q % 2), PIECE_C)]
                         pltpu.make_async_copy(source.at[below], target, sems.at[s, q]).start()
 
+        expand_table(table, held, left_table, right_table, table_sem)
         for s in range(2):
             for q in range(8):
                 piece_copy(s, q, own, 0).wait()
@@ -120,34 +135,38 @@
             out[...] = power[:, pl.ds(start, 64), :]
 
 
-def forward(info, own, right, below, probe, tables):
+def forward(info, own, right, below, probe, table):
     full = lambda *shape: pl.BlockSpec(shape, lambda k: (0,) * len(shape))
     return pl.pallas_call(
         forward_kernel,
         grid=(3,),
-        in_specs=[SMEM] + [ANY] * 6 + [
+        in_specs=[SMEM] + [HBM] * 6 + [
                   pl.BlockSpec((1, 2, SIDE, SIDE), lambda k: (k, 0, 0, 0)),
-                  full(512, 512), full(512, 512)],
+                  HBM],
         out_specs=[pl.BlockSpec((2, 1, 2, SIDE, SIDE), lambda k: (0, k, 0, 0, 0)),
                    full(2, 2, SIDE, SIDE)] + [full(2, 64, SIDE)] * 4,
-        out_shape=[jax.ShapeDtypeStruct((2, 3, 2, SIDE, SIDE), F32),
+        out_shape=[pltpu.HBM((2, 3, 2, SIDE, SIDE), F32),
                    jax.ShapeDtypeStruct((2, 2, SIDE, SIDE), F32)]
         + [jax.ShapeDtypeStruct((2, 64, SIDE), F32)] * 4,
-        scratch_shapes=[pltpu.VMEM((2, SIDE, SIDE), F32), pltpu.SemaphoreType.DMA((2, 8))],
-        compiler_params=pltpu.CompilerParams(vmem_limit_bytes=VMEM_BYTES),
+        scratch_shapes=[pltpu.VMEM((2, SIDE, SIDE), F32), pltpu.VMEM((2, SIDE, SIDE), BF16), pltpu.VMEM((512, 512), BF16),
+                        pltpu.VMEM((512, 512), BF16),
+                        pltpu.SemaphoreType.DMA((2, 8)), pltpu.SemaphoreType.DMA],
+        compiler_params=pltpu.CompilerParams(vmem_limit_bytes=FORWARD_BYTES),
         cost_estimate=pl.CostEstimate(flops=1700000000, bytes_accessed=12000000, transcendentals=0),
         name="forward",
-    )(info, own, right, *below, probe, *tables)
-
-
-def backward_kernel(info, far, probe, patch, f0, f1, f2, f3, left_table, right_table,
-                    mine, theirs, g0, g1, g2, g3, factor, grad):
+    )(info, own, right, *below, probe, table)
+
+
+def backward_kernel(info, far, probe, patch, f0, f1, f2, f3, table,
+                    mine, theirs, g0, g1, g2, g3, factor, grad, held, left_table, right_table,
+                    table_sem):
     mode = pl.program_id(0)
     me = info[5]
     first = info[6] == 0
 
     @pl.when(mode == 0)
     def _():
+        expand_table(table, held, left_table, right_table, table_sem)
         for j, part in enumerate((f0, f1, f2, f3)):
             start = pl.multiple_of(lax.rem(me + N_MODE - j, N_MODE) * 64, 64)
             factor[:, pl.ds(start, 64), :] = part[...]
@@ -183,7 +202,7 @@
                 out[:, q] = grad[:, :, pl.ds(start, SUB), PIECE_C * (q % 2):PIECE_C * (q % 2 + 1)]
 
 
-def backward(info, far, probe, patch, factors, tables):
+def backward(info, far, probe, patch, factors, table):
     full = lambda *shape: pl.BlockSpec(shape, lambda k: (0,) * len(shape))
     return pl.pallas_call(
         backward_kernel,
@@ -192,16 +211,19 @@
                   pl.BlockSpec((2, 1, 2, SIDE, SIDE), lambda k: (0, k, 0, 0, 0)),
                   pl.BlockSpec((1, 2, SIDE, SIDE), lambda k: (k, 0, 0, 0)),
                   full(2, 2, SIDE, SIDE)] + [full(2, 64, SIDE)] * 4
-        + [full(512, 512), full(512, 512)],
+        + [HBM],
         out_specs=[pl.BlockSpec((1, SIDE, SIDE), lambda k: (k, 0, 0))] * 2
         + [full(2, 8, 2, SUB, PIECE_C)] * 4,
         out_shape=[jax.ShapeDtypeStruct((3, SIDE, SIDE), F32)] * 2
         + [jax.ShapeDtypeStruct((2, 8, 2, SUB, PIECE_C), F32)] * 4,
-        scratch_shapes=[pltpu.VMEM((2, SIDE, SIDE), F32), pltpu.VMEM((2, 2, SIDE, SIDE), F32)],
+        scratch_shapes=[pltpu.VMEM((2, SIDE, SIDE), F32), pltpu.VMEM((2, 2, SIDE, SIDE), F32),
+                        pltpu.VMEM((2, SIDE, SIDE), BF16), pltpu.VMEM((512, 512), BF16),
+                        pltpu.VMEM((512, 512), BF16),
+                        pltpu.SemaphoreType.DMA],
         compiler_params=pltpu.CompilerParams(vmem_limit_bytes=VMEM_BYTES),
         cost_estimate=pl.CostEstimate(flops=1700000000, bytes_accessed=12000000, transcendentals=0),
         name="backward",
-    )(info, far, probe, patch, *factors, *tables)
+    )(info, far, probe, patch, *factors, table)
 
 
 def scatter_kernel(info, g0, g1, g2, g3, own, right, low, corner, canvas):
@@ -228,6 +250,7 @@
         out_specs=[VMEM] * 4,
         out_shape=[pieces(24), pieces(7), pieces(13), pieces(4)],
         scratch_shapes=[pltpu.VMEM((45, 2, SUB, PIECE_C), F32)],
+        compiler_params=pltpu.CompilerParams(vmem_limit_bytes=SMALL_BYTES),
         cost_estimate=pl.CostEstimate(flops=1000000, bytes_accessed=2000000, transcendentals=0),
         name="scatter",
     )(info, *parts)
@@ -288,23 +311,17 @@
         out_shape=jax.ShapeDtypeStruct(shape, F32),
         scratch_shapes=[pltpu.VMEM(shape, F32), pltpu.VMEM((TILE_R * TILE_C, SUB, PIECE_C), F32),
                         pltpu.SMEM((3, SUB, PIECE_C), F32), pltpu.SemaphoreType.DMA((4,))],
-        compiler_params=pltpu.CompilerParams(vmem_limit_bytes=VMEM_BYTES),
+        compiler_params=pltpu.CompilerParams(vmem_limit_bytes=SMALL_BYTES),
         cost_estimate=pl.CostEstimate(flops=1000000, bytes_accessed=2000000, transcendentals=0),
         name="update",
     )(info, pieces, own, right, low, corner, light)
 
 
-def join_pieces_kernel(info, n0, n1, n2, n3, out, held, in_sems, out_sems):
-    parts = (n0, n1, n2, n3)
-    reads = [pltpu.make_async_copy(part, held.at[j], in_sems.at[j]) for j, part in enumerate(parts)]
-    for read in reads:
-        read.start()
+def join_pieces_kernel(info, n0, n1, n2, n3, out, sems):
     writes = []
-    for j, read in enumerate(reads):
+    for j, part in enumerate((n0, n1, n2, n3)):
         start = pl.multiple_of(lax.rem(info[5] + N_MODE - j, N_MODE) * SUB, SUB)
-        read.wait()
-        writes.append(pltpu.make_async_copy(
-            held.at[j], out.at[:, :, pl.ds(start, SUB), :], out_sems.at[j]))
+        writes.append(pltpu.make_async_copy(part, out.at[:, :, pl.ds(start, SUB), :], sems.at[j]))
         writes[j].start()
     for write in writes:
         write.wait()
@@ -316,28 +333,22 @@
         in_specs=[SMEM] + [ANY] * 4,
         out_specs=pl.BlockSpec(memory_space=pltpu.HBM),
         out_shape=jax.ShapeDtypeStruct((TILE_R * TILE_C, 2, PIECE_R, PIECE_C), F32),
-        scratch_shapes=[pltpu.VMEM((N_MODE, TILE_R * TILE_C, 2, SUB, PIECE_C), F32),
-                        pltpu.SemaphoreType.DMA((N_MODE,)), pltpu.SemaphoreType.DMA((N_MODE,))],
-        compiler_params=pltpu.CompilerParams(vmem_limit_bytes=VMEM_BYTES),
+        scratch_shapes=[pltpu.SemaphoreType.DMA((N_MODE,))],
+        compiler_params=pltpu.CompilerParams(vmem_limit_bytes=2 * 1024 * 1024),
         cost_estimate=pl.CostEstimate(flops=0, bytes_accessed=3000000, transcendentals=0),
         name="join_pieces",
     )(info, *parts)
 
 
-def join_channels_kernel(info, mine, theirs, out, held, in_sems, out_sems):
+def join_channels_kernel(info, mine, theirs, out, sems):
     core = info[6]
-    steps = [(source, half, k) for k in range(3) for half, source in enumerate((mine, theirs))]
-    reads = [pltpu.make_async_copy(source.at[k], held.at[half, k], in_sems.at[half, k])
-             for source, half, k in steps]
-    for read in reads:
-        read.start()
     writes = []
-    for (source, half, k), read in zip(steps, reads):
-        read.wait()
+    for half, source in enumerate((mine, theirs)):
         channel = core if half == 0 else 1 - core
-        writes.append(pltpu.make_async_copy(
-            held.at[half, k], out.at[k, channel], out_sems.at[half, k]))
-        writes[-1].start()
+        for k in range(3):
+            writes.append(pltpu.make_async_copy(
+                source.at[k], out.at[k, channel], sems.at[half, k]))
+            writes[-1].start()
     for write in writes:
         write.wait()
 
@@ -348,9 +359,8 @@
         in_specs=[SMEM, ANY, ANY],
         out_specs=pl.BlockSpec(memory_space=pltpu.HBM),
         out_shape=jax.ShapeDtypeStruct((3, 2, SIDE, SIDE), F32),
-        scratch_shapes=[pltpu.VMEM((2, 3, SIDE, SIDE), F32),
-                        pltpu.SemaphoreType.DMA((2, 3)), pltpu.SemaphoreType.DMA((2, 3))],
-        compiler_params=pltpu.CompilerParams(vmem_limit_bytes=VMEM_BYTES),
+        scratch_shapes=[pltpu.SemaphoreType.DMA((2, 3))],
+        compiler_params=pltpu.CompilerParams(vmem_limit_bytes=2 * 1024 * 1024),
         cost_estimate=pl.CostEstimate(flops=0, bytes_accessed=3000000, transcendentals=0),
         name="join_channels",
     )(info, mine, theirs)
@@ -359,7 +369,7 @@
 def body(object_pieces, probe_modes, intensity, positions, counts):
     tile_index = lax.axis_index("tile")
     mode_index = lax.axis_index("mode")
-    tables = fourier_blocks()
+    table = fourier_table()
     tile_grid = object_pieces.reshape(TILE_R, TILE_C, 2, PIECE_R, PIECE_C)
     own_rows = lax.dynamic_slice_in_dim(object_pieces[:12], mode_index * SUB, SUB, axis=2)
     low = shifted(own_rows, -DEV_COLS)
@@ -378,7 +388,7 @@
     light = lax.psum_scatter(light_parts, "mode", scatter_dimension=0, tiled=True)
     below = [below] + [turned(below, j) for j in (1, 2, 3)]
 
-    far, patch, *powers = forward(info, object_pieces, right, below, probe_modes, tables)
+    far, patch, *powers = forward(info, object_pieces, right, below, probe_modes, table)
     received = [turned(powers[j], j) for j in (1, 2, 3)]
     power = (powers[0] + received[0]) + (received[1] + received[2])
     own_intensity = lax.dynamic_slice_in_dim(intensity, mode_index * 64, 64, axis=1)
@@ -386,7 +396,7 @@
     factor = live[:, None, None] * (jnp.sqrt(own_intensity) / jnp.sqrt(power + far_floor) - 1.0)
     factors = [factor] + [turned(factor, j) for j in (1, 2, 3)]
 
-    mine, theirs, *grads = backward(info, far, probe_modes, patch, factors, tables)
+    mine, theirs, *grads = backward(info, far, probe_modes, patch, factors, table)
 
     groups = [list(range(core, N_TILE, 2)) for core in range(2)]
     exchange = lambda blocks: lax.all_to_all(

time: 187 us -> 179 us (0.957)
  Pallas kernels: 26.7 us -> 19 us
    pallas_call x1, Pallas kernels: 7.42 us -> 4.82 us  [backward(): pl.pallas_call(backward_kernel, grid=(3,), in_specs=[SMEM, pl.BlockSpec((...]
    unnamed x52 -> x24, local copies, waits for them, and re-layouts: 3.66 us -> 3.98 us
  transfers between devices with their start and end apart: 26 -> 26, of which waited for: 18 -> 19; matrix products, arithmetic and copies ran while one was open for 3% -> 4% of each run, Pallas kernels for 3% -> 1%
where the time goes in v5:
time: 179 us; the launch traced here: 178 us
  waiting for transfers between devices  78.3 us (44%)
  starting transfers between devices  50.5 us (28%)
  Pallas kernels  19 us (11%)
  between operations  15 us (8%)
  local copies, waits for them, and re-layouts  12.2 us (7%)
  other arithmetic  3.37 us (2%)
    ppermute x15, waiting for transfers between devices, turned(): lax.ppermute(block, 'mode', [(i, (i + distance) % N_MODE) for i in range(...  52.8 us
    ppermute x6, waiting for transfers between devices, shifted(): lax.ppermute(block, 'tile', [(d, (d + distance) % N_TILE) for d in range(...  21.2 us
    all_to_all x2, starting transfers between devices, body(): lax.all_to_all(blocks, 'tile', 0, 0, axis_index_groups=groups, tiled=True)  18.8 us
    ppermute x6, starting transfers between devices, shifted(): lax.ppermute(block, 'tile', [(d, (d + distance) % N_TILE) for d in range(...  16.6 us
    ppermute x15, starting transfers between devices, turned(): lax.ppermute(block, 'mode', [(i, (i + distance) % N_MODE) for i in range(...  11.4 us
    pallas_call x1, Pallas kernels, forward(): pl.pallas_call(forward_kernel, grid=(3,), in_specs=[SMEM] + [HBM] * 6 + [...  8.27 us
    pallas_call x1, Pallas kernels, backward(): pl.pallas_call(backward_kernel, grid=(3,), in_specs=[SMEM, pl.BlockSpec((...  4.82 us
    unnamed x24, local copies, waits for them, and re-layouts  3.98 us
  transfers between devices with their start and end apart: 26, of which 19 were waited for; matrix products, arithmetic and copies ran while one was open for 4% of the time, Pallas kernels for 1%

profile of v5, /device:TPU:39, one launch (start us, length us, event | category | flops | bytes accessed | tf_op | source)
XLA Modules:
  0.0 178.3 jit_solution(13142435394710952102)
XLA Ops:
  7.2 1.1 slice-done
  8.3 8.5 %collective-permute-start.1 = (f32[12,2,16,128]{3,2,1,0:T(8,128)S(1)}, f32[12,2,16,128]{3,2,1,0:T(8,128)S(1)}, u32[]{:S(2)}, u32[]{:S(2)}) collective-permute-start(f32[12,2,16,128]{3,2,1,0:T(8,128)S(1)} %constant_dynamic-slice_fusion), channel_id=1, source_target_pairs={{0,224},{4,228},{8,232},{12,236},{16,240},{20,244},{24,248},{28,25... | collective-permute-start | bytes 589832 | tf_op jit(solution)/shard_map/ppermute | solution.py:38
  16.9 0.7 collective-permute-start.2
  17.5 1.0 slice_bitcast_fusion
  18.5 0.4 collective-permute-start
  18.9 0.2 slice_reduce_fusion
  19.1 7.3 %collective-permute-done.2 = f32[3,2,16,128]{3,2,1,0:T(8,128)S(1)} collective-permute-done((f32[3,2,16,128]{3,2,1,0:T(8,128)S(1)}, f32[3,2,16,128]{3,2,1,0:T(8,128)S(1)}, u32[]{:S(2)}, u32[]{:S(2)}) %collective-permute-start.2) | collective-permute-done | bytes 49184 | tf_op jit(solution)/shard_map/ppermute | solution.py:38
  26.5 0.3 collective-permute-start.3
  26.7 2.1 %collective-permute-start.4 = (f32[15,2,16,128]{3,2,1,0:T(8,128)S(1)}, f32[15,2,16,128]{3,2,1,0:T(8,128)S(1)}, u32[]{:S(2)}, u32[]{:S(2)}) collective-permute-start(f32[15,2,16,128]{3,2,1,0:T(8,128)S(1)} %pad_maximum_fusion.b0), channel_id=1, source_target_pairs={{0,2},{1,3},{2,0},{3,1},{4,6},{5,7},{6,4},{7,5},{8,10},{9,11},{10,... | collective-permute-start | bytes 737288 | tf_op jit(solution)/shard_map/ppermute | solution.py:42
  29.6 0.6 fusion
  30.1 0.6 fusion.1
  30.7 3.0 %stack.15.info = s32[8]{0:T(128)} concatenate(s32[1]{0:T(128)} %get-tuple-element.65, s32[1]{0:T(128)} %get-tuple-element.63, s32[1]{0:T(128)} %get-tuple-element.64, s32[1]{0:T(128)} %get-tuple-element.62, s32[1]{0:T(128)} %copy.13, s32[1]{0:T(128)} %bitcast, s32[1]{0:T(128)} %bitcast.1, s32[1]{0:T(128)} %bitcast.2), dimensions={0} | concatenate | bytes 64 | tf_op jit(solution)/shard_map/stack | solution.py:383
  33.8 0.7 collective-permute-done.4.b2
  34.5 6.9 %collective-permute-done.5.b3 = f32[15,2,16,128]{3,2,1,0:T(8,128)} collective-permute-done((f32[15,2,16,128]{3,2,1,0:T(8,128)S(1)}, f32[15,2,16,128]{3,2,1,0:T(8,128)}, u32[]{:S(2)}, u32[]{:S(2)}) %collective-permute-start.5) | collective-permute-done | bytes 245792 | tf_op jit(solution)/shard_map/ppermute | solution.py:42
  41.4 8.3 %forward.1 = (f32[2,3,2,256,256]{4,3,2,1,0:T(8,128)}, f32[2,2,256,256]{3,2,1,0:T(8,128)}, f32[2,64,256]{2,1,0:T(8,128)}, f32[2,64,256]{2,1,0:T(8,128)}, f32[2,64,256]{2,1,0:T(8,128)}, /*index=5*/f32[2,64,256]{2,1,0:T(8,128)}) custom-call(s32[8]{0:T(128)} %stack.15.info, f32[24,2,64,128]{3,2,1,0:T(8,128)} %pieces.1, f32[6,2,64,128]{3,2,1,0:T(8,128)} %copy-done.9, ...), custom_call_target="tpu_custom_call" | custom-call | flops 1700000000 | bytes 12000000 | tf_op jit(solution)/shard_map/forward/pallas_call | solution.py:140
  49.7 0.1 collective-permute-start.6
  49.8 0.9 collective-permute-start.7
  50.7 0.7 collective-permute-start.8
  51.5 3.1 %collective-permute-done.6 = f32[2,64,256]{2,1,0:T(8,128)S(1)} collective-permute-done((f32[2,64,256]{2,1,0:T(8,128)}, f32[2,64,256]{2,1,0:T(8,128)S(1)}, u32[]{:S(2)}, u32[]{:S(2)}) %collective-permute-start.6) | collective-permute-done | bytes 131104 | tf_op jit(solution)/shard_map/ppermute | solution.py:42
  54.5 1.0 collective-permute-done.7
  55.5 2.1 %collective-permute-done.8 = f32[2,64,256]{2,1,0:T(8,128)S(1)} collective-permute-done((f32[2,64,256]{2,1,0:T(8,128)}, f32[2,64,256]{2,1,0:T(8,128)S(1)}, u32[]{:S(2)}, u32[]{:S(2)}) %collective-permute-start.8) | collective-permute-done | bytes 131104 | tf_op jit(solution)/shard_map/ppermute | solution.py:42
  57.6 1.0 add_multiply_fusion.f0
  58.6 0.6 collective-permute-start.10
  59.2 2.2 %collective-permute-start.11 = (f32[2,64,256]{2,1,0:T(8,128)S(1)}, f32[2,64,256]{2,1,0:T(8,128)S(1)}, u32[]{:S(2)}, u32[]{:S(2)}) collective-permute-start(f32[2,64,256]{2,1,0:T(8,128)S(1)} %add_multiply_fusion.f0), channel_id=1, source_target_pairs={{0,3},{1,0},{2,1},{3,2},{4,7},{5,4},{6,5},{7,6},{8,11},{9,8},{10,9... | collective-permute-start | bytes 393224 | tf_op jit(solution)/shard_map/ppermute | solution.py:42
  61.4 0.5 collective-permute-start.9
  61.9 2.2 %collective-permute-done.10.f2 = f32[2,64,256]{2,1,0:T(8,128)S(1)} collective-permute-done((f32[2,64,256]{2,1,0:T(8,128)S(1)}, f32[2,64,256]{2,1,0:T(8,128)S(1)}, u32[]{:S(2)}, u32[]{:S(2)}) %collective-permute-start.10) | collective-permute-done | bytes 131104 | tf_op jit(solution)/shard_map/ppermute | solution.py:42
  64.1 1.3 collective-permute-done.11.f3
  65.4 1.1 collective-permute-done.9.f1
  66.6 1.9 %copy-done.2 = f32[2,3,2,256,256]{4,3,2,1,0:T(8,128)S(1)} copy-done((f32[2,3,2,256,256]{4,3,2,1,0:T(8,128)S(1)}, f32[2,3,2,256,256]{4,3,2,1,0:T(8,128)}, u32[]{:S(2)}) %copy-start.2) | copy-done | bytes 3145752
  68.5 1.2 copy-done.3
  69.7 4.8 %backward.1 = (f32[3,256,256]{2,1,0:T(8,128)S(1)}, f32[3,256,256]{2,1,0:T(8,128)S(1)}, f32[2,8,2,16,128]{4,3,2,1,0:T(8,128)S(1)}, f32[2,8,2,16,128]{4,3,2,1,0:T(...) custom-call(s32[8]{0:T(128)S(1)} %copy-done.6, f32[2,3,2,256,256]{4,3,2,1,0:T(8,128)S(1)} %copy-done.2, ...), custom_call_target="tpu_custom_call" | custom-call | flops 1700000000 | bytes 12000000 | tf_op jit(solution)/shard_map/backward/pallas_call | solution.py:207
  74.5 3.1 %collective-permute-start.12 = (f32[3,256,256]{2,1,0:T(8,128)S(1)}, f32[3,256,256]{2,1,0:T(8,128)S(1)}, u32[]{:S(2)}, u32[]{:S(2)}) collective-permute-start(f32[3,256,256]{2,1,0:T(8,128)S(1)} %get-tuple-element.39), channel_id=1, source_target_pairs={{0,4},{4,0},{8,12},{12,8},{16,20},{20,16},{24,28},{28,24},{32,36},... | collective-permute-start | bytes 2359304 | tf_op jit(solution)/shard_map/ppermute | solution.py:46
  77.6 1.9 %collective-permute-done.12 = f32[3,256,256]{2,1,0:T(8,128)S(1)} collective-permute-done((f32[3,256,256]{2,1,0:T(8,128)S(1)}, f32[3,256,256]{2,1,0:T(8,128)S(1)}, u32[]{:S(2)}, u32[]{:S(2)}) %collective-permute-start.12) | collective-permute-done | bytes 786464 | tf_op jit(solution)/shard_map/ppermute | solution.py:46
  79.5 1.0 add.46
  80.5 12.5 %all-to-all-start = ((f32[32,24,256]{2,1,0:T(8,128)}), f32[32,24,256]{2,1,0:T(8,128)}, u32[]{:S(2)}, u32[]{:S(2)}) async-start(f32[32,24,256]{2,1,0:T(8,128)} %bitcast.21), calls=%async_computation | async-start | bytes 1572864 | tf_op jit(solution)/shard_map/all_to_all | solution.py:402
  93.1 0.1 multiply_reduce_fusion
  93.2 0.7 copy.12
  94.0 1.5 collective-permute-start.13
  95.4 0.7 collective-permute-start.14
  96.1 0.3 collective-permute-start.15
  96.3 4.7 %collective-permute-done.13.g1 = f32[2,8,2,16,128]{4,3,2,1,0:T(8,128)S(1)} collective-permute-done((f32[2,8,2,16,128]{4,3,2,1,0:T(8,128)S(1)}, f32[2,8,2,16,128]{4,3,2,1,0:T(8,128)S(1)}, u32[]{:S(2)}, u32[]{:S(2)}) %collective-permute-start.13) | collective-permute-done | bytes 262176 | tf_op jit(solution)/shard_map/ppermute | solution.py:42
  101.0 2.5 %collective-permute-done.14.g2 = f32[2,8,2,16,128]{4,3,2,1,0:T(8,128)S(1)} collective-permute-done((f32[2,8,2,16,128]{4,3,2,1,0:T(8,128)S(1)}, f32[2,8,2,16,128]{4,3,2,1,0:T(8,128)S(1)}, u32[]{:S(2)}, u32[]{:S(2)}) %collective-permute-start.14) | collective-permute-done | bytes 262176 | tf_op jit(solution)/shard_map/ppermute | solution.py:42
  103.5 7.6 %collective-permute-done.15.g3 = f32[2,8,2,16,128]{4,3,2,1,0:T(8,128)S(1)} collective-permute-done((f32[2,8,2,16,128]{4,3,2,1,0:T(8,128)S(1)}, f32[2,8,2,16,128]{4,3,2,1,0:T(8,128)S(1)}, u32[]{:S(2)}, u32[]{:S(2)}) %collective-permute-start.15) | collective-permute-done | bytes 262176 | tf_op jit(solution)/shard_map/ppermute | solution.py:42
  111.2 0.7 scatter.1
  111.9 4.0 %collective-permute-start.17 = (f32[13,2,16,128]{3,2,1,0:T(8,128)S(1)}, f32[13,2,16,128]{3,2,1,0:T(8,128)S(1)}, u32[]{:S(2)}, u32[]{:S(2)}) collective-permute-start(f32[13,2,16,128]{3,2,1,0:T(8,128)S(1)} %get-tuple-element.45), channel_id=1, source_target_pairs={{0,32},{4,36},{8,40},{12,44},{16,48},{20,52},{24,56},{28,60},{32,6... | collective-permute-start | bytes 638984 | tf_op jit(solution)/shard_map/ppermute | solution.py:38
  115.9 0.9 collective-permute-start.16
  116.7 2.2 %collective-permute-start.18 = (f32[4,2,16,128]{3,2,1,0:T(8,128)S(1)}, f32[4,2,16,128]{3,2,1,0:T(8,128)S(1)}, u32[]{:S(2)}, u32[]{:S(2)}) collective-permute-start(f32[4,2,16,128]{3,2,1,0:T(8,128)S(1)} %get-tuple-element.46), channel_id=1, source_target_pairs={{0,36},{4,40},{8,44},{12,48},{16,52},{20,56},{24,60},{28,64},{32,6... | collective-permute-start | bytes 196616 | tf_op jit(solution)/shard_map/ppermute | solution.py:38
  118.9 13.9 %collective-permute-done.18.corner = f32[4,2,16,128]{3,2,1,0:T(8,128)S(1)} collective-permute-done((f32[4,2,16,128]{3,2,1,0:T(8,128)S(1)}, f32[4,2,16,128]{3,2,1,0:T(8,128)S(1)}, u32[]{:S(2)}, u32[]{:S(2)}) %collective-permute-start.18) | collective-permute-done | bytes 65568 | tf_op jit(solution)/shard_map/ppermute | solution.py:38
  132.8 1.2 reduce_sum.18
  134.0 0.8 copy-done.5
  134.9 1.7 update.1.n0
  136.6 0.9 broadcast_in_dim.2
  137.5 6.2 %all-to-all-start.1 = ((f32[32,24,256]{2,1,0:T(8,128)}), f32[32,24,256]{2,1,0:T(8,128)S(1)}, u32[]{:S(2)}, u32[]{:S(2)}) async-start(f32[32,24,256]{2,1,0:T(8,128)} %broadcast_in_dim.2), calls=%async_computation.2 | async-start | bytes 1572864 | tf_op jit(solution)/shard_map/all_to_all | solution.py:402
  143.8 0.1 collective-permute-start.19
  143.9 0.8 collective-permute-start.20
  144.7 0.8 collective-permute-start.21
  145.4 9.0 %collective-permute-done.19.n1 = f32[24,2,16,128]{3,2,1,0:T(8,128)S(1)} collective-permute-done((f32[24,2,16,128]{3,2,1,0:T(8,128)S(1)}, f32[24,2,16,128]{3,2,1,0:T(8,128)S(1)}, u32[]{:S(2)}, u32[]{:S(2)}) %collective-permute-start.19) | collective-permute-done | bytes 393248 | tf_op jit(solution)/shard_map/ppermute | solution.py:42
  154.4 1.6 collective-permute-done.20.n2
  156.1 8.9 %collective-permute-done.21.n3 = f32[24,2,16,128]{3,2,1,0:T(8,128)S(1)} collective-permute-done((f32[24,2,16,128]{3,2,1,0:T(8,128)S(1)}, f32[24,2,16,128]{3,2,1,0:T(8,128)S(1)}, u32[]{:S(2)}, u32[]{:S(2)}) %collective-permute-start.21) | collective-permute-done | bytes 393248 | tf_op jit(solution)/shard_map/ppermute | solution.py:42
  164.9 2.2 %all-to-all-done.1 = f32[32,24,256]{2,1,0:T(8,128)S(1)} async-done(((f32[32,24,256]{2,1,0:T(8,128)}), f32[32,24,256]{2,1,0:T(8,128)S(1)}, u32[]{:S(2)}, u32[]{:S(2)}) %all-to-all-start.1) | async-done | bytes 786464 | tf_op jit(solution)/shard_map/all_to_all | solution.py:402
  167.1 0.7 collective-permute-start.22
  167.8 1.7 join_pieces.1
  169.5 0.2 collective-permute-done.22.theirs
  169.7 1.7 join_channels.1
  (37 shorter events, 0.2 us)
Async XLA Ops:
  7.2 1.1 slice-start
  7.2 11.7 %copy-start.8 = (s32[2,2]{1,0:T(2,128)S(1)}, s32[2,2]{1,0:T(2,128)}, u32[]{:S(2)}) copy-start(s32[2,2]{1,0:T(2,128)} %param.9) | copy-start | bytes 52
  8.3 18.1 %collective-permute-start.1 = (f32[12,2,16,128]{3,2,1,0:T(8,128)S(1)}, f32[12,2,16,128]{3,2,1,0:T(8,128)S(1)}, u32[]{:S(2)}, u32[]{:S(2)}) collective-permute-start(f32[12,2,16,128]{3,2,1,0:T(8,128)S(1)} %constant_dynamic-slice_fusion), channel_id=1, source_target_pairs={{0,224},{4,228},{8,232},{12,236},{16,240},{20,244},{24,248},{28,25... | collective-permute-start | bytes 589832 | tf_op jit(solution)/shard_map/ppermute | solution.py:38
  16.9 9.6 %collective-permute-start.2 = (f32[3,2,16,128]{3,2,1,0:T(8,128)S(1)}, f32[3,2,16,128]{3,2,1,0:T(8,128)S(1)}, u32[]{:S(2)}, u32[]{:S(2)}) collective-permute-start(f32[3,2,16,128]{3,2,1,0:T(8,128)S(1)} %slice.35), channel_id=1, source_target_pairs={{0,220},{4,224},{8,228},{12,232},{16,236},{20,240},{24,244},{28,24... | collective-permute-start | bytes 147464 | tf_op jit(solution)/shard_map/ppermute | solution.py:38
  18.5 15.2 %collective-permute-start = (f32[6,2,64,128]{3,2,1,0:T(8,128)S(1)}, f32[6,2,64,128]{3,2,1,0:T(8,128)S(1)}, u32[]{:S(2)}, u32[]{:S(2)}) collective-permute-start(f32[6,2,64,128]{3,2,1,0:T(8,128)S(1)} %slice_bitcast_fusion), channel_id=1, source_target_pairs={{0,252},{4,0},{8,4},{12,8},{16,12},{20,16},{24,20},{28,24},{32,28}... | collective-permute-start | bytes 1179656 | tf_op jit(solution)/shard_map/ppermute | solution.py:38
  26.5 15.0 %copy-start.7 = (f32[15,2,16,128]{3,2,1,0:T(8,128)}, f32[15,2,16,128]{3,2,1,0:T(8,128)S(1)}, u32[]{:S(2)}) copy-start(f32[15,2,16,128]{3,2,1,0:T(8,128)S(1)} %pad_maximum_fusion.b0) | copy-start | bytes 737284
  26.5 7.3 %collective-permute-start.3 = (f32[15,2,16,128]{3,2,1,0:T(8,128)S(1)}, f32[15,2,16,128]{3,2,1,0:T(8,128)S(1)}, u32[]{:S(2)}, u32[]{:S(2)}) collective-permute-start(f32[15,2,16,128]{3,2,1,0:T(8,128)S(1)} %pad_maximum_fusion.b0), channel_id=1, source_target_pairs={{0,1},{1,2},{2,3},{3,0},{4,5},{5,6},{6,7},{7,4},{8,9},{9,10},{10,1... | collective-permute-start | bytes 737288 | tf_op jit(solution)/shard_map/ppermute | solution.py:42
  26.7 7.7 %collective-permute-start.4 = (f32[15,2,16,128]{3,2,1,0:T(8,128)S(1)}, f32[15,2,16,128]{3,2,1,0:T(8,128)S(1)}, u32[]{:S(2)}, u32[]{:S(2)}) collective-permute-start(f32[15,2,16,128]{3,2,1,0:T(8,128)S(1)} %pad_maximum_fusion.b0), channel_id=1, source_target_pairs={{0,2},{1,3},{2,0},{3,1},{4,6},{5,7},{6,4},{7,5},{8,10},{9,11},{10,... | collective-permute-start | bytes 737288 | tf_op jit(solution)/shard_map/ppermute | solution.py:42
  28.9 12.5 %collective-permute-start.5 = (f32[15,2,16,128]{3,2,1,0:T(8,128)S(1)}, f32[15,2,16,128]{3,2,1,0:T(8,128)}, u32[]{:S(2)}, u32[]{:S(2)}) collective-permute-start(f32[15,2,16,128]{3,2,1,0:T(8,128)S(1)} %pad_maximum_fusion.b0), channel_id=1, source_target_pairs={{0,3},{1,0},{2,1},{3,2},{4,7},{5,4},{6,5},{7,6},{8,11},{9,8},{10,9... | collective-permute-start | bytes 737288 | tf_op jit(solution)/shard_map/ppermute | solution.py:42
  33.8 32.8 %copy-start = (f32[3,2,256,256]{3,2,1,0:T(8,128)S(1)}, f32[3,2,256,256]{3,2,1,0:T(8,128)}, u32[]{:S(2)}) copy-start(f32[3,2,256,256]{3,2,1,0:T(8,128)} %probe.3) | copy-start | bytes 4718596
  33.8 32.8 %copy-start.4 = (bf16[2,256,256]{2,1,0:T(8,128)(2,1)S(1)}, bf16[2,256,256]{2,1,0:T(8,128)(2,1)}, u32[]{:S(2)}) copy-start(bf16[2,256,256]{2,1,0:T(8,128)(2,1)} %constant.88.clone.table) | copy-start | bytes 786436
  33.8 32.8 %copy-start.6 = (s32[8]{0:T(128)S(1)}, s32[8]{0:T(128)}, u32[]{:S(2)}) copy-start(s32[8]{0:T(128)} %stack.15.info) | copy-start | bytes 100
  33.8 7.7 %copy-start.9 = (f32[6,2,64,128]{3,2,1,0:T(8,128)}, f32[6,2,64,128]{3,2,1,0:T(8,128)S(1)}, u32[]{:S(2)}) copy-start(f32[6,2,64,128]{3,2,1,0:T(8,128)S(1)} %collective-permute-done.right) | copy-start | bytes 1179652
  33.8 7.6 %copy-start.10 = (f32[15,2,16,128]{3,2,1,0:T(8,128)}, f32[15,2,16,128]{3,2,1,0:T(8,128)S(1)}, u32[]{:S(2)}) copy-start(f32[15,2,16,128]{3,2,1,0:T(8,128)S(1)} %collective-permute-done.3.b1) | copy-start | bytes 737284
  34.5 7.0 %copy-start.11 = (f32[15,2,16,128]{3,2,1,0:T(8,128)}, f32[15,2,16,128]{3,2,1,0:T(8,128)S(1)}, u32[]{:S(2)}) copy-start(f32[15,2,16,128]{3,2,1,0:T(8,128)S(1)} %collective-permute-done.4.b2) | copy-start | bytes 737284
  49.7 4.8 %collective-permute-start.6 = (f32[2,64,256]{2,1,0:T(8,128)}, f32[2,64,256]{2,1,0:T(8,128)S(1)}, u32[]{:S(2)}, u32[]{:S(2)}) collective-permute-start(f32[2,64,256]{2,1,0:T(8,128)} %get-tuple-element.35), channel_id=1, source_target_pairs={{0,1},{1,2},{2,3},{3,0},{4,5},{5,6},{6,7},{7,4},{8,9},{9,10},{10,1... | collective-permute-start | bytes 393224 | tf_op jit(solution)/shard_map/ppermute | solution.py:42
  49.8 5.7 %collective-permute-start.7 = (f32[2,64,256]{2,1,0:T(8,128)}, f32[2,64,256]{2,1,0:T(8,128)S(1)}, u32[]{:S(2)}, u32[]{:S(2)}) collective-permute-start(f32[2,64,256]{2,1,0:T(8,128)} %get-tuple-element.36), channel_id=1, source_target_pairs={{0,2},{1,3},{2,0},{3,1},{4,6},{5,7},{6,4},{7,5},{8,10},{9,11},{10,... | collective-permute-start | bytes 393224 | tf_op jit(solution)/shard_map/ppermute | solution.py:42
  50.7 6.9 %collective-permute-start.8 = (f32[2,64,256]{2,1,0:T(8,128)}, f32[2,64,256]{2,1,0:T(8,128)S(1)}, u32[]{:S(2)}, u32[]{:S(2)}) collective-permute-start(f32[2,64,256]{2,1,0:T(8,128)} %get-tuple-element.37), channel_id=1, source_target_pairs={{0,3},{1,0},{2,1},{3,2},{4,7},{5,4},{6,5},{7,6},{8,11},{9,8},{10,9... | collective-permute-start | bytes 393224 | tf_op jit(solution)/shard_map/ppermute | solution.py:42
  58.6 5.5 %collective-permute-start.10 = (f32[2,64,256]{2,1,0:T(8,128)S(1)}, f32[2,64,256]{2,1,0:T(8,128)S(1)}, u32[]{:S(2)}, u32[]{:S(2)}) collective-permute-start(f32[2,64,256]{2,1,0:T(8,128)S(1)} %add_multiply_fusion.f0), channel_id=1, source_target_pairs={{0,2},{1,3},{2,0},{3,1},{4,6},{5,7},{6,4},{7,5},{8,10},{9,11},{10,... | collective-permute-start | bytes 393224 | tf_op jit(solution)/shard_map/ppermute | solution.py:42
  59.2 6.2 %collective-permute-start.11 = (f32[2,64,256]{2,1,0:T(8,128)S(1)}, f32[2,64,256]{2,1,0:T(8,128)S(1)}, u32[]{:S(2)}, u32[]{:S(2)}) collective-permute-start(f32[2,64,256]{2,1,0:T(8,128)S(1)} %add_multiply_fusion.f0), channel_id=1, source_target_pairs={{0,3},{1,0},{2,1},{3,2},{4,7},{5,4},{6,5},{7,6},{8,11},{9,8},{10,9... | collective-permute-start | bytes 393224 | tf_op jit(solution)/shard_map/ppermute | solution.py:42
  61.4 5.1 %collective-permute-start.9 = (f32[2,64,256]{2,1,0:T(8,128)S(1)}, f32[2,64,256]{2,1,0:T(8,128)S(1)}, u32[]{:S(2)}, u32[]{:S(2)}) collective-permute-start(f32[2,64,256]{2,1,0:T(8,128)S(1)} %add_multiply_fusion.f0), channel_id=1, source_target_pairs={{0,1},{1,2},{2,3},{3,0},{4,5},{5,6},{6,7},{7,4},{8,9},{9,10},{10,1... | collective-permute-start | bytes 393224 | tf_op jit(solution)/shard_map/ppermute | solution.py:42
  66.6 1.9 %copy-start.2 = (f32[2,3,2,256,256]{4,3,2,1,0:T(8,128)S(1)}, f32[2,3,2,256,256]{4,3,2,1,0:T(8,128)}, u32[]{:S(2)}) copy-start(f32[2,3,2,256,256]{4,3,2,1,0:T(8,128)} %get-tuple-element.32.far) | copy-start | bytes 9437188
  68.5 1.2 copy-start.3
  74.5 5.0 %collective-permute-start.12 = (f32[3,256,256]{2,1,0:T(8,128)S(1)}, f32[3,256,256]{2,1,0:T(8,128)S(1)}, u32[]{:S(2)}, u32[]{:S(2)}) collective-permute-start(f32[3,256,256]{2,1,0:T(8,128)S(1)} %get-tuple-element.39), channel_id=1, source_target_pairs={{0,4},{4,0},{8,12},{12,8},{16,20},{20,16},{24,28},{28,24},{32,36},... | collective-permute-start | bytes 2359304 | tf_op jit(solution)/shard_map/ppermute | solution.py:46
  80.5 52.3 %all-to-all-start = ((f32[32,24,256]{2,1,0:T(8,128)}), f32[32,24,256]{2,1,0:T(8,128)}, u32[]{:S(2)}, u32[]{:S(2)}) async-start(f32[32,24,256]{2,1,0:T(8,128)} %bitcast.21), calls=%async_computation | async-start | bytes 1572864 | tf_op jit(solution)/shard_map/all_to_all | solution.py:402
  93.0 41.0 %reduce-scatter.2.cloned.1.call-start = ((), (), s32[]{:S(2)}) async-start(), calls=%async_computation.3 | async-start | bytes 327680 | tf_op jit(solution)/shard_map/reduce_scatter | solution.py:388
  93.2 40.8 %copy-start.1 = (f32[24,2,64,128]{3,2,1,0:T(8,128)S(1)}, f32[24,2,64,128]{3,2,1,0:T(8,128)}, u32[]{:S(2)}) copy-start(f32[24,2,64,128]{3,2,1,0:T(8,128)} %pieces.1) | copy-start | bytes 4718596
  94.0 7.1 %collective-permute-start.13 = (f32[2,8,2,16,128]{4,3,2,1,0:T(8,128)S(1)}, f32[2,8,2,16,128]{4,3,2,1,0:T(8,128)S(1)}, u32[]{:S(2)}, u32[]{:S(2)}) collective-permute-start(f32[2,8,2,16,128]{4,3,2,1,0:T(8,128)S(1)} %get-tuple-element.41), channel_id=1, source_target_pairs={{0,1},{1,2},{2,3},{3,0},{4,5},{5,6},{6,7},{7,4},{8,9},{9,10},{10,1... | collective-permute-start | bytes 786440 | tf_op jit(solution)/shard_map/ppermute | solution.py:42
  95.4 8.1 %collective-permute-start.14 = (f32[2,8,2,16,128]{4,3,2,1,0:T(8,128)S(1)}, f32[2,8,2,16,128]{4,3,2,1,0:T(8,128)S(1)}, u32[]{:S(2)}, u32[]{:S(2)}) collective-permute-start(f32[2,8,2,16,128]{4,3,2,1,0:T(8,128)S(1)} %get-tuple-element.42), channel_id=1, source_target_pairs={{0,2},{1,3},{2,0},{3,1},{4,6},{5,7},{6,4},{7,5},{8,10},{9,11},{10,... | collective-permute-start | bytes 786440 | tf_op jit(solution)/shard_map/ppermute | solution.py:42
  96.1 15.1 %collective-permute-start.15 = (f32[2,8,2,16,128]{4,3,2,1,0:T(8,128)S(1)}, f32[2,8,2,16,128]{4,3,2,1,0:T(8,128)S(1)}, u32[]{:S(2)}, u32[]{:S(2)}) collective-permute-start(f32[2,8,2,16,128]{4,3,2,1,0:T(8,128)S(1)} %get-tuple-element.43), channel_id=1, source_target_pairs={{0,3},{1,0},{2,1},{3,2},{4,7},{5,4},{6,5},{7,6},{8,11},{9,8},{10,9... | collective-permute-start | bytes 786440 | tf_op jit(solution)/shard_map/ppermute | solution.py:42
  111.9 20.9 %collective-permute-start.17 = (f32[13,2,16,128]{3,2,1,0:T(8,128)S(1)}, f32[13,2,16,128]{3,2,1,0:T(8,128)S(1)}, u32[]{:S(2)}, u32[]{:S(2)}) collective-permute-start(f32[13,2,16,128]{3,2,1,0:T(8,128)S(1)} %get-tuple-element.45), channel_id=1, source_target_pairs={{0,32},{4,36},{8,40},{12,44},{16,48},{20,52},{24,56},{28,60},{32,6... | collective-permute-start | bytes 638984 | tf_op jit(solution)/shard_map/ppermute | solution.py:38
  115.9 16.9 %collective-permute-start.16 = (f32[7,2,16,128]{3,2,1,0:T(8,128)S(1)}, f32[7,2,16,128]{3,2,1,0:T(8,128)S(1)}, u32[]{:S(2)}, u32[]{:S(2)}) collective-permute-start(f32[7,2,16,128]{3,2,1,0:T(8,128)S(1)} %get-tuple-element.44), channel_id=1, source_target_pairs={{0,4},{4,8},{8,12},{12,16},{16,20},{20,24},{24,28},{28,32},{32,36}... | collective-permute-start | bytes 344072 | tf_op jit(solution)/shard_map/ppermute | solution.py:38
  116.7 16.1 %collective-permute-start.18 = (f32[4,2,16,128]{3,2,1,0:T(8,128)S(1)}, f32[4,2,16,128]{3,2,1,0:T(8,128)S(1)}, u32[]{:S(2)}, u32[]{:S(2)}) collective-permute-start(f32[4,2,16,128]{3,2,1,0:T(8,128)S(1)} %get-tuple-element.46), channel_id=1, source_target_pairs={{0,36},{4,40},{8,44},{12,48},{16,52},{20,56},{24,60},{28,64},{32,6... | collective-permute-start | bytes 196616 | tf_op jit(solution)/shard_map/ppermute | solution.py:38
  134.0 0.8 copy-start.5
  137.5 29.6 %all-to-all-start.1 = ((f32[32,24,256]{2,1,0:T(8,128)}), f32[32,24,256]{2,1,0:T(8,128)S(1)}, u32[]{:S(2)}, u32[]{:S(2)}) async-start(f32[32,24,256]{2,1,0:T(8,128)} %broadcast_in_dim.2), calls=%async_computation.2 | async-start | bytes 1572864 | tf_op jit(solution)/shard_map/all_to_all | solution.py:402
  143.8 10.6 %collective-permute-start.19 = (f32[24,2,16,128]{3,2,1,0:T(8,128)S(1)}, f32[24,2,16,128]{3,2,1,0:T(8,128)S(1)}, u32[]{:S(2)}, u32[]{:S(2)}) collective-permute-start(f32[24,2,16,128]{3,2,1,0:T(8,128)S(1)} %update.1.n0), channel_id=1, source_target_pairs={{0,1},{1,2},{2,3},{3,0},{4,5},{5,6},{6,7},{7,4},{8,9},{9,10},{10,1... | collective-permute-start | bytes 1179656 | tf_op jit(solution)/shard_map/ppermute | solution.py:42
  143.9 12.2 %collective-permute-start.20 = (f32[24,2,16,128]{3,2,1,0:T(8,128)S(1)}, f32[24,2,16,128]{3,2,1,0:T(8,128)S(1)}, u32[]{:S(2)}, u32[]{:S(2)}) collective-permute-start(f32[24,2,16,128]{3,2,1,0:T(8,128)S(1)} %update.1.n0), channel_id=1, source_target_pairs={{0,2},{1,3},{2,0},{3,1},{4,6},{5,7},{6,4},{7,5},{8,10},{9,11},{10,... | collective-permute-start | bytes 1179656 | tf_op jit(solution)/shard_map/ppermute | solution.py:42
  144.7 20.3 %collective-permute-start.21 = (f32[24,2,16,128]{3,2,1,0:T(8,128)S(1)}, f32[24,2,16,128]{3,2,1,0:T(8,128)S(1)}, u32[]{:S(2)}, u32[]{:S(2)}) collective-permute-start(f32[24,2,16,128]{3,2,1,0:T(8,128)S(1)} %update.1.n0), channel_id=1, source_target_pairs={{0,3},{1,0},{2,1},{3,2},{4,7},{5,4},{6,5},{7,6},{8,11},{9,8},{10,9... | collective-permute-start | bytes 1179656 | tf_op jit(solution)/shard_map/ppermute | solution.py:42
  167.1 2.6 %collective-permute-start.22 = (f32[3,256,256]{2,1,0:T(8,128)S(1)}, f32[3,256,256]{2,1,0:T(8,128)S(1)}, u32[]{:S(2)}, u32[]{:S(2)}) collective-permute-start(f32[3,256,256]{2,1,0:T(8,128)S(1)} %bitcast.18), channel_id=1, source_target_pairs={{0,4},{4,0},{8,12},{12,8},{16,20},{20,16},{24,28},{28,24},{32,36},... | collective-permute-start | bytes 2359304 | tf_op jit(solution)/shard_map/ppermute | solution.py:46
Sparse Core Ops, SparseCore 0:
  97.0 21.0 reduce-scatter.1

commit v6 on v5

--- a/solution.py
+++ b/solution.py
@@ -20,7 +20,7 @@
 N_CHIP = N_TILE // 2
 PART = 3 * SIDE // N_CHIP
 VMEM_BYTES = 24 * 1024 * 1024
-FORWARD_BYTES = 56 * 1024 * 1024
+FORWARD_BYTES = 40 * 1024 * 1024
 SMALL_BYTES = 8 * 1024 * 1024
 
 far_floor = 0.1
@@ -44,6 +44,10 @@
 
 def core_swap(block):
     return lax.ppermute(block, "tile", [(d, d ^ 1) for d in range(N_TILE)])
+
+
+def in_hbm(block):
+    return pltpu.with_memory_space_constraint(block, pltpu.HBM)
 
 
 def fourier_table():
@@ -388,7 +392,8 @@
     light = lax.psum_scatter(light_parts, "mode", scatter_dimension=0, tiled=True)
     below = [below] + [turned(below, j) for j in (1, 2, 3)]
 
-    far, patch, *powers = forward(info, object_pieces, right, below, probe_modes, table)
+    far, patch, *powers = forward(info, in_hbm(object_pieces), in_hbm(right),
+                                  [in_hbm(block) for block in below], probe_modes, in_hbm(table))
     received = [turned(powers[j], j) for j in (1, 2, 3)]
     power = (powers[0] + received[0]) + (received[1] + received[2])
     own_intensity = lax.dynamic_slice_in_dim(intensity, mode_index * 64, 64, axis=1)
@@ -396,7 +401,7 @@
     factor = live[:, None, None] * (jnp.sqrt(own_intensity) / jnp.sqrt(power + far_floor) - 1.0)
     factors = [factor] + [turned(factor, j) for j in (1, 2, 3)]
 
-    mine, theirs, *grads = backward(info, far, probe_modes, patch, factors, table)
+    mine, theirs, *grads = backward(info, in_hbm(far), probe_modes, patch, factors, in_hbm(table))
 
     groups = [list(range(core, N_TILE, 2)) for core in range(2)]
     exchange = lambda blocks: lax.all_to_all(
@@ -412,7 +417,7 @@
         (pieces, from_left, from_above, from_corner))
     share = jnp.sum(pieces, axis=0)
 
-    new = update(info, object_pieces, own, from_left, from_above, from_corner, light[0])
+    new = update(info, object_pieces, own, from_left, from_above, from_corner, in_hbm(light[0]))
     share, new = lax.optimization_barrier((share, new))
     gathered = exchange(jnp.broadcast_to(share[None], (N_CHIP, PART, SIDE)))
     new_parts = [new] + [turned(new, j) for j in (1, 2, 3)]

time: 179 us -> 176 us (0.983)
  local copies, waits for them, and re-layouts: 12.2 us -> 8.39 us
    unnamed x24 -> x20, local copies, waits for them, and re-layouts: 3.98 us -> 0.73 us
where the time goes in v6:
time: 176 us; the launch traced here: 175 us
  waiting for transfers between devices  78 us (44%)
  starting transfers between devices  51.2 us (29%)
  Pallas kernels  19.2 us (11%)
  between operations  14.9 us (8%)
  local copies, waits for them, and re-layouts  8.39 us (5%)
  other arithmetic  3.31 us (2%)
    ppermute x15, waiting for transfers between devices, turned(): lax.ppermute(block, 'mode', [(i, (i + distance) % N_MODE) for i in range(...  53 us
    ppermute x6, waiting for transfers between devices, shifted(): lax.ppermute(block, 'tile', [(d, (d + distance) % N_TILE) for d in range(...  20.7 us
    all_to_all x2, starting transfers between devices, body(): lax.all_to_all(blocks, 'tile', 0, 0, axis_index_groups=groups, tiled=True)  19.6 us
    ppermute x6, starting transfers between devices, shifted(): lax.ppermute(block, 'tile', [(d, (d + distance) % N_TILE) for d in range(...  16.6 us
    ppermute x15, starting transfers between devices, turned(): lax.ppermute(block, 'mode', [(i, (i + distance) % N_MODE) for i in range(...  11.3 us
    pallas_call x1, Pallas kernels, forward(): pl.pallas_call(forward_kernel, grid=(3,), in_specs=[SMEM] + [HBM] * 6 + [...  6.88 us
    pallas_call x1, Pallas kernels, backward(): pl.pallas_call(backward_kernel, grid=(3,), in_specs=[SMEM, pl.BlockSpec((...  6.12 us
    ppermute x2, starting transfers between devices, core_swap(): return lax.ppermute(block, 'tile', [(d, d ^ 1) for d in range(N_TILE)])  3.71 us
  transfers between devices with their start and end apart: 26, of which 19 were waited for; matrix products, arithmetic and copies ran while one was open for 4% of the time, Pallas kernels for 1%

profile of v6, /device:TPU:39, one launch (start us, length us, event | category | flops | bytes accessed | tf_op | source)
XLA Modules:
  0.0 175.0 jit_solution(1768132896589475979)
XLA Ops:
  7.2 1.1 slice-done
  8.3 8.5 %collective-permute-start.1 = (f32[12,2,16,128]{3,2,1,0:T(8,128)S(1)}, f32[12,2,16,128]{3,2,1,0:T(8,128)S(1)}, u32[]{:S(2)}, u32[]{:S(2)}) collective-permute-start(f32[12,2,16,128]{3,2,1,0:T(8,128)S(1)} %constant_dynamic-slice_fusion), channel_id=1, source_target_pairs={{0,224},{4,228},{8,232},{12,236},{16,240},{20,244},{24,248},{28,25... | collective-permute-start | bytes 589832 | tf_op jit(solution)/shard_map/ppermute | solution.py:38
  16.9 0.7 collective-permute-start.2
  17.5 1.0 slice_bitcast_fusion
  18.5 0.4 collective-permute-start
  18.9 0.2 slice_reduce_fusion
  19.1 7.3 %collective-permute-done.2 = f32[3,2,16,128]{3,2,1,0:T(8,128)S(1)} collective-permute-done((f32[3,2,16,128]{3,2,1,0:T(8,128)S(1)}, f32[3,2,16,128]{3,2,1,0:T(8,128)S(1)}, u32[]{:S(2)}, u32[]{:S(2)}) %collective-permute-start.2) | collective-permute-done | bytes 49184 | tf_op jit(solution)/shard_map/ppermute | solution.py:38
  26.5 0.3 collective-permute-start.3
  26.7 2.1 %collective-permute-start.4 = (f32[15,2,16,128]{3,2,1,0:T(8,128)S(1)}, f32[15,2,16,128]{3,2,1,0:T(8,128)S(1)}, u32[]{:S(2)}, u32[]{:S(2)}) collective-permute-start(f32[15,2,16,128]{3,2,1,0:T(8,128)S(1)} %pad_maximum_fusion.b0), channel_id=1, source_target_pairs={{0,2},{1,3},{2,0},{3,1},{4,6},{5,7},{6,4},{7,5},{8,10},{9,11},{10,... | collective-permute-start | bytes 737288 | tf_op jit(solution)/shard_map/ppermute | solution.py:42
  29.6 0.6 fusion
  30.1 0.6 fusion.1
  30.7 2.5 %stack.15.info = s32[8]{0:T(128)S(1)} concatenate(s32[1]{0:T(128)} %get-tuple-element.65, s32[1]{0:T(128)} %get-tuple-element.63, s32[1]{0:T(128)} %get-tuple-element.64, s32[1]{0:T(128)} %get-tuple-element.62, s32[1]{0:T(128)} %copy.13, s32[1]{0:T(128)} %bitcast, s32[1]{0:T(128)} %bitcast.1, s32[1]{0:T(128)} %bitcast.2), dimensions={0} | concatenate | bytes 64 | tf_op jit(solution)/shard_map/stack | solution.py:387
  33.3 1.2 collective-permute-done.4.b2
  34.5 0.7 copy-done.9
  35.2 6.3 %collective-permute-done.5.b3 = f32[15,2,16,128]{3,2,1,0:T(8,128)} collective-permute-done((f32[15,2,16,128]{3,2,1,0:T(8,128)S(1)}, f32[15,2,16,128]{3,2,1,0:T(8,128)}, u32[]{:S(2)}, u32[]{:S(2)}) %collective-permute-start.5) | collective-permute-done | bytes 245792 | tf_op jit(solution)/shard_map/ppermute | solution.py:42
  41.4 6.9 %forward.1 = (f32[2,3,2,256,256]{4,3,2,1,0:T(8,128)}, f32[2,2,256,256]{3,2,1,0:T(8,128)S(1)}, f32[2,64,256]{2,1,0:T(8,128)S(1)}, f32[2,64,256]{2,1,0:T(8,128)S(1...) custom-call(s32[8]{0:T(128)S(1)} %stack.15.info, f32[24,2,64,128]{3,2,1,0:T(8,128)} %pieces.1, ...), custom_call_target="tpu_custom_call" | custom-call | flops 1700000000 | bytes 12000000 | tf_op jit(solution)/shard_map/forward/pallas_call | solution.py:144
  48.3 0.1 collective-permute-start.6
  48.4 0.9 collective-permute-start.7
  49.3 0.7 collective-permute-start.8
  50.1 2.9 %collective-permute-done.6 = f32[2,64,256]{2,1,0:T(8,128)S(1)} collective-permute-done((f32[2,64,256]{2,1,0:T(8,128)S(1)}, f32[2,64,256]{2,1,0:T(8,128)S(1)}, u32[]{:S(2)}, u32[]{:S(2)}) %collective-permute-start.6) | collective-permute-done | bytes 131104 | tf_op jit(solution)/shard_map/ppermute | solution.py:42
  52.9 1.0 collective-permute-done.7
  53.9 2.0 %collective-permute-done.8 = f32[2,64,256]{2,1,0:T(8,128)S(1)} collective-permute-done((f32[2,64,256]{2,1,0:T(8,128)S(1)}, f32[2,64,256]{2,1,0:T(8,128)S(1)}, u32[]{:S(2)}, u32[]{:S(2)}) %collective-permute-start.8) | collective-permute-done | bytes 131104 | tf_op jit(solution)/shard_map/ppermute | solution.py:42
  55.9 1.0 add_multiply_fusion.f0
  56.9 0.5 collective-permute-start.10
  57.4 2.4 %collective-permute-start.11 = (f32[2,64,256]{2,1,0:T(8,128)S(1)}, f32[2,64,256]{2,1,0:T(8,128)S(1)}, u32[]{:S(2)}, u32[]{:S(2)}) collective-permute-start(f32[2,64,256]{2,1,0:T(8,128)S(1)} %add_multiply_fusion.f0), channel_id=1, source_target_pairs={{0,3},{1,0},{2,1},{3,2},{4,7},{5,4},{6,5},{7,6},{8,11},{9,8},{10,9... | collective-permute-start | bytes 393224 | tf_op jit(solution)/shard_map/ppermute | solution.py:42
  59.8 0.3 collective-permute-start.9
  60.1 2.3 %collective-permute-done.10.f2 = f32[2,64,256]{2,1,0:T(8,128)S(1)} collective-permute-done((f32[2,64,256]{2,1,0:T(8,128)S(1)}, f32[2,64,256]{2,1,0:T(8,128)S(1)}, u32[]{:S(2)}, u32[]{:S(2)}) %collective-permute-start.10) | collective-permute-done | bytes 131104 | tf_op jit(solution)/shard_map/ppermute | solution.py:42
  62.4 1.3 collective-permute-done.11.f3
  63.7 1.3 collective-permute-done.9.f1
  65.0 6.1 %backward.1 = (f32[3,256,256]{2,1,0:T(8,128)S(1)}, f32[3,256,256]{2,1,0:T(8,128)S(1)}, f32[2,8,2,16,128]{4,3,2,1,0:T(8,128)S(1)}, f32[2,8,2,16,128]{4,3,2,1,0:T(...) custom-call(s32[8]{0:T(128)S(1)} %stack.15.info, ...), custom_call_target="tpu_custom_call" | custom-call | flops 1700000000 | bytes 12000000 | tf_op jit(solution)/shard_map/backward/pallas_call | solution.py:211
  71.1 3.0 %collective-permute-start.12 = (f32[3,256,256]{2,1,0:T(8,128)S(1)}, f32[3,256,256]{2,1,0:T(8,128)S(1)}, u32[]{:S(2)}, u32[]{:S(2)}) collective-permute-start(f32[3,256,256]{2,1,0:T(8,128)S(1)} %get-tuple-element.39), channel_id=1, source_target_pairs={{0,4},{4,0},{8,12},{12,8},{16,20},{20,16},{24,28},{28,24},{32,36},... | collective-permute-start | bytes 2359304 | tf_op jit(solution)/shard_map/ppermute | solution.py:46
  74.1 1.9 %collective-permute-done.12 = f32[3,256,256]{2,1,0:T(8,128)S(1)} collective-permute-done((f32[3,256,256]{2,1,0:T(8,128)S(1)}, f32[3,256,256]{2,1,0:T(8,128)S(1)}, u32[]{:S(2)}, u32[]{:S(2)}) %collective-permute-start.12) | collective-permute-done | bytes 786464 | tf_op jit(solution)/shard_map/ppermute | solution.py:46
  76.1 1.0 add.46
  77.0 12.6 %all-to-all-start = ((f32[32,24,256]{2,1,0:T(8,128)}), f32[32,24,256]{2,1,0:T(8,128)}, u32[]{:S(2)}, u32[]{:S(2)}) async-start(f32[32,24,256]{2,1,0:T(8,128)} %bitcast.6), calls=%async_computation | async-start | bytes 1572864 | tf_op jit(solution)/shard_map/all_to_all | solution.py:407
  89.7 0.0 reduce-scatter.2.cloned.1.call-start
  89.7 0.1 multiply_reduce_fusion
  89.8 0.7 copy.12
  90.6 1.3 collective-permute-start.13
  91.9 0.6 collective-permute-start.14
  92.5 0.4 collective-permute-start.15
  93.0 4.9 %collective-permute-done.13.g1 = f32[2,8,2,16,128]{4,3,2,1,0:T(8,128)S(1)} collective-permute-done((f32[2,8,2,16,128]{4,3,2,1,0:T(8,128)}, f32[2,8,2,16,128]{4,3,2,1,0:T(8,128)S(1)}, u32[]{:S(2)}, u32[]{:S(2)}) %collective-permute-start.13) | collective-permute-done | bytes 262176 | tf_op jit(solution)/shard_map/ppermute | solution.py:42
  97.8 2.4 %collective-permute-done.14.g2 = f32[2,8,2,16,128]{4,3,2,1,0:T(8,128)S(1)} collective-permute-done((f32[2,8,2,16,128]{4,3,2,1,0:T(8,128)}, f32[2,8,2,16,128]{4,3,2,1,0:T(8,128)S(1)}, u32[]{:S(2)}, u32[]{:S(2)}) %collective-permute-start.14) | collective-permute-done | bytes 262176 | tf_op jit(solution)/shard_map/ppermute | solution.py:42
  100.2 7.9 %collective-permute-done.15.g3 = f32[2,8,2,16,128]{4,3,2,1,0:T(8,128)S(1)} collective-permute-done((f32[2,8,2,16,128]{4,3,2,1,0:T(8,128)}, f32[2,8,2,16,128]{4,3,2,1,0:T(8,128)S(1)}, u32[]{:S(2)}, u32[]{:S(2)}) %collective-permute-start.15) | collective-permute-done | bytes 262176 | tf_op jit(solution)/shard_map/ppermute | solution.py:42
  108.2 0.7 scatter.1
  108.9 4.3 %collective-permute-start.17 = (f32[13,2,16,128]{3,2,1,0:T(8,128)S(1)}, f32[13,2,16,128]{3,2,1,0:T(8,128)S(1)}, u32[]{:S(2)}, u32[]{:S(2)}) collective-permute-start(f32[13,2,16,128]{3,2,1,0:T(8,128)S(1)} %get-tuple-element.45), channel_id=1, source_target_pairs={{0,32},{4,36},{8,40},{12,44},{16,48},{20,52},{24,56},{28,60},{32,6... | collective-permute-start | bytes 638984 | tf_op jit(solution)/shard_map/ppermute | solution.py:38
  113.2 0.9 collective-permute-start.16
  114.1 1.8 %collective-permute-start.18 = (f32[4,2,16,128]{3,2,1,0:T(8,128)S(1)}, f32[4,2,16,128]{3,2,1,0:T(8,128)S(1)}, u32[]{:S(2)}, u32[]{:S(2)}) collective-permute-start(f32[4,2,16,128]{3,2,1,0:T(8,128)S(1)} %get-tuple-element.46), channel_id=1, source_target_pairs={{0,36},{4,40},{8,44},{12,48},{16,52},{20,56},{24,60},{28,64},{32,6... | collective-permute-start | bytes 196616 | tf_op jit(solution)/shard_map/ppermute | solution.py:38
  115.9 13.4 %collective-permute-done.18.corner = f32[4,2,16,128]{3,2,1,0:T(8,128)S(1)} collective-permute-done((f32[4,2,16,128]{3,2,1,0:T(8,128)S(1)}, f32[4,2,16,128]{3,2,1,0:T(8,128)S(1)}, u32[]{:S(2)}, u32[]{:S(2)}) %collective-permute-start.18) | collective-permute-done | bytes 65568 | tf_op jit(solution)/shard_map/ppermute | solution.py:38
  129.3 1.2 reduce_sum.18
  130.5 0.0 reduce-scatter.2.cloned.1.call-done
  130.6 2.0 %update.1.n0 = f32[24,2,16,128]{3,2,1,0:T(8,128)S(1)} custom-call(s32[8]{0:T(128)S(1)} %stack.15.info, f32[24,2,64,128]{3,2,1,0:T(8,128)S(1)} %copy-done.1, f32[24,2,16,128]{3,2,1,0:T(8,128)S(1)} %get-tuple-element.48.own, f32[7,2,16,128]{3,2,1,0:T(8,128)S(1)} %collective-permute-done.16.right, f32[13,2,16,128]{3,2,1,0:T(8,128)S(1)} %collective-permute-done.17.low, ...), custom_call_target="tpu_custom_call" | custom-call | flops 1000000 | bytes 2000000 | tf_op jit(solution)/shard_map/update/pallas_call | solution.py:311
  132.6 0.9 broadcast_in_dim.2
  133.5 7.0 %all-to-all-start.1 = ((f32[32,24,256]{2,1,0:T(8,128)}), f32[32,24,256]{2,1,0:T(8,128)S(1)}, u32[]{:S(2)}, u32[]{:S(2)}) async-start(f32[32,24,256]{2,1,0:T(8,128)} %broadcast_in_dim.2), calls=%async_computation.2 | async-start | bytes 1572864 | tf_op jit(solution)/shard_map/all_to_all | solution.py:407
  140.5 0.1 collective-permute-start.19
  140.6 0.2 collective-permute-start.20
  140.8 1.2 collective-permute-start.21
  142.0 8.8 %collective-permute-done.19.n1 = f32[24,2,16,128]{3,2,1,0:T(8,128)S(1)} collective-permute-done((f32[24,2,16,128]{3,2,1,0:T(8,128)S(1)}, f32[24,2,16,128]{3,2,1,0:T(8,128)S(1)}, u32[]{:S(2)}, u32[]{:S(2)}) %collective-permute-start.19) | collective-permute-done | bytes 393248 | tf_op jit(solution)/shard_map/ppermute | solution.py:42
  150.8 1.6 collective-permute-done.20.n2
  152.4 9.2 %collective-permute-done.21.n3 = f32[24,2,16,128]{3,2,1,0:T(8,128)S(1)} collective-permute-done((f32[24,2,16,128]{3,2,1,0:T(8,128)S(1)}, f32[24,2,16,128]{3,2,1,0:T(8,128)S(1)}, u32[]{:S(2)}, u32[]{:S(2)}) %collective-permute-start.21) | collective-permute-done | bytes 393248 | tf_op jit(solution)/shard_map/ppermute | solution.py:42
  161.6 2.2 %all-to-all-done.1 = f32[32,24,256]{2,1,0:T(8,128)S(1)} async-done(((f32[32,24,256]{2,1,0:T(8,128)}), f32[32,24,256]{2,1,0:T(8,128)S(1)}, u32[]{:S(2)}, u32[]{:S(2)}) %all-to-all-start.1) | async-done | bytes 786464 | tf_op jit(solution)/shard_map/all_to_all | solution.py:407
  163.8 0.7 collective-permute-start.22
  164.5 1.7 join_pieces.1
  166.2 0.2 collective-permute-done.22.theirs
  166.4 1.7 join_channels.1
  (33 shorter events, 0.1 us)
Async XLA Ops:
  7.2 1.1 slice-start
  7.2 11.7 %copy-start.6 = (s32[2,2]{1,0:T(2,128)S(1)}, s32[2,2]{1,0:T(2,128)}, u32[]{:S(2)}) copy-start(s32[2,2]{1,0:T(2,128)} %param.9) | copy-start | bytes 52
  7.2 34.2 %copy-start = (f32[3,2,256,256]{3,2,1,0:T(8,128)S(1)}, f32[3,2,256,256]{3,2,1,0:T(8,128)}, u32[]{:S(2)}) copy-start(f32[3,2,256,256]{3,2,1,0:T(8,128)} %probe.3) | copy-start | bytes 4718596
  8.3 18.1 %collective-permute-start.1 = (f32[12,2,16,128]{3,2,1,0:T(8,128)S(1)}, f32[12,2,16,128]{3,2,1,0:T(8,128)S(1)}, u32[]{:S(2)}, u32[]{:S(2)}) collective-permute-start(f32[12,2,16,128]{3,2,1,0:T(8,128)S(1)} %constant_dynamic-slice_fusion), channel_id=1, source_target_pairs={{0,224},{4,228},{8,232},{12,236},{16,240},{20,244},{24,248},{28,25... | collective-permute-start | bytes 589832 | tf_op jit(solution)/shard_map/ppermute | solution.py:38
  16.9 9.6 %collective-permute-start.2 = (f32[3,2,16,128]{3,2,1,0:T(8,128)S(1)}, f32[3,2,16,128]{3,2,1,0:T(8,128)S(1)}, u32[]{:S(2)}, u32[]{:S(2)}) collective-permute-start(f32[3,2,16,128]{3,2,1,0:T(8,128)S(1)} %slice.35), channel_id=1, source_target_pairs={{0,220},{4,224},{8,228},{12,232},{16,236},{20,240},{24,244},{28,24... | collective-permute-start | bytes 147464 | tf_op jit(solution)/shard_map/ppermute | solution.py:38
  18.5 14.7 %collective-permute-start = (f32[6,2,64,128]{3,2,1,0:T(8,128)S(1)}, f32[6,2,64,128]{3,2,1,0:T(8,128)S(1)}, u32[]{:S(2)}, u32[]{:S(2)}) collective-permute-start(f32[6,2,64,128]{3,2,1,0:T(8,128)S(1)} %slice_bitcast_fusion), channel_id=1, source_target_pairs={{0,252},{4,0},{8,4},{12,8},{16,12},{20,16},{24,20},{28,24},{32,28}... | collective-permute-start | bytes 1179656 | tf_op jit(solution)/shard_map/ppermute | solution.py:38
  26.5 15.0 %copy-start.5 = (f32[15,2,16,128]{3,2,1,0:T(8,128)}, f32[15,2,16,128]{3,2,1,0:T(8,128)S(1)}, u32[]{:S(2)}) copy-start(f32[15,2,16,128]{3,2,1,0:T(8,128)S(1)} %pad_maximum_fusion.b0) | copy-start | bytes 737284
  26.5 6.8 %collective-permute-start.3 = (f32[15,2,16,128]{3,2,1,0:T(8,128)S(1)}, f32[15,2,16,128]{3,2,1,0:T(8,128)S(1)}, u32[]{:S(2)}, u32[]{:S(2)}) collective-permute-start(f32[15,2,16,128]{3,2,1,0:T(8,128)S(1)} %pad_maximum_fusion.b0), channel_id=1, source_target_pairs={{0,1},{1,2},{2,3},{3,0},{4,5},{5,6},{6,7},{7,4},{8,9},{9,10},{10,1... | collective-permute-start | bytes 737288 | tf_op jit(solution)/shard_map/ppermute | solution.py:42
  26.7 7.7 %collective-permute-start.4 = (f32[15,2,16,128]{3,2,1,0:T(8,128)S(1)}, f32[15,2,16,128]{3,2,1,0:T(8,128)S(1)}, u32[]{:S(2)}, u32[]{:S(2)}) collective-permute-start(f32[15,2,16,128]{3,2,1,0:T(8,128)S(1)} %pad_maximum_fusion.b0), channel_id=1, source_target_pairs={{0,2},{1,3},{2,0},{3,1},{4,6},{5,7},{6,4},{7,5},{8,10},{9,11},{10,... | collective-permute-start | bytes 737288 | tf_op jit(solution)/shard_map/ppermute | solution.py:42
  28.9 12.5 %collective-permute-start.5 = (f32[15,2,16,128]{3,2,1,0:T(8,128)S(1)}, f32[15,2,16,128]{3,2,1,0:T(8,128)}, u32[]{:S(2)}, u32[]{:S(2)}) collective-permute-start(f32[15,2,16,128]{3,2,1,0:T(8,128)S(1)} %pad_maximum_fusion.b0), channel_id=1, source_target_pairs={{0,3},{1,0},{2,1},{3,2},{4,7},{5,4},{6,5},{7,6},{8,11},{9,8},{10,9... | collective-permute-start | bytes 737288 | tf_op jit(solution)/shard_map/ppermute | solution.py:42
  33.2 1.2 copy-start.7
  33.3 1.2 copy-start.8
  34.5 0.7 copy-start.9
  48.3 4.6 %collective-permute-start.6 = (f32[2,64,256]{2,1,0:T(8,128)S(1)}, f32[2,64,256]{2,1,0:T(8,128)S(1)}, u32[]{:S(2)}, u32[]{:S(2)}) collective-permute-start(f32[2,64,256]{2,1,0:T(8,128)S(1)} %get-tuple-element.35), channel_id=1, source_target_pairs={{0,1},{1,2},{2,3},{3,0},{4,5},{5,6},{6,7},{7,4},{8,9},{9,10},{10,1... | collective-permute-start | bytes 393224 | tf_op jit(solution)/shard_map/ppermute | solution.py:42
  48.4 5.5 %collective-permute-start.7 = (f32[2,64,256]{2,1,0:T(8,128)S(1)}, f32[2,64,256]{2,1,0:T(8,128)S(1)}, u32[]{:S(2)}, u32[]{:S(2)}) collective-permute-start(f32[2,64,256]{2,1,0:T(8,128)S(1)} %get-tuple-element.36), channel_id=1, source_target_pairs={{0,2},{1,3},{2,0},{3,1},{4,6},{5,7},{6,4},{7,5},{8,10},{9,11},{10,... | collective-permute-start | bytes 393224 | tf_op jit(solution)/shard_map/ppermute | solution.py:42
  49.3 6.6 %collective-permute-start.8 = (f32[2,64,256]{2,1,0:T(8,128)S(1)}, f32[2,64,256]{2,1,0:T(8,128)S(1)}, u32[]{:S(2)}, u32[]{:S(2)}) collective-permute-start(f32[2,64,256]{2,1,0:T(8,128)S(1)} %get-tuple-element.37), channel_id=1, source_target_pairs={{0,3},{1,0},{2,1},{3,2},{4,7},{5,4},{6,5},{7,6},{8,11},{9,8},{10,9... | collective-permute-start | bytes 393224 | tf_op jit(solution)/shard_map/ppermute | solution.py:42
  56.9 5.5 %collective-permute-start.10 = (f32[2,64,256]{2,1,0:T(8,128)S(1)}, f32[2,64,256]{2,1,0:T(8,128)S(1)}, u32[]{:S(2)}, u32[]{:S(2)}) collective-permute-start(f32[2,64,256]{2,1,0:T(8,128)S(1)} %add_multiply_fusion.f0), channel_id=1, source_target_pairs={{0,2},{1,3},{2,0},{3,1},{4,6},{5,7},{6,4},{7,5},{8,10},{9,11},{10,... | collective-permute-start | bytes 393224 | tf_op jit(solution)/shard_map/ppermute | solution.py:42
  57.4 6.3 %collective-permute-start.11 = (f32[2,64,256]{2,1,0:T(8,128)S(1)}, f32[2,64,256]{2,1,0:T(8,128)S(1)}, u32[]{:S(2)}, u32[]{:S(2)}) collective-permute-start(f32[2,64,256]{2,1,0:T(8,128)S(1)} %add_multiply_fusion.f0), channel_id=1, source_target_pairs={{0,3},{1,0},{2,1},{3,2},{4,7},{5,4},{6,5},{7,6},{8,11},{9,8},{10,9... | collective-permute-start | bytes 393224 | tf_op jit(solution)/shard_map/ppermute | solution.py:42
  59.8 5.2 %collective-permute-start.9 = (f32[2,64,256]{2,1,0:T(8,128)S(1)}, f32[2,64,256]{2,1,0:T(8,128)S(1)}, u32[]{:S(2)}, u32[]{:S(2)}) collective-permute-start(f32[2,64,256]{2,1,0:T(8,128)S(1)} %add_multiply_fusion.f0), channel_id=1, source_target_pairs={{0,1},{1,2},{2,3},{3,0},{4,5},{5,6},{6,7},{7,4},{8,9},{9,10},{10,1... | collective-permute-start | bytes 393224 | tf_op jit(solution)/shard_map/ppermute | solution.py:42
  71.1 6.0 %copy-start.2 = (f32[2,8,2,16,128]{4,3,2,1,0:T(8,128)}, f32[2,8,2,16,128]{4,3,2,1,0:T(8,128)S(1)}, u32[]{:S(2)}) copy-start(f32[2,8,2,16,128]{4,3,2,1,0:T(8,128)S(1)} %get-tuple-element.43) | copy-start | bytes 786436
  71.1 5.9 %copy-start.3 = (f32[2,8,2,16,128]{4,3,2,1,0:T(8,128)}, f32[2,8,2,16,128]{4,3,2,1,0:T(8,128)S(1)}, u32[]{:S(2)}) copy-start(f32[2,8,2,16,128]{4,3,2,1,0:T(8,128)S(1)} %get-tuple-element.42) | copy-start | bytes 786436
  71.1 5.9 %copy-start.4 = (f32[2,8,2,16,128]{4,3,2,1,0:T(8,128)}, f32[2,8,2,16,128]{4,3,2,1,0:T(8,128)S(1)}, u32[]{:S(2)}) copy-start(f32[2,8,2,16,128]{4,3,2,1,0:T(8,128)S(1)} %get-tuple-element.41) | copy-start | bytes 786436
  71.1 4.9 %collective-permute-start.12 = (f32[3,256,256]{2,1,0:T(8,128)S(1)}, f32[3,256,256]{2,1,0:T(8,128)S(1)}, u32[]{:S(2)}, u32[]{:S(2)}) collective-permute-start(f32[3,256,256]{2,1,0:T(8,128)S(1)} %get-tuple-element.39), channel_id=1, source_target_pairs={{0,4},{4,0},{8,12},{12,8},{16,20},{20,16},{24,28},{28,24},{32,36},... | collective-permute-start | bytes 2359304 | tf_op jit(solution)/shard_map/ppermute | solution.py:46
  77.0 52.3 %all-to-all-start = ((f32[32,24,256]{2,1,0:T(8,128)}), f32[32,24,256]{2,1,0:T(8,128)}, u32[]{:S(2)}, u32[]{:S(2)}) async-start(f32[32,24,256]{2,1,0:T(8,128)} %bitcast.6), calls=%async_computation | async-start | bytes 1572864 | tf_op jit(solution)/shard_map/all_to_all | solution.py:407
  89.7 40.9 %reduce-scatter.2.cloned.1.call-start = ((), (), s32[]{:S(2)}) async-start(), calls=%async_computation.3 | async-start | bytes 327680 | tf_op jit(solution)/shard_map/reduce_scatter | solution.py:392
  89.8 40.7 %copy-start.1 = (f32[24,2,64,128]{3,2,1,0:T(8,128)S(1)}, f32[24,2,64,128]{3,2,1,0:T(8,128)}, u32[]{:S(2)}) copy-start(f32[24,2,64,128]{3,2,1,0:T(8,128)} %pieces.1) | copy-start | bytes 4718596
  90.6 7.3 %collective-permute-start.13 = (f32[2,8,2,16,128]{4,3,2,1,0:T(8,128)}, f32[2,8,2,16,128]{4,3,2,1,0:T(8,128)S(1)}, u32[]{:S(2)}, u32[]{:S(2)}) collective-permute-start(f32[2,8,2,16,128]{4,3,2,1,0:T(8,128)} %copy-done.4), channel_id=1, source_target_pairs={{0,1},{1,2},{2,3},{3,0},{4,5},{5,6},{6,7},{7,4},{8,9},{9,10},{10,1... | collective-permute-start | bytes 786440 | tf_op jit(solution)/shard_map/ppermute | solution.py:42
  91.9 8.3 %collective-permute-start.14 = (f32[2,8,2,16,128]{4,3,2,1,0:T(8,128)}, f32[2,8,2,16,128]{4,3,2,1,0:T(8,128)S(1)}, u32[]{:S(2)}, u32[]{:S(2)}) collective-permute-start(f32[2,8,2,16,128]{4,3,2,1,0:T(8,128)} %copy-done.3), channel_id=1, source_target_pairs={{0,2},{1,3},{2,0},{3,1},{4,6},{5,7},{6,4},{7,5},{8,10},{9,11},{10,... | collective-permute-start | bytes 786440 | tf_op jit(solution)/shard_map/ppermute | solution.py:42
  92.5 15.6 %collective-permute-start.15 = (f32[2,8,2,16,128]{4,3,2,1,0:T(8,128)}, f32[2,8,2,16,128]{4,3,2,1,0:T(8,128)S(1)}, u32[]{:S(2)}, u32[]{:S(2)}) collective-permute-start(f32[2,8,2,16,128]{4,3,2,1,0:T(8,128)} %copy-done.2), channel_id=1, source_target_pairs={{0,3},{1,0},{2,1},{3,2},{4,7},{5,4},{6,5},{7,6},{8,11},{9,8},{10,9... | collective-permute-start | bytes 786440 | tf_op jit(solution)/shard_map/ppermute | solution.py:42
  108.9 20.4 %collective-permute-start.17 = (f32[13,2,16,128]{3,2,1,0:T(8,128)S(1)}, f32[13,2,16,128]{3,2,1,0:T(8,128)S(1)}, u32[]{:S(2)}, u32[]{:S(2)}) collective-permute-start(f32[13,2,16,128]{3,2,1,0:T(8,128)S(1)} %get-tuple-element.45), channel_id=1, source_target_pairs={{0,32},{4,36},{8,40},{12,44},{16,48},{20,52},{24,56},{28,60},{32,6... | collective-permute-start | bytes 638984 | tf_op jit(solution)/shard_map/ppermute | solution.py:38
  113.2 16.1 %collective-permute-start.16 = (f32[7,2,16,128]{3,2,1,0:T(8,128)S(1)}, f32[7,2,16,128]{3,2,1,0:T(8,128)S(1)}, u32[]{:S(2)}, u32[]{:S(2)}) collective-permute-start(f32[7,2,16,128]{3,2,1,0:T(8,128)S(1)} %get-tuple-element.44), channel_id=1, source_target_pairs={{0,4},{4,8},{8,12},{12,16},{16,20},{20,24},{24,28},{28,32},{32,36}... | collective-permute-start | bytes 344072 | tf_op jit(solution)/shard_map/ppermute | solution.py:38
  114.1 15.2 %collective-permute-start.18 = (f32[4,2,16,128]{3,2,1,0:T(8,128)S(1)}, f32[4,2,16,128]{3,2,1,0:T(8,128)S(1)}, u32[]{:S(2)}, u32[]{:S(2)}) collective-permute-start(f32[4,2,16,128]{3,2,1,0:T(8,128)S(1)} %get-tuple-element.46), channel_id=1, source_target_pairs={{0,36},{4,40},{8,44},{12,48},{16,52},{20,56},{24,60},{28,64},{32,6... | collective-permute-start | bytes 196616 | tf_op jit(solution)/shard_map/ppermute | solution.py:38
  133.5 30.3 %all-to-all-start.1 = ((f32[32,24,256]{2,1,0:T(8,128)}), f32[32,24,256]{2,1,0:T(8,128)S(1)}, u32[]{:S(2)}, u32[]{:S(2)}) async-start(f32[32,24,256]{2,1,0:T(8,128)} %broadcast_in_dim.2), calls=%async_computation.2 | async-start | bytes 1572864 | tf_op jit(solution)/shard_map/all_to_all | solution.py:407
  140.5 10.3 %collective-permute-start.19 = (f32[24,2,16,128]{3,2,1,0:T(8,128)S(1)}, f32[24,2,16,128]{3,2,1,0:T(8,128)S(1)}, u32[]{:S(2)}, u32[]{:S(2)}) collective-permute-start(f32[24,2,16,128]{3,2,1,0:T(8,128)S(1)} %update.1.n0), channel_id=1, source_target_pairs={{0,1},{1,2},{2,3},{3,0},{4,5},{5,6},{6,7},{7,4},{8,9},{9,10},{10,1... | collective-permute-start | bytes 1179656 | tf_op jit(solution)/shard_map/ppermute | solution.py:42
  140.6 11.9 %collective-permute-start.20 = (f32[24,2,16,128]{3,2,1,0:T(8,128)S(1)}, f32[24,2,16,128]{3,2,1,0:T(8,128)S(1)}, u32[]{:S(2)}, u32[]{:S(2)}) collective-permute-start(f32[24,2,16,128]{3,2,1,0:T(8,128)S(1)} %update.1.n0), channel_id=1, source_target_pairs={{0,2},{1,3},{2,0},{3,1},{4,6},{5,7},{6,4},{7,5},{8,10},{9,11},{10,... | collective-permute-start | bytes 1179656 | tf_op jit(solution)/shard_map/ppermute | solution.py:42
  140.8 20.8 %collective-permute-start.21 = (f32[24,2,16,128]{3,2,1,0:T(8,128)S(1)}, f32[24,2,16,128]{3,2,1,0:T(8,128)S(1)}, u32[]{:S(2)}, u32[]{:S(2)}) collective-permute-start(f32[24,2,16,128]{3,2,1,0:T(8,128)S(1)} %update.1.n0), channel_id=1, source_target_pairs={{0,3},{1,0},{2,1},{3,2},{4,7},{5,4},{6,5},{7,6},{8,11},{9,8},{10,9... | collective-permute-start | bytes 1179656 | tf_op jit(solution)/shard_map/ppermute | solution.py:42
  163.8 2.6 %collective-permute-start.22 = (f32[3,256,256]{2,1,0:T(8,128)S(1)}, f32[3,256,256]{2,1,0:T(8,128)S(1)}, u32[]{:S(2)}, u32[]{:S(2)}) collective-permute-start(f32[3,256,256]{2,1,0:T(8,128)S(1)} %bitcast.18), channel_id=1, source_target_pairs={{0,4},{4,0},{8,12},{12,8},{16,20},{20,16},{24,28},{28,24},{32,36},... | collective-permute-start | bytes 2359304 | tf_op jit(solution)/shard_map/ppermute | solution.py:46
Sparse Core Ops, SparseCore 0:
  93.0 21.2 reduce-scatter.1

commit v7 on v6

--- a/solution.py
+++ b/solution.py
@@ -370,6 +370,23 @@
     )(info, mine, theirs)
 
 
+def spread_sum_kernel(pieces, out):
+    total = jnp.sum(pieces[...], axis=0)
+    out[...] = jnp.broadcast_to(total[None], out.shape)
+
+
+def spread_sum(pieces):
+    return pl.pallas_call(
+        spread_sum_kernel,
+        in_specs=[VMEM],
+        out_specs=VMEM,
+        out_shape=jax.ShapeDtypeStruct(pieces.shape, F32),
+        compiler_params=pltpu.CompilerParams(vmem_limit_bytes=SMALL_BYTES),
+        cost_estimate=pl.CostEstimate(flops=200000, bytes_accessed=1600000, transcendentals=0),
+        name="spread_sum",
+    )(pieces)
+
+
 def body(object_pieces, probe_modes, intensity, positions, counts):
     tile_index = lax.axis_index("tile")
     mode_index = lax.axis_index("mode")
@@ -413,13 +430,13 @@
     from_above = shifted(to_low, DEV_COLS)
     from_corner = shifted(to_corner, DEV_COLS + 1)
     from_left = shifted(to_right, 1)
-    pieces, from_left, from_above, from_corner = lax.optimization_barrier(
-        (pieces, from_left, from_above, from_corner))
-    share = jnp.sum(pieces, axis=0)
+    shares = spread_sum(pieces)
+    shares, from_left, from_above, from_corner = lax.optimization_barrier(
+        (shares, from_left, from_above, from_corner))
 
     new = update(info, object_pieces, own, from_left, from_above, from_corner, in_hbm(light[0]))
-    share, new = lax.optimization_barrier((share, new))
-    gathered = exchange(jnp.broadcast_to(share[None], (N_CHIP, PART, SIDE)))
+    shares, new = lax.optimization_barrier((shares, new))
+    gathered = exchange(shares)
     new_parts = [new] + [turned(new, j) for j in (1, 2, 3)]
     gathered, *new_parts = lax.optimization_barrier((gathered, *new_parts))
     gathered = gathered.reshape(3, SIDE, SIDE)

time: 176 us -> 181 us (1.028)
  local copies, waits for them, and re-layouts: 8.39 us -> 14 us
  Pallas kernels: 19.2 us -> 22 us
  waiting for transfers between devices: 78 us -> 75.9 us
    unnamed x20 -> x36, local copies, waits for them, and re-layouts: 0.73 us -> 7.1 us
    pallas_call x0 -> x1, Pallas kernels: none -> 2.1 us  [spread_sum(): pl.pallas_call(spread_sum_kernel, in_specs=[VMEM], out_specs=VMEM, out_sh...]
    ppermute x6, waiting for transfers between devices: 20.7 us -> 18.8 us  [shifted(): lax.ppermute(block, 'tile', [(d, (d + distance) % N_TILE) for d in range(...]
  transfers between devices with their start and end apart: 26 -> 26, of which waited for: 19 -> 19; matrix products, arithmetic and copies ran while one was open for 4% -> 3% of each run, Pallas kernels for 1% -> 3%
where the time goes in v7:
time: 181 us; the launch traced here: 180 us
  waiting for transfers between devices  75.9 us (42%)
  starting transfers between devices  51.2 us (28%)
  Pallas kernels  22 us (12%)
  between operations  14.9 us (8%)
  local copies, waits for them, and re-layouts  14 us (8%)
  other arithmetic  2.11 us (1%)
    ppermute x15, waiting for transfers between devices, turned(): lax.ppermute(block, 'mode', [(i, (i + distance) % N_MODE) for i in range(...  52.8 us
    all_to_all x2, starting transfers between devices, body(): lax.all_to_all(blocks, 'tile', 0, 0, axis_index_groups=groups, tiled=True)  19.6 us
    ppermute x6, waiting for transfers between devices, shifted(): lax.ppermute(block, 'tile', [(d, (d + distance) % N_TILE) for d in range(...  18.8 us
    ppermute x6, starting transfers between devices, shifted(): lax.ppermute(block, 'tile', [(d, (d + distance) % N_TILE) for d in range(...  16.5 us
    ppermute x15, starting transfers between devices, turned(): lax.ppermute(block, 'mode', [(i, (i + distance) % N_MODE) for i in range(...  11.3 us
    unnamed x36, local copies, waits for them, and re-layouts  7.1 us
    pallas_call x1, Pallas kernels, forward(): pl.pallas_call(forward_kernel, grid=(3,), in_specs=[SMEM] + [HBM] * 6 + [...  6.87 us
    pallas_call x1, Pallas kernels, backward(): pl.pallas_call(backward_kernel, grid=(3,), in_specs=[SMEM, pl.BlockSpec((...  6.11 us
  transfers between devices with their start and end apart: 26, of which 19 were waited for; matrix products, arithmetic and copies ran while one was open for 3% of the time, Pallas kernels for 3%

profile of v7, /device:TPU:39, one launch (start us, length us, event | category | flops | bytes accessed | tf_op | source)
XLA Modules:
  0.0 180.1 jit_solution(5295658564745695577)
XLA Ops:
  7.2 1.1 slice-done
  8.3 8.5 %collective-permute-start.1 = (f32[12,2,16,128]{3,2,1,0:T(8,128)S(1)}, f32[12,2,16,128]{3,2,1,0:T(8,128)S(1)}, u32[]{:S(2)}, u32[]{:S(2)}) collective-permute-start(f32[12,2,16,128]{3,2,1,0:T(8,128)S(1)} %constant_dynamic-slice_fusion), channel_id=1, source_target_pairs={{0,224},{4,228},{8,232},{12,236},{16,240},{20,244},{24,248},{28,25... | collective-permute-start | bytes 589832 | tf_op jit(solution)/shard_map/ppermute | solution.py:38
  16.9 0.7 collective-permute-start.2
  17.5 1.0 slice_bitcast_fusion
  18.5 0.4 collective-permute-start
  19.1 7.3 %collective-permute-done.2 = f32[3,2,16,128]{3,2,1,0:T(8,128)S(1)} collective-permute-done((f32[3,2,16,128]{3,2,1,0:T(8,128)S(1)}, f32[3,2,16,128]{3,2,1,0:T(8,128)S(1)}, u32[]{:S(2)}, u32[]{:S(2)}) %collective-permute-start.2) | collective-permute-done | bytes 49184 | tf_op jit(solution)/shard_map/ppermute | solution.py:38
  26.5 0.3 collective-permute-start.3
  26.7 2.1 %collective-permute-start.4 = (f32[15,2,16,128]{3,2,1,0:T(8,128)S(1)}, f32[15,2,16,128]{3,2,1,0:T(8,128)S(1)}, u32[]{:S(2)}, u32[]{:S(2)}) collective-permute-start(f32[15,2,16,128]{3,2,1,0:T(8,128)S(1)} %pad_maximum_fusion.b0), channel_id=1, source_target_pairs={{0,2},{1,3},{2,0},{3,1},{4,6},{5,7},{6,4},{7,5},{8,10},{9,11},{10,... | collective-permute-start | bytes 737288 | tf_op jit(solution)/shard_map/ppermute | solution.py:42
  29.6 0.6 fusion
  30.1 0.7 fusion.1
  30.8 2.6 %stack.15.info = s32[8]{0:T(128)S(1)} concatenate(s32[1]{0:T(128)} %get-tuple-element.65, s32[1]{0:T(128)} %get-tuple-element.63, s32[1]{0:T(128)} %get-tuple-element.64, s32[1]{0:T(128)} %get-tuple-element.62, s32[1]{0:T(128)} %copy.13, s32[1]{0:T(128)} %bitcast, s32[1]{0:T(128)} %bitcast.1, s32[1]{0:T(128)} %bitcast.2), dimensions={0} | concatenate | bytes 64 | tf_op jit(solution)/shard_map/stack | solution.py:404
  33.4 1.1 collective-permute-done.4.b2
  34.5 0.7 copy-done.17
  35.2 6.2 %collective-permute-done.5.b3 = f32[15,2,16,128]{3,2,1,0:T(8,128)} collective-permute-done((f32[15,2,16,128]{3,2,1,0:T(8,128)S(1)}, f32[15,2,16,128]{3,2,1,0:T(8,128)}, u32[]{:S(2)}, u32[]{:S(2)}) %collective-permute-start.5) | collective-permute-done | bytes 245792 | tf_op jit(solution)/shard_map/ppermute | solution.py:42
  41.4 6.9 %forward.1 = (f32[2,3,2,256,256]{4,3,2,1,0:T(8,128)}, f32[2,2,256,256]{3,2,1,0:T(8,128)S(1)}, f32[2,64,256]{2,1,0:T(8,128)S(1)}, f32[2,64,256]{2,1,0:T(8,128)S(1...) custom-call(s32[8]{0:T(128)S(1)} %stack.15.info, f32[24,2,64,128]{3,2,1,0:T(8,128)} %pieces.1, ...), custom_call_target="tpu_custom_call" | custom-call | flops 1700000000 | bytes 12000000 | tf_op jit(solution)/shard_map/forward/pallas_call | solution.py:144
  48.4 0.9 collective-permute-start.7
  49.3 0.7 collective-permute-start.8
  50.1 2.8 %collective-permute-done.6 = f32[2,64,256]{2,1,0:T(8,128)S(1)} collective-permute-done((f32[2,64,256]{2,1,0:T(8,128)S(1)}, f32[2,64,256]{2,1,0:T(8,128)S(1)}, u32[]{:S(2)}, u32[]{:S(2)}) %collective-permute-start.6) | collective-permute-done | bytes 131104 | tf_op jit(solution)/shard_map/ppermute | solution.py:42
  52.9 1.0 collective-permute-done.7
  53.9 2.0 %collective-permute-done.8 = f32[2,64,256]{2,1,0:T(8,128)S(1)} collective-permute-done((f32[2,64,256]{2,1,0:T(8,128)S(1)}, f32[2,64,256]{2,1,0:T(8,128)S(1)}, u32[]{:S(2)}, u32[]{:S(2)}) %collective-permute-start.8) | collective-permute-done | bytes 131104 | tf_op jit(solution)/shard_map/ppermute | solution.py:42
  55.9 1.0 add_multiply_fusion.f0
  56.8 0.5 collective-permute-start.10
  57.3 2.4 %collective-permute-start.11 = (f32[2,64,256]{2,1,0:T(8,128)S(1)}, f32[2,64,256]{2,1,0:T(8,128)S(1)}, u32[]{:S(2)}, u32[]{:S(2)}) collective-permute-start(f32[2,64,256]{2,1,0:T(8,128)S(1)} %add_multiply_fusion.f0), channel_id=1, source_target_pairs={{0,3},{1,0},{2,1},{3,2},{4,7},{5,4},{6,5},{7,6},{8,11},{9,8},{10,9... | collective-permute-start | bytes 393224 | tf_op jit(solution)/shard_map/ppermute | solution.py:42
  59.8 0.3 collective-permute-start.9
  60.0 2.3 %collective-permute-done.10.f2 = f32[2,64,256]{2,1,0:T(8,128)S(1)} collective-permute-done((f32[2,64,256]{2,1,0:T(8,128)S(1)}, f32[2,64,256]{2,1,0:T(8,128)S(1)}, u32[]{:S(2)}, u32[]{:S(2)}) %collective-permute-start.10) | collective-permute-done | bytes 131104 | tf_op jit(solution)/shard_map/ppermute | solution.py:42
  62.4 1.3 collective-permute-done.11.f3
  63.7 1.2 collective-permute-done.9.f1
  64.9 6.1 %backward.1 = (f32[3,256,256]{2,1,0:T(8,128)S(1)}, f32[3,256,256]{2,1,0:T(8,128)S(1)}, f32[2,8,2,16,128]{4,3,2,1,0:T(8,128)S(1)}, f32[2,8,2,16,128]{4,3,2,1,0:T(...) custom-call(s32[8]{0:T(128)S(1)} %stack.15.info, ...), custom_call_target="tpu_custom_call" | custom-call | flops 1700000000 | bytes 12000000 | tf_op jit(solution)/shard_map/backward/pallas_call | solution.py:211
  71.0 3.1 %collective-permute-start.12 = (f32[3,256,256]{2,1,0:T(8,128)S(1)}, f32[3,256,256]{2,1,0:T(8,128)S(1)}, u32[]{:S(2)}, u32[]{:S(2)}) collective-permute-start(f32[3,256,256]{2,1,0:T(8,128)S(1)} %get-tuple-element.39), channel_id=1, source_target_pairs={{0,4},{4,0},{8,12},{12,8},{16,20},{20,16},{24,28},{28,24},{32,36},... | collective-permute-start | bytes 2359304 | tf_op jit(solution)/shard_map/ppermute | solution.py:46
  74.2 1.9 %collective-permute-done.12 = f32[3,256,256]{2,1,0:T(8,128)S(1)} collective-permute-done((f32[3,256,256]{2,1,0:T(8,128)S(1)}, f32[3,256,256]{2,1,0:T(8,128)S(1)}, u32[]{:S(2)}, u32[]{:S(2)}) %collective-permute-start.12) | collective-permute-done | bytes 786464 | tf_op jit(solution)/shard_map/ppermute | solution.py:46
  76.1 1.0 add.46
  77.1 12.6 %all-to-all-start = ((f32[32,24,256]{2,1,0:T(8,128)}), f32[32,24,256]{2,1,0:T(8,128)}, u32[]{:S(2)}, u32[]{:S(2)}) async-start(f32[32,24,256]{2,1,0:T(8,128)} %bitcast.6), calls=%async_computation | async-start | bytes 1572864 | tf_op jit(solution)/shard_map/all_to_all | solution.py:424
  89.8 0.7 copy.12
  90.6 1.3 collective-permute-start.13
  91.9 0.6 collective-permute-start.14
  92.6 0.4 collective-permute-start.15
  93.0 4.9 %collective-permute-done.13.g1 = f32[2,8,2,16,128]{4,3,2,1,0:T(8,128)S(1)} collective-permute-done((f32[2,8,2,16,128]{4,3,2,1,0:T(8,128)}, f32[2,8,2,16,128]{4,3,2,1,0:T(8,128)S(1)}, u32[]{:S(2)}, u32[]{:S(2)}) %collective-permute-start.13) | collective-permute-done | bytes 262176 | tf_op jit(solution)/shard_map/ppermute | solution.py:42
  97.9 2.4 %collective-permute-done.14.g2 = f32[2,8,2,16,128]{4,3,2,1,0:T(8,128)S(1)} collective-permute-done((f32[2,8,2,16,128]{4,3,2,1,0:T(8,128)}, f32[2,8,2,16,128]{4,3,2,1,0:T(8,128)S(1)}, u32[]{:S(2)}, u32[]{:S(2)}) %collective-permute-start.14) | collective-permute-done | bytes 262176 | tf_op jit(solution)/shard_map/ppermute | solution.py:42
  100.3 7.9 %collective-permute-done.15.g3 = f32[2,8,2,16,128]{4,3,2,1,0:T(8,128)S(1)} collective-permute-done((f32[2,8,2,16,128]{4,3,2,1,0:T(8,128)}, f32[2,8,2,16,128]{4,3,2,1,0:T(8,128)S(1)}, u32[]{:S(2)}, u32[]{:S(2)}) %collective-permute-start.15) | collective-permute-done | bytes 262176 | tf_op jit(solution)/shard_map/ppermute | solution.py:42
  108.2 1.4 scatter.1
  109.6 0.7 copy-done.2
  110.3 4.2 %collective-permute-start.17 = (f32[13,2,16,128]{3,2,1,0:T(8,128)}, f32[13,2,16,128]{3,2,1,0:T(8,128)S(1)}, u32[]{:S(2)}, u32[]{:S(2)}) collective-permute-start(f32[13,2,16,128]{3,2,1,0:T(8,128)} %get-tuple-element.45), channel_id=1, source_target_pairs={{0,32},{4,36},{8,40},{12,44},{16,48},{20,52},{24,56},{28,60},{32,6... | collective-permute-start | bytes 638984 | tf_op jit(solution)/shard_map/ppermute | solution.py:38
  114.5 0.9 collective-permute-start.16
  115.5 1.8 %collective-permute-start.18 = (f32[4,2,16,128]{3,2,1,0:T(8,128)}, f32[4,2,16,128]{3,2,1,0:T(8,128)S(1)}, u32[]{:S(2)}, u32[]{:S(2)}) collective-permute-start(f32[4,2,16,128]{3,2,1,0:T(8,128)} %get-tuple-element.46), channel_id=1, source_target_pairs={{0,36},{4,40},{8,44},{12,48},{16,52},{20,56},{24,60},{28,64},{32,6... | collective-permute-start | bytes 196616 | tf_op jit(solution)/shard_map/ppermute | solution.py:38
  117.3 2.1 %spread_sum.1 = f32[32,24,256]{2,1,0:T(8,128)} custom-call(f32[32,24,256]{2,1,0:T(8,128)} %all-to-all-done.pieces), custom_call_target="tpu_custom_call" | custom-call | flops 200000 | bytes 1600000 | tf_op jit(solution)/shard_map/spread_sum/pallas_call | solution.py:379
  119.4 11.4 %collective-permute-done.18.corner = f32[4,2,16,128]{3,2,1,0:T(8,128)S(1)} collective-permute-done((f32[4,2,16,128]{3,2,1,0:T(8,128)}, f32[4,2,16,128]{3,2,1,0:T(8,128)S(1)}, u32[]{:S(2)}, u32[]{:S(2)}) %collective-permute-start.18) | collective-permute-done | bytes 65568 | tf_op jit(solution)/shard_map/ppermute | solution.py:38
  130.8 0.6 copy-done.8
  131.5 0.6 copy-done.6
  132.1 0.7 copy-done.4
  132.8 1.0 copy-done.3
  133.8 0.9 copy-done.5
  134.7 0.9 copy-done.7
  135.6 0.8 copy-done.9
  136.5 2.0 %update.1.n0 = f32[24,2,16,128]{3,2,1,0:T(8,128)S(1)} custom-call(s32[8]{0:T(128)S(1)} %stack.15.info, f32[24,2,64,128]{3,2,1,0:T(8,128)S(1)} %copy-done.1, f32[24,2,16,128]{3,2,1,0:T(8,128)S(1)} %copy-done.3, f32[7,2,16,128]{3,2,1,0:T(8,128)S(1)} %copy-done.7, f32[13,2,16,128]{3,2,1,0:T(8,128)S(1)} %copy-done.5, f32[4,2,16,128]{3,2,1,0:T(8,128)S(1)} %copy-done.9, ...), custom_call_target="tpu_custom_call" | custom-call | flops 1000000 | bytes 2000000 | tf_op jit(solution)/shard_map/update/pallas_call | solution.py:311
  138.5 7.0 %all-to-all-start.1 = ((f32[32,24,256]{2,1,0:T(8,128)}), f32[32,24,256]{2,1,0:T(8,128)S(1)}, u32[]{:S(2)}, u32[]{:S(2)}) async-start(f32[32,24,256]{2,1,0:T(8,128)} %spread_sum.1), calls=%async_computation.2 | async-start | bytes 1572864 | tf_op jit(solution)/shard_map/all_to_all | solution.py:424
  145.6 0.3 collective-permute-start.20
  145.9 1.2 collective-permute-start.21
  147.1 8.8 %collective-permute-done.19.n1 = f32[24,2,16,128]{3,2,1,0:T(8,128)S(1)} collective-permute-done((f32[24,2,16,128]{3,2,1,0:T(8,128)S(1)}, f32[24,2,16,128]{3,2,1,0:T(8,128)S(1)}, u32[]{:S(2)}, u32[]{:S(2)}) %collective-permute-start.19) | collective-permute-done | bytes 393248 | tf_op jit(solution)/shard_map/ppermute | solution.py:42
  155.9 1.6 collective-permute-done.20.n2
  157.5 9.2 %collective-permute-done.21.n3 = f32[24,2,16,128]{3,2,1,0:T(8,128)S(1)} collective-permute-done((f32[24,2,16,128]{3,2,1,0:T(8,128)S(1)}, f32[24,2,16,128]{3,2,1,0:T(8,128)S(1)}, u32[]{:S(2)}, u32[]{:S(2)}) %collective-permute-start.21) | collective-permute-done | bytes 393248 | tf_op jit(solution)/shard_map/ppermute | solution.py:42
  166.7 2.2 %all-to-all-done.1 = f32[32,24,256]{2,1,0:T(8,128)S(1)} async-done(((f32[32,24,256]{2,1,0:T(8,128)}), f32[32,24,256]{2,1,0:T(8,128)S(1)}, u32[]{:S(2)}, u32[]{:S(2)}) %all-to-all-start.1) | async-done | bytes 786464 | tf_op jit(solution)/shard_map/all_to_all | solution.py:424
  168.9 0.7 collective-permute-start.22
  169.6 1.7 join_pieces.1
  171.5 1.7 join_channels.1
  (48 shorter events, 0.9 us)
Async XLA Ops:
  7.2 1.1 slice-start
  7.2 11.7 %copy-start.14 = (s32[2,2]{1,0:T(2,128)S(1)}, s32[2,2]{1,0:T(2,128)}, u32[]{:S(2)}) copy-start(s32[2,2]{1,0:T(2,128)} %param.9) | copy-start | bytes 52
  7.2 34.2 %copy-start = (f32[3,2,256,256]{3,2,1,0:T(8,128)S(1)}, f32[3,2,256,256]{3,2,1,0:T(8,128)}, u32[]{:S(2)}) copy-start(f32[3,2,256,256]{3,2,1,0:T(8,128)} %probe.3) | copy-start | bytes 4718596
  8.3 18.1 %collective-permute-start.1 = (f32[12,2,16,128]{3,2,1,0:T(8,128)S(1)}, f32[12,2,16,128]{3,2,1,0:T(8,128)S(1)}, u32[]{:S(2)}, u32[]{:S(2)}) collective-permute-start(f32[12,2,16,128]{3,2,1,0:T(8,128)S(1)} %constant_dynamic-slice_fusion), channel_id=1, source_target_pairs={{0,224},{4,228},{8,232},{12,236},{16,240},{20,244},{24,248},{28,25... | collective-permute-start | bytes 589832 | tf_op jit(solution)/shard_map/ppermute | solution.py:38
  16.9 9.6 %collective-permute-start.2 = (f32[3,2,16,128]{3,2,1,0:T(8,128)S(1)}, f32[3,2,16,128]{3,2,1,0:T(8,128)S(1)}, u32[]{:S(2)}, u32[]{:S(2)}) collective-permute-start(f32[3,2,16,128]{3,2,1,0:T(8,128)S(1)} %slice.35), channel_id=1, source_target_pairs={{0,220},{4,224},{8,228},{12,232},{16,236},{20,240},{24,244},{28,24... | collective-permute-start | bytes 147464 | tf_op jit(solution)/shard_map/ppermute | solution.py:38
  18.5 14.8 %collective-permute-start = (f32[6,2,64,128]{3,2,1,0:T(8,128)S(1)}, f32[6,2,64,128]{3,2,1,0:T(8,128)S(1)}, u32[]{:S(2)}, u32[]{:S(2)}) collective-permute-start(f32[6,2,64,128]{3,2,1,0:T(8,128)S(1)} %slice_bitcast_fusion), channel_id=1, source_target_pairs={{0,252},{4,0},{8,4},{12,8},{16,12},{20,16},{24,20},{28,24},{32,28}... | collective-permute-start | bytes 1179656 | tf_op jit(solution)/shard_map/ppermute | solution.py:38
  26.5 15.0 %copy-start.13 = (f32[15,2,16,128]{3,2,1,0:T(8,128)}, f32[15,2,16,128]{3,2,1,0:T(8,128)S(1)}, u32[]{:S(2)}) copy-start(f32[15,2,16,128]{3,2,1,0:T(8,128)S(1)} %pad_maximum_fusion.b0) | copy-start | bytes 737284
  26.5 6.9 %collective-permute-start.3 = (f32[15,2,16,128]{3,2,1,0:T(8,128)S(1)}, f32[15,2,16,128]{3,2,1,0:T(8,128)S(1)}, u32[]{:S(2)}, u32[]{:S(2)}) collective-permute-start(f32[15,2,16,128]{3,2,1,0:T(8,128)S(1)} %pad_maximum_fusion.b0), channel_id=1, source_target_pairs={{0,1},{1,2},{2,3},{3,0},{4,5},{5,6},{6,7},{7,4},{8,9},{9,10},{10,1... | collective-permute-start | bytes 737288 | tf_op jit(solution)/shard_map/ppermute | solution.py:42
  26.7 7.7 %collective-permute-start.4 = (f32[15,2,16,128]{3,2,1,0:T(8,128)S(1)}, f32[15,2,16,128]{3,2,1,0:T(8,128)S(1)}, u32[]{:S(2)}, u32[]{:S(2)}) collective-permute-start(f32[15,2,16,128]{3,2,1,0:T(8,128)S(1)} %pad_maximum_fusion.b0), channel_id=1, source_target_pairs={{0,2},{1,3},{2,0},{3,1},{4,6},{5,7},{6,4},{7,5},{8,10},{9,11},{10,... | collective-permute-start | bytes 737288 | tf_op jit(solution)/shard_map/ppermute | solution.py:42
  28.9 12.5 %collective-permute-start.5 = (f32[15,2,16,128]{3,2,1,0:T(8,128)S(1)}, f32[15,2,16,128]{3,2,1,0:T(8,128)}, u32[]{:S(2)}, u32[]{:S(2)}) collective-permute-start(f32[15,2,16,128]{3,2,1,0:T(8,128)S(1)} %pad_maximum_fusion.b0), channel_id=1, source_target_pairs={{0,3},{1,0},{2,1},{3,2},{4,7},{5,4},{6,5},{7,6},{8,11},{9,8},{10,9... | collective-permute-start | bytes 737288 | tf_op jit(solution)/shard_map/ppermute | solution.py:42
  33.4 1.1 copy-start.15
  33.4 1.1 copy-start.16
  34.5 0.7 copy-start.17
  48.3 4.6 %collective-permute-start.6 = (f32[2,64,256]{2,1,0:T(8,128)S(1)}, f32[2,64,256]{2,1,0:T(8,128)S(1)}, u32[]{:S(2)}, u32[]{:S(2)}) collective-permute-start(f32[2,64,256]{2,1,0:T(8,128)S(1)} %get-tuple-element.35), channel_id=1, source_target_pairs={{0,1},{1,2},{2,3},{3,0},{4,5},{5,6},{6,7},{7,4},{8,9},{9,10},{10,1... | collective-permute-start | bytes 393224 | tf_op jit(solution)/shard_map/ppermute | solution.py:42
  48.4 5.5 %collective-permute-start.7 = (f32[2,64,256]{2,1,0:T(8,128)S(1)}, f32[2,64,256]{2,1,0:T(8,128)S(1)}, u32[]{:S(2)}, u32[]{:S(2)}) collective-permute-start(f32[2,64,256]{2,1,0:T(8,128)S(1)} %get-tuple-element.36), channel_id=1, source_target_pairs={{0,2},{1,3},{2,0},{3,1},{4,6},{5,7},{6,4},{7,5},{8,10},{9,11},{10,... | collective-permute-start | bytes 393224 | tf_op jit(solution)/shard_map/ppermute | solution.py:42
  49.3 6.5 %collective-permute-start.8 = (f32[2,64,256]{2,1,0:T(8,128)S(1)}, f32[2,64,256]{2,1,0:T(8,128)S(1)}, u32[]{:S(2)}, u32[]{:S(2)}) collective-permute-start(f32[2,64,256]{2,1,0:T(8,128)S(1)} %get-tuple-element.37), channel_id=1, source_target_pairs={{0,3},{1,0},{2,1},{3,2},{4,7},{5,4},{6,5},{7,6},{8,11},{9,8},{10,9... | collective-permute-start | bytes 393224 | tf_op jit(solution)/shard_map/ppermute | solution.py:42
  56.8 5.5 %collective-permute-start.10 = (f32[2,64,256]{2,1,0:T(8,128)S(1)}, f32[2,64,256]{2,1,0:T(8,128)S(1)}, u32[]{:S(2)}, u32[]{:S(2)}) collective-permute-start(f32[2,64,256]{2,1,0:T(8,128)S(1)} %add_multiply_fusion.f0), channel_id=1, source_target_pairs={{0,2},{1,3},{2,0},{3,1},{4,6},{5,7},{6,4},{7,5},{8,10},{9,11},{10,... | collective-permute-start | bytes 393224 | tf_op jit(solution)/shard_map/ppermute | solution.py:42
  57.3 6.3 %collective-permute-start.11 = (f32[2,64,256]{2,1,0:T(8,128)S(1)}, f32[2,64,256]{2,1,0:T(8,128)S(1)}, u32[]{:S(2)}, u32[]{:S(2)}) collective-permute-start(f32[2,64,256]{2,1,0:T(8,128)S(1)} %add_multiply_fusion.f0), channel_id=1, source_target_pairs={{0,3},{1,0},{2,1},{3,2},{4,7},{5,4},{6,5},{7,6},{8,11},{9,8},{10,9... | collective-permute-start | bytes 393224 | tf_op jit(solution)/shard_map/ppermute | solution.py:42
  59.8 5.1 %collective-permute-start.9 = (f32[2,64,256]{2,1,0:T(8,128)S(1)}, f32[2,64,256]{2,1,0:T(8,128)S(1)}, u32[]{:S(2)}, u32[]{:S(2)}) collective-permute-start(f32[2,64,256]{2,1,0:T(8,128)S(1)} %add_multiply_fusion.f0), channel_id=1, source_target_pairs={{0,1},{1,2},{2,3},{3,0},{4,5},{5,6},{6,7},{7,4},{8,9},{9,10},{10,1... | collective-permute-start | bytes 393224 | tf_op jit(solution)/shard_map/ppermute | solution.py:42
  71.0 6.0 %copy-start.10 = (f32[2,8,2,16,128]{4,3,2,1,0:T(8,128)}, f32[2,8,2,16,128]{4,3,2,1,0:T(8,128)S(1)}, u32[]{:S(2)}) copy-start(f32[2,8,2,16,128]{4,3,2,1,0:T(8,128)S(1)} %get-tuple-element.43) | copy-start | bytes 786436
  71.0 6.0 %copy-start.11 = (f32[2,8,2,16,128]{4,3,2,1,0:T(8,128)}, f32[2,8,2,16,128]{4,3,2,1,0:T(8,128)S(1)}, u32[]{:S(2)}) copy-start(f32[2,8,2,16,128]{4,3,2,1,0:T(8,128)S(1)} %get-tuple-element.42) | copy-start | bytes 786436
  71.0 6.0 %copy-start.12 = (f32[2,8,2,16,128]{4,3,2,1,0:T(8,128)}, f32[2,8,2,16,128]{4,3,2,1,0:T(8,128)S(1)}, u32[]{:S(2)}) copy-start(f32[2,8,2,16,128]{4,3,2,1,0:T(8,128)S(1)} %get-tuple-element.41) | copy-start | bytes 786436
  71.0 5.0 %collective-permute-start.12 = (f32[3,256,256]{2,1,0:T(8,128)S(1)}, f32[3,256,256]{2,1,0:T(8,128)S(1)}, u32[]{:S(2)}, u32[]{:S(2)}) collective-permute-start(f32[3,256,256]{2,1,0:T(8,128)S(1)} %get-tuple-element.39), channel_id=1, source_target_pairs={{0,4},{4,0},{8,12},{12,8},{16,20},{20,16},{24,28},{28,24},{32,36},... | collective-permute-start | bytes 2359304 | tf_op jit(solution)/shard_map/ppermute | solution.py:46
  77.1 40.2 %all-to-all-start = ((f32[32,24,256]{2,1,0:T(8,128)}), f32[32,24,256]{2,1,0:T(8,128)}, u32[]{:S(2)}, u32[]{:S(2)}) async-start(f32[32,24,256]{2,1,0:T(8,128)} %bitcast.6), calls=%async_computation | async-start | bytes 1572864 | tf_op jit(solution)/shard_map/all_to_all | solution.py:424
  89.7 43.1 %reduce-scatter.2.cloned.1.call-start = ((), (), s32[]{:S(2)}) async-start(), calls=%async_computation.3 | async-start | bytes 327680 | tf_op jit(solution)/shard_map/reduce_scatter | solution.py:409
  90.6 42.2 %copy-start.1 = (f32[24,2,64,128]{3,2,1,0:T(8,128)S(1)}, f32[24,2,64,128]{3,2,1,0:T(8,128)}, u32[]{:S(2)}) copy-start(f32[24,2,64,128]{3,2,1,0:T(8,128)} %pieces.1) | copy-start | bytes 4718596
  90.6 7.3 %collective-permute-start.13 = (f32[2,8,2,16,128]{4,3,2,1,0:T(8,128)}, f32[2,8,2,16,128]{4,3,2,1,0:T(8,128)S(1)}, u32[]{:S(2)}, u32[]{:S(2)}) collective-permute-start(f32[2,8,2,16,128]{4,3,2,1,0:T(8,128)} %copy-done.12), channel_id=1, source_target_pairs={{0,1},{1,2},{2,3},{3,0},{4,5},{5,6},{6,7},{7,4},{8,9},{9,10},{10,1... | collective-permute-start | bytes 786440 | tf_op jit(solution)/shard_map/ppermute | solution.py:42
  91.9 8.3 %collective-permute-start.14 = (f32[2,8,2,16,128]{4,3,2,1,0:T(8,128)}, f32[2,8,2,16,128]{4,3,2,1,0:T(8,128)S(1)}, u32[]{:S(2)}, u32[]{:S(2)}) collective-permute-start(f32[2,8,2,16,128]{4,3,2,1,0:T(8,128)} %copy-done.11), channel_id=1, source_target_pairs={{0,2},{1,3},{2,0},{3,1},{4,6},{5,7},{6,4},{7,5},{8,10},{9,11},{10,... | collective-permute-start | bytes 786440 | tf_op jit(solution)/shard_map/ppermute | solution.py:42
  92.6 15.6 %collective-permute-start.15 = (f32[2,8,2,16,128]{4,3,2,1,0:T(8,128)}, f32[2,8,2,16,128]{4,3,2,1,0:T(8,128)S(1)}, u32[]{:S(2)}, u32[]{:S(2)}) collective-permute-start(f32[2,8,2,16,128]{4,3,2,1,0:T(8,128)} %copy-done.10), channel_id=1, source_target_pairs={{0,3},{1,0},{2,1},{3,2},{4,7},{5,4},{6,5},{7,6},{8,11},{9,8},{10,9... | collective-permute-start | bytes 786440 | tf_op jit(solution)/shard_map/ppermute | solution.py:42
  109.6 0.7 copy-start.2
  110.3 21.8 %collective-permute-start.17 = (f32[13,2,16,128]{3,2,1,0:T(8,128)}, f32[13,2,16,128]{3,2,1,0:T(8,128)S(1)}, u32[]{:S(2)}, u32[]{:S(2)}) collective-permute-start(f32[13,2,16,128]{3,2,1,0:T(8,128)} %get-tuple-element.45), channel_id=1, source_target_pairs={{0,32},{4,36},{8,40},{12,44},{16,48},{20,52},{24,56},{28,60},{32,6... | collective-permute-start | bytes 638984 | tf_op jit(solution)/shard_map/ppermute | solution.py:38
  114.5 16.9 %collective-permute-start.16 = (f32[7,2,16,128]{3,2,1,0:T(8,128)}, f32[7,2,16,128]{3,2,1,0:T(8,128)S(1)}, u32[]{:S(2)}, u32[]{:S(2)}) collective-permute-start(f32[7,2,16,128]{3,2,1,0:T(8,128)} %get-tuple-element.44), channel_id=1, source_target_pairs={{0,4},{4,8},{8,12},{12,16},{16,20},{20,24},{24,28},{28,32},{32,36}... | collective-permute-start | bytes 344072 | tf_op jit(solution)/shard_map/ppermute | solution.py:38
  115.5 15.3 %collective-permute-start.18 = (f32[4,2,16,128]{3,2,1,0:T(8,128)}, f32[4,2,16,128]{3,2,1,0:T(8,128)S(1)}, u32[]{:S(2)}, u32[]{:S(2)}) collective-permute-start(f32[4,2,16,128]{3,2,1,0:T(8,128)} %get-tuple-element.46), channel_id=1, source_target_pairs={{0,36},{4,40},{8,44},{12,48},{16,52},{20,56},{24,60},{28,64},{32,6... | collective-permute-start | bytes 196616 | tf_op jit(solution)/shard_map/ppermute | solution.py:38
  130.8 0.6 copy-start.8
  131.5 0.7 copy-start.6
  132.1 0.7 copy-start.4
  132.8 1.0 copy-start.3
  133.8 0.9 copy-start.5
  134.7 0.9 copy-start.7
  135.6 0.8 copy-start.9
  138.5 30.4 %all-to-all-start.1 = ((f32[32,24,256]{2,1,0:T(8,128)}), f32[32,24,256]{2,1,0:T(8,128)S(1)}, u32[]{:S(2)}, u32[]{:S(2)}) async-start(f32[32,24,256]{2,1,0:T(8,128)} %spread_sum.1), calls=%async_computation.2 | async-start | bytes 1572864 | tf_op jit(solution)/shard_map/all_to_all | solution.py:424
  145.5 10.3 %collective-permute-start.19 = (f32[24,2,16,128]{3,2,1,0:T(8,128)S(1)}, f32[24,2,16,128]{3,2,1,0:T(8,128)S(1)}, u32[]{:S(2)}, u32[]{:S(2)}) collective-permute-start(f32[24,2,16,128]{3,2,1,0:T(8,128)S(1)} %update.1.n0), channel_id=1, source_target_pairs={{0,1},{1,2},{2,3},{3,0},{4,5},{5,6},{6,7},{7,4},{8,9},{9,10},{10,1... | collective-permute-start | bytes 1179656 | tf_op jit(solution)/shard_map/ppermute | solution.py:42
  145.6 11.9 %collective-permute-start.20 = (f32[24,2,16,128]{3,2,1,0:T(8,128)S(1)}, f32[24,2,16,128]{3,2,1,0:T(8,128)S(1)}, u32[]{:S(2)}, u32[]{:S(2)}) collective-permute-start(f32[24,2,16,128]{3,2,1,0:T(8,128)S(1)} %update.1.n0), channel_id=1, source_target_pairs={{0,2},{1,3},{2,0},{3,1},{4,6},{5,7},{6,4},{7,5},{8,10},{9,11},{10,... | collective-permute-start | bytes 1179656 | tf_op jit(solution)/shard_map/ppermute | solution.py:42
  145.9 20.8 %collective-permute-start.21 = (f32[24,2,16,128]{3,2,1,0:T(8,128)S(1)}, f32[24,2,16,128]{3,2,1,0:T(8,128)S(1)}, u32[]{:S(2)}, u32[]{:S(2)}) collective-permute-start(f32[24,2,16,128]{3,2,1,0:T(8,128)S(1)} %update.1.n0), channel_id=1, source_target_pairs={{0,3},{1,0},{2,1},{3,2},{4,7},{5,4},{6,5},{7,6},{8,11},{9,8},{10,9... | collective-permute-start | bytes 1179656 | tf_op jit(solution)/shard_map/ppermute | solution.py:42
  168.9 2.6 %collective-permute-start.22 = (f32[3,256,256]{2,1,0:T(8,128)S(1)}, f32[3,256,256]{2,1,0:T(8,128)S(1)}, u32[]{:S(2)}, u32[]{:S(2)}) collective-permute-start(f32[3,256,256]{2,1,0:T(8,128)S(1)} %bitcast.18), channel_id=1, source_target_pairs={{0,4},{4,0},{8,12},{12,8},{16,20},{20,16},{24,28},{28,24},{32,36},... | collective-permute-start | bytes 2359304 | tf_op jit(solution)/shard_map/ppermute | solution.py:46
Sparse Core Ops, SparseCore 0:
  93.0 21.2 reduce-scatter.1

commit v8 on v6

--- a/solution.py
+++ b/solution.py
@@ -413,13 +413,13 @@
     from_above = shifted(to_low, DEV_COLS)
     from_corner = shifted(to_corner, DEV_COLS + 1)
     from_left = shifted(to_right, 1)
-    pieces, from_left, from_above, from_corner = lax.optimization_barrier(
-        (pieces, from_left, from_above, from_corner))
-    share = jnp.sum(pieces, axis=0)
+    shares = jnp.broadcast_to(jnp.sum(pieces, axis=0)[None], (N_CHIP, PART, SIDE))
+    shares, from_left, from_above, from_corner = lax.optimization_barrier(
+        (shares, from_left, from_above, from_corner))
 
     new = update(info, object_pieces, own, from_left, from_above, from_corner, in_hbm(light[0]))
-    share, new = lax.optimization_barrier((share, new))
-    gathered = exchange(jnp.broadcast_to(share[None], (N_CHIP, PART, SIDE)))
+    shares, new = lax.optimization_barrier((shares, new))
+    gathered = exchange(shares)
     new_parts = [new] + [turned(new, j) for j in (1, 2, 3)]
     gathered, *new_parts = lax.optimization_barrier((gathered, *new_parts))
     gathered = gathered.reshape(3, SIDE, SIDE)

time: 176 us -> 174 us (0.989)
  transfers between devices with their start and end apart: 26 -> 26, of which waited for: 19 -> 19; matrix products, arithmetic and copies ran while one was open for 4% -> 5% of each run, Pallas kernels for 1% -> 1%
where the time goes in v8:
time: 174 us
  waiting for transfers between devices  76.8 us (44%)
  starting transfers between devices  51.2 us (29%)
  Pallas kernels  19.2 us (11%)
  between operations  14.9 us (9%)
  local copies, waits for them, and re-layouts  8.39 us (5%)
  other arithmetic  3.3 us (2%)
    ppermute x15, waiting for transfers between devices, turned(): lax.ppermute(block, 'mode', [(i, (i + distance) % N_MODE) for i in range(...  53 us
    all_to_all x2, starting transfers between devices, body(): lax.all_to_all(blocks, 'tile', 0, 0, axis_index_groups=groups, tiled=True)  19.6 us
    ppermute x6, waiting for transfers between devices, shifted(): lax.ppermute(block, 'tile', [(d, (d + distance) % N_TILE) for d in range(...  19.5 us
    ppermute x6, starting transfers between devices, shifted(): lax.ppermute(block, 'tile', [(d, (d + distance) % N_TILE) for d in range(...  16.6 us
    ppermute x15, starting transfers between devices, turned(): lax.ppermute(block, 'mode', [(i, (i + distance) % N_MODE) for i in range(...  11.3 us
    pallas_call x1, Pallas kernels, forward(): pl.pallas_call(forward_kernel, grid=(3,), in_specs=[SMEM] + [HBM] * 6 + [...  6.88 us
    pallas_call x1, Pallas kernels, backward(): pl.pallas_call(backward_kernel, grid=(3,), in_specs=[SMEM, pl.BlockSpec((...  6.12 us
    ppermute x2, starting transfers between devices, core_swap(): return lax.ppermute(block, 'tile', [(d, d ^ 1) for d in range(N_TILE)])  3.69 us
  transfers between devices with their start and end apart: 26, of which 19 were waited for; matrix products, arithmetic and copies ran while one was open for 5% of the time, Pallas kernels for 1%

profile of v8, /device:TPU:39, one launch (start us, length us, event | category | flops | bytes accessed | tf_op | source)
XLA Modules:
  0.0 173.8 jit_solution(17105560521946504091)
XLA Ops:
  7.2 1.1 slice-done
  8.3 8.5 %collective-permute-start.1 = (f32[12,2,16,128]{3,2,1,0:T(8,128)S(1)}, f32[12,2,16,128]{3,2,1,0:T(8,128)S(1)}, u32[]{:S(2)}, u32[]{:S(2)}) collective-permute-start(f32[12,2,16,128]{3,2,1,0:T(8,128)S(1)} %constant_dynamic-slice_fusion), channel_id=1, source_target_pairs={{0,224},{4,228},{8,232},{12,236},{16,240},{20,244},{24,248},{28,25... | collective-permute-start | bytes 589832 | tf_op jit(solution)/shard_map/ppermute | solution.py:38
  16.9 0.7 collective-permute-start.2
  17.5 1.0 slice_bitcast_fusion
  18.5 0.4 collective-permute-start
  18.9 0.2 slice_reduce_fusion
  19.1 7.3 %collective-permute-done.2 = f32[3,2,16,128]{3,2,1,0:T(8,128)S(1)} collective-permute-done((f32[3,2,16,128]{3,2,1,0:T(8,128)S(1)}, f32[3,2,16,128]{3,2,1,0:T(8,128)S(1)}, u32[]{:S(2)}, u32[]{:S(2)}) %collective-permute-start.2) | collective-permute-done | bytes 49184 | tf_op jit(solution)/shard_map/ppermute | solution.py:38
  26.5 0.3 collective-permute-start.3
  26.7 2.1 %collective-permute-start.4 = (f32[15,2,16,128]{3,2,1,0:T(8,128)S(1)}, f32[15,2,16,128]{3,2,1,0:T(8,128)S(1)}, u32[]{:S(2)}, u32[]{:S(2)}) collective-permute-start(f32[15,2,16,128]{3,2,1,0:T(8,128)S(1)} %pad_maximum_fusion.b0), channel_id=1, source_target_pairs={{0,2},{1,3},{2,0},{3,1},{4,6},{5,7},{6,4},{7,5},{8,10},{9,11},{10,... | collective-permute-start | bytes 737288 | tf_op jit(solution)/shard_map/ppermute | solution.py:42
  29.6 0.6 fusion
  30.1 0.6 fusion.1
  30.7 2.5 %stack.15.info = s32[8]{0:T(128)S(1)} concatenate(s32[1]{0:T(128)} %get-tuple-element.65, s32[1]{0:T(128)} %get-tuple-element.63, s32[1]{0:T(128)} %get-tuple-element.64, s32[1]{0:T(128)} %get-tuple-element.62, s32[1]{0:T(128)} %copy.13, s32[1]{0:T(128)} %bitcast, s32[1]{0:T(128)} %bitcast.1, s32[1]{0:T(128)} %bitcast.2), dimensions={0} | concatenate | bytes 64 | tf_op jit(solution)/shard_map/stack | solution.py:387
  33.3 1.2 collective-permute-done.4.b2
  34.5 0.7 copy-done.9
  35.2 6.3 %collective-permute-done.5.b3 = f32[15,2,16,128]{3,2,1,0:T(8,128)} collective-permute-done((f32[15,2,16,128]{3,2,1,0:T(8,128)S(1)}, f32[15,2,16,128]{3,2,1,0:T(8,128)}, u32[]{:S(2)}, u32[]{:S(2)}) %collective-permute-start.5) | collective-permute-done | bytes 245792 | tf_op jit(solution)/shard_map/ppermute | solution.py:42
  41.4 6.9 %forward.1 = (f32[2,3,2,256,256]{4,3,2,1,0:T(8,128)}, f32[2,2,256,256]{3,2,1,0:T(8,128)S(1)}, f32[2,64,256]{2,1,0:T(8,128)S(1)}, f32[2,64,256]{2,1,0:T(8,128)S(1...) custom-call(s32[8]{0:T(128)S(1)} %stack.15.info, f32[24,2,64,128]{3,2,1,0:T(8,128)} %pieces.1, ...), custom_call_target="tpu_custom_call" | custom-call | flops 1700000000 | bytes 12000000 | tf_op jit(solution)/shard_map/forward/pallas_call | solution.py:144
  48.3 0.1 collective-permute-start.6
  48.4 0.9 collective-permute-start.7
  49.3 0.7 collective-permute-start.8
  50.1 2.9 %collective-permute-done.6 = f32[2,64,256]{2,1,0:T(8,128)S(1)} collective-permute-done((f32[2,64,256]{2,1,0:T(8,128)S(1)}, f32[2,64,256]{2,1,0:T(8,128)S(1)}, u32[]{:S(2)}, u32[]{:S(2)}) %collective-permute-start.6) | collective-permute-done | bytes 131104 | tf_op jit(solution)/shard_map/ppermute | solution.py:42
  52.9 1.0 collective-permute-done.7
  53.9 2.0 %collective-permute-done.8 = f32[2,64,256]{2,1,0:T(8,128)S(1)} collective-permute-done((f32[2,64,256]{2,1,0:T(8,128)S(1)}, f32[2,64,256]{2,1,0:T(8,128)S(1)}, u32[]{:S(2)}, u32[]{:S(2)}) %collective-permute-start.8) | collective-permute-done | bytes 131104 | tf_op jit(solution)/shard_map/ppermute | solution.py:42
  55.9 1.0 add_multiply_fusion.f0
  56.9 0.5 collective-permute-start.10
  57.4 2.4 %collective-permute-start.11 = (f32[2,64,256]{2,1,0:T(8,128)S(1)}, f32[2,64,256]{2,1,0:T(8,128)S(1)}, u32[]{:S(2)}, u32[]{:S(2)}) collective-permute-start(f32[2,64,256]{2,1,0:T(8,128)S(1)} %add_multiply_fusion.f0), channel_id=1, source_target_pairs={{0,3},{1,0},{2,1},{3,2},{4,7},{5,4},{6,5},{7,6},{8,11},{9,8},{10,9... | collective-permute-start | bytes 393224 | tf_op jit(solution)/shard_map/ppermute | solution.py:42
  59.8 0.3 collective-permute-start.9
  60.1 2.3 %collective-permute-done.10.f2 = f32[2,64,256]{2,1,0:T(8,128)S(1)} collective-permute-done((f32[2,64,256]{2,1,0:T(8,128)S(1)}, f32[2,64,256]{2,1,0:T(8,128)S(1)}, u32[]{:S(2)}, u32[]{:S(2)}) %collective-permute-start.10) | collective-permute-done | bytes 131104 | tf_op jit(solution)/shard_map/ppermute | solution.py:42
  62.4 1.3 collective-permute-done.11.f3
  63.7 1.3 collective-permute-done.9.f1
  65.0 6.1 %backward.1 = (f32[3,256,256]{2,1,0:T(8,128)S(1)}, f32[3,256,256]{2,1,0:T(8,128)S(1)}, f32[2,8,2,16,128]{4,3,2,1,0:T(8,128)S(1)}, f32[2,8,2,16,128]{4,3,2,1,0:T(...) custom-call(s32[8]{0:T(128)S(1)} %stack.15.info, ...), custom_call_target="tpu_custom_call" | custom-call | flops 1700000000 | bytes 12000000 | tf_op jit(solution)/shard_map/backward/pallas_call | solution.py:211
  71.1 3.0 %collective-permute-start.12 = (f32[3,256,256]{2,1,0:T(8,128)S(1)}, f32[3,256,256]{2,1,0:T(8,128)S(1)}, u32[]{:S(2)}, u32[]{:S(2)}) collective-permute-start(f32[3,256,256]{2,1,0:T(8,128)S(1)} %get-tuple-element.39), channel_id=1, source_target_pairs={{0,4},{4,0},{8,12},{12,8},{16,20},{20,16},{24,28},{28,24},{32,36},... | collective-permute-start | bytes 2359304 | tf_op jit(solution)/shard_map/ppermute | solution.py:46
  74.1 1.9 %collective-permute-done.12 = f32[3,256,256]{2,1,0:T(8,128)S(1)} collective-permute-done((f32[3,256,256]{2,1,0:T(8,128)S(1)}, f32[3,256,256]{2,1,0:T(8,128)S(1)}, u32[]{:S(2)}, u32[]{:S(2)}) %collective-permute-start.12) | collective-permute-done | bytes 786464 | tf_op jit(solution)/shard_map/ppermute | solution.py:46
  76.1 1.0 add.46
  77.0 12.6 %all-to-all-start = ((f32[32,24,256]{2,1,0:T(8,128)}), f32[32,24,256]{2,1,0:T(8,128)}, u32[]{:S(2)}, u32[]{:S(2)}) async-start(f32[32,24,256]{2,1,0:T(8,128)} %bitcast.6), calls=%async_computation | async-start | bytes 1572864 | tf_op jit(solution)/shard_map/all_to_all | solution.py:407
  89.6 0.0 reduce-scatter.2.cloned.1.call-start
  89.7 0.1 multiply_reduce_fusion
  89.8 0.7 copy.12
  90.5 0.0 reduce-scatter.2.cloned.1.call-update
  90.5 1.4 collective-permute-start.13
  91.9 0.6 collective-permute-start.14
  92.5 0.4 collective-permute-start.15
  92.9 4.9 %collective-permute-done.13.g1 = f32[2,8,2,16,128]{4,3,2,1,0:T(8,128)S(1)} collective-permute-done((f32[2,8,2,16,128]{4,3,2,1,0:T(8,128)}, f32[2,8,2,16,128]{4,3,2,1,0:T(8,128)S(1)}, u32[]{:S(2)}, u32[]{:S(2)}) %collective-permute-start.13) | collective-permute-done | bytes 262176 | tf_op jit(solution)/shard_map/ppermute | solution.py:42
  97.8 2.4 %collective-permute-done.14.g2 = f32[2,8,2,16,128]{4,3,2,1,0:T(8,128)S(1)} collective-permute-done((f32[2,8,2,16,128]{4,3,2,1,0:T(8,128)}, f32[2,8,2,16,128]{4,3,2,1,0:T(8,128)S(1)}, u32[]{:S(2)}, u32[]{:S(2)}) %collective-permute-start.14) | collective-permute-done | bytes 262176 | tf_op jit(solution)/shard_map/ppermute | solution.py:42
  100.2 7.9 %collective-permute-done.15.g3 = f32[2,8,2,16,128]{4,3,2,1,0:T(8,128)S(1)} collective-permute-done((f32[2,8,2,16,128]{4,3,2,1,0:T(8,128)}, f32[2,8,2,16,128]{4,3,2,1,0:T(8,128)S(1)}, u32[]{:S(2)}, u32[]{:S(2)}) %collective-permute-start.15) | collective-permute-done | bytes 262176 | tf_op jit(solution)/shard_map/ppermute | solution.py:42
  108.2 0.7 scatter.1
  108.9 4.3 %collective-permute-start.17 = (f32[13,2,16,128]{3,2,1,0:T(8,128)S(1)}, f32[13,2,16,128]{3,2,1,0:T(8,128)S(1)}, u32[]{:S(2)}, u32[]{:S(2)}) collective-permute-start(f32[13,2,16,128]{3,2,1,0:T(8,128)S(1)} %get-tuple-element.45), channel_id=1, source_target_pairs={{0,32},{4,36},{8,40},{12,44},{16,48},{20,52},{24,56},{28,60},{32,6... | collective-permute-start | bytes 638984 | tf_op jit(solution)/shard_map/ppermute | solution.py:38
  113.2 0.9 collective-permute-start.16
  114.1 1.8 %collective-permute-start.18 = (f32[4,2,16,128]{3,2,1,0:T(8,128)S(1)}, f32[4,2,16,128]{3,2,1,0:T(8,128)S(1)}, u32[]{:S(2)}, u32[]{:S(2)}) collective-permute-start(f32[4,2,16,128]{3,2,1,0:T(8,128)S(1)} %get-tuple-element.46), channel_id=1, source_target_pairs={{0,36},{4,40},{8,44},{12,48},{16,52},{20,56},{24,60},{28,64},{32,6... | collective-permute-start | bytes 196616 | tf_op jit(solution)/shard_map/ppermute | solution.py:38
  115.9 1.2 reduce_sum.18
  117.1 12.2 %collective-permute-done.18.corner = f32[4,2,16,128]{3,2,1,0:T(8,128)S(1)} collective-permute-done((f32[4,2,16,128]{3,2,1,0:T(8,128)S(1)}, f32[4,2,16,128]{3,2,1,0:T(8,128)S(1)}, u32[]{:S(2)}, u32[]{:S(2)}) %collective-permute-start.18) | collective-permute-done | bytes 65568 | tf_op jit(solution)/shard_map/ppermute | solution.py:38
  129.3 0.9 broadcast_in_dim.2
  130.2 2.0 %update.1.n0 = f32[24,2,16,128]{3,2,1,0:T(8,128)S(1)} custom-call(s32[8]{0:T(128)S(1)} %stack.15.info, f32[24,2,64,128]{3,2,1,0:T(8,128)S(1)} %copy-done.1, f32[24,2,16,128]{3,2,1,0:T(8,128)S(1)} %get-tuple-element.48.own, f32[7,2,16,128]{3,2,1,0:T(8,128)S(1)} %collective-permute-done.16.right, f32[13,2,16,128]{3,2,1,0:T(8,128)S(1)} %collective-permute-done.17.low, ...), custom_call_target="tpu_custom_call" | custom-call | flops 1000000 | bytes 2000000 | tf_op jit(solution)/shard_map/update/pallas_call | solution.py:311
  132.2 7.0 %all-to-all-start.1 = ((f32[32,24,256]{2,1,0:T(8,128)}), f32[32,24,256]{2,1,0:T(8,128)S(1)}, u32[]{:S(2)}, u32[]{:S(2)}) async-start(f32[32,24,256]{2,1,0:T(8,128)} %broadcast_in_dim.2), calls=%async_computation.2 | async-start | bytes 1572864 | tf_op jit(solution)/shard_map/all_to_all | solution.py:407
  139.3 0.1 collective-permute-start.19
  139.3 0.2 collective-permute-start.20
  139.6 1.2 collective-permute-start.21
  140.8 8.9 %collective-permute-done.19.n1 = f32[24,2,16,128]{3,2,1,0:T(8,128)S(1)} collective-permute-done((f32[24,2,16,128]{3,2,1,0:T(8,128)S(1)}, f32[24,2,16,128]{3,2,1,0:T(8,128)S(1)}, u32[]{:S(2)}, u32[]{:S(2)}) %collective-permute-start.19) | collective-permute-done | bytes 393248 | tf_op jit(solution)/shard_map/ppermute | solution.py:42
  149.7 1.6 collective-permute-done.20.n2
  151.3 9.1 %collective-permute-done.21.n3 = f32[24,2,16,128]{3,2,1,0:T(8,128)S(1)} collective-permute-done((f32[24,2,16,128]{3,2,1,0:T(8,128)S(1)}, f32[24,2,16,128]{3,2,1,0:T(8,128)S(1)}, u32[]{:S(2)}, u32[]{:S(2)}) %collective-permute-start.21) | collective-permute-done | bytes 393248 | tf_op jit(solution)/shard_map/ppermute | solution.py:42
  160.4 2.2 %all-to-all-done.1 = f32[32,24,256]{2,1,0:T(8,128)S(1)} async-done(((f32[32,24,256]{2,1,0:T(8,128)}), f32[32,24,256]{2,1,0:T(8,128)S(1)}, u32[]{:S(2)}, u32[]{:S(2)}) %all-to-all-start.1) | async-done | bytes 786464 | tf_op jit(solution)/shard_map/all_to_all | solution.py:407
  162.6 0.7 collective-permute-start.22
  163.3 1.7 join_pieces.1
  165.0 0.2 collective-permute-done.22.theirs
  165.2 1.7 join_channels.1
  (33 shorter events, 0.1 us)
Async XLA Ops:
  7.2 1.1 slice-start
  7.2 11.7 %copy-start.6 = (s32[2,2]{1,0:T(2,128)S(1)}, s32[2,2]{1,0:T(2,128)}, u32[]{:S(2)}) copy-start(s32[2,2]{1,0:T(2,128)} %param.9) | copy-start | bytes 52
  7.2 34.2 %copy-start = (f32[3,2,256,256]{3,2,1,0:T(8,128)S(1)}, f32[3,2,256,256]{3,2,1,0:T(8,128)}, u32[]{:S(2)}) copy-start(f32[3,2,256,256]{3,2,1,0:T(8,128)} %probe.3) | copy-start | bytes 4718596
  8.3 18.1 %collective-permute-start.1 = (f32[12,2,16,128]{3,2,1,0:T(8,128)S(1)}, f32[12,2,16,128]{3,2,1,0:T(8,128)S(1)}, u32[]{:S(2)}, u32[]{:S(2)}) collective-permute-start(f32[12,2,16,128]{3,2,1,0:T(8,128)S(1)} %constant_dynamic-slice_fusion), channel_id=1, source_target_pairs={{0,224},{4,228},{8,232},{12,236},{16,240},{20,244},{24,248},{28,25... | collective-permute-start | bytes 589832 | tf_op jit(solution)/shard_map/ppermute | solution.py:38
  16.9 9.6 %collective-permute-start.2 = (f32[3,2,16,128]{3,2,1,0:T(8,128)S(1)}, f32[3,2,16,128]{3,2,1,0:T(8,128)S(1)}, u32[]{:S(2)}, u32[]{:S(2)}) collective-permute-start(f32[3,2,16,128]{3,2,1,0:T(8,128)S(1)} %slice.35), channel_id=1, source_target_pairs={{0,220},{4,224},{8,228},{12,232},{16,236},{20,240},{24,244},{28,24... | collective-permute-start | bytes 147464 | tf_op jit(solution)/shard_map/ppermute | solution.py:38
  18.5 14.7 %collective-permute-start = (f32[6,2,64,128]{3,2,1,0:T(8,128)S(1)}, f32[6,2,64,128]{3,2,1,0:T(8,128)S(1)}, u32[]{:S(2)}, u32[]{:S(2)}) collective-permute-start(f32[6,2,64,128]{3,2,1,0:T(8,128)S(1)} %slice_bitcast_fusion), channel_id=1, source_target_pairs={{0,252},{4,0},{8,4},{12,8},{16,12},{20,16},{24,20},{28,24},{32,28}... | collective-permute-start | bytes 1179656 | tf_op jit(solution)/shard_map/ppermute | solution.py:38
  26.5 15.0 %copy-start.5 = (f32[15,2,16,128]{3,2,1,0:T(8,128)}, f32[15,2,16,128]{3,2,1,0:T(8,128)S(1)}, u32[]{:S(2)}) copy-start(f32[15,2,16,128]{3,2,1,0:T(8,128)S(1)} %pad_maximum_fusion.b0) | copy-start | bytes 737284
  26.5 6.8 %collective-permute-start.3 = (f32[15,2,16,128]{3,2,1,0:T(8,128)S(1)}, f32[15,2,16,128]{3,2,1,0:T(8,128)S(1)}, u32[]{:S(2)}, u32[]{:S(2)}) collective-permute-start(f32[15,2,16,128]{3,2,1,0:T(8,128)S(1)} %pad_maximum_fusion.b0), channel_id=1, source_target_pairs={{0,1},{1,2},{2,3},{3,0},{4,5},{5,6},{6,7},{7,4},{8,9},{9,10},{10,1... | collective-permute-start | bytes 737288 | tf_op jit(solution)/shard_map/ppermute | solution.py:42
  26.7 7.7 %collective-permute-start.4 = (f32[15,2,16,128]{3,2,1,0:T(8,128)S(1)}, f32[15,2,16,128]{3,2,1,0:T(8,128)S(1)}, u32[]{:S(2)}, u32[]{:S(2)}) collective-permute-start(f32[15,2,16,128]{3,2,1,0:T(8,128)S(1)} %pad_maximum_fusion.b0), channel_id=1, source_target_pairs={{0,2},{1,3},{2,0},{3,1},{4,6},{5,7},{6,4},{7,5},{8,10},{9,11},{10,... | collective-permute-start | bytes 737288 | tf_op jit(solution)/shard_map/ppermute | solution.py:42
  28.9 12.5 %collective-permute-start.5 = (f32[15,2,16,128]{3,2,1,0:T(8,128)S(1)}, f32[15,2,16,128]{3,2,1,0:T(8,128)}, u32[]{:S(2)}, u32[]{:S(2)}) collective-permute-start(f32[15,2,16,128]{3,2,1,0:T(8,128)S(1)} %pad_maximum_fusion.b0), channel_id=1, source_target_pairs={{0,3},{1,0},{2,1},{3,2},{4,7},{5,4},{6,5},{7,6},{8,11},{9,8},{10,9... | collective-permute-start | bytes 737288 | tf_op jit(solution)/shard_map/ppermute | solution.py:42
  33.2 1.2 copy-start.7
  33.3 1.2 copy-start.8
  34.5 0.7 copy-start.9
  48.3 4.6 %collective-permute-start.6 = (f32[2,64,256]{2,1,0:T(8,128)S(1)}, f32[2,64,256]{2,1,0:T(8,128)S(1)}, u32[]{:S(2)}, u32[]{:S(2)}) collective-permute-start(f32[2,64,256]{2,1,0:T(8,128)S(1)} %get-tuple-element.35), channel_id=1, source_target_pairs={{0,1},{1,2},{2,3},{3,0},{4,5},{5,6},{6,7},{7,4},{8,9},{9,10},{10,1... | collective-permute-start | bytes 393224 | tf_op jit(solution)/shard_map/ppermute | solution.py:42
  48.4 5.5 %collective-permute-start.7 = (f32[2,64,256]{2,1,0:T(8,128)S(1)}, f32[2,64,256]{2,1,0:T(8,128)S(1)}, u32[]{:S(2)}, u32[]{:S(2)}) collective-permute-start(f32[2,64,256]{2,1,0:T(8,128)S(1)} %get-tuple-element.36), channel_id=1, source_target_pairs={{0,2},{1,3},{2,0},{3,1},{4,6},{5,7},{6,4},{7,5},{8,10},{9,11},{10,... | collective-permute-start | bytes 393224 | tf_op jit(solution)/shard_map/ppermute | solution.py:42
  49.3 6.6 %collective-permute-start.8 = (f32[2,64,256]{2,1,0:T(8,128)S(1)}, f32[2,64,256]{2,1,0:T(8,128)S(1)}, u32[]{:S(2)}, u32[]{:S(2)}) collective-permute-start(f32[2,64,256]{2,1,0:T(8,128)S(1)} %get-tuple-element.37), channel_id=1, source_target_pairs={{0,3},{1,0},{2,1},{3,2},{4,7},{5,4},{6,5},{7,6},{8,11},{9,8},{10,9... | collective-permute-start | bytes 393224 | tf_op jit(solution)/shard_map/ppermute | solution.py:42
  56.9 5.5 %collective-permute-start.10 = (f32[2,64,256]{2,1,0:T(8,128)S(1)}, f32[2,64,256]{2,1,0:T(8,128)S(1)}, u32[]{:S(2)}, u32[]{:S(2)}) collective-permute-start(f32[2,64,256]{2,1,0:T(8,128)S(1)} %add_multiply_fusion.f0), channel_id=1, source_target_pairs={{0,2},{1,3},{2,0},{3,1},{4,6},{5,7},{6,4},{7,5},{8,10},{9,11},{10,... | collective-permute-start | bytes 393224 | tf_op jit(solution)/shard_map/ppermute | solution.py:42
  57.4 6.3 %collective-permute-start.11 = (f32[2,64,256]{2,1,0:T(8,128)S(1)}, f32[2,64,256]{2,1,0:T(8,128)S(1)}, u32[]{:S(2)}, u32[]{:S(2)}) collective-permute-start(f32[2,64,256]{2,1,0:T(8,128)S(1)} %add_multiply_fusion.f0), channel_id=1, source_target_pairs={{0,3},{1,0},{2,1},{3,2},{4,7},{5,4},{6,5},{7,6},{8,11},{9,8},{10,9... | collective-permute-start | bytes 393224 | tf_op jit(solution)/shard_map/ppermute | solution.py:42
  59.8 5.2 %collective-permute-start.9 = (f32[2,64,256]{2,1,0:T(8,128)S(1)}, f32[2,64,256]{2,1,0:T(8,128)S(1)}, u32[]{:S(2)}, u32[]{:S(2)}) collective-permute-start(f32[2,64,256]{2,1,0:T(8,128)S(1)} %add_multiply_fusion.f0), channel_id=1, source_target_pairs={{0,1},{1,2},{2,3},{3,0},{4,5},{5,6},{6,7},{7,4},{8,9},{9,10},{10,1... | collective-permute-start | bytes 393224 | tf_op jit(solution)/shard_map/ppermute | solution.py:42
  71.1 6.0 %copy-start.2 = (f32[2,8,2,16,128]{4,3,2,1,0:T(8,128)}, f32[2,8,2,16,128]{4,3,2,1,0:T(8,128)S(1)}, u32[]{:S(2)}) copy-start(f32[2,8,2,16,128]{4,3,2,1,0:T(8,128)S(1)} %get-tuple-element.43) | copy-start | bytes 786436
  71.1 5.9 %copy-start.3 = (f32[2,8,2,16,128]{4,3,2,1,0:T(8,128)}, f32[2,8,2,16,128]{4,3,2,1,0:T(8,128)S(1)}, u32[]{:S(2)}) copy-start(f32[2,8,2,16,128]{4,3,2,1,0:T(8,128)S(1)} %get-tuple-element.42) | copy-start | bytes 786436
  71.1 5.9 %copy-start.4 = (f32[2,8,2,16,128]{4,3,2,1,0:T(8,128)}, f32[2,8,2,16,128]{4,3,2,1,0:T(8,128)S(1)}, u32[]{:S(2)}) copy-start(f32[2,8,2,16,128]{4,3,2,1,0:T(8,128)S(1)} %get-tuple-element.41) | copy-start | bytes 786436
  71.1 4.9 %collective-permute-start.12 = (f32[3,256,256]{2,1,0:T(8,128)S(1)}, f32[3,256,256]{2,1,0:T(8,128)S(1)}, u32[]{:S(2)}, u32[]{:S(2)}) collective-permute-start(f32[3,256,256]{2,1,0:T(8,128)S(1)} %get-tuple-element.39), channel_id=1, source_target_pairs={{0,4},{4,0},{8,12},{12,8},{16,20},{20,16},{24,28},{28,24},{32,36},... | collective-permute-start | bytes 2359304 | tf_op jit(solution)/shard_map/ppermute | solution.py:46
  77.0 38.9 %all-to-all-start = ((f32[32,24,256]{2,1,0:T(8,128)}), f32[32,24,256]{2,1,0:T(8,128)}, u32[]{:S(2)}, u32[]{:S(2)}) async-start(f32[32,24,256]{2,1,0:T(8,128)} %bitcast.6), calls=%async_computation | async-start | bytes 1572864 | tf_op jit(solution)/shard_map/all_to_all | solution.py:407
  89.6 40.6 %reduce-scatter.2.cloned.1.call-start = ((), (), s32[]{:S(2)}) async-start(), calls=%async_computation.3 | async-start | bytes 327680 | tf_op jit(solution)/shard_map/reduce_scatter | solution.py:392
  90.5 39.7 %copy-start.1 = (f32[24,2,64,128]{3,2,1,0:T(8,128)S(1)}, f32[24,2,64,128]{3,2,1,0:T(8,128)}, u32[]{:S(2)}) copy-start(f32[24,2,64,128]{3,2,1,0:T(8,128)} %pieces.1) | copy-start | bytes 4718596
  90.5 7.3 %collective-permute-start.13 = (f32[2,8,2,16,128]{4,3,2,1,0:T(8,128)}, f32[2,8,2,16,128]{4,3,2,1,0:T(8,128)S(1)}, u32[]{:S(2)}, u32[]{:S(2)}) collective-permute-start(f32[2,8,2,16,128]{4,3,2,1,0:T(8,128)} %copy-done.4), channel_id=1, source_target_pairs={{0,1},{1,2},{2,3},{3,0},{4,5},{5,6},{6,7},{7,4},{8,9},{9,10},{10,1... | collective-permute-start | bytes 786440 | tf_op jit(solution)/shard_map/ppermute | solution.py:42
  91.9 8.3 %collective-permute-start.14 = (f32[2,8,2,16,128]{4,3,2,1,0:T(8,128)}, f32[2,8,2,16,128]{4,3,2,1,0:T(8,128)S(1)}, u32[]{:S(2)}, u32[]{:S(2)}) collective-permute-start(f32[2,8,2,16,128]{4,3,2,1,0:T(8,128)} %copy-done.3), channel_id=1, source_target_pairs={{0,2},{1,3},{2,0},{3,1},{4,6},{5,7},{6,4},{7,5},{8,10},{9,11},{10,... | collective-permute-start | bytes 786440 | tf_op jit(solution)/shard_map/ppermute | solution.py:42
  92.5 15.6 %collective-permute-start.15 = (f32[2,8,2,16,128]{4,3,2,1,0:T(8,128)}, f32[2,8,2,16,128]{4,3,2,1,0:T(8,128)S(1)}, u32[]{:S(2)}, u32[]{:S(2)}) collective-permute-start(f32[2,8,2,16,128]{4,3,2,1,0:T(8,128)} %copy-done.2), channel_id=1, source_target_pairs={{0,3},{1,0},{2,1},{3,2},{4,7},{5,4},{6,5},{7,6},{8,11},{9,8},{10,9... | collective-permute-start | bytes 786440 | tf_op jit(solution)/shard_map/ppermute | solution.py:42
  108.9 20.4 %collective-permute-start.17 = (f32[13,2,16,128]{3,2,1,0:T(8,128)S(1)}, f32[13,2,16,128]{3,2,1,0:T(8,128)S(1)}, u32[]{:S(2)}, u32[]{:S(2)}) collective-permute-start(f32[13,2,16,128]{3,2,1,0:T(8,128)S(1)} %get-tuple-element.45), channel_id=1, source_target_pairs={{0,32},{4,36},{8,40},{12,44},{16,48},{20,52},{24,56},{28,60},{32,6... | collective-permute-start | bytes 638984 | tf_op jit(solution)/shard_map/ppermute | solution.py:38
  113.2 16.1 %collective-permute-start.16 = (f32[7,2,16,128]{3,2,1,0:T(8,128)S(1)}, f32[7,2,16,128]{3,2,1,0:T(8,128)S(1)}, u32[]{:S(2)}, u32[]{:S(2)}) collective-permute-start(f32[7,2,16,128]{3,2,1,0:T(8,128)S(1)} %get-tuple-element.44), channel_id=1, source_target_pairs={{0,4},{4,8},{8,12},{12,16},{16,20},{20,24},{24,28},{28,32},{32,36}... | collective-permute-start | bytes 344072 | tf_op jit(solution)/shard_map/ppermute | solution.py:38
  114.1 15.2 %collective-permute-start.18 = (f32[4,2,16,128]{3,2,1,0:T(8,128)S(1)}, f32[4,2,16,128]{3,2,1,0:T(8,128)S(1)}, u32[]{:S(2)}, u32[]{:S(2)}) collective-permute-start(f32[4,2,16,128]{3,2,1,0:T(8,128)S(1)} %get-tuple-element.46), channel_id=1, source_target_pairs={{0,36},{4,40},{8,44},{12,48},{16,52},{20,56},{24,60},{28,64},{32,6... | collective-permute-start | bytes 196616 | tf_op jit(solution)/shard_map/ppermute | solution.py:38
  132.2 30.4 %all-to-all-start.1 = ((f32[32,24,256]{2,1,0:T(8,128)}), f32[32,24,256]{2,1,0:T(8,128)S(1)}, u32[]{:S(2)}, u32[]{:S(2)}) async-start(f32[32,24,256]{2,1,0:T(8,128)} %broadcast_in_dim.2), calls=%async_computation.2 | async-start | bytes 1572864 | tf_op jit(solution)/shard_map/all_to_all | solution.py:407
  139.3 10.4 %collective-permute-start.19 = (f32[24,2,16,128]{3,2,1,0:T(8,128)S(1)}, f32[24,2,16,128]{3,2,1,0:T(8,128)S(1)}, u32[]{:S(2)}, u32[]{:S(2)}) collective-permute-start(f32[24,2,16,128]{3,2,1,0:T(8,128)S(1)} %update.1.n0), channel_id=1, source_target_pairs={{0,1},{1,2},{2,3},{3,0},{4,5},{5,6},{6,7},{7,4},{8,9},{9,10},{10,1... | collective-permute-start | bytes 1179656 | tf_op jit(solution)/shard_map/ppermute | solution.py:42
  139.3 12.0 %collective-permute-start.20 = (f32[24,2,16,128]{3,2,1,0:T(8,128)S(1)}, f32[24,2,16,128]{3,2,1,0:T(8,128)S(1)}, u32[]{:S(2)}, u32[]{:S(2)}) collective-permute-start(f32[24,2,16,128]{3,2,1,0:T(8,128)S(1)} %update.1.n0), channel_id=1, source_target_pairs={{0,2},{1,3},{2,0},{3,1},{4,6},{5,7},{6,4},{7,5},{8,10},{9,11},{10,... | collective-permute-start | bytes 1179656 | tf_op jit(solution)/shard_map/ppermute | solution.py:42
  139.6 20.8 %collective-permute-start.21 = (f32[24,2,16,128]{3,2,1,0:T(8,128)S(1)}, f32[24,2,16,128]{3,2,1,0:T(8,128)S(1)}, u32[]{:S(2)}, u32[]{:S(2)}) collective-permute-start(f32[24,2,16,128]{3,2,1,0:T(8,128)S(1)} %update.1.n0), channel_id=1, source_target_pairs={{0,3},{1,0},{2,1},{3,2},{4,7},{5,4},{6,5},{7,6},{8,11},{9,8},{10,9... | collective-permute-start | bytes 1179656 | tf_op jit(solution)/shard_map/ppermute | solution.py:42
  162.6 2.6 %collective-permute-start.22 = (f32[3,256,256]{2,1,0:T(8,128)S(1)}, f32[3,256,256]{2,1,0:T(8,128)S(1)}, u32[]{:S(2)}, u32[]{:S(2)}) collective-permute-start(f32[3,256,256]{2,1,0:T(8,128)S(1)} %bitcast.18), channel_id=1, source_target_pairs={{0,4},{4,0},{8,12},{12,8},{16,20},{20,16},{24,28},{28,24},{32,36},... | collective-permute-start | bytes 2359304 | tf_op jit(solution)/shard_map/ppermute | solution.py:46
Sparse Core Ops, SparseCore 0:
  93.0 21.2 reduce-scatter.1

commit v9 on v8

--- a/solution.py
+++ b/solution.py
@@ -59,9 +59,7 @@
 
 
 def expand_table(table, held, left, right, sem):
-    fetch = pltpu.make_async_copy(table, held, sem)
-    fetch.start()
-    fetch.wait()
+    pltpu.make_async_copy(table, held, sem).wait()
     re, im = held[0], held[1]
     for out in (left, right):
         out[:SIDE, :SIDE] = re
@@ -88,6 +86,7 @@
 
     @pl.when(mode == 0)
     def _():
+        pltpu.make_async_copy(table, held, table_sem).start()
         for s in range(2):
             for q in range(8):
                 row = info[2 * s] + q // 2
@@ -170,10 +169,11 @@
 
     @pl.when(mode == 0)
     def _():
-        expand_table(table, held, left_table, right_table, table_sem)
+        pltpu.make_async_copy(table, held, table_sem).start()
         for j, part in enumerate((f0, f1, f2, f3)):
             start = pl.multiple_of(lax.rem(me + N_MODE - j, N_MODE) * 64, 64)
             factor[:, pl.ds(start, 64), :] = part[...]
+        expand_table(table, held, left_table, right_table, table_sem)
 
     probe_re, probe_im = probe[0, 0], probe[0, 1]
     own_term, other_term = 0.0, 0.0

time: 174 us -> 174 us (level)
  no operation moved by 1% of the time
where the time goes in v9:
time: 174 us; the launch traced here: 173 us
  waiting for transfers between devices  76.2 us (44%)
  starting transfers between devices  51.8 us (30%)
  Pallas kernels  18.8 us (11%)
  between operations  14.9 us (9%)
  local copies, waits for them, and re-layouts  8.39 us (5%)
  other arithmetic  3.3 us (2%)
    ppermute x15, waiting for transfers between devices, turned(): lax.ppermute(block, 'mode', [(i, (i + distance) % N_MODE) for i in range(...  52.5 us
    all_to_all x2, starting transfers between devices, body(): lax.all_to_all(blocks, 'tile', 0, 0, axis_index_groups=groups, tiled=True)  19.6 us
    ppermute x6, waiting for transfers between devices, shifted(): lax.ppermute(block, 'tile', [(d, (d + distance) % N_TILE) for d in range(...  19.4 us
    ppermute x6, starting transfers between devices, shifted(): lax.ppermute(block, 'tile', [(d, (d + distance) % N_TILE) for d in range(...  16.6 us
    ppermute x15, starting transfers between devices, turned(): lax.ppermute(block, 'mode', [(i, (i + distance) % N_MODE) for i in range(...  11.3 us
    pallas_call x1, Pallas kernels, forward(): pl.pallas_call(forward_kernel, grid=(3,), in_specs=[SMEM] + [HBM] * 6 + [...  6.53 us
    pallas_call x1, Pallas kernels, backward(): pl.pallas_call(backward_kernel, grid=(3,), in_specs=[SMEM, pl.BlockSpec((...  6.08 us
    ppermute x2, starting transfers between devices, core_swap(): return lax.ppermute(block, 'tile', [(d, d ^ 1) for d in range(N_TILE)])  4.34 us
  transfers between devices with their start and end apart: 26, of which 19 were waited for; matrix products, arithmetic and copies ran while one was open for 5% of the time, Pallas kernels for 1%

profile of v9, /device:TPU:39, one launch (start us, length us, event | category | flops | bytes accessed | tf_op | source)
XLA Modules:
  0.0 173.5 jit_solution(11968260007948545139)
XLA Ops:
  7.2 1.1 slice-done
  8.3 8.5 %collective-permute-start.1 = (f32[12,2,16,128]{3,2,1,0:T(8,128)S(1)}, f32[12,2,16,128]{3,2,1,0:T(8,128)S(1)}, u32[]{:S(2)}, u32[]{:S(2)}) collective-permute-start(f32[12,2,16,128]{3,2,1,0:T(8,128)S(1)} %constant_dynamic-slice_fusion), channel_id=1, source_target_pairs={{0,224},{4,228},{8,232},{12,236},{16,240},{20,244},{24,248},{28,25... | collective-permute-start | bytes 589832 | tf_op jit(solution)/shard_map/ppermute | solution.py:38
  16.9 0.7 collective-permute-start.2
  17.5 1.0 slice_bitcast_fusion
  18.5 0.4 collective-permute-start
  18.9 0.2 slice_reduce_fusion
  19.1 7.3 %collective-permute-done.2 = f32[3,2,16,128]{3,2,1,0:T(8,128)S(1)} collective-permute-done((f32[3,2,16,128]{3,2,1,0:T(8,128)S(1)}, f32[3,2,16,128]{3,2,1,0:T(8,128)S(1)}, u32[]{:S(2)}, u32[]{:S(2)}) %collective-permute-start.2) | collective-permute-done | bytes 49184 | tf_op jit(solution)/shard_map/ppermute | solution.py:38
  26.5 0.3 collective-permute-start.3
  26.7 2.1 %collective-permute-start.4 = (f32[15,2,16,128]{3,2,1,0:T(8,128)S(1)}, f32[15,2,16,128]{3,2,1,0:T(8,128)S(1)}, u32[]{:S(2)}, u32[]{:S(2)}) collective-permute-start(f32[15,2,16,128]{3,2,1,0:T(8,128)S(1)} %pad_maximum_fusion.b0), channel_id=1, source_target_pairs={{0,2},{1,3},{2,0},{3,1},{4,6},{5,7},{6,4},{7,5},{8,10},{9,11},{10,... | collective-permute-start | bytes 737288 | tf_op jit(solution)/shard_map/ppermute | solution.py:42
  29.6 0.6 fusion
  30.1 0.6 fusion.1
  30.7 2.5 %stack.15.info = s32[8]{0:T(128)S(1)} concatenate(s32[1]{0:T(128)} %get-tuple-element.65, s32[1]{0:T(128)} %get-tuple-element.63, s32[1]{0:T(128)} %get-tuple-element.64, s32[1]{0:T(128)} %get-tuple-element.62, s32[1]{0:T(128)} %copy.13, s32[1]{0:T(128)} %bitcast, s32[1]{0:T(128)} %bitcast.1, s32[1]{0:T(128)} %bitcast.2), dimensions={0} | concatenate | bytes 64 | tf_op jit(solution)/shard_map/stack | solution.py:387
  33.3 1.2 collective-permute-done.4.b2
  34.5 0.7 copy-done.9
  35.2 6.3 %collective-permute-done.5.b3 = f32[15,2,16,128]{3,2,1,0:T(8,128)} collective-permute-done((f32[15,2,16,128]{3,2,1,0:T(8,128)S(1)}, f32[15,2,16,128]{3,2,1,0:T(8,128)}, u32[]{:S(2)}, u32[]{:S(2)}) %collective-permute-start.5) | collective-permute-done | bytes 245792 | tf_op jit(solution)/shard_map/ppermute | solution.py:42
  41.4 6.5 %forward.1 = (f32[2,3,2,256,256]{4,3,2,1,0:T(8,128)}, f32[2,2,256,256]{3,2,1,0:T(8,128)S(1)}, f32[2,64,256]{2,1,0:T(8,128)S(1)}, f32[2,64,256]{2,1,0:T(8,128)S(1...) custom-call(s32[8]{0:T(128)S(1)} %stack.15.info, f32[24,2,64,128]{3,2,1,0:T(8,128)} %pieces.1, ...), custom_call_target="tpu_custom_call" | custom-call | flops 1700000000 | bytes 12000000 | tf_op jit(solution)/shard_map/forward/pallas_call | solution.py:143
  48.0 0.1 collective-permute-start.6
  48.1 0.9 collective-permute-start.7
  49.0 0.7 collective-permute-start.8
  49.7 2.8 %collective-permute-done.6 = f32[2,64,256]{2,1,0:T(8,128)S(1)} collective-permute-done((f32[2,64,256]{2,1,0:T(8,128)S(1)}, f32[2,64,256]{2,1,0:T(8,128)S(1)}, u32[]{:S(2)}, u32[]{:S(2)}) %collective-permute-start.6) | collective-permute-done | bytes 131104 | tf_op jit(solution)/shard_map/ppermute | solution.py:42
  52.5 1.1 collective-permute-done.7
  53.5 1.9 %collective-permute-done.8 = f32[2,64,256]{2,1,0:T(8,128)S(1)} collective-permute-done((f32[2,64,256]{2,1,0:T(8,128)S(1)}, f32[2,64,256]{2,1,0:T(8,128)S(1)}, u32[]{:S(2)}, u32[]{:S(2)}) %collective-permute-start.8) | collective-permute-done | bytes 131104 | tf_op jit(solution)/shard_map/ppermute | solution.py:42
  55.4 1.0 add_multiply_fusion.f0
  56.4 0.5 collective-permute-start.10
  56.9 2.4 %collective-permute-start.11 = (f32[2,64,256]{2,1,0:T(8,128)S(1)}, f32[2,64,256]{2,1,0:T(8,128)S(1)}, u32[]{:S(2)}, u32[]{:S(2)}) collective-permute-start(f32[2,64,256]{2,1,0:T(8,128)S(1)} %add_multiply_fusion.f0), channel_id=1, source_target_pairs={{0,3},{1,0},{2,1},{3,2},{4,7},{5,4},{6,5},{7,6},{8,11},{9,8},{10,9... | collective-permute-start | bytes 393224 | tf_op jit(solution)/shard_map/ppermute | solution.py:42
  59.3 0.3 collective-permute-start.9
  59.6 2.3 %collective-permute-done.10.f2 = f32[2,64,256]{2,1,0:T(8,128)S(1)} collective-permute-done((f32[2,64,256]{2,1,0:T(8,128)S(1)}, f32[2,64,256]{2,1,0:T(8,128)S(1)}, u32[]{:S(2)}, u32[]{:S(2)}) %collective-permute-start.10) | collective-permute-done | bytes 131104 | tf_op jit(solution)/shard_map/ppermute | solution.py:42
  61.9 1.3 collective-permute-done.11.f3
  63.2 0.8 collective-permute-done.9.f1
  64.1 6.1 %backward.1 = (f32[3,256,256]{2,1,0:T(8,128)S(1)}, f32[3,256,256]{2,1,0:T(8,128)S(1)}, f32[2,8,2,16,128]{4,3,2,1,0:T(8,128)S(1)}, f32[2,8,2,16,128]{4,3,2,1,0:T(...) custom-call(s32[8]{0:T(128)S(1)} %stack.15.info, ...), custom_call_target="tpu_custom_call" | custom-call | flops 1700000000 | bytes 12000000 | tf_op jit(solution)/shard_map/backward/pallas_call | solution.py:211
  70.2 3.6 %collective-permute-start.12 = (f32[3,256,256]{2,1,0:T(8,128)S(1)}, f32[3,256,256]{2,1,0:T(8,128)S(1)}, u32[]{:S(2)}, u32[]{:S(2)}) collective-permute-start(f32[3,256,256]{2,1,0:T(8,128)S(1)} %get-tuple-element.39), channel_id=1, source_target_pairs={{0,4},{4,0},{8,12},{12,8},{16,20},{20,16},{24,28},{28,24},{32,36},... | collective-permute-start | bytes 2359304 | tf_op jit(solution)/shard_map/ppermute | solution.py:46
  73.8 1.9 %collective-permute-done.12 = f32[3,256,256]{2,1,0:T(8,128)S(1)} collective-permute-done((f32[3,256,256]{2,1,0:T(8,128)S(1)}, f32[3,256,256]{2,1,0:T(8,128)S(1)}, u32[]{:S(2)}, u32[]{:S(2)}) %collective-permute-start.12) | collective-permute-done | bytes 786464 | tf_op jit(solution)/shard_map/ppermute | solution.py:46
  75.8 1.0 add.46
  76.7 12.6 %all-to-all-start = ((f32[32,24,256]{2,1,0:T(8,128)}), f32[32,24,256]{2,1,0:T(8,128)}, u32[]{:S(2)}, u32[]{:S(2)}) async-start(f32[32,24,256]{2,1,0:T(8,128)} %bitcast.6), calls=%async_computation | async-start | bytes 1572864 | tf_op jit(solution)/shard_map/all_to_all | solution.py:407
  89.3 0.0 reduce-scatter.2.cloned.1.call-start
  89.4 0.1 multiply_reduce_fusion
  89.5 0.7 copy.12
  90.2 0.0 reduce-scatter.2.cloned.1.call-update
  90.3 1.3 collective-permute-start.13
  91.6 0.6 collective-permute-start.14
  92.2 0.4 collective-permute-start.15
  92.7 4.9 %collective-permute-done.13.g1 = f32[2,8,2,16,128]{4,3,2,1,0:T(8,128)S(1)} collective-permute-done((f32[2,8,2,16,128]{4,3,2,1,0:T(8,128)}, f32[2,8,2,16,128]{4,3,2,1,0:T(8,128)S(1)}, u32[]{:S(2)}, u32[]{:S(2)}) %collective-permute-start.13) | collective-permute-done | bytes 262176 | tf_op jit(solution)/shard_map/ppermute | solution.py:42
  97.5 2.4 %collective-permute-done.14.g2 = f32[2,8,2,16,128]{4,3,2,1,0:T(8,128)S(1)} collective-permute-done((f32[2,8,2,16,128]{4,3,2,1,0:T(8,128)}, f32[2,8,2,16,128]{4,3,2,1,0:T(8,128)S(1)}, u32[]{:S(2)}, u32[]{:S(2)}) %collective-permute-start.14) | collective-permute-done | bytes 262176 | tf_op jit(solution)/shard_map/ppermute | solution.py:42
  99.9 7.9 %collective-permute-done.15.g3 = f32[2,8,2,16,128]{4,3,2,1,0:T(8,128)S(1)} collective-permute-done((f32[2,8,2,16,128]{4,3,2,1,0:T(8,128)}, f32[2,8,2,16,128]{4,3,2,1,0:T(8,128)S(1)}, u32[]{:S(2)}, u32[]{:S(2)}) %collective-permute-start.15) | collective-permute-done | bytes 262176 | tf_op jit(solution)/shard_map/ppermute | solution.py:42
  107.9 0.7 scatter.1
  108.6 4.3 %collective-permute-start.17 = (f32[13,2,16,128]{3,2,1,0:T(8,128)S(1)}, f32[13,2,16,128]{3,2,1,0:T(8,128)S(1)}, u32[]{:S(2)}, u32[]{:S(2)}) collective-permute-start(f32[13,2,16,128]{3,2,1,0:T(8,128)S(1)} %get-tuple-element.45), channel_id=1, source_target_pairs={{0,32},{4,36},{8,40},{12,44},{16,48},{20,52},{24,56},{28,60},{32,6... | collective-permute-start | bytes 638984 | tf_op jit(solution)/shard_map/ppermute | solution.py:38
  112.9 0.9 collective-permute-start.16
  113.8 1.8 %collective-permute-start.18 = (f32[4,2,16,128]{3,2,1,0:T(8,128)S(1)}, f32[4,2,16,128]{3,2,1,0:T(8,128)S(1)}, u32[]{:S(2)}, u32[]{:S(2)}) collective-permute-start(f32[4,2,16,128]{3,2,1,0:T(8,128)S(1)} %get-tuple-element.46), channel_id=1, source_target_pairs={{0,36},{4,40},{8,44},{12,48},{16,52},{20,56},{24,60},{28,64},{32,6... | collective-permute-start | bytes 196616 | tf_op jit(solution)/shard_map/ppermute | solution.py:38
  115.6 1.2 reduce_sum.18
  116.8 12.1 %collective-permute-done.18.corner = f32[4,2,16,128]{3,2,1,0:T(8,128)S(1)} collective-permute-done((f32[4,2,16,128]{3,2,1,0:T(8,128)S(1)}, f32[4,2,16,128]{3,2,1,0:T(8,128)S(1)}, u32[]{:S(2)}, u32[]{:S(2)}) %collective-permute-start.18) | collective-permute-done | bytes 65568 | tf_op jit(solution)/shard_map/ppermute | solution.py:38
  128.9 0.9 broadcast_in_dim.2
  129.8 2.0 %update.1.n0 = f32[24,2,16,128]{3,2,1,0:T(8,128)S(1)} custom-call(s32[8]{0:T(128)S(1)} %stack.15.info, f32[24,2,64,128]{3,2,1,0:T(8,128)S(1)} %copy-done.1, f32[24,2,16,128]{3,2,1,0:T(8,128)S(1)} %get-tuple-element.48.own, f32[7,2,16,128]{3,2,1,0:T(8,128)S(1)} %collective-permute-done.16.right, f32[13,2,16,128]{3,2,1,0:T(8,128)S(1)} %collective-permute-done.17.low, ...), custom_call_target="tpu_custom_call" | custom-call | flops 1000000 | bytes 2000000 | tf_op jit(solution)/shard_map/update/pallas_call | solution.py:311
  131.9 7.0 %all-to-all-start.1 = ((f32[32,24,256]{2,1,0:T(8,128)}), f32[32,24,256]{2,1,0:T(8,128)S(1)}, u32[]{:S(2)}, u32[]{:S(2)}) async-start(f32[32,24,256]{2,1,0:T(8,128)} %broadcast_in_dim.2), calls=%async_computation.2 | async-start | bytes 1572864 | tf_op jit(solution)/shard_map/all_to_all | solution.py:407
  138.9 0.1 collective-permute-start.19
  139.0 0.2 collective-permute-start.20
  139.2 1.2 collective-permute-start.21
  140.5 8.8 %collective-permute-done.19.n1 = f32[24,2,16,128]{3,2,1,0:T(8,128)S(1)} collective-permute-done((f32[24,2,16,128]{3,2,1,0:T(8,128)S(1)}, f32[24,2,16,128]{3,2,1,0:T(8,128)S(1)}, u32[]{:S(2)}, u32[]{:S(2)}) %collective-permute-start.19) | collective-permute-done | bytes 393248 | tf_op jit(solution)/shard_map/ppermute | solution.py:42
  149.2 1.6 collective-permute-done.20.n2
  150.9 9.2 %collective-permute-done.21.n3 = f32[24,2,16,128]{3,2,1,0:T(8,128)S(1)} collective-permute-done((f32[24,2,16,128]{3,2,1,0:T(8,128)S(1)}, f32[24,2,16,128]{3,2,1,0:T(8,128)S(1)}, u32[]{:S(2)}, u32[]{:S(2)}) %collective-permute-start.21) | collective-permute-done | bytes 393248 | tf_op jit(solution)/shard_map/ppermute | solution.py:42
  160.1 2.2 %all-to-all-done.1 = f32[32,24,256]{2,1,0:T(8,128)S(1)} async-done(((f32[32,24,256]{2,1,0:T(8,128)}), f32[32,24,256]{2,1,0:T(8,128)S(1)}, u32[]{:S(2)}, u32[]{:S(2)}) %all-to-all-start.1) | async-done | bytes 786464 | tf_op jit(solution)/shard_map/all_to_all | solution.py:407
  162.3 0.7 collective-permute-start.22
  163.0 1.7 join_pieces.1
  164.7 0.2 collective-permute-done.22.theirs
  164.9 1.7 join_channels.1
  (33 shorter events, 0.1 us)
Async XLA Ops:
  7.2 1.1 slice-start
  7.2 11.7 %copy-start.6 = (s32[2,2]{1,0:T(2,128)S(1)}, s32[2,2]{1,0:T(2,128)}, u32[]{:S(2)}) copy-start(s32[2,2]{1,0:T(2,128)} %param.9) | copy-start | bytes 52
  7.2 34.2 %copy-start = (f32[3,2,256,256]{3,2,1,0:T(8,128)S(1)}, f32[3,2,256,256]{3,2,1,0:T(8,128)}, u32[]{:S(2)}) copy-start(f32[3,2,256,256]{3,2,1,0:T(8,128)} %probe.3) | copy-start | bytes 4718596
  8.3 18.1 %collective-permute-start.1 = (f32[12,2,16,128]{3,2,1,0:T(8,128)S(1)}, f32[12,2,16,128]{3,2,1,0:T(8,128)S(1)}, u32[]{:S(2)}, u32[]{:S(2)}) collective-permute-start(f32[12,2,16,128]{3,2,1,0:T(8,128)S(1)} %constant_dynamic-slice_fusion), channel_id=1, source_target_pairs={{0,224},{4,228},{8,232},{12,236},{16,240},{20,244},{24,248},{28,25... | collective-permute-start | bytes 589832 | tf_op jit(solution)/shard_map/ppermute | solution.py:38
  16.9 9.6 %collective-permute-start.2 = (f32[3,2,16,128]{3,2,1,0:T(8,128)S(1)}, f32[3,2,16,128]{3,2,1,0:T(8,128)S(1)}, u32[]{:S(2)}, u32[]{:S(2)}) collective-permute-start(f32[3,2,16,128]{3,2,1,0:T(8,128)S(1)} %slice.35), channel_id=1, source_target_pairs={{0,220},{4,224},{8,228},{12,232},{16,236},{20,240},{24,244},{28,24... | collective-permute-start | bytes 147464 | tf_op jit(solution)/shard_map/ppermute | solution.py:38
  18.5 14.7 %collective-permute-start = (f32[6,2,64,128]{3,2,1,0:T(8,128)S(1)}, f32[6,2,64,128]{3,2,1,0:T(8,128)S(1)}, u32[]{:S(2)}, u32[]{:S(2)}) collective-permute-start(f32[6,2,64,128]{3,2,1,0:T(8,128)S(1)} %slice_bitcast_fusion), channel_id=1, source_target_pairs={{0,252},{4,0},{8,4},{12,8},{16,12},{20,16},{24,20},{28,24},{32,28}... | collective-permute-start | bytes 1179656 | tf_op jit(solution)/shard_map/ppermute | solution.py:38
  26.5 15.0 %copy-start.5 = (f32[15,2,16,128]{3,2,1,0:T(8,128)}, f32[15,2,16,128]{3,2,1,0:T(8,128)S(1)}, u32[]{:S(2)}) copy-start(f32[15,2,16,128]{3,2,1,0:T(8,128)S(1)} %pad_maximum_fusion.b0) | copy-start | bytes 737284
  26.5 6.8 %collective-permute-start.3 = (f32[15,2,16,128]{3,2,1,0:T(8,128)S(1)}, f32[15,2,16,128]{3,2,1,0:T(8,128)S(1)}, u32[]{:S(2)}, u32[]{:S(2)}) collective-permute-start(f32[15,2,16,128]{3,2,1,0:T(8,128)S(1)} %pad_maximum_fusion.b0), channel_id=1, source_target_pairs={{0,1},{1,2},{2,3},{3,0},{4,5},{5,6},{6,7},{7,4},{8,9},{9,10},{10,1... | collective-permute-start | bytes 737288 | tf_op jit(solution)/shard_map/ppermute | solution.py:42
  26.7 7.7 %collective-permute-start.4 = (f32[15,2,16,128]{3,2,1,0:T(8,128)S(1)}, f32[15,2,16,128]{3,2,1,0:T(8,128)S(1)}, u32[]{:S(2)}, u32[]{:S(2)}) collective-permute-start(f32[15,2,16,128]{3,2,1,0:T(8,128)S(1)} %pad_maximum_fusion.b0), channel_id=1, source_target_pairs={{0,2},{1,3},{2,0},{3,1},{4,6},{5,7},{6,4},{7,5},{8,10},{9,11},{10,... | collective-permute-start | bytes 737288 | tf_op jit(solution)/shard_map/ppermute | solution.py:42
  28.9 12.5 %collective-permute-start.5 = (f32[15,2,16,128]{3,2,1,0:T(8,128)S(1)}, f32[15,2,16,128]{3,2,1,0:T(8,128)}, u32[]{:S(2)}, u32[]{:S(2)}) collective-permute-start(f32[15,2,16,128]{3,2,1,0:T(8,128)S(1)} %pad_maximum_fusion.b0), channel_id=1, source_target_pairs={{0,3},{1,0},{2,1},{3,2},{4,7},{5,4},{6,5},{7,6},{8,11},{9,8},{10,9... | collective-permute-start | bytes 737288 | tf_op jit(solution)/shard_map/ppermute | solution.py:42
  33.2 1.2 copy-start.7
  33.3 1.2 copy-start.8
  34.5 0.7 copy-start.9
  48.0 4.5 %collective-permute-start.6 = (f32[2,64,256]{2,1,0:T(8,128)S(1)}, f32[2,64,256]{2,1,0:T(8,128)S(1)}, u32[]{:S(2)}, u32[]{:S(2)}) collective-permute-start(f32[2,64,256]{2,1,0:T(8,128)S(1)} %get-tuple-element.35), channel_id=1, source_target_pairs={{0,1},{1,2},{2,3},{3,0},{4,5},{5,6},{6,7},{7,4},{8,9},{9,10},{10,1... | collective-permute-start | bytes 393224 | tf_op jit(solution)/shard_map/ppermute | solution.py:42
  48.1 5.5 %collective-permute-start.7 = (f32[2,64,256]{2,1,0:T(8,128)S(1)}, f32[2,64,256]{2,1,0:T(8,128)S(1)}, u32[]{:S(2)}, u32[]{:S(2)}) collective-permute-start(f32[2,64,256]{2,1,0:T(8,128)S(1)} %get-tuple-element.36), channel_id=1, source_target_pairs={{0,2},{1,3},{2,0},{3,1},{4,6},{5,7},{6,4},{7,5},{8,10},{9,11},{10,... | collective-permute-start | bytes 393224 | tf_op jit(solution)/shard_map/ppermute | solution.py:42
  49.0 6.5 %collective-permute-start.8 = (f32[2,64,256]{2,1,0:T(8,128)S(1)}, f32[2,64,256]{2,1,0:T(8,128)S(1)}, u32[]{:S(2)}, u32[]{:S(2)}) collective-permute-start(f32[2,64,256]{2,1,0:T(8,128)S(1)} %get-tuple-element.37), channel_id=1, source_target_pairs={{0,3},{1,0},{2,1},{3,2},{4,7},{5,4},{6,5},{7,6},{8,11},{9,8},{10,9... | collective-permute-start | bytes 393224 | tf_op jit(solution)/shard_map/ppermute | solution.py:42
  56.4 5.5 %collective-permute-start.10 = (f32[2,64,256]{2,1,0:T(8,128)S(1)}, f32[2,64,256]{2,1,0:T(8,128)S(1)}, u32[]{:S(2)}, u32[]{:S(2)}) collective-permute-start(f32[2,64,256]{2,1,0:T(8,128)S(1)} %add_multiply_fusion.f0), channel_id=1, source_target_pairs={{0,2},{1,3},{2,0},{3,1},{4,6},{5,7},{6,4},{7,5},{8,10},{9,11},{10,... | collective-permute-start | bytes 393224 | tf_op jit(solution)/shard_map/ppermute | solution.py:42
  56.9 6.3 %collective-permute-start.11 = (f32[2,64,256]{2,1,0:T(8,128)S(1)}, f32[2,64,256]{2,1,0:T(8,128)S(1)}, u32[]{:S(2)}, u32[]{:S(2)}) collective-permute-start(f32[2,64,256]{2,1,0:T(8,128)S(1)} %add_multiply_fusion.f0), channel_id=1, source_target_pairs={{0,3},{1,0},{2,1},{3,2},{4,7},{5,4},{6,5},{7,6},{8,11},{9,8},{10,9... | collective-permute-start | bytes 393224 | tf_op jit(solution)/shard_map/ppermute | solution.py:42
  59.3 4.8 %collective-permute-start.9 = (f32[2,64,256]{2,1,0:T(8,128)S(1)}, f32[2,64,256]{2,1,0:T(8,128)S(1)}, u32[]{:S(2)}, u32[]{:S(2)}) collective-permute-start(f32[2,64,256]{2,1,0:T(8,128)S(1)} %add_multiply_fusion.f0), channel_id=1, source_target_pairs={{0,1},{1,2},{2,3},{3,0},{4,5},{5,6},{6,7},{7,4},{8,9},{9,10},{10,1... | collective-permute-start | bytes 393224 | tf_op jit(solution)/shard_map/ppermute | solution.py:42
  70.2 6.6 %copy-start.2 = (f32[2,8,2,16,128]{4,3,2,1,0:T(8,128)}, f32[2,8,2,16,128]{4,3,2,1,0:T(8,128)S(1)}, u32[]{:S(2)}) copy-start(f32[2,8,2,16,128]{4,3,2,1,0:T(8,128)S(1)} %get-tuple-element.43) | copy-start | bytes 786436
  70.2 6.6 %copy-start.3 = (f32[2,8,2,16,128]{4,3,2,1,0:T(8,128)}, f32[2,8,2,16,128]{4,3,2,1,0:T(8,128)S(1)}, u32[]{:S(2)}) copy-start(f32[2,8,2,16,128]{4,3,2,1,0:T(8,128)S(1)} %get-tuple-element.42) | copy-start | bytes 786436
  70.2 6.6 %copy-start.4 = (f32[2,8,2,16,128]{4,3,2,1,0:T(8,128)}, f32[2,8,2,16,128]{4,3,2,1,0:T(8,128)S(1)}, u32[]{:S(2)}) copy-start(f32[2,8,2,16,128]{4,3,2,1,0:T(8,128)S(1)} %get-tuple-element.41) | copy-start | bytes 786436
  70.2 5.6 %collective-permute-start.12 = (f32[3,256,256]{2,1,0:T(8,128)S(1)}, f32[3,256,256]{2,1,0:T(8,128)S(1)}, u32[]{:S(2)}, u32[]{:S(2)}) collective-permute-start(f32[3,256,256]{2,1,0:T(8,128)S(1)} %get-tuple-element.39), channel_id=1, source_target_pairs={{0,4},{4,0},{8,12},{12,8},{16,20},{20,16},{24,28},{28,24},{32,36},... | collective-permute-start | bytes 2359304 | tf_op jit(solution)/shard_map/ppermute | solution.py:46
  76.7 38.9 %all-to-all-start = ((f32[32,24,256]{2,1,0:T(8,128)}), f32[32,24,256]{2,1,0:T(8,128)}, u32[]{:S(2)}, u32[]{:S(2)}) async-start(f32[32,24,256]{2,1,0:T(8,128)} %bitcast.6), calls=%async_computation | async-start | bytes 1572864 | tf_op jit(solution)/shard_map/all_to_all | solution.py:407
  89.3 40.5 %reduce-scatter.2.cloned.1.call-start = ((), (), s32[]{:S(2)}) async-start(), calls=%async_computation.3 | async-start | bytes 327680 | tf_op jit(solution)/shard_map/reduce_scatter | solution.py:392
  90.2 39.6 %copy-start.1 = (f32[24,2,64,128]{3,2,1,0:T(8,128)S(1)}, f32[24,2,64,128]{3,2,1,0:T(8,128)}, u32[]{:S(2)}) copy-start(f32[24,2,64,128]{3,2,1,0:T(8,128)} %pieces.1) | copy-start | bytes 4718596
  90.3 7.3 %collective-permute-start.13 = (f32[2,8,2,16,128]{4,3,2,1,0:T(8,128)}, f32[2,8,2,16,128]{4,3,2,1,0:T(8,128)S(1)}, u32[]{:S(2)}, u32[]{:S(2)}) collective-permute-start(f32[2,8,2,16,128]{4,3,2,1,0:T(8,128)} %copy-done.4), channel_id=1, source_target_pairs={{0,1},{1,2},{2,3},{3,0},{4,5},{5,6},{6,7},{7,4},{8,9},{9,10},{10,1... | collective-permute-start | bytes 786440 | tf_op jit(solution)/shard_map/ppermute | solution.py:42
  91.6 8.3 %collective-permute-start.14 = (f32[2,8,2,16,128]{4,3,2,1,0:T(8,128)}, f32[2,8,2,16,128]{4,3,2,1,0:T(8,128)S(1)}, u32[]{:S(2)}, u32[]{:S(2)}) collective-permute-start(f32[2,8,2,16,128]{4,3,2,1,0:T(8,128)} %copy-done.3), channel_id=1, source_target_pairs={{0,2},{1,3},{2,0},{3,1},{4,6},{5,7},{6,4},{7,5},{8,10},{9,11},{10,... | collective-permute-start | bytes 786440 | tf_op jit(solution)/shard_map/ppermute | solution.py:42
  92.2 15.6 %collective-permute-start.15 = (f32[2,8,2,16,128]{4,3,2,1,0:T(8,128)}, f32[2,8,2,16,128]{4,3,2,1,0:T(8,128)S(1)}, u32[]{:S(2)}, u32[]{:S(2)}) collective-permute-start(f32[2,8,2,16,128]{4,3,2,1,0:T(8,128)} %copy-done.2), channel_id=1, source_target_pairs={{0,3},{1,0},{2,1},{3,2},{4,7},{5,4},{6,5},{7,6},{8,11},{9,8},{10,9... | collective-permute-start | bytes 786440 | tf_op jit(solution)/shard_map/ppermute | solution.py:42
  108.6 20.3 %collective-permute-start.17 = (f32[13,2,16,128]{3,2,1,0:T(8,128)S(1)}, f32[13,2,16,128]{3,2,1,0:T(8,128)S(1)}, u32[]{:S(2)}, u32[]{:S(2)}) collective-permute-start(f32[13,2,16,128]{3,2,1,0:T(8,128)S(1)} %get-tuple-element.45), channel_id=1, source_target_pairs={{0,32},{4,36},{8,40},{12,44},{16,48},{20,52},{24,56},{28,60},{32,6... | collective-permute-start | bytes 638984 | tf_op jit(solution)/shard_map/ppermute | solution.py:38
  112.9 16.0 %collective-permute-start.16 = (f32[7,2,16,128]{3,2,1,0:T(8,128)S(1)}, f32[7,2,16,128]{3,2,1,0:T(8,128)S(1)}, u32[]{:S(2)}, u32[]{:S(2)}) collective-permute-start(f32[7,2,16,128]{3,2,1,0:T(8,128)S(1)} %get-tuple-element.44), channel_id=1, source_target_pairs={{0,4},{4,8},{8,12},{12,16},{16,20},{20,24},{24,28},{28,32},{32,36}... | collective-permute-start | bytes 344072 | tf_op jit(solution)/shard_map/ppermute | solution.py:38
  113.8 15.1 %collective-permute-start.18 = (f32[4,2,16,128]{3,2,1,0:T(8,128)S(1)}, f32[4,2,16,128]{3,2,1,0:T(8,128)S(1)}, u32[]{:S(2)}, u32[]{:S(2)}) collective-permute-start(f32[4,2,16,128]{3,2,1,0:T(8,128)S(1)} %get-tuple-element.46), channel_id=1, source_target_pairs={{0,36},{4,40},{8,44},{12,48},{16,52},{20,56},{24,60},{28,64},{32,6... | collective-permute-start | bytes 196616 | tf_op jit(solution)/shard_map/ppermute | solution.py:38
  131.9 30.4 %all-to-all-start.1 = ((f32[32,24,256]{2,1,0:T(8,128)}), f32[32,24,256]{2,1,0:T(8,128)S(1)}, u32[]{:S(2)}, u32[]{:S(2)}) async-start(f32[32,24,256]{2,1,0:T(8,128)} %broadcast_in_dim.2), calls=%async_computation.2 | async-start | bytes 1572864 | tf_op jit(solution)/shard_map/all_to_all | solution.py:407
  138.9 10.3 %collective-permute-start.19 = (f32[24,2,16,128]{3,2,1,0:T(8,128)S(1)}, f32[24,2,16,128]{3,2,1,0:T(8,128)S(1)}, u32[]{:S(2)}, u32[]{:S(2)}) collective-permute-start(f32[24,2,16,128]{3,2,1,0:T(8,128)S(1)} %update.1.n0), channel_id=1, source_target_pairs={{0,1},{1,2},{2,3},{3,0},{4,5},{5,6},{6,7},{7,4},{8,9},{9,10},{10,1... | collective-permute-start | bytes 1179656 | tf_op jit(solution)/shard_map/ppermute | solution.py:42
  139.0 11.9 %collective-permute-start.20 = (f32[24,2,16,128]{3,2,1,0:T(8,128)S(1)}, f32[24,2,16,128]{3,2,1,0:T(8,128)S(1)}, u32[]{:S(2)}, u32[]{:S(2)}) collective-permute-start(f32[24,2,16,128]{3,2,1,0:T(8,128)S(1)} %update.1.n0), channel_id=1, source_target_pairs={{0,2},{1,3},{2,0},{3,1},{4,6},{5,7},{6,4},{7,5},{8,10},{9,11},{10,... | collective-permute-start | bytes 1179656 | tf_op jit(solution)/shard_map/ppermute | solution.py:42
  139.2 20.8 %collective-permute-start.21 = (f32[24,2,16,128]{3,2,1,0:T(8,128)S(1)}, f32[24,2,16,128]{3,2,1,0:T(8,128)S(1)}, u32[]{:S(2)}, u32[]{:S(2)}) collective-permute-start(f32[24,2,16,128]{3,2,1,0:T(8,128)S(1)} %update.1.n0), channel_id=1, source_target_pairs={{0,3},{1,0},{2,1},{3,2},{4,7},{5,4},{6,5},{7,6},{8,11},{9,8},{10,9... | collective-permute-start | bytes 1179656 | tf_op jit(solution)/shard_map/ppermute | solution.py:42
  162.3 2.6 %collective-permute-start.22 = (f32[3,256,256]{2,1,0:T(8,128)S(1)}, f32[3,256,256]{2,1,0:T(8,128)S(1)}, u32[]{:S(2)}, u32[]{:S(2)}) collective-permute-start(f32[3,256,256]{2,1,0:T(8,128)S(1)} %bitcast.18), channel_id=1, source_target_pairs={{0,4},{4,0},{8,12},{12,8},{16,20},{20,16},{24,28},{28,24},{32,36},... | collective-permute-start | bytes 2359304 | tf_op jit(solution)/shard_map/ppermute | solution.py:46
Sparse Core Ops, SparseCore 0:
  92.7 21.2 reduce-scatter.1
